TPU v7x, 32 devices: a whole 2x2x4 slice. The times are simulated.
32 devices in a mesh: rep: 2 (over y), tp: 8 (over z, x), dp: 2 (over core).
Axes of the slice: x: 2, y: 2, z: 4, core: 2. Of those that a mesh axis runs over, the one named last changes fastest.
Arguments:
- state_hidden: bfloat16 [8, 8192], P(('rep', 'dp'), 'tp'), parts along dimension 0, may hold values from -40 to 40
- action_seeds: int32 [8, 64], P(('rep', 'dp')), parts along dimension 0, may hold values from 0 to 65520
- action_mean: float32 [256], P('rep'), parts along dimension 0, may hold values from -4 to 4
- action_spread: float32 [256], P('rep'), parts along dimension 0, may hold values from 0.5 to 2
- action_weight: bfloat16 [128, 8192], P(None, 'tp'), may hold values from -0.5 to 0.5
- norm_gain: float32 [8192], P('tp'), may hold values from 0.1 to 1.9
- gate_weight: bfloat16 [8192, 24576], P('dp', 'tp'), may hold values from -0.0625 to 0.0625
- up_weight: bfloat16 [8192, 24576], P('dp', 'tp'), may hold values from -0.0625 to 0.0625
- down_weight: bfloat16 [24576, 8192], P('tp', 'dp'), may hold values from -0.0546875 to 0.0546875
- head_gain: float32 [8192], P('tp'), may hold values from 0.1 to 1.9
- value_weight: float32 [8192], P('tp'), may hold values from -0.0625 to 0.0625
Outputs:
- output_rows: bfloat16 [8, 64, 8192], P(('rep', 'dp'), None, 'tp'), parts along dimension 0
- values: float32 [8, 64], P(('rep', 'dp')), parts along dimension 0
There are 2 independent parts, one for each index of `rep`. A program takes and returns all parts, laid end to end along the dimension named above; an argument that names none is the same for every part. Nothing has to cross between parts.
All inputs are finite; a program needn't handle non-finite values.
Results may differ from a plain program's by a relative error of at most 0.014.
Values may be sent and summed in bfloat16 or wider, within the bound.
No kernel may reach another device: no remote copies, remote signals or barrier semaphores. Data moves between devices by JAX's collectives and lax.ppermute only.
A program may use at most 448 MiB of HBM per device.

v0:
```python
import math

import jax
import jax.numpy as jnp
from jax import lax
from jax.sharding import PartitionSpec as P

epsilon = 1e-05
modulus = 251


def action_features(action_seeds, action_mean, action_spread):
    harmonic = jnp.arange(1, action_mean.shape[0] + 1, dtype=jnp.int32)
    phases = action_seeds[:, :, None] * harmonic % modulus
    angles = phases.astype(jnp.float32) * (2.0 * math.pi / modulus)
    return (action_mean + action_spread * jnp.cos(angles)).astype(jnp.bfloat16)


def head_value(output_rows, head_gain, value_weight):
    wide_out = output_rows.astype(jnp.float32)
    scale = lax.rsqrt(jnp.mean(wide_out * wide_out, axis=1) + epsilon)
    return jnp.sum(wide_out * (head_gain * value_weight), axis=1) * scale


def local(
    state_hidden,
    action_seeds,
    action_mean,
    action_spread,
    action_weight,
    norm_gain,
    gate_weight,
    up_weight,
    down_weight,
    head_gain,
    value_weight,
):
    state_count, cand_count = action_seeds.shape
    row_count = state_count * cand_count
    local_cols = action_weight.shape[1]
    features = action_features(action_seeds, action_mean, action_spread)
    embedded = jnp.dot(
        features.reshape(row_count, features.shape[2]),
        action_weight,
        preferred_element_type=jnp.float32,
    )
    inputs_local = (
        (
            state_hidden.astype(jnp.float32)[:, None, :]
            + embedded.reshape(state_count, cand_count, local_cols)
        )
        .reshape(row_count, local_cols)
        .astype(jnp.bfloat16)
    )
    gathered, gain_full = (
        lax.all_gather(inputs_local, "tp", axis=1, tiled=True),
        lax.all_gather(norm_gain.astype(jnp.bfloat16), "tp", axis=0, tiled=True).astype(
            norm_gain.dtype
        ),
    )
    scale = lax.rsqrt(
        jnp.mean(jnp.square(gathered.astype(jnp.float32)), axis=1, keepdims=True) + epsilon
    )
    normed = (gathered.astype(jnp.float32) * scale * gain_full).astype(jnp.bfloat16)
    gate_sum = jnp.dot(
        normed,
        lax.all_gather(gate_weight, "dp", axis=0, tiled=True),
        preferred_element_type=jnp.float32,
    )
    up_sum = jnp.dot(
        normed,
        lax.all_gather(up_weight, "dp", axis=0, tiled=True),
        preferred_element_type=jnp.float32,
    )
    hidden = (jax.nn.silu(gate_sum) * up_sum).astype(jnp.bfloat16)
    partial_terms = jnp.dot(
        hidden,
        lax.all_gather(down_weight, "dp", axis=1, tiled=True),
        preferred_element_type=jnp.float32,
    )
    summed_local = lax.psum_scatter(partial_terms, "tp", scatter_dimension=1, tiled=True)
    output_local = (inputs_local.astype(jnp.float32) + summed_local).astype(jnp.bfloat16)
    output_full, head_full, value_full = (
        lax.all_gather(output_local, "tp", axis=1, tiled=True),
        lax.all_gather(head_gain.astype(jnp.bfloat16), "tp", axis=0, tiled=True).astype(
            head_gain.dtype
        ),
        lax.all_gather(value_weight.astype(jnp.bfloat16), "tp", axis=0, tiled=True).astype(
            value_weight.dtype
        ),
    )
    values = head_value(output_full, head_full, value_full)
    return (
        output_local.reshape(state_count, cand_count, local_cols),
        values.reshape(state_count, cand_count),
    )


def solution(mesh):
    return jax.shard_map(
        local,
        mesh=mesh,
        in_specs=(
            P(("rep", "dp"), "tp"),
            P(("rep", "dp"), None),
            P("rep"),
            P("rep"),
            P(None, "tp"),
            P("tp"),
            P("dp", "tp"),
            P("dp", "tp"),
            P("tp", "dp"),
            P("tp"),
            P("tp"),
        ),
        out_specs=(P(("rep", "dp"), None, "tp"), P(("rep", "dp"), None)),
        check_vma=False,
    )
```

profile of v0, /device:TPU:0, one launch (start us, length us, event | category | flops | bytes accessed | tf_op | source)
XLA Modules:
  0.0 462.0 jit_solution(15725198353235282980)
XLA Ops:
  7.2 0.0 all-gather.6.cloned.1.call-start
  7.2 0.7 convert_element_type.56
  8.0 0.2 copy-done
  8.1 1.9 fusion.12
  10.0 0.0 all-gather.6.cloned.1.call-update
  10.1 0.0 all-gather.8.cloned.1.call-start
  10.1 0.7 all-gather.8.cloned.1.call-update
  10.8 0.0 all-gather.10.cloned.1.call-start
  10.9 0.7 all-gather.10.cloned.1.call-update
  11.6 0.0 all-gather.12.cloned.1.call-start
  11.6 0.5 all-gather.12.cloned.1.call-update
  12.1 0.0 reduce-scatter.2.cloned.1.call-start
  12.2 0.1 copy-done.4
  12.2 27.9 %all_gather.25 = bf16[8192]{0:T(1024)(128)(2,1)S(1)} all-gather(bf16[1024]{0:T(1024)(128)(2,1)S(1)} %convert_element_type.63), channel_id=1, replica_groups=mesh['rep'=2,'tp'=8,'dp'=2] {'tp'}, dimensions={0}, use_global_device_ids=true | all-gather | bytes 18432 | tf_op jit(solution)/shard_map/all_gather | solution.py:57
  40.2 22.6 %all-gather.6.cloned.1.call-done = bf16[128,8192]{1,0:T(8,128)(2,1)} async-done(((bf16[128,1024]{1,0:T(8,128)(2,1)}), bf16[128,8192]{1,0:T(8,128)(2,1)}) %all-gather.6.cloned.1.call-update) | async-done | bytes 2097168 | tf_op jit(solution)/shard_map/all_gather | solution.py:56
  62.8 2.1 fusion
  64.9 71.1 %all-gather.8.cloned.1.call-done = bf16[8192,3072]{1,0:T(8,128)(2,1)} async-done(((bf16[4096,3072]{1,0:T(8,128)(2,1)}), bf16[8192,3072]{1,0:T(8,128)(2,1)}) %all-gather.8.cloned.1.call-update) | async-done | bytes 50331664 | tf_op jit(solution)/shard_map/all_gather | solution.py:67
  136.1 29.1 %fusion.16 = f32[128,3072]{1,0:T(8,128)} fusion(bf16[8192,3072]{1,0:T(8,128)(2,1)} %all-gather.8.cloned.1.call-done, bf16[128,8192]{1,0:T(8,128)(2,1)} %all-gather.6.cloned.1.call-done, f32[8192]{0:T(1024)S(1)} %convert_element_type.64, f32[128]{0:T(128)S(1)} %add_rsqrt_fusion), kind=kOutput, calls=%fused_computation.20 | convolution fusion | flops 6446645248 | bytes 54034944 | tf_op jit(solution)/shard_map/dot_general | solution.py:65
  165.2 46.8 %all-gather.10.cloned.1.call-done = bf16[8192,3072]{1,0:T(8,128)(2,1)} async-done(((bf16[4096,3072]{1,0:T(8,128)(2,1)}), bf16[8192,3072]{1,0:T(8,128)(2,1)}) %all-gather.10.cloned.1.call-update) | async-done | bytes 50331664 | tf_op jit(solution)/shard_map/all_gather | solution.py:72
  212.0 26.6 %fusion.5.clone.4 = bf16[128,3072]{1,0:T(8,128)(2,1)S(1)} fusion(bf16[8192,3072]{1,0:T(8,128)(2,1)} %all-gather.10.cloned.1.call-done, f32[128,3072]{1,0:T(8,128)} %fusion.16, bf16[128,8192]{1,0:T(8,128)(2,1)S(1)} %copy-done.2, f32[8192]{0:T(1024)S(1)} %convert_element_type.64, f32[128]{0:T(128)S(1)} %add_rsqrt_fusion), kind=kOutput, calls=%fused_computation.10.clone.clone.clone.1 | convolution fusion | flops 6449004544 | bytes 54821376 | tf_op jit(solution)/shard_map/dot_general | solution.py:70
  238.6 49.1 %all-gather.12.cloned.1.call-done = bf16[3072,8192]{1,0:T(8,128)(2,1)} async-done(((bf16[3072,4096]{1,0:T(8,128)(2,1)}), bf16[3072,8192]{1,0:T(8,128)(2,1)}) %all-gather.12.cloned.1.call-update) | async-done | bytes 50331664 | tf_op jit(solution)/shard_map/all_gather | solution.py:78
  287.8 20.1 %fusion.6 = f32[128,8192]{1,0:T(8,128)} fusion(bf16[3072,8192]{1,0:T(8,128)(2,1)} %all-gather.12.cloned.1.call-done, bf16[128,3072]{1,0:T(8,128)(2,1)S(1)} %fusion.5.clone.4), kind=kOutput, calls=%fused_computation.11 | convolution fusion | flops 6442450944 | bytes 55312384 | tf_op jit(solution)/shard_map/dot_general | solution.py:76
  307.8 0.0 reduce-scatter.2.cloned.1.call-update
  307.9 0.0 all-gather.14.cloned.1.call-start
  307.9 89.7 %reduce-scatter.2.cloned.1.call-done = f32[128,1024]{1,0:T(8,128)} async-done(((f32[128,8192]{1,0:T(8,128)}), f32[128,1024]{1,0:T(8,128)}) %reduce-scatter.2.cloned.1.call-update) | async-done | bytes 524304 | tf_op jit(solution)/shard_map/reduce_scatter | solution.py:81
  397.7 1.8 add_convert_fusion
  399.5 0.0 all-gather.14.cloned.1.call-update
  399.5 26.0 %all_gather.30 = bf16[8192]{0:T(1024)(128)(2,1)S(1)} all-gather(bf16[1024]{0:T(1024)(128)(2,1)S(1)} %convert_element_type.69), channel_id=1, replica_groups=mesh['rep'=2,'tp'=8,'dp'=2] {'tp'}, dimensions={0}, use_global_device_ids=true | all-gather | bytes 18432 | tf_op jit(solution)/shard_map/all_gather | solution.py:85
  425.6 26.4 %all_gather.31 = bf16[8192]{0:T(1024)(128)(2,1)S(1)} all-gather(bf16[1024]{0:T(1024)(128)(2,1)S(1)} %convert_element_type.71), channel_id=1, replica_groups=mesh['rep'=2,'tp'=8,'dp'=2] {'tp'}, dimensions={0}, use_global_device_ids=true | all-gather | bytes 18432 | tf_op jit(solution)/shard_map/all_gather | solution.py:88
  452.0 0.0 all-gather.14.cloned.1.call-done
  452.1 2.4 fusion.4
  454.5 0.7 mul.95
  (20 shorter events, 0.1 us)
Async XLA Ops:
  7.2 1.0 copy-start
  7.2 55.6 %all-gather.6.cloned.1.call-start = ((), (), s32[]{:S(2)}) async-start(), calls=%async_computation.1 | async-start | bytes 2359296 | tf_op jit(solution)/shard_map/all_gather | solution.py:56
  10.1 126.0 %all-gather.8.cloned.1.call-start = ((), (), s32[]{:S(2)}) async-start(), calls=%async_computation.2 | async-start | bytes 75497472 | tf_op jit(solution)/shard_map/all_gather | solution.py:67
  10.8 201.2 %all-gather.10.cloned.1.call-start = ((), (), s32[]{:S(2)}) async-start(), calls=%async_computation.3 | async-start | bytes 75497472 | tf_op jit(solution)/shard_map/all_gather | solution.py:72
  11.5 0.7 copy-start.4
  11.6 276.2 %all-gather.12.cloned.1.call-start = ((), (), s32[]{:S(2)}) async-start(), calls=%async_computation.4 | async-start | bytes 75497472 | tf_op jit(solution)/shard_map/all_gather | solution.py:78
  12.1 385.5 %reduce-scatter.2.cloned.1.call-start = ((), (), s32[]{:S(2)}) async-start(), calls=%async_computation.5 | async-start | bytes 4718592 | tf_op jit(solution)/shard_map/reduce_scatter | solution.py:81
  64.9 147.1 %copy-start.2 = (bf16[128,8192]{1,0:T(8,128)(2,1)S(1)}, bf16[128,8192]{1,0:T(8,128)(2,1)}, u32[]{:S(2)}) copy-start(bf16[128,8192]{1,0:T(8,128)(2,1)} %all-gather.6.cloned.1.call-done) | copy-start | bytes 6291460
  287.8 167.4 %copy-start.1 = (bf16[128,1024]{1,0:T(8,128)(2,1)S(1)}, bf16[128,1024]{1,0:T(8,128)(2,1)}, u32[]{:S(2)}) copy-start(bf16[128,1024]{1,0:T(8,128)(2,1)} %param.15) | copy-start | bytes 786436
  307.8 89.8 %copy-start.3 = (bf16[2,64,1024]{2,1,0:T(8,128)(2,1)S(1)}, bf16[2,64,1024]{2,1,0:T(8,128)(2,1)}, u32[]{:S(2)}) copy-start(bf16[2,64,1024]{2,1,0:T(8,128)(2,1)} %fusion.12) | copy-start | bytes 786436
  307.8 91.7 %copy-start.5 = (f32[1024]{0:T(1024)S(1)}, f32[1024]{0:T(1024)}, u32[]{:S(2)}) copy-start(f32[1024]{0:T(1024)} %param.20) | copy-start | bytes 12292
  307.8 91.7 %copy-start.6 = (f32[1024]{0:T(1024)S(1)}, f32[1024]{0:T(1024)}, u32[]{:S(2)}) copy-start(f32[1024]{0:T(1024)} %param.21) | copy-start | bytes 12292
  307.9 144.2 %all-gather.14.cloned.1.call-start = ((), (), s32[]{:S(2)}) async-start(), calls=%async_computation.6 | async-start | bytes 2359296 | tf_op jit(solution)/shard_map/all_gather | solution.py:84
Sparse Core Ops, SparseCore 0:
  10.8 52.0 all-gather.5
  64.4 71.6 all-gather.7
  137.6 74.3 all-gather.9
  213.4 74.3 all-gather.11
  308.0 89.6 reduce-scatter.1
  400.5 49.2 all-gather.13
where the time goes:
time: 462 us
  waiting for transfers between devices  281 us (61%)
  blocking collectives  80.4 us (17%)
  matrix products  77.7 us (17%)
  between operations  14.2 us (3%)
  other arithmetic  7.04 us (2%)
    reduce_scatter x1, waiting for transfers between devices, local(): lax.psum_scatter(partial_terms, 'tp', scatter_dimension=1, tiled=True)  89.7 us
    all_gather x1, waiting for transfers between devices, local(): lax.all_gather(gate_weight, 'dp', axis=0, tiled=True)  71.1 us
    all_gather x1, waiting for transfers between devices, local(): lax.all_gather(down_weight, 'dp', axis=1, tiled=True)  49.1 us
    all_gather x1, waiting for transfers between devices, local(): lax.all_gather(up_weight, 'dp', axis=0, tiled=True)  46.8 us
    dot_general x1, matrix products, local(): jnp.dot(normed, lax.all_gather(gate_weight, 'dp', axis=0, tiled=True), pr...  29.1 us
    all_gather x1, blocking collectives, local(): lax.all_gather(norm_gain.astype(jnp.bfloat16), 'tp', axis=0, tiled=True)  27.9 us
    dot_general x1, matrix products, local(): jnp.dot(normed, lax.all_gather(up_weight, 'dp', axis=0, tiled=True), pref...  26.6 us
    all_gather x1, blocking collectives, local(): lax.all_gather(value_weight.astype(jnp.bfloat16), 'tp', axis=0, tiled=True)  26.4 us
  transfers between devices with their start and end apart: 6, of which 5 were waited for; matrix products, arithmetic and copies ran while one was open for 13% of the time, Pallas kernels for 0%

commit v1 on v0

--- a/solution.py
+++ b/solution.py
@@ -7,6 +7,7 @@
 
 epsilon = 1e-05
 modulus = 251
+PAD = 8
 
 
 def action_features(action_seeds, action_mean, action_spread):
@@ -22,7 +23,7 @@
     return jnp.sum(wide_out * (head_gain * value_weight), axis=1) * scale
 
 
-def local(
+def local_gathered(
     state_hidden,
     action_seeds,
     action_mean,
@@ -96,7 +97,174 @@
     )
 
 
+RING = 8
+
+
+def chip_of(pos):
+    pos = pos % RING
+    z, x = (pos, 0) if pos < 4 else (7 - pos, 1)
+    return 2 * z + x
+
+
+def core_of(pos):
+    return chip_of(pos) // 4
+
+
+def send(array, pairs):
+    return lax.ppermute(
+        array, ("tp", "dp"), [(2 * st + sd, 2 * dt + dd) for (st, sd), (dt, dd) in pairs]
+    )
+
+
+def local_ring(
+    state_hidden,
+    action_seeds,
+    action_mean,
+    action_spread,
+    action_weight,
+    norm_gain,
+    gate_weight,
+    up_weight,
+    down_weight,
+    head_gain,
+    value_weight,
+):
+    f32, bf16 = jnp.float32, jnp.bfloat16
+    states, cands = action_seeds.shape
+    rows = states * cands
+    act, cols = action_weight.shape
+    half = act // 2
+    full_width = gate_weight.shape[0] * 2
+    tp, dp = lax.axis_index("tp"), lax.axis_index("dp")
+    z, x = tp // 2, tp % 2
+    swap_core = [((t, d), (t, 1 - d)) for t in range(8) for d in range(2)]
+    swap_x = [((t, d), (t ^ 1, d)) for t in range(8) for d in range(2)]
+
+    piece = jnp.concatenate(
+        [
+            lax.dynamic_slice_in_dim(action_weight, dp * half, half, 0),
+            state_hidden,
+            norm_gain.astype(bf16)[None],
+            jnp.zeros((PAD - states - 1, cols), bf16),
+        ],
+        axis=0,
+    )
+    own, across = [], []
+    for j in range(4):
+        pairs = []
+        for t in range(8):
+            for d in range(2):
+                zz, xx = t // 2, t % 2
+                to = (2 * (zz % 2) + d) ^ j
+                pairs.append(((t, d), (2 * to + xx, zz // 2)))
+        got = send(piece, pairs)
+        own.append(got)
+        across.append(send(got, swap_x))
+    own, across = jnp.stack(own), jnp.stack(across)
+    blocks = jnp.stack([jnp.where(x == 0, own, across), jnp.where(x == 0, across, own)])
+    order = jnp.stack([z ^ k for k in range(4)])
+    blocks = jnp.take(blocks, order, axis=1)
+    blocks = blocks.reshape(2, 2, 2, half + PAD, cols)
+    blocks = blocks.transpose(2, 3, 1, 0, 4).reshape(2, half + PAD, 4 * cols)
+    weight_half = blocks[:, :half].reshape(act, 4 * cols)
+    state_half = blocks[:, half : half + states].reshape(2 * states, 4 * cols)
+    gain_half = blocks[0, half + states]
+
+    features = action_features(action_seeds, action_mean, action_spread).reshape(rows, act)
+    other_features = send(features, swap_core)
+    all_features = jnp.where(
+        dp == 0,
+        jnp.concatenate([features, other_features]),
+        jnp.concatenate([other_features, features]),
+    )
+    row_state = jnp.arange(2 * rows) // cands
+    onehot = (row_state[:, None] == jnp.arange(PAD)[None]).astype(bf16)
+    wide_features = jnp.concatenate([all_features, onehot], axis=1)
+
+    basis = jnp.concatenate(
+        [weight_half, state_half, jnp.zeros((PAD - 2 * states, 4 * cols), bf16)]
+    )
+    lhs = (basis.astype(f32) * gain_half.astype(f32)[None]).astype(bf16)
+
+    gate_own = jnp.dot(lhs, gate_weight, preferred_element_type=f32)
+    gate_other = send(gate_own.astype(bf16), swap_core)
+    up_own = jnp.dot(lhs, up_weight, preferred_element_type=f32)
+    up_other = send(up_own.astype(bf16), swap_core)
+
+    inputs_half = jnp.dot(wide_features, basis, preferred_element_type=f32).astype(bf16)
+    squares = jnp.sum(jnp.square(inputs_half.astype(f32)), axis=1)
+    squares = squares + send(squares, swap_core)
+    scale = lax.rsqrt(squares / full_width + epsilon)[:, None]
+
+    gate_basis = (gate_own + gate_other.astype(f32)).astype(bf16)
+    up_basis = (up_own + up_other.astype(f32)).astype(bf16)
+    gate_sum = scale * jnp.dot(wide_features, gate_basis, preferred_element_type=f32)
+    up_sum = scale * jnp.dot(wide_features, up_basis, preferred_element_type=f32)
+    hidden = (jax.nn.silu(gate_sum) * up_sum).astype(bf16)
+
+    partial = jnp.dot(hidden, down_weight, preferred_element_type=f32).astype(bf16)
+
+    embedded = jnp.dot(features, action_weight, preferred_element_type=f32)
+    inputs_local = (
+        (state_hidden.astype(f32)[:, None, :] + embedded.reshape(states, cands, cols))
+        .reshape(rows, cols)
+        .astype(bf16)
+    )
+
+    pos = jnp.where(x == 0, z, 7 - z)
+
+    def share(to, part):
+        to = to % RING
+        chip = jnp.where(to < 4, 2 * to, 2 * (7 - to) + 1)
+        block = jnp.clip(chip - 4 * dp, 0, 3)
+        return lax.dynamic_slice(partial, (part * rows, block * cols), (rows, cols))
+
+    chains = [(1, 0, 4), (-1, 1, 4), (1, 1, 3), (-1, 0, 3)]
+    held = [None] * len(chains)
+    for step in range(4):
+        for index, (way, part, hops) in enumerate(chains):
+            at = step - (4 - hops)
+            if at < 0:
+                continue
+            left = hops - at
+            value = share(pos + way * left, part)
+            if held[index] is not None:
+                value = (value.astype(f32) + held[index].astype(f32)).astype(bf16)
+            pairs = []
+            for p in range(RING):
+                to = (p + way * left) % RING
+                core = core_of(to)
+                pairs.append(
+                    ((chip_of(p), core), (chip_of(p + way), part if left == 1 else core))
+                )
+            held[index] = send(value, pairs)
+    mine = z // 2 == dp
+    crossing = share(pos, 1 - dp)
+    crossed = send(crossing, [((t, t // 4), (t, 1 - t // 4)) for t in range(8)])
+    summed = jnp.where(mine, share(pos, dp), crossed).astype(f32)
+    for got in held:
+        summed = summed + got.astype(f32)
+    output_local = (inputs_local.astype(f32) + summed).astype(bf16)
+
+    wide_out = output_local.astype(f32)
+    sums = jnp.stack(
+        [
+            jnp.sum(wide_out * wide_out, axis=1),
+            jnp.sum(wide_out * (head_gain * value_weight), axis=1),
+        ]
+    )
+    total = sums
+    for k in range(1, 8):
+        total = total + send(sums, [((t, d), (t ^ k, d)) for t in range(8) for d in range(2)])
+    values = total[1] * lax.rsqrt(total[0] / full_width + epsilon)
+    return (
+        output_local.reshape(states, cands, cols),
+        values.reshape(states, cands),
+    )
+
+
 def solution(mesh):
+    local = local_ring if mesh.shape["tp"] == RING and mesh.shape["dp"] == 2 else local_gathered
     return jax.shard_map(
         local,
         mesh=mesh,

time: 462 us -> 154 us (0.33)
  waiting for transfers between devices: 281 us -> 39.3 us
  blocking collectives: 80.4 us -> 0 us
  starting transfers between devices: 0.24 us -> 52.5 us
  matrix products: 77.7 us -> 45.4 us
  between operations: 14.2 us -> 1.32 us
    all_gather x5 -> x0, waiting for transfers between devices: 190 us -> none  [the longest x1 71.1 us: local(): lax.all_gather(gate_weight, 'dp', axis=0, tiled=True)]
    reduce_scatter x1 -> x0, waiting for transfers between devices: 89.7 us -> none  [local(): lax.psum_scatter(partial_terms, 'tp', scatter_dimension=1, tiled=True)]
    all_gather x3 -> x0, blocking collectives: 80.4 us -> none  [the longest x1 27.9 us: local(): lax.all_gather(norm_gain.astype(jnp.bfloat16), 'tp', axis=0, tiled=True)]
    ppermute x0 -> x34, starting transfers between devices: none -> 52.5 us  [send(): lax.ppermute(array, ('tp', 'dp'), [(2 * st + sd, 2 * dt + dd) for (st, sd...]
    ppermute x0 -> x34, waiting for transfers between devices: none -> 39.3 us  [send(): lax.ppermute(array, ('tp', 'dp'), [(2 * st + sd, 2 * dt + dd) for (st, sd...]
    dot_general x4 -> x6, matrix products: 77.7 us -> 45.4 us  [the longest x1 14.4 us: local_ring(): jnp.dot(hidden, down_weight, preferred_element_type=f32).astype(bf16)]
  transfers between devices with their start and end apart: 6 -> 34, of which waited for: 5 -> 15; matrix products, arithmetic and copies ran while one was open for 13% -> 14% of each run, Pallas kernels for 0% -> 0%
where the time goes in v1:
time: 154 us; the launch traced here: 153 us
  starting transfers between devices  52.5 us (34%)
  matrix products  45.4 us (29%)
  waiting for transfers between devices  39.3 us (26%)
  other arithmetic  10.1 us (7%)
  local copies, waits for them, and re-layouts  4.78 us (3%)
    ppermute x34, starting transfers between devices, send(): lax.ppermute(array, ('tp', 'dp'), [(2 * st + sd, 2 * dt + dd) for (st, sd...  52.5 us
    ppermute x34, waiting for transfers between devices, send(): lax.ppermute(array, ('tp', 'dp'), [(2 * st + sd, 2 * dt + dd) for (st, sd...  39.3 us
    dot_general x1, matrix products, local_ring(): jnp.dot(hidden, down_weight, preferred_element_type=f32).astype(bf16)  14.4 us
    dot_general x1, matrix products, local_ring(): up_own = jnp.dot(lhs, up_weight, preferred_element_type=f32)  13.4 us
    dot_general x1, matrix products, local_ring(): gate_own = jnp.dot(lhs, gate_weight, preferred_element_type=f32)  12.8 us
    convert_element_type x5, other arithmetic, local_ring(): value = (value.astype(f32) + held[index].astype(f32)).astype(bf16)  3.55 us
    dot_general x1, matrix products, local_ring(): jnp.dot(wide_features, gate_basis, preferred_element_type=f32)  3.38 us
  transfers between devices with their start and end apart: 34, of which 15 were waited for; matrix products, arithmetic and copies ran while one was open for 14% of the time, Pallas kernels for 0%

profile of v1, /device:TPU:0, one launch (start us, length us, event | category | flops | bytes accessed | tf_op | source)
XLA Modules:
  0.0 153.3 jit_solution(6093410565923717929)
XLA Ops:
  2.5 7.0 %collective-permute-start.4 = (bf16[72,1024]{1,0:T(8,128)(2,1)S(1)}, bf16[72,1024]{1,0:T(8,128)(2,1)S(1)}, u32[]{:S(2)}, u32[]{:S(2)}) collective-permute-start(bf16[72,1024]{1,0:T(8,128)(2,1)S(1)} %maximum_maximum_fusion.1), channel_id=1, source_target_pairs={{0,12},{1,8},{2,14},{3,10},{4,4},{5,0},{6,6},{7,2},{8,13},{9,9},{1... | collective-permute-start | bytes 442376 | tf_op jit(solution)/shard_map/ppermute | solution.py:114
  9.5 2.0 %collective-permute-start.2 = (bf16[72,1024]{1,0:T(8,128)(2,1)S(1)}, bf16[72,1024]{1,0:T(8,128)(2,1)S(1)}, u32[]{:S(2)}, u32[]{:S(2)}) collective-permute-start(bf16[72,1024]{1,0:T(8,128)(2,1)S(1)} %maximum_maximum_fusion.1), channel_id=1, source_target_pairs={{0,4},{1,0},{2,6},{3,2},{4,12},{5,8},{6,14},{7,10},{8,5},{9,1},{10... | collective-permute-start | bytes 442376 | tf_op jit(solution)/shard_map/ppermute | solution.py:114
  14.0 2.5 %collective-permute-start = (bf16[128,128]{1,0:T(8,128)(2,1)S(1)}, bf16[128,128]{1,0:T(8,128)(2,1)S(1)}, u32[]{:S(2)}, u32[]{:S(2)}) collective-permute-start(bf16[128,128]{1,0:T(8,128)(2,1)S(1)} %fusion.27), channel_id=1, source_target_pairs={{0,1},{1,0},{2,3},{3,2},{4,5},{5,4},{6,7},{7,6},{8,9},{9,8},{10,11... | collective-permute-start | bytes 98312 | tf_op jit(solution)/shard_map/ppermute | solution.py:114
  16.9 1.5 collective-permute-start.8
  18.9 1.5 collective-permute-start.6
  21.2 2.4 %collective-permute-done.8 = bf16[72,1024]{1,0:T(8,128)(2,1)S(1)} collective-permute-done((bf16[72,1024]{1,0:T(8,128)(2,1)S(1)}, bf16[72,1024]{1,0:T(8,128)(2,1)S(1)}, u32[]{:S(2)}, u32[]{:S(2)}) %collective-permute-start.8) | collective-permute-done | bytes 147488 | tf_op jit(solution)/shard_map/ppermute | solution.py:114
  23.6 3.2 %collective-permute-done.7 = bf16[72,1024]{1,0:T(8,128)(2,1)S(1)} collective-permute-done((bf16[72,1024]{1,0:T(8,128)(2,1)S(1)}, bf16[72,1024]{1,0:T(8,128)(2,1)S(1)}, u32[]{:S(2)}, u32[]{:S(2)}) %collective-permute-start.7) | collective-permute-done | bytes 147488 | tf_op jit(solution)/shard_map/ppermute | solution.py:114
  26.7 3.2 %collective-permute-done.6 = bf16[72,1024]{1,0:T(8,128)(2,1)S(1)} collective-permute-done((bf16[72,1024]{1,0:T(8,128)(2,1)S(1)}, bf16[72,1024]{1,0:T(8,128)(2,1)S(1)}, u32[]{:S(2)}, u32[]{:S(2)}) %collective-permute-start.6) | collective-permute-done | bytes 147488 | tf_op jit(solution)/shard_map/ppermute | solution.py:114
  29.9 2.2 %collective-permute-done.5 = bf16[72,1024]{1,0:T(8,128)(2,1)S(1)} collective-permute-done((bf16[72,1024]{1,0:T(8,128)(2,1)S(1)}, bf16[72,1024]{1,0:T(8,128)(2,1)S(1)}, u32[]{:S(2)}, u32[]{:S(2)}) %collective-permute-start.5) | collective-permute-done | bytes 147488 | tf_op jit(solution)/shard_map/ppermute | solution.py:114
  33.0 1.4 fusion.8
  35.7 12.8 %fusion.53 = (bf16[136,3072]{1,0:T(8,128)(2,1)}, f32[136,3072]{1,0:T(8,128)S(1)}) fusion(bf16[4096,3072]{1,0:T(8,128)(2,1)} %param.17, f32[4096]{0:T(1024)S(1)} %bitcast.42, bf16[136]{0:T(256)(128)(2,1)S(1)} %pad.4.clone, bf16[4,4096]{1,0:T(4,128)(2,1)S(1)} %reshape.501, bf16[128,4096]{1,0:T(8,128)(2,1)S(1)} %bitcast.38), kind=kOutput, calls=%fused_computation.107 | convolution fusion | flops 3427426304 | bytes 28770576 | tf_op jit(solution)/shard_map/dot_general | solution.py:189
  48.5 13.4 %fusion.54 = (bf16[136,3072]{1,0:T(8,128)(2,1)}, f32[136,3072]{1,0:T(8,128)}) fusion(bf16[4096,3072]{1,0:T(8,128)(2,1)} %param.18, f32[4096]{0:T(1024)S(1)} %bitcast.43, bf16[136]{0:T(256)(128)(2,1)S(1)} %pad.4.clone, bf16[4,4096]{1,0:T(4,128)(2,1)S(1)} %reshape.501, bf16[128,4096]{1,0:T(8,128)(2,1)S(1)} %bitcast.39), kind=kOutput, calls=%fused_computation.108 | convolution fusion | flops 3427426304 | bytes 28770576 | tf_op jit(solution)/shard_map/dot_general | solution.py:191
  64.5 3.4 %convolution_multiply_fusion.1 = f32[256,3072]{1,0:T(8,128)} fusion(f32[256]{0:T(256)S(1)} %add_rsqrt_fusion, f32[136,3072]{1,0:T(8,128)S(1)} %get-tuple-element.20, bf16[136,3072]{1,0:T(8,128)(2,1)} %collective-permute-done.10, bf16[256,8]{1,0:T(8,128)(2,1)S(1)} %fusion.15, bf16[256,128]{1,0:T(8,128)(2,1)S(1)} %maximum_select_fusion), kind=kOutput, calls=%fused_computation.7 | convolution fusion | flops 216088576 | bytes 5723136 | tf_op jit(solution)/shard_map/dot_general | solution.py:201
  67.9 14.4 %convolution_convert_fusion = bf16[256,4096]{1,0:T(8,128)(2,1)S(1)} fusion(bf16[3072,4096]{1,0:T(8,128)(2,1)} %param.19, f32[256,3072]{1,0:T(8,128)} %convolution_multiply_fusion.1, f32[256]{0:T(256)S(1)} %add_rsqrt_fusion, f32[136,3072]{1,0:T(8,128)} %get-tuple-element.22, bf16[136,3072]{1,0:T(8,128)(2,1)} %collective-permute-done.11, ...), kind=kOutput, calls=%fused_computation.1 | convolution fusion | flops 6664306688 | bytes 32986112 | tf_op jit(solution)/shard_map/dot_general | solution.py:205
  86.0 1.4 collective-permute-start.21
  90.2 3.1 %collective-permute-done.24 = bf16[128,1024]{1,0:T(8,128)(2,1)} collective-permute-done((bf16[128,1024]{1,0:T(8,128)(2,1)}, bf16[128,1024]{1,0:T(8,128)(2,1)}, u32[]{:S(2)}, u32[]{:S(2)}) %collective-permute-start.24) | collective-permute-done | bytes 262176 | tf_op jit(solution)/shard_map/ppermute | solution.py:114
  93.3 13.9 %collective-permute-done.15 = bf16[128,1024]{1,0:T(8,128)(2,1)S(1)} collective-permute-done((bf16[128,1024]{1,0:T(8,128)(2,1)S(1)}, bf16[128,1024]{1,0:T(8,128)(2,1)S(1)}, u32[]{:S(2)}, u32[]{:S(2)}) %collective-permute-start.15) | collective-permute-done | bytes 262176 | tf_op jit(solution)/shard_map/ppermute | solution.py:114
  107.2 2.2 %add_convert_fusion.12 = (bf16[128,1024]{1,0:T(8,128)(2,1)}, bf16[128,1024]{1,0:T(8,128)(2,1)}, bf16[128,1024]{1,0:T(8,128)(2,1)}, bf16[128,1024]{1,0:T(8,128)(2,1)S(1)}) fusion(bf16[128,1024]{1,0:T(8,128)(2,1)S(1)} %collective-permute-done.15, bf16[256,4096]{1,0:T(8,128)(2,1)S(1)} %convolution_convert_fusion, s32[]{:T(128)S(6)} %select_n.252, ...), kind=kLoop, calls=%fused_computation.40 | loop fusion | flops 2097152 | bytes 3145744 | tf_op jit(solution)/shard_map/convert_element_type | solution.py:232
  109.4 1.4 collective-permute-start.18
  110.9 2.2 %collective-permute-start.25 = (bf16[128,1024]{1,0:T(8,128)(2,1)}, bf16[128,1024]{1,0:T(8,128)(2,1)S(1)}, u32[]{:S(2)}, u32[]{:S(2)}) collective-permute-start(bf16[128,1024]{1,0:T(8,128)(2,1)} %get-tuple-element.11), channel_id=1, source_target_pairs={{0,2},{4,0},{8,4},{12,8},{15,13},{11,15},{7,11},{3,7},{16,18},{20,... | collective-permute-start | bytes 786440 | tf_op jit(solution)/shard_map/ppermute | solution.py:114
  114.4 3.5 %collective-permute-done.18 = bf16[128,1024]{1,0:T(8,128)(2,1)S(1)} collective-permute-done((bf16[128,1024]{1,0:T(8,128)(2,1)S(1)}, bf16[128,1024]{1,0:T(8,128)(2,1)S(1)}, u32[]{:S(2)}, u32[]{:S(2)}) %collective-permute-start.18) | collective-permute-done | bytes 262176 | tf_op jit(solution)/shard_map/ppermute | solution.py:114
  117.9 1.9 %collective-permute-start.19 = (bf16[128,1024]{1,0:T(8,128)(2,1)S(1)}, bf16[128,1024]{1,0:T(8,128)(2,1)S(1)}, u32[]{:S(2)}, u32[]{:S(2)}) collective-permute-start(bf16[128,1024]{1,0:T(8,128)(2,1)S(1)} %add_convert_fusion.10), channel_id=1, source_target_pairs={{0,2},{4,0},{8,4},{12,8},{15,13},{11,15},{7,11},{3,7},{16,18},{20,... | collective-permute-start | bytes 786440 | tf_op jit(solution)/shard_map/ppermute | solution.py:114
  119.9 2.0 %collective-permute-start.12 = (bf16[128,1024]{1,0:T(8,128)(2,1)}, bf16[128,1024]{1,0:T(8,128)(2,1)}, u32[]{:S(2)}, u32[]{:S(2)}) collective-permute-start(bf16[128,1024]{1,0:T(8,128)(2,1)} %get-tuple-element.5), channel_id=1, source_target_pairs={{0,1},{2,3},{4,5},{6,7},{9,8},{11,10},{13,12},{15,14},{16,17},{18,... | collective-permute-start | bytes 786440 | tf_op jit(solution)/shard_map/ppermute | solution.py:114
  121.9 3.9 %collective-permute-start.16 = (bf16[128,1024]{1,0:T(8,128)(2,1)}, bf16[128,1024]{1,0:T(8,128)(2,1)}, u32[]{:S(2)}, u32[]{:S(2)}) collective-permute-start(bf16[128,1024]{1,0:T(8,128)(2,1)} %get-tuple-element.10), channel_id=1, source_target_pairs={{0,4},{5,8},{9,12},{13,14},{15,10},{10,6},{6,2},{2,0},{16,20},{21,... | collective-permute-start | bytes 786440 | tf_op jit(solution)/shard_map/ppermute | solution.py:114
  127.3 1.9 %collective-permute-start.26 = (bf16[128,1024]{1,0:T(8,128)(2,1)}, bf16[128,1024]{1,0:T(8,128)(2,1)S(1)}, u32[]{:S(2)}, u32[]{:S(2)}) collective-permute-start(bf16[128,1024]{1,0:T(8,128)(2,1)} %get-tuple-element.15), channel_id=1, source_target_pairs={{0,2},{4,0},{8,4},{13,8},{15,12},{11,14},{7,10},{2,6},{16,18},{20,... | collective-permute-start | bytes 786440 | tf_op jit(solution)/shard_map/ppermute | solution.py:114
  129.2 1.9 %collective-permute-start.23 = (bf16[128,1024]{1,0:T(8,128)(2,1)}, bf16[128,1024]{1,0:T(8,128)(2,1)S(1)}, u32[]{:S(2)}, u32[]{:S(2)}) collective-permute-start(bf16[128,1024]{1,0:T(8,128)(2,1)} %get-tuple-element.16), channel_id=1, source_target_pairs={{0,5},{5,9},{9,13},{13,15},{15,11},{10,7},{6,3},{2,1},{16,21},{21,... | collective-permute-start | bytes 786440 | tf_op jit(solution)/shard_map/ppermute | solution.py:114
  133.1 2.7 %collective-permute-done.26 = bf16[128,1024]{1,0:T(8,128)(2,1)S(1)} collective-permute-done((bf16[128,1024]{1,0:T(8,128)(2,1)}, bf16[128,1024]{1,0:T(8,128)(2,1)S(1)}, u32[]{:S(2)}, u32[]{:S(2)}) %collective-permute-start.26) | collective-permute-done | bytes 262176 | tf_op jit(solution)/shard_map/ppermute | solution.py:114
  136.2 2.0 %fusion.11 = (f32[128]{0:T(128)S(1)}, f32[128]{0:T(128)S(1)}, bf16[128,1024]{1,0:T(8,128)(2,1)}) fusion(f32[1024]{0:T(1024)S(1)} %mul.282, bf16[128,1024]{1,0:T(8,128)(2,1)S(1)} %collective-permute-done.26, bf16[128,1024]{1,0:T(8,128)(2,1)S(1)} %collective-permute-done.23, bf16[128,1024]{1,0:T(8,128)(2,1)S(1)} %collective-permute-done.20, ...), kind=kLoop, calls=%fused_computation.29 | loop fusion | flops 2359040 | bytes 2102281 | tf_op jit(solution)/shard_map/reduce_sum | solution.py:252
  138.3 4.8 %collective-permute-start.32 = (f32[2,128]{1,0:T(2,128)S(1)}, f32[2,128]{1,0:T(2,128)S(1)}, u32[]{:S(2)}, u32[]{:S(2)}) collective-permute-start(f32[2,128]{1,0:T(2,128)S(1)} %pad_maximum_fusion.8), channel_id=1, source_target_pairs={{0,12},{1,13},{2,14},{3,15},{4,8},{5,9},{6,10},{7,11},{8,4},{9,5},... | collective-permute-start | bytes 3080 | tf_op jit(solution)/shard_map/ppermute | solution.py:114
  143.1 2.4 %collective-permute-start.31 = (f32[2,128]{1,0:T(2,128)S(1)}, f32[2,128]{1,0:T(2,128)S(1)}, u32[]{:S(2)}, u32[]{:S(2)}) collective-permute-start(f32[2,128]{1,0:T(2,128)S(1)} %pad_maximum_fusion.8), channel_id=1, source_target_pairs={{0,10},{1,11},{2,8},{3,9},{4,14},{5,15},{6,12},{7,13},{8,2},{9,3},... | collective-permute-start | bytes 3080 | tf_op jit(solution)/shard_map/ppermute | solution.py:114
  147.1 1.9 %collective-permute-start.28 = (f32[2,128]{1,0:T(2,128)S(1)}, f32[2,128]{1,0:T(2,128)S(1)}, u32[]{:S(2)}, u32[]{:S(2)}) collective-permute-start(f32[2,128]{1,0:T(2,128)S(1)} %pad_maximum_fusion.8), channel_id=1, source_target_pairs={{0,4},{1,5},{2,6},{3,7},{4,0},{5,1},{6,2},{7,3},{8,12},{9,13},{10,... | collective-permute-start | bytes 3080 | tf_op jit(solution)/shard_map/ppermute | solution.py:114
  150.7 1.9 %collective-permute-done.27 = f32[2,128]{1,0:T(2,128)S(1)} collective-permute-done((f32[2,128]{1,0:T(2,128)S(1)}, f32[2,128]{1,0:T(2,128)S(1)}, u32[]{:S(2)}, u32[]{:S(2)}) %collective-permute-start.27) | collective-permute-done | bytes 1056 | tf_op jit(solution)/shard_map/ppermute | solution.py:114
  (99 shorter events, 26.2 us)
Async XLA Ops:
  2.5 14.4 %collective-permute-start.4 = (bf16[72,1024]{1,0:T(8,128)(2,1)S(1)}, bf16[72,1024]{1,0:T(8,128)(2,1)S(1)}, u32[]{:S(2)}, u32[]{:S(2)}) collective-permute-start(bf16[72,1024]{1,0:T(8,128)(2,1)S(1)} %maximum_maximum_fusion.1), channel_id=1, source_target_pairs={{0,12},{1,8},{2,14},{3,10},{4,4},{5,0},{6,6},{7,2},{8,13},{9,9},{1... | collective-permute-start | bytes 442376 | tf_op jit(solution)/shard_map/ppermute | solution.py:114
  9.4 8.9 %collective-permute-start.3 = (bf16[72,1024]{1,0:T(8,128)(2,1)S(1)}, bf16[72,1024]{1,0:T(8,128)(2,1)S(1)}, u32[]{:S(2)}, u32[]{:S(2)}) collective-permute-start(bf16[72,1024]{1,0:T(8,128)(2,1)S(1)} %maximum_maximum_fusion.1), channel_id=1, source_target_pairs={{0,8},{1,12},{2,10},{3,14},{4,0},{5,4},{6,2},{7,6},{8,9},{9,13},{1... | collective-permute-start | bytes 442376 | tf_op jit(solution)/shard_map/ppermute | solution.py:114
  9.5 9.4 %collective-permute-start.2 = (bf16[72,1024]{1,0:T(8,128)(2,1)S(1)}, bf16[72,1024]{1,0:T(8,128)(2,1)S(1)}, u32[]{:S(2)}, u32[]{:S(2)}) collective-permute-start(bf16[72,1024]{1,0:T(8,128)(2,1)S(1)} %maximum_maximum_fusion.1), channel_id=1, source_target_pairs={{0,4},{1,0},{2,6},{3,2},{4,12},{5,8},{6,14},{7,10},{8,5},{9,1},{10... | collective-permute-start | bytes 442376 | tf_op jit(solution)/shard_map/ppermute | solution.py:114
  11.5 8.9 %collective-permute-start.1 = (bf16[72,1024]{1,0:T(8,128)(2,1)S(1)}, bf16[72,1024]{1,0:T(8,128)(2,1)S(1)}, u32[]{:S(2)}, u32[]{:S(2)}) collective-permute-start(bf16[72,1024]{1,0:T(8,128)(2,1)S(1)} %maximum_maximum_fusion.1), channel_id=1, source_target_pairs={{0,0},{1,4},{2,2},{3,6},{4,8},{5,12},{6,10},{7,14},{8,1},{9,5},{10... | collective-permute-start | bytes 442376 | tf_op jit(solution)/shard_map/ppermute | solution.py:114
  14.0 7.1 %collective-permute-start = (bf16[128,128]{1,0:T(8,128)(2,1)S(1)}, bf16[128,128]{1,0:T(8,128)(2,1)S(1)}, u32[]{:S(2)}, u32[]{:S(2)}) collective-permute-start(bf16[128,128]{1,0:T(8,128)(2,1)S(1)} %fusion.27), channel_id=1, source_target_pairs={{0,1},{1,0},{2,3},{3,2},{4,5},{5,4},{6,7},{7,6},{8,9},{9,8},{10,11... | collective-permute-start | bytes 98312 | tf_op jit(solution)/shard_map/ppermute | solution.py:114
  16.9 6.7 %collective-permute-start.8 = (bf16[72,1024]{1,0:T(8,128)(2,1)S(1)}, bf16[72,1024]{1,0:T(8,128)(2,1)S(1)}, u32[]{:S(2)}, u32[]{:S(2)}) collective-permute-start(bf16[72,1024]{1,0:T(8,128)(2,1)S(1)} %collective-permute-done.4), channel_id=1, source_target_pairs={{0,2},{1,3},{2,0},{3,1},{4,6},{5,7},{6,4},{7,5},{8,10},{9,11},{10,... | collective-permute-start | bytes 442376 | tf_op jit(solution)/shard_map/ppermute | solution.py:114
  18.4 8.4 %collective-permute-start.7 = (bf16[72,1024]{1,0:T(8,128)(2,1)S(1)}, bf16[72,1024]{1,0:T(8,128)(2,1)S(1)}, u32[]{:S(2)}, u32[]{:S(2)}) collective-permute-start(bf16[72,1024]{1,0:T(8,128)(2,1)S(1)} %collective-permute-done.3), channel_id=1, source_target_pairs={{0,2},{1,3},{2,0},{3,1},{4,6},{5,7},{6,4},{7,5},{8,10},{9,11},{10,... | collective-permute-start | bytes 442376 | tf_op jit(solution)/shard_map/ppermute | solution.py:114
  18.9 11.0 %collective-permute-start.6 = (bf16[72,1024]{1,0:T(8,128)(2,1)S(1)}, bf16[72,1024]{1,0:T(8,128)(2,1)S(1)}, u32[]{:S(2)}, u32[]{:S(2)}) collective-permute-start(bf16[72,1024]{1,0:T(8,128)(2,1)S(1)} %collective-permute-done.2), channel_id=1, source_target_pairs={{0,2},{1,3},{2,0},{3,1},{4,6},{5,7},{6,4},{7,5},{8,10},{9,11},{10,... | collective-permute-start | bytes 442376 | tf_op jit(solution)/shard_map/ppermute | solution.py:114
  20.4 11.7 %collective-permute-start.5 = (bf16[72,1024]{1,0:T(8,128)(2,1)S(1)}, bf16[72,1024]{1,0:T(8,128)(2,1)S(1)}, u32[]{:S(2)}, u32[]{:S(2)}) collective-permute-start(bf16[72,1024]{1,0:T(8,128)(2,1)S(1)} %collective-permute-done.1), channel_id=1, source_target_pairs={{0,2},{1,3},{2,0},{3,1},{4,6},{5,7},{6,4},{7,5},{8,10},{9,11},{10,... | collective-permute-start | bytes 442376 | tf_op jit(solution)/shard_map/ppermute | solution.py:114
  48.5 16.0 %collective-permute-start.10 = (bf16[136,3072]{1,0:T(8,128)(2,1)}, bf16[136,3072]{1,0:T(8,128)(2,1)}, u32[]{:S(2)}, u32[]{:S(2)}) collective-permute-start(bf16[136,3072]{1,0:T(8,128)(2,1)} %get-tuple-element.19), channel_id=1, source_target_pairs={{0,1},{1,0},{2,3},{3,2},{4,5},{5,4},{6,7},{7,6},{8,9},{9,8},{10,11... | collective-permute-start | bytes 2506760 | tf_op jit(solution)/shard_map/ppermute | solution.py:114
  61.9 6.0 %collective-permute-start.11 = (bf16[136,3072]{1,0:T(8,128)(2,1)}, bf16[136,3072]{1,0:T(8,128)(2,1)}, u32[]{:S(2)}, u32[]{:S(2)}) collective-permute-start(bf16[136,3072]{1,0:T(8,128)(2,1)} %get-tuple-element.21), channel_id=1, source_target_pairs={{0,1},{1,0},{2,3},{3,2},{4,5},{5,4},{6,7},{7,6},{8,9},{9,8},{10,11... | collective-permute-start | bytes 2506760 | tf_op jit(solution)/shard_map/ppermute | solution.py:114
  84.0 4.8 %collective-permute-start.14 = (bf16[128,1024]{1,0:T(8,128)(2,1)S(1)}, bf16[128,1024]{1,0:T(8,128)(2,1)S(1)}, u32[]{:S(2)}, u32[]{:S(2)}) collective-permute-start(bf16[128,1024]{1,0:T(8,128)(2,1)S(1)} %add_convert_fusion.14), channel_id=1, source_target_pairs={{1,5},{5,9},{9,13},{12,14},{14,10},{10,6},{6,2},{3,1},{17,21},{21,... | collective-permute-start | bytes 786440 | tf_op jit(solution)/shard_map/ppermute | solution.py:114
  84.7 8.6 %collective-permute-start.24 = (bf16[128,1024]{1,0:T(8,128)(2,1)}, bf16[128,1024]{1,0:T(8,128)(2,1)}, u32[]{:S(2)}, u32[]{:S(2)}) collective-permute-start(bf16[128,1024]{1,0:T(8,128)(2,1)} %get-tuple-element.6), channel_id=1, source_target_pairs={{1,3},{4,0},{8,4},{12,8},{14,12},{11,15},{7,11},{3,7},{17,19},{20,... | collective-permute-start | bytes 786440 | tf_op jit(solution)/shard_map/ppermute | solution.py:114
  86.0 7.3 %collective-permute-start.21 = (bf16[128,1024]{1,0:T(8,128)(2,1)S(1)}, bf16[128,1024]{1,0:T(8,128)(2,1)}, u32[]{:S(2)}, u32[]{:S(2)}) collective-permute-start(bf16[128,1024]{1,0:T(8,128)(2,1)S(1)} %get-tuple-element.7), channel_id=1, source_target_pairs={{1,5},{5,9},{9,13},{12,14},{14,10},{10,6},{6,2},{3,1},{17,21},{21,... | collective-permute-start | bytes 786440 | tf_op jit(solution)/shard_map/ppermute | solution.py:114
  87.4 5.9 %collective-permute-start.17 = (bf16[128,1024]{1,0:T(8,128)(2,1)S(1)}, bf16[128,1024]{1,0:T(8,128)(2,1)}, u32[]{:S(2)}, u32[]{:S(2)}) collective-permute-start(bf16[128,1024]{1,0:T(8,128)(2,1)S(1)} %get-tuple-element.8), channel_id=1, source_target_pairs={{1,3},{5,1},{8,4},{12,8},{14,12},{10,14},{7,11},{3,7},{17,19},{21,... | collective-permute-start | bytes 786440 | tf_op jit(solution)/shard_map/ppermute | solution.py:114
  88.8 18.3 %collective-permute-start.15 = (bf16[128,1024]{1,0:T(8,128)(2,1)S(1)}, bf16[128,1024]{1,0:T(8,128)(2,1)S(1)}, u32[]{:S(2)}, u32[]{:S(2)}) collective-permute-start(bf16[128,1024]{1,0:T(8,128)(2,1)S(1)} %add_convert_fusion.13), channel_id=1, source_target_pairs={{1,5},{5,9},{9,13},{13,15},{14,10},{10,6},{6,2},{2,0},{17,21},{21,... | collective-permute-start | bytes 786440 | tf_op jit(solution)/shard_map/ppermute | solution.py:114
  109.4 8.4 %collective-permute-start.18 = (bf16[128,1024]{1,0:T(8,128)(2,1)S(1)}, bf16[128,1024]{1,0:T(8,128)(2,1)S(1)}, u32[]{:S(2)}, u32[]{:S(2)}) collective-permute-start(bf16[128,1024]{1,0:T(8,128)(2,1)S(1)} %get-tuple-element.13), channel_id=1, source_target_pairs={{1,3},{4,0},{8,4},{12,8},{14,12},{11,15},{7,11},{3,7},{17,19},{20,... | collective-permute-start | bytes 786440 | tf_op jit(solution)/shard_map/ppermute | solution.py:114
  110.9 14.9 %collective-permute-start.25 = (bf16[128,1024]{1,0:T(8,128)(2,1)}, bf16[128,1024]{1,0:T(8,128)(2,1)S(1)}, u32[]{:S(2)}, u32[]{:S(2)}) collective-permute-start(bf16[128,1024]{1,0:T(8,128)(2,1)} %get-tuple-element.11), channel_id=1, source_target_pairs={{0,2},{4,0},{8,4},{12,8},{15,13},{11,15},{7,11},{3,7},{16,18},{20,... | collective-permute-start | bytes 786440 | tf_op jit(solution)/shard_map/ppermute | solution.py:114
  113.1 12.8 %collective-permute-start.22 = (bf16[128,1024]{1,0:T(8,128)(2,1)}, bf16[128,1024]{1,0:T(8,128)(2,1)S(1)}, u32[]{:S(2)}, u32[]{:S(2)}) collective-permute-start(bf16[128,1024]{1,0:T(8,128)(2,1)} %get-tuple-element.12), channel_id=1, source_target_pairs={{1,5},{5,9},{9,13},{13,15},{14,10},{10,6},{6,2},{2,0},{17,21},{21,... | collective-permute-start | bytes 786440 | tf_op jit(solution)/shard_map/ppermute | solution.py:114
  117.9 8.3 %collective-permute-start.19 = (bf16[128,1024]{1,0:T(8,128)(2,1)S(1)}, bf16[128,1024]{1,0:T(8,128)(2,1)S(1)}, u32[]{:S(2)}, u32[]{:S(2)}) collective-permute-start(bf16[128,1024]{1,0:T(8,128)(2,1)S(1)} %add_convert_fusion.10), channel_id=1, source_target_pairs={{0,2},{4,0},{8,4},{12,8},{15,13},{11,15},{7,11},{3,7},{16,18},{20,... | collective-permute-start | bytes 786440 | tf_op jit(solution)/shard_map/ppermute | solution.py:114
  119.9 13.2 %collective-permute-start.12 = (bf16[128,1024]{1,0:T(8,128)(2,1)}, bf16[128,1024]{1,0:T(8,128)(2,1)}, u32[]{:S(2)}, u32[]{:S(2)}) collective-permute-start(bf16[128,1024]{1,0:T(8,128)(2,1)} %get-tuple-element.5), channel_id=1, source_target_pairs={{0,1},{2,3},{4,5},{6,7},{9,8},{11,10},{13,12},{15,14},{16,17},{18,... | collective-permute-start | bytes 786440 | tf_op jit(solution)/shard_map/ppermute | solution.py:114
  121.9 11.2 %collective-permute-start.16 = (bf16[128,1024]{1,0:T(8,128)(2,1)}, bf16[128,1024]{1,0:T(8,128)(2,1)}, u32[]{:S(2)}, u32[]{:S(2)}) collective-permute-start(bf16[128,1024]{1,0:T(8,128)(2,1)} %get-tuple-element.10), channel_id=1, source_target_pairs={{0,4},{5,8},{9,12},{13,14},{15,10},{10,6},{6,2},{2,0},{16,20},{21,... | collective-permute-start | bytes 786440 | tf_op jit(solution)/shard_map/ppermute | solution.py:114
  127.3 8.5 %collective-permute-start.26 = (bf16[128,1024]{1,0:T(8,128)(2,1)}, bf16[128,1024]{1,0:T(8,128)(2,1)S(1)}, u32[]{:S(2)}, u32[]{:S(2)}) collective-permute-start(bf16[128,1024]{1,0:T(8,128)(2,1)} %get-tuple-element.15), channel_id=1, source_target_pairs={{0,2},{4,0},{8,4},{13,8},{15,12},{11,14},{7,10},{2,6},{16,18},{20,... | collective-permute-start | bytes 786440 | tf_op jit(solution)/shard_map/ppermute | solution.py:114
  129.2 6.6 %collective-permute-start.23 = (bf16[128,1024]{1,0:T(8,128)(2,1)}, bf16[128,1024]{1,0:T(8,128)(2,1)S(1)}, u32[]{:S(2)}, u32[]{:S(2)}) collective-permute-start(bf16[128,1024]{1,0:T(8,128)(2,1)} %get-tuple-element.16), channel_id=1, source_target_pairs={{0,5},{5,9},{9,13},{13,15},{15,11},{10,7},{6,3},{2,1},{16,21},{21,... | collective-permute-start | bytes 786440 | tf_op jit(solution)/shard_map/ppermute | solution.py:114
  131.1 5.2 %collective-permute-start.20 = (bf16[128,1024]{1,0:T(8,128)(2,1)S(1)}, bf16[128,1024]{1,0:T(8,128)(2,1)S(1)}, u32[]{:S(2)}, u32[]{:S(2)}) collective-permute-start(bf16[128,1024]{1,0:T(8,128)(2,1)S(1)} %get-tuple-element.14), channel_id=1, source_target_pairs={{0,3},{4,1},{8,5},{13,9},{15,13},{11,15},{7,11},{2,7},{16,19},{20,... | collective-permute-start | bytes 786440 | tf_op jit(solution)/shard_map/ppermute | solution.py:114
  138.2 8.9 %collective-permute-start.33 = (f32[2,128]{1,0:T(2,128)S(1)}, f32[2,128]{1,0:T(2,128)S(1)}, u32[]{:S(2)}, u32[]{:S(2)}) collective-permute-start(f32[2,128]{1,0:T(2,128)S(1)} %pad_maximum_fusion.8), channel_id=1, source_target_pairs={{0,14},{1,15},{2,12},{3,13},{4,10},{5,11},{6,8},{7,9},{8,6},{9,7},... | collective-permute-start | bytes 3080 | tf_op jit(solution)/shard_map/ppermute | solution.py:114
  138.3 10.7 %collective-permute-start.32 = (f32[2,128]{1,0:T(2,128)S(1)}, f32[2,128]{1,0:T(2,128)S(1)}, u32[]{:S(2)}, u32[]{:S(2)}) collective-permute-start(f32[2,128]{1,0:T(2,128)S(1)} %pad_maximum_fusion.8), channel_id=1, source_target_pairs={{0,12},{1,13},{2,14},{3,15},{4,8},{5,9},{6,10},{7,11},{8,4},{9,5},... | collective-permute-start | bytes 3080 | tf_op jit(solution)/shard_map/ppermute | solution.py:114
  143.1 6.3 %collective-permute-start.31 = (f32[2,128]{1,0:T(2,128)S(1)}, f32[2,128]{1,0:T(2,128)S(1)}, u32[]{:S(2)}, u32[]{:S(2)}) collective-permute-start(f32[2,128]{1,0:T(2,128)S(1)} %pad_maximum_fusion.8), channel_id=1, source_target_pairs={{0,10},{1,11},{2,8},{3,9},{4,14},{5,15},{6,12},{7,13},{8,2},{9,3},... | collective-permute-start | bytes 3080 | tf_op jit(solution)/shard_map/ppermute | solution.py:114
  145.6 4.5 %collective-permute-start.30 = (f32[2,128]{1,0:T(2,128)S(1)}, f32[2,128]{1,0:T(2,128)S(1)}, u32[]{:S(2)}, u32[]{:S(2)}) collective-permute-start(f32[2,128]{1,0:T(2,128)S(1)} %pad_maximum_fusion.8), channel_id=1, source_target_pairs={{0,8},{1,9},{2,10},{3,11},{4,12},{5,13},{6,14},{7,15},{8,0},{9,1},... | collective-permute-start | bytes 3080 | tf_op jit(solution)/shard_map/ppermute | solution.py:114
  145.9 4.5 %collective-permute-start.29 = (f32[2,128]{1,0:T(2,128)S(1)}, f32[2,128]{1,0:T(2,128)S(1)}, u32[]{:S(2)}, u32[]{:S(2)}) collective-permute-start(f32[2,128]{1,0:T(2,128)S(1)} %pad_maximum_fusion.8), channel_id=1, source_target_pairs={{0,6},{1,7},{2,4},{3,5},{4,2},{5,3},{6,0},{7,1},{8,14},{9,15},{10,... | collective-permute-start | bytes 3080 | tf_op jit(solution)/shard_map/ppermute | solution.py:114
  147.1 3.6 %collective-permute-start.28 = (f32[2,128]{1,0:T(2,128)S(1)}, f32[2,128]{1,0:T(2,128)S(1)}, u32[]{:S(2)}, u32[]{:S(2)}) collective-permute-start(f32[2,128]{1,0:T(2,128)S(1)} %pad_maximum_fusion.8), channel_id=1, source_target_pairs={{0,4},{1,5},{2,6},{3,7},{4,0},{5,1},{6,2},{7,3},{8,12},{9,13},{10,... | collective-permute-start | bytes 3080 | tf_op jit(solution)/shard_map/ppermute | solution.py:114
  149.0 3.6 %collective-permute-start.27 = (f32[2,128]{1,0:T(2,128)S(1)}, f32[2,128]{1,0:T(2,128)S(1)}, u32[]{:S(2)}, u32[]{:S(2)}) collective-permute-start(f32[2,128]{1,0:T(2,128)S(1)} %pad_maximum_fusion.8), channel_id=1, source_target_pairs={{0,2},{1,3},{2,0},{3,1},{4,6},{5,7},{6,4},{7,5},{8,10},{9,11},{10,... | collective-permute-start | bytes 3080 | tf_op jit(solution)/shard_map/ppermute | solution.py:114
  (9 other events, 141.2 us)

commit v2 on v0

--- a/solution.py
+++ b/solution.py
@@ -1,8 +1,11 @@
+import functools
 import math
 
 import jax
 import jax.numpy as jnp
 from jax import lax
+from jax.experimental import pallas as pl
+from jax.experimental.pallas import tpu as pltpu
 from jax.sharding import PartitionSpec as P
 
 epsilon = 1e-05
@@ -22,7 +25,7 @@
     return jnp.sum(wide_out * (head_gain * value_weight), axis=1) * scale
 
 
-def local(
+def local_gathered(
     state_hidden,
     action_seeds,
     action_mean,
@@ -96,7 +99,333 @@
     )
 
 
+TP = 8
+SMALL = 16
+MIB = 1024 * 1024
+
+
+def send(array, pairs):
+    return lax.ppermute(
+        array, ("tp", "dp"), [(2 * st + sd, 2 * dt + dd) for (st, sd), (dt, dd) in pairs]
+    )
+
+
+def basis_body(block_count, accumulate, square, narrow, *refs):
+    refs = list(refs)
+    refs.pop(0)
+    blocks = [refs.pop(0) for _ in range(block_count)]
+    features = refs.pop(0) if square else None
+    gate_ref, up_ref = refs.pop(0), refs.pop(0)
+    before = refs.pop(0) if accumulate else None
+    total = refs.pop(0)
+    narrow_ref = refs.pop(0) if narrow else None
+    square_ref = refs.pop(0) if square else None
+    lhs = refs.pop(0)
+    tile, block = pl.program_id(0), pl.program_id(1)
+    states_at = features.shape[1] - SMALL if square else blocks[0].shape[0] - SMALL
+
+    for index, ref in enumerate(blocks):
+
+        @pl.when((tile == 0) & (block == index))
+        def _(index=index, ref=ref):
+            gain = ref[states_at + 4 : states_at + 5, :].astype(jnp.float32)
+            lhs[index] = (ref[...].astype(jnp.float32) * gain).astype(jnp.bfloat16)
+            if square:
+                rows = jnp.dot(features[...], ref[...], preferred_element_type=jnp.float32)
+                rows = rows.astype(jnp.bfloat16).astype(jnp.float32)
+                rows = rows * rows
+                part = rows[:, :128]
+                for at in range(128, rows.shape[1], 128):
+                    part += rows[:, at : at + 128]
+                if index == 0:
+                    square_ref[...] = part
+                else:
+                    square_ref[...] += part
+
+    gate = jnp.dot(lhs[block], gate_ref[...], preferred_element_type=jnp.float32)
+    up = jnp.dot(lhs[block], up_ref[...], preferred_element_type=jnp.float32)
+
+    def first():
+        if accumulate:
+            total[0] = before[0] + gate
+            total[1] = before[1] + up
+        else:
+            total[0] = gate
+            total[1] = up
+
+    def later():
+        total[0] += gate
+        total[1] += up
+
+    if block_count == 1:
+        first()
+    else:
+        pl.when(block == 0)(first)
+        pl.when(block > 0)(later)
+    if narrow:
+
+        @pl.when(block == block_count - 1)
+        def _():
+            narrow_ref[...] = total[...].astype(jnp.bfloat16)
+
+
+def basis_products(
+    blocks, which, features, gate_weight, up_weight, before, columns, square, narrow, tile
+):
+    count = len(blocks)
+    m, k = blocks[0].shape
+    start, stop = columns
+    width = stop - start
+    tiles, base = width // tile, start // tile
+    whole = lambda *shape: pl.BlockSpec(shape, lambda j, b, s: (0,) * len(shape))
+    weight = pl.BlockSpec((k, tile), lambda j, b, s: (s[b], base + j))
+    specs, operands = [whole(m, k)] * count, list(blocks)
+    if square:
+        specs.append(whole(*features.shape))
+        operands.append(features)
+    specs += [weight, weight]
+    operands += [gate_weight, up_weight]
+    if before is not None:
+        specs.append(pl.BlockSpec((2, m, tile), lambda j, b, s: (0, 0, base + j)))
+        operands.append(before)
+    part = pl.BlockSpec((2, m, tile), lambda j, b, s: (0, 0, j))
+    outs = [jax.ShapeDtypeStruct((2, m, width), jnp.float32)]
+    out_specs = [part]
+    if narrow:
+        outs.append(jax.ShapeDtypeStruct((2, m, width), jnp.bfloat16))
+        out_specs.append(part)
+    if square:
+        outs.append(jax.ShapeDtypeStruct((features.shape[0], 128), jnp.float32))
+        out_specs.append(whole(features.shape[0], 128))
+    return pl.pallas_call(
+        functools.partial(basis_body, count, before is not None, square, narrow),
+        out_shape=outs,
+        grid_spec=pltpu.PrefetchScalarGridSpec(
+            num_scalar_prefetch=1,
+            grid=(tiles, count),
+            in_specs=specs,
+            out_specs=out_specs,
+            scratch_shapes=[pltpu.VMEM((count, m, k), jnp.bfloat16)],
+        ),
+        compiler_params=pltpu.CompilerParams(
+            dimension_semantics=("arbitrary", "arbitrary"), vmem_limit_bytes=32 * MIB
+        ),
+        cost_estimate=pl.CostEstimate(
+            flops=4 * m * k * width * count,
+            bytes_accessed=4 * k * width * count,
+            transcendentals=0,
+        ),
+    )(which, *operands)
+
+
+def hidden_body(width, own, other, features, square_own, square_other, hidden):
+    squares = jnp.sum(square_own[...] + square_other[...], axis=1, keepdims=True)
+    scale = lax.rsqrt(squares / width + epsilon)
+    basis = (own[...] + other[...].astype(jnp.float32)).astype(jnp.bfloat16)
+    gate = scale * jnp.dot(features[...], basis[0], preferred_element_type=jnp.float32)
+    up = scale * jnp.dot(features[...], basis[1], preferred_element_type=jnp.float32)
+    hidden[...] = (gate / (1.0 + jnp.exp(-gate)) * up).astype(jnp.bfloat16)
+
+
+def hidden_units(own, other, features, square_own, square_other, width, tile):
+    _, m, units = own.shape
+    rows = features.shape[0]
+    whole = lambda *shape: pl.BlockSpec(shape, lambda j: (0,) * len(shape))
+    part = pl.BlockSpec((2, m, tile), lambda j: (0, 0, j))
+    return pl.pallas_call(
+        functools.partial(hidden_body, width),
+        out_shape=jax.ShapeDtypeStruct((rows, units), jnp.bfloat16),
+        grid=(units // tile,),
+        in_specs=[part, part, whole(rows, m), whole(rows, 128), whole(rows, 128)],
+        out_specs=pl.BlockSpec((rows, tile), lambda j: (0, j)),
+        compiler_params=pltpu.CompilerParams(vmem_limit_bytes=16 * MIB),
+        cost_estimate=pl.CostEstimate(
+            flops=4 * m * rows * units, bytes_accessed=12 * m * units, transcendentals=rows * units
+        ),
+    )(own, other, features, square_own, square_other)
+
+
+def down_body(count, which, *refs):
+    hidden = refs[:count]
+    weight, *outs = refs[count:]
+    total = None
+    at = 0
+    for ref in hidden:
+        depth = ref.shape[1]
+        term = jnp.dot(ref[...], weight[at : at + depth, :], preferred_element_type=jnp.float32)
+        total = term if total is None else total + term
+        at += depth
+    rows = total.shape[0] // 2
+    for part in range(2):
+        outs[part][...] = total[part * rows : (part + 1) * rows].astype(jnp.bfloat16)
+
+
+def down_products(hidden, down_weight, which, width, tile):
+    rows = hidden[0].shape[0]
+    depth = down_weight.shape[0]
+    tiles = width // tile
+    half = pl.BlockSpec((rows // 2, tile), lambda j, s: (0, j))
+    return pl.pallas_call(
+        functools.partial(down_body, len(hidden)),
+        out_shape=[jax.ShapeDtypeStruct((rows // 2, width), jnp.bfloat16)] * 2,
+        grid_spec=pltpu.PrefetchScalarGridSpec(
+            num_scalar_prefetch=1,
+            grid=(tiles,),
+            in_specs=[pl.BlockSpec(h.shape, lambda j, s: (0, 0)) for h in hidden]
+            + [pl.BlockSpec((depth, tile), lambda j, s: (0, s[0] * tiles + j))],
+            out_specs=[half, half],
+        ),
+        compiler_params=pltpu.CompilerParams(vmem_limit_bytes=32 * MIB),
+        cost_estimate=pl.CostEstimate(
+            flops=2 * rows * depth * width, bytes_accessed=2 * depth * width, transcendentals=0
+        ),
+    )(which, *hidden, down_weight)
+
+
+def local_blocks(
+    state_hidden,
+    action_seeds,
+    action_mean,
+    action_spread,
+    action_weight,
+    norm_gain,
+    gate_weight,
+    up_weight,
+    down_weight,
+    head_gain,
+    value_weight,
+):
+    f32, bf16 = jnp.float32, jnp.bfloat16
+    states, cands = action_seeds.shape
+    rows = states * cands
+    act, cols = action_weight.shape
+    half = act // 2
+    units = gate_weight.shape[1]
+    full_width = gate_weight.shape[0] * 2
+    tp, dp = lax.axis_index("tp"), lax.axis_index("dp")
+    home = tp // 4 == dp
+    place = tp % 4
+    every = [(t, d) for t in range(TP) for d in range(2)]
+    swap_core = [((t, d), (t, 1 - d)) for t, d in every]
+
+    seeds = jnp.concatenate([action_seeds // 256, action_seeds % 256]).astype(bf16)
+    seeds_row = jnp.pad(seeds.reshape(1, -1), ((0, 0), (0, cols - seeds.size)))
+    piece = jnp.concatenate(
+        [
+            lax.dynamic_slice_in_dim(action_weight, dp * half, half, 0),
+            state_hidden,
+            norm_gain.astype(bf16)[None],
+            seeds_row,
+            jnp.zeros((SMALL - states - 2, cols), bf16),
+        ],
+        axis=0,
+    )
+    first = send(
+        piece,
+        [((t, t // 4), (t ^ 4, t // 4)) for t in range(TP)]
+        + [((t, 1 - t // 4), (t, t // 4)) for t in range(TP)],
+    )
+    second = send(piece, [((t, 1 - t // 4), (t ^ 4, t // 4)) for t in range(TP)])
+    same = jnp.where(home, piece, first)
+    other = jnp.where(home, first, second)
+    low = jnp.where(dp == 0, same, other)
+    high = jnp.where(dp == 0, other, same)
+    block = jnp.concatenate(
+        [
+            low[:half],
+            high[:half],
+            low[half : half + states],
+            high[half : half + states],
+            low[half + states : half + states + 1],
+            jnp.zeros((SMALL - 2 * states - 1, cols), bf16),
+        ]
+    )
+
+    near = {k: send(block, [((t, d), (t ^ k, d)) for t, d in every]) for k in (2, 1, 3)}
+
+    all_seeds = jnp.concatenate(
+        [part[half + states + 1, : seeds.size].reshape(2, states, cands) for part in (low, high)],
+        axis=1,
+    ).astype(jnp.int32)
+    all_seeds = all_seeds[0] * 256 + all_seeds[1]
+    features = action_features(all_seeds, action_mean, action_spread).reshape(2 * rows, act)
+    row_state = jnp.arange(2 * rows) // cands
+    onehot = (row_state[:, None] == jnp.arange(SMALL)[None]).astype(bf16)
+    features = jnp.concatenate([features, onehot], axis=1)
+
+    index = lambda *ks: jnp.stack([place ^ k for k in ks]).astype(jnp.int32)
+    weights = (gate_weight, up_weight)
+    tile = 512
+    basis, square0 = basis_products(
+        [block], index(0), features, *weights, None, (0, units), True, False, tile
+    )
+    basis, square2 = basis_products(
+        [near[2]], index(2), features, *weights, basis, (0, units), True, False, tile
+    )
+    cut = units // 2
+    rest = [near[1], near[3]]
+    own_a, narrow_a, square13 = basis_products(
+        rest, index(1, 3), features, *weights, basis, (0, cut), True, True, tile
+    )
+    square = square0 + square2 + square13
+    other_a = send(narrow_a, swap_core)
+    other_square = send(square, swap_core)
+    own_b, narrow_b = basis_products(
+        rest, index(1, 3), features, *weights, basis, (cut, units), False, True, tile
+    )
+    other_b = send(narrow_b, swap_core)
+    hidden = [
+        hidden_units(own, other, features, square, other_square, full_width, tile)
+        for own, other in ((own_a, other_a), (own_b, other_b))
+    ]
+
+    partial = {
+        k: down_products(hidden, down_weight, index(k), cols, 256) for k in (3, 1, 2, 0)
+    }
+    sums = []
+    for part in range(2):
+        total = partial[0][part].astype(f32)
+        for k in (3, 1, 2):
+            got = send(partial[k][part], [((t, d), (t ^ k, d)) for t, d in every])
+            total = total + got.astype(f32)
+        sums.append(total.astype(bf16))
+    far = [
+        send(sums[part], [((t, 1 - t // 4), (t ^ 4, part)) for t in range(TP)])
+        for part in range(2)
+    ]
+    crossed = send(
+        jnp.where(dp == 0, sums[1], sums[0]), [((t, t // 4), (t, 1 - t // 4)) for t in range(TP)]
+    )
+
+    own_features = lax.dynamic_slice(features, (dp * rows, 0), (rows, act))
+    embedded = jnp.dot(own_features, action_weight, preferred_element_type=f32)
+    inputs_local = (
+        (state_hidden.astype(f32)[:, None, :] + embedded.reshape(states, cands, cols))
+        .reshape(rows, cols)
+        .astype(bf16)
+    )
+    mine = jnp.where(home, jnp.where(dp == 0, sums[0], sums[1]), crossed).astype(f32)
+    summed = mine + jnp.where(dp == 0, far[0], far[1]).astype(f32)
+    output_local = (inputs_local.astype(f32) + summed).astype(bf16)
+
+    wide_out = output_local.astype(f32)
+    totals = jnp.stack(
+        [
+            jnp.sum(wide_out * wide_out, axis=1),
+            jnp.sum(wide_out * (head_gain * value_weight), axis=1),
+        ]
+    )
+    totals = lax.all_to_all(jnp.broadcast_to(totals, (TP, 2, rows)), "tp", 0, 0)
+    totals = jnp.sum(totals, axis=0)
+    values = totals[1] * lax.rsqrt(totals[0] / full_width + epsilon)
+    return (
+        output_local.reshape(states, cands, cols),
+        values.reshape(states, cands),
+    )
+
+
 def solution(mesh):
+    local = local_blocks if mesh.shape["tp"] == TP and mesh.shape["dp"] == 2 else local_gathered
     return jax.shard_map(
         local,
         mesh=mesh,

time: 462 us -> 128 us (0.28)
  waiting for transfers between devices: 281 us -> 29.4 us
  matrix products: 77.7 us -> 0.22 us
  blocking collectives: 80.4 us -> 9.94 us
  Pallas kernels: 0 us -> 54 us
  starting transfers between devices: 0.24 us -> 25.8 us
  between operations: 14.2 us -> 1.03 us
    all_gather x5 -> x0, waiting for transfers between devices: 190 us -> none  [the longest x1 71.1 us: local(): lax.all_gather(gate_weight, 'dp', axis=0, tiled=True)]
    reduce_scatter x1 -> x0, waiting for transfers between devices: 89.7 us -> none  [local(): lax.psum_scatter(partial_terms, 'tp', scatter_dimension=1, tiled=True)]
    all_gather x3 -> x0, blocking collectives: 80.4 us -> none  [the longest x1 27.9 us: local(): lax.all_gather(norm_gain.astype(jnp.bfloat16), 'tp', axis=0, tiled=True)]
    dot_general x4 -> x1, matrix products: 77.7 us -> 0.22 us  [local_blocks(): embedded = jnp.dot(own_features, action_weight, preferred_element_type=f32)]
    pallas_call x0 -> x10, Pallas kernels: none -> 54 us  [the longest x4 32.4 us: basis_products(): pl.pallas_call(functools.partial(basis_body, count, before is not None, s...]
    ppermute x0 -> x17, waiting for transfers between devices: none -> 29.4 us  [send(): lax.ppermute(array, ('tp', 'dp'), [(2 * st + sd, 2 * dt + dd) for (st, sd...]
    ppermute x0 -> x17, starting transfers between devices: none -> 25.8 us  [send(): lax.ppermute(array, ('tp', 'dp'), [(2 * st + sd, 2 * dt + dd) for (st, sd...]
    all_to_all x0 -> x1, blocking collectives: none -> 9.94 us  [local_blocks(): totals = lax.all_to_all(jnp.broadcast_to(totals, (TP, 2, rows)), 'tp', 0, 0)]
  transfers between devices with their start and end apart: 6 -> 17, of which waited for: 5 -> 8; matrix products, arithmetic and copies ran while one was open for 13% -> 2% of each run, Pallas kernels for 0% -> 31%
where the time goes in v2:
time: 128 us; the launch traced here: 127 us
  Pallas kernels  54 us (42%)
  waiting for transfers between devices  29.4 us (23%)
  starting transfers between devices  25.8 us (20%)
  blocking collectives  9.94 us (8%)
  other arithmetic  4.37 us (3%)
  local copies, waits for them, and re-layouts  2.24 us (2%)
    pallas_call x4, Pallas kernels, basis_products(): pl.pallas_call(functools.partial(basis_body, count, before is not None, s...  32.4 us
    ppermute x17, waiting for transfers between devices, send(): lax.ppermute(array, ('tp', 'dp'), [(2 * st + sd, 2 * dt + dd) for (st, sd...  29.4 us
    ppermute x17, starting transfers between devices, send(): lax.ppermute(array, ('tp', 'dp'), [(2 * st + sd, 2 * dt + dd) for (st, sd...  25.8 us
    pallas_call x4, Pallas kernels, down_products(): pl.pallas_call(functools.partial(down_body, len(hidden)), out_shape=[jax....  18.9 us
    all_to_all x1, blocking collectives, local_blocks(): totals = lax.all_to_all(jnp.broadcast_to(totals, (TP, 2, rows)), 'tp', 0, 0)  9.94 us
    pallas_call x2, Pallas kernels, hidden_units(): pl.pallas_call(functools.partial(hidden_body, width), out_shape=jax.Shape...  2.7 us
  transfers between devices with their start and end apart: 17, of which 8 were waited for; matrix products, arithmetic and copies ran while one was open for 2% of the time, Pallas kernels for 31%

profile of v2, /device:TPU:0, one launch (start us, length us, event | category | flops | bytes accessed | tf_op | source)
XLA Modules:
  0.0 127.1 jit_solution(10189747256695968425)
XLA Ops:
  0.7 0.7 convert_element_type.82
  2.2 0.9 concatenate.17
  3.1 4.1 %collective-permute-start = (bf16[80,1024]{1,0:T(8,128)(2,1)S(1)}, bf16[80,1024]{1,0:T(8,128)(2,1)S(1)}, u32[]{:S(2)}, u32[]{:S(2)}) collective-permute-start(bf16[80,1024]{1,0:T(8,128)(2,1)S(1)} %concatenate.17), channel_id=1, source_target_pairs={{0,8},{2,10},{4,12},{6,14},{9,1},{11,3},{13,5},{15,7},{1,0},{3,2},... | collective-permute-start | bytes 491528 | tf_op jit(solution)/shard_map/ppermute | solution.py:108
  8.1 2.4 %collective-permute-done = bf16[80,1024]{1,0:T(8,128)(2,1)S(1)} collective-permute-done((bf16[80,1024]{1,0:T(8,128)(2,1)S(1)}, bf16[80,1024]{1,0:T(8,128)(2,1)S(1)}, u32[]{:S(2)}, u32[]{:S(2)}) %collective-permute-start) | collective-permute-done | bytes 163872 | tf_op jit(solution)/shard_map/ppermute | solution.py:108
  10.8 1.6 %collective-permute-start.2 = (bf16[144,1024]{1,0:T(8,128)(2,1)S(1)}, bf16[144,1024]{1,0:T(8,128)(2,1)S(1)}, u32[]{:S(2)}, u32[]{:S(2)}) collective-permute-start(bf16[144,1024]{1,0:T(8,128)(2,1)S(1)} %concatenate.20.refs_1_), channel_id=1, source_target_pairs={{0,2},{1,3},{2,0},{3,1},{4,6},{5,7},{6,4},{7,5},{8,10},{9,11},{10,... | collective-permute-start | bytes 884744 | tf_op jit(solution)/shard_map/ppermute | solution.py:108
  12.4 6.2 %collective-permute-start.3 = (bf16[144,1024]{1,0:T(8,128)(2,1)S(1)}, bf16[144,1024]{1,0:T(8,128)(2,1)S(1)}, u32[]{:S(2)}, u32[]{:S(2)}) collective-permute-start(bf16[144,1024]{1,0:T(8,128)(2,1)S(1)} %concatenate.20.refs_1_), channel_id=1, source_target_pairs={{0,6},{1,7},{2,4},{3,5},{4,2},{5,3},{6,0},{7,1},{8,14},{9,15},{10,... | collective-permute-start | bytes 884744 | tf_op jit(solution)/shard_map/ppermute | solution.py:108
  18.9 1.3 fusion.9
  20.2 7.6 %shard_map.122 = (f32[2,144,3072]{2,1,0:T(8,128)S(1)}, f32[256,128]{1,0:T(8,128)S(1)}) custom-call(s32[1]{0:T(128)} %bitcast.1.refs_0_.which, bf16[144,1024]{1,0:T(8,128)(2,1)S(1)} %concatenate.20.refs_1_, bf16[256,144]{1,0:T(8,128)(2,1)S(1)} %pad_maximum_fusion.refs_2_.refs_3_.features, bf16[4096,3072]{1,0:T(8,128)(2,1)} %refs_3_.5, bf16[4096,3072]{1,0:T(8,128)(2,1)} %refs_4_.7), custom_call_target="tpu_custom_call" | custom-call | flops 1811939328 | bytes 12582912 | tf_op jit(solution)/shard_map/pallas_call | solution.py:200
  27.8 4.4 %collective-permute-done.4.refs_1_ = bf16[144,1024]{1,0:T(8,128)(2,1)S(1)} collective-permute-done((bf16[144,1024]{1,0:T(8,128)(2,1)S(1)}, bf16[144,1024]{1,0:T(8,128)(2,1)S(1)}, u32[]{:S(2)}, u32[]{:S(2)}) %collective-permute-start.4) | collective-permute-done | bytes 294944 | tf_op jit(solution)/shard_map/ppermute | solution.py:108
  32.2 7.6 %shard_map.123 = (f32[2,144,3072]{2,1,0:T(8,128)S(1)}, f32[256,128]{1,0:T(8,128)S(1)}) custom-call(s32[1]{0:T(128)} %bitcast.4.refs_0_.which, bf16[144,1024]{1,0:T(8,128)(2,1)S(1)} %collective-permute-done.4.refs_1_, bf16[256,144]{1,0:T(8,128)(2,1)S(1)} %pad_maximum_fusion.refs_2_.refs_3_.features, bf16[4096,3072]{1,0:T(8,128)(2,1)} %refs_3_.5, ...), custom_call_target="tpu_custom_call" | custom-call | flops 1811939328 | bytes 12582912 | tf_op jit(solution)/shard_map/pallas_call | solution.py:200
  39.8 8.9 %shard_map.124 = (f32[2,144,1536]{2,1,0:T(8,128)S(1)}, bf16[2,144,1536]{2,1,0:T(8,128)(2,1)S(1)}, f32[256,128]{1,0:T(8,128)S(1)}) custom-call(s32[2]{0:T(128)S(1)} %pad_add_fusion.refs_0_, bf16[144,1024]{1,0:T(8,128)(2,1)S(1)} %collective-permute-done.2.refs_1_, bf16[144,1024]{1,0:T(8,128)(2,1)S(1)} %collective-permute-done.3.refs_2_, ...), custom_call_target="tpu_custom_call" | custom-call | flops 1811939328 | bytes 12582912 | tf_op jit(solution)/shard_map/pallas_call | solution.py:200
  48.8 8.3 %shard_map.126 = (f32[2,144,1536]{2,1,0:T(8,128)S(1)}, bf16[2,144,1536]{2,1,0:T(8,128)(2,1)S(1)}) custom-call(s32[2]{0:T(128)S(1)} %pad_add_fusion.refs_0_, bf16[144,1024]{1,0:T(8,128)(2,1)S(1)} %collective-permute-done.2.refs_1_, bf16[144,1024]{1,0:T(8,128)(2,1)S(1)} %collective-permute-done.3.refs_2_, bf16[4096,3072]{1,0:T(8,128)(2,1)} %refs_3_.5, ...), custom_call_target="tpu_custom_call" | custom-call | flops 1811939328 | bytes 12582912 | tf_op jit(solution)/shard_map/pallas_call | solution.py:200
  57.8 2.1 %collective-permute-done.6.square_other = f32[256,128]{1,0:T(8,128)S(1)} collective-permute-done((f32[256,128]{1,0:T(8,128)S(1)}, f32[256,128]{1,0:T(8,128)S(1)}, u32[]{:S(2)}, u32[]{:S(2)}) %collective-permute-start.6) | collective-permute-done | bytes 131104 | tf_op jit(solution)/shard_map/ppermute | solution.py:108
  60.0 1.3 %shard_map.125.refs_0_ = bf16[256,1536]{1,0:T(8,128)(2,1)S(1)} custom-call(f32[2,144,1536]{2,1,0:T(8,128)S(1)} %get-tuple-element.21.own, bf16[2,144,1536]{2,1,0:T(8,128)(2,1)S(1)} %collective-permute-done.5.other, bf16[256,144]{1,0:T(8,128)(2,1)S(1)} %pad_maximum_fusion.refs_2_.refs_3_.features, f32[256,128]{1,0:T(8,128)S(1)} %add_add_fusion.square_own, ...), custom_call_target="tpu_custom_call" | custom-call | flops 226492416 | bytes 2654208 | tf_op jit(solution)/shard_map/pallas_call | solution.py:235
  61.3 1.4 %shard_map.127.refs_1_ = bf16[256,1536]{1,0:T(8,128)(2,1)S(1)} custom-call(f32[2,144,1536]{2,1,0:T(8,128)S(1)} %get-tuple-element.26.own, bf16[2,144,1536]{2,1,0:T(8,128)(2,1)S(1)} %collective-permute-done.7.other, bf16[256,144]{1,0:T(8,128)(2,1)S(1)} %pad_maximum_fusion.refs_2_.refs_3_.features, f32[256,128]{1,0:T(8,128)S(1)} %add_add_fusion.square_own, ...), custom_call_target="tpu_custom_call" | custom-call | flops 226492416 | bytes 2654208 | tf_op jit(solution)/shard_map/pallas_call | solution.py:235
  62.7 4.7 %shard_map.131 = (bf16[128,1024]{1,0:T(8,128)(2,1)S(1)}, bf16[128,1024]{1,0:T(8,128)(2,1)S(1)}) custom-call(s32[1]{0:T(128)} %bitcast.4.refs_0_.which, bf16[256,1536]{1,0:T(8,128)(2,1)S(1)} %shard_map.125.refs_0_, bf16[256,1536]{1,0:T(8,128)(2,1)S(1)} %shard_map.127.refs_1_, bf16[3072,4096]{1,0:T(8,128)(2,1)} %refs_2_.7), custom_call_target="tpu_custom_call" | custom-call | flops 1610612736 | bytes 6291456 | tf_op jit(solution)/shard_map/pallas_call | solution.py:268
  67.4 1.8 %collective-permute-start.13 = (bf16[128,1024]{1,0:T(8,128)(2,1)S(1)}, bf16[128,1024]{1,0:T(8,128)(2,1)S(1)}, u32[]{:S(2)}, u32[]{:S(2)}) collective-permute-start(bf16[128,1024]{1,0:T(8,128)(2,1)S(1)} %get-tuple-element.35), channel_id=1, source_target_pairs={{0,4},{1,5},{2,6},{3,7},{4,0},{5,1},{6,2},{7,3},{8,12},{9,13},{10,... | collective-permute-start | bytes 786440 | tf_op jit(solution)/shard_map/ppermute | solution.py:108
  69.3 4.7 %shard_map.130 = (bf16[128,1024]{1,0:T(8,128)(2,1)S(1)}, bf16[128,1024]{1,0:T(8,128)(2,1)S(1)}) custom-call(s32[1]{0:T(128)} %bitcast.2.which, bf16[256,1536]{1,0:T(8,128)(2,1)S(1)} %shard_map.125.refs_0_, bf16[256,1536]{1,0:T(8,128)(2,1)S(1)} %shard_map.127.refs_1_, bf16[3072,4096]{1,0:T(8,128)(2,1)} %refs_2_.7), custom_call_target="tpu_custom_call" | custom-call | flops 1610612736 | bytes 6291456 | tf_op jit(solution)/shard_map/pallas_call | solution.py:268
  74.0 1.6 %collective-permute-start.12 = (bf16[128,1024]{1,0:T(8,128)(2,1)S(1)}, bf16[128,1024]{1,0:T(8,128)(2,1)S(1)}, u32[]{:S(2)}, u32[]{:S(2)}) collective-permute-start(bf16[128,1024]{1,0:T(8,128)(2,1)S(1)} %get-tuple-element.34), channel_id=1, source_target_pairs={{0,2},{1,3},{2,0},{3,1},{4,6},{5,7},{6,4},{7,5},{8,10},{9,11},{10,... | collective-permute-start | bytes 786440 | tf_op jit(solution)/shard_map/ppermute | solution.py:108
  75.6 4.7 %shard_map.129 = (bf16[128,1024]{1,0:T(8,128)(2,1)S(1)}, bf16[128,1024]{1,0:T(8,128)(2,1)S(1)}) custom-call(s32[1]{0:T(128)} %bitcast.3.which, bf16[256,1536]{1,0:T(8,128)(2,1)S(1)} %shard_map.125.refs_0_, bf16[256,1536]{1,0:T(8,128)(2,1)S(1)} %shard_map.127.refs_1_, bf16[3072,4096]{1,0:T(8,128)(2,1)} %refs_2_.7), custom_call_target="tpu_custom_call" | custom-call | flops 1610612736 | bytes 6291456 | tf_op jit(solution)/shard_map/pallas_call | solution.py:268
  80.6 1.7 %collective-permute-start.10 = (bf16[128,1024]{1,0:T(8,128)(2,1)S(1)}, bf16[128,1024]{1,0:T(8,128)(2,1)S(1)}, u32[]{:S(2)}, u32[]{:S(2)}) collective-permute-start(bf16[128,1024]{1,0:T(8,128)(2,1)S(1)} %get-tuple-element.31), channel_id=1, source_target_pairs={{0,4},{1,5},{2,6},{3,7},{4,0},{5,1},{6,2},{7,3},{8,12},{9,13},{10,... | collective-permute-start | bytes 786440 | tf_op jit(solution)/shard_map/ppermute | solution.py:108
  82.3 1.5 %collective-permute-start.9 = (bf16[128,1024]{1,0:T(8,128)(2,1)S(1)}, bf16[128,1024]{1,0:T(8,128)(2,1)S(1)}, u32[]{:S(2)}, u32[]{:S(2)}) collective-permute-start(bf16[128,1024]{1,0:T(8,128)(2,1)S(1)} %get-tuple-element.30), channel_id=1, source_target_pairs={{0,2},{1,3},{2,0},{3,1},{4,6},{5,7},{6,4},{7,5},{8,10},{9,11},{10,... | collective-permute-start | bytes 786440 | tf_op jit(solution)/shard_map/ppermute | solution.py:108
  84.2 4.7 %shard_map.128 = (bf16[128,1024]{1,0:T(8,128)(2,1)S(1)}, bf16[128,1024]{1,0:T(8,128)(2,1)S(1)}) custom-call(s32[1]{0:T(128)} %bitcast.1.refs_0_.which, bf16[256,1536]{1,0:T(8,128)(2,1)S(1)} %shard_map.125.refs_0_, bf16[256,1536]{1,0:T(8,128)(2,1)S(1)} %shard_map.127.refs_1_, bf16[3072,4096]{1,0:T(8,128)(2,1)} %refs_2_.7), custom_call_target="tpu_custom_call" | custom-call | flops 1610612736 | bytes 6291456 | tf_op jit(solution)/shard_map/pallas_call | solution.py:268
  88.9 1.6 %collective-permute-done.11 = bf16[128,1024]{1,0:T(8,128)(2,1)S(1)} collective-permute-done((bf16[128,1024]{1,0:T(8,128)(2,1)S(1)}, bf16[128,1024]{1,0:T(8,128)(2,1)S(1)}, u32[]{:S(2)}, u32[]{:S(2)}) %collective-permute-start.11) | collective-permute-done | bytes 262176 | tf_op jit(solution)/shard_map/ppermute | solution.py:108
  90.5 4.7 %collective-permute-done.10 = bf16[128,1024]{1,0:T(8,128)(2,1)S(1)} collective-permute-done((bf16[128,1024]{1,0:T(8,128)(2,1)S(1)}, bf16[128,1024]{1,0:T(8,128)(2,1)S(1)}, u32[]{:S(2)}, u32[]{:S(2)}) %collective-permute-start.10) | collective-permute-done | bytes 262176 | tf_op jit(solution)/shard_map/ppermute | solution.py:108
  95.2 0.8 collective-permute-done.9
  96.0 4.5 %collective-permute-done.8 = bf16[128,1024]{1,0:T(8,128)(2,1)S(1)} collective-permute-done((bf16[128,1024]{1,0:T(8,128)(2,1)S(1)}, bf16[128,1024]{1,0:T(8,128)(2,1)S(1)}, u32[]{:S(2)}, u32[]{:S(2)}) %collective-permute-start.8) | collective-permute-done | bytes 262176 | tf_op jit(solution)/shard_map/ppermute | solution.py:108
  100.9 1.3 %collective-permute-start.15 = (bf16[128,1024]{1,0:T(8,128)(2,1)S(1)}, bf16[128,1024]{1,0:T(8,128)(2,1)S(1)}, u32[]{:S(2)}, u32[]{:S(2)}) collective-permute-start(bf16[128,1024]{1,0:T(8,128)(2,1)S(1)} %get-tuple-element.41), channel_id=1, source_target_pairs={{1,8},{3,10},{5,12},{7,14},{8,0},{10,2},{12,4},{14,6},{17,24},{19,... | collective-permute-start | bytes 786440 | tf_op jit(solution)/shard_map/ppermute | solution.py:108
  102.9 3.3 %collective-permute-start.14 = (bf16[128,1024]{1,0:T(8,128)(2,1)S(1)}, bf16[128,1024]{1,0:T(8,128)(2,1)S(1)}, u32[]{:S(2)}, u32[]{:S(2)}) collective-permute-start(bf16[128,1024]{1,0:T(8,128)(2,1)S(1)} %get-tuple-element.39), channel_id=1, source_target_pairs={{0,1},{2,3},{4,5},{6,7},{9,8},{11,10},{13,12},{15,14},{16,17},{18,... | collective-permute-start | bytes 786440 | tf_op jit(solution)/shard_map/ppermute | solution.py:108
  106.6 8.9 %collective-permute-done.15 = bf16[128,1024]{1,0:T(8,128)(2,1)S(1)} collective-permute-done((bf16[128,1024]{1,0:T(8,128)(2,1)S(1)}, bf16[128,1024]{1,0:T(8,128)(2,1)S(1)}, u32[]{:S(2)}, u32[]{:S(2)}) %collective-permute-start.15) | collective-permute-done | bytes 262176 | tf_op jit(solution)/shard_map/ppermute | solution.py:108
  115.5 1.0 fusion.2
  116.5 9.9 %all_to_all.5 = f32[8,2,128]{2,1,0:T(2,128)S(1)} all-to-all(f32[8,2,128]{2,1,0:T(2,128)S(1)} %broadcast_in_dim.11), channel_id=1, replica_groups=mesh['rep'=2,'tp'=8,'dp'=2] {'tp'}, dimensions={0} | all-to-all | bytes 16384 | tf_op jit(solution)/shard_map/all_to_all | solution.py:418
  (61 shorter events, 5.7 us)
Async XLA Ops:
  0.6 1.6 %copy-start = (bf16[128,1024]{1,0:T(8,128)(2,1)S(1)}, bf16[128,1024]{1,0:T(8,128)(2,1)}, u32[]{:S(2)}) copy-start(bf16[128,1024]{1,0:T(8,128)(2,1)} %param.15) | copy-start | bytes 786436
  3.1 7.4 %collective-permute-start = (bf16[80,1024]{1,0:T(8,128)(2,1)S(1)}, bf16[80,1024]{1,0:T(8,128)(2,1)S(1)}, u32[]{:S(2)}, u32[]{:S(2)}) collective-permute-start(bf16[80,1024]{1,0:T(8,128)(2,1)S(1)} %concatenate.17), channel_id=1, source_target_pairs={{0,8},{2,10},{4,12},{6,14},{9,1},{11,3},{13,5},{15,7},{1,0},{3,2},... | collective-permute-start | bytes 491528 | tf_op jit(solution)/shard_map/ppermute | solution.py:108
  7.2 3.3 %collective-permute-start.1 = (bf16[80,1024]{1,0:T(8,128)(2,1)S(1)}, bf16[80,1024]{1,0:T(8,128)(2,1)S(1)}, u32[]{:S(2)}, u32[]{:S(2)}) collective-permute-start(bf16[80,1024]{1,0:T(8,128)(2,1)S(1)} %concatenate.17), channel_id=1, source_target_pairs={{1,8},{3,10},{5,12},{7,14},{8,1},{10,3},{12,5},{14,7},{17,24},{19,... | collective-permute-start | bytes 491528 | tf_op jit(solution)/shard_map/ppermute | solution.py:108
  10.8 29.0 %collective-permute-start.2 = (bf16[144,1024]{1,0:T(8,128)(2,1)S(1)}, bf16[144,1024]{1,0:T(8,128)(2,1)S(1)}, u32[]{:S(2)}, u32[]{:S(2)}) collective-permute-start(bf16[144,1024]{1,0:T(8,128)(2,1)S(1)} %concatenate.20.refs_1_), channel_id=1, source_target_pairs={{0,2},{1,3},{2,0},{3,1},{4,6},{5,7},{6,4},{7,5},{8,10},{9,11},{10,... | collective-permute-start | bytes 884744 | tf_op jit(solution)/shard_map/ppermute | solution.py:108
  12.4 27.4 %collective-permute-start.3 = (bf16[144,1024]{1,0:T(8,128)(2,1)S(1)}, bf16[144,1024]{1,0:T(8,128)(2,1)S(1)}, u32[]{:S(2)}, u32[]{:S(2)}) collective-permute-start(bf16[144,1024]{1,0:T(8,128)(2,1)S(1)} %concatenate.20.refs_1_), channel_id=1, source_target_pairs={{0,6},{1,7},{2,4},{3,5},{4,2},{5,3},{6,0},{7,1},{8,14},{9,15},{10,... | collective-permute-start | bytes 884744 | tf_op jit(solution)/shard_map/ppermute | solution.py:108
  18.6 13.6 %collective-permute-start.4 = (bf16[144,1024]{1,0:T(8,128)(2,1)S(1)}, bf16[144,1024]{1,0:T(8,128)(2,1)S(1)}, u32[]{:S(2)}, u32[]{:S(2)}) collective-permute-start(bf16[144,1024]{1,0:T(8,128)(2,1)S(1)} %concatenate.20.refs_1_), channel_id=1, source_target_pairs={{0,4},{1,5},{2,6},{3,7},{4,0},{5,1},{6,2},{7,3},{8,12},{9,13},{10,... | collective-permute-start | bytes 884744 | tf_op jit(solution)/shard_map/ppermute | solution.py:108
  48.7 11.2 %collective-permute-start.5 = (bf16[2,144,1536]{2,1,0:T(8,128)(2,1)S(1)}, bf16[2,144,1536]{2,1,0:T(8,128)(2,1)S(1)}, u32[]{:S(2)}, u32[]{:S(2)}) collective-permute-start(bf16[2,144,1536]{2,1,0:T(8,128)(2,1)S(1)} %get-tuple-element.22), channel_id=1, source_target_pairs={{0,1},{1,0},{2,3},{3,2},{4,5},{5,4},{6,7},{7,6},{8,9},{9,8},{10,11... | collective-permute-start | bytes 2654216 | tf_op jit(solution)/shard_map/ppermute | solution.py:108
  57.2 4.2 %collective-permute-start.7 = (bf16[2,144,1536]{2,1,0:T(8,128)(2,1)S(1)}, bf16[2,144,1536]{2,1,0:T(8,128)(2,1)S(1)}, u32[]{:S(2)}, u32[]{:S(2)}) collective-permute-start(bf16[2,144,1536]{2,1,0:T(8,128)(2,1)S(1)} %get-tuple-element.27), channel_id=1, source_target_pairs={{0,1},{1,0},{2,3},{3,2},{4,5},{5,4},{6,7},{7,6},{8,9},{9,8},{10,11... | collective-permute-start | bytes 2654216 | tf_op jit(solution)/shard_map/ppermute | solution.py:108
  57.7 2.2 %collective-permute-start.6 = (f32[256,128]{1,0:T(8,128)S(1)}, f32[256,128]{1,0:T(8,128)S(1)}, u32[]{:S(2)}, u32[]{:S(2)}) collective-permute-start(f32[256,128]{1,0:T(8,128)S(1)} %add_add_fusion.square_own), channel_id=1, source_target_pairs={{0,1},{1,0},{2,3},{3,2},{4,5},{5,4},{6,7},{7,6},{8,9},{9,8},{10,11... | collective-permute-start | bytes 393224 | tf_op jit(solution)/shard_map/ppermute | solution.py:108
  67.4 16.4 %collective-permute-start.13 = (bf16[128,1024]{1,0:T(8,128)(2,1)S(1)}, bf16[128,1024]{1,0:T(8,128)(2,1)S(1)}, u32[]{:S(2)}, u32[]{:S(2)}) collective-permute-start(bf16[128,1024]{1,0:T(8,128)(2,1)S(1)} %get-tuple-element.35), channel_id=1, source_target_pairs={{0,4},{1,5},{2,6},{3,7},{4,0},{5,1},{6,2},{7,3},{8,12},{9,13},{10,... | collective-permute-start | bytes 786440 | tf_op jit(solution)/shard_map/ppermute | solution.py:108
  74.0 14.9 %collective-permute-start.12 = (bf16[128,1024]{1,0:T(8,128)(2,1)S(1)}, bf16[128,1024]{1,0:T(8,128)(2,1)S(1)}, u32[]{:S(2)}, u32[]{:S(2)}) collective-permute-start(bf16[128,1024]{1,0:T(8,128)(2,1)S(1)} %get-tuple-element.34), channel_id=1, source_target_pairs={{0,2},{1,3},{2,0},{3,1},{4,6},{5,7},{6,4},{7,5},{8,10},{9,11},{10,... | collective-permute-start | bytes 786440 | tf_op jit(solution)/shard_map/ppermute | solution.py:108
  80.3 10.2 %collective-permute-start.11 = (bf16[128,1024]{1,0:T(8,128)(2,1)S(1)}, bf16[128,1024]{1,0:T(8,128)(2,1)S(1)}, u32[]{:S(2)}, u32[]{:S(2)}) collective-permute-start(bf16[128,1024]{1,0:T(8,128)(2,1)S(1)} %get-tuple-element.33), channel_id=1, source_target_pairs={{0,6},{1,7},{2,4},{3,5},{4,2},{5,3},{6,0},{7,1},{8,14},{9,15},{10,... | collective-permute-start | bytes 786440 | tf_op jit(solution)/shard_map/ppermute | solution.py:108
  80.6 14.6 %collective-permute-start.10 = (bf16[128,1024]{1,0:T(8,128)(2,1)S(1)}, bf16[128,1024]{1,0:T(8,128)(2,1)S(1)}, u32[]{:S(2)}, u32[]{:S(2)}) collective-permute-start(bf16[128,1024]{1,0:T(8,128)(2,1)S(1)} %get-tuple-element.31), channel_id=1, source_target_pairs={{0,4},{1,5},{2,6},{3,7},{4,0},{5,1},{6,2},{7,3},{8,12},{9,13},{10,... | collective-permute-start | bytes 786440 | tf_op jit(solution)/shard_map/ppermute | solution.py:108
  82.3 13.7 %collective-permute-start.9 = (bf16[128,1024]{1,0:T(8,128)(2,1)S(1)}, bf16[128,1024]{1,0:T(8,128)(2,1)S(1)}, u32[]{:S(2)}, u32[]{:S(2)}) collective-permute-start(bf16[128,1024]{1,0:T(8,128)(2,1)S(1)} %get-tuple-element.30), channel_id=1, source_target_pairs={{0,2},{1,3},{2,0},{3,1},{4,6},{5,7},{6,4},{7,5},{8,10},{9,11},{10,... | collective-permute-start | bytes 786440 | tf_op jit(solution)/shard_map/ppermute | solution.py:108
  83.9 22.4 %copy-start.2 = (f32[1024]{0:T(1024)S(1)}, f32[1024]{0:T(1024)}, u32[]{:S(2)}) copy-start(f32[1024]{0:T(1024)} %param.20) | copy-start | bytes 12292
  83.9 22.4 %copy-start.3 = (f32[1024]{0:T(1024)S(1)}, f32[1024]{0:T(1024)}, u32[]{:S(2)}) copy-start(f32[1024]{0:T(1024)} %param.21) | copy-start | bytes 12292
  83.9 22.4 %copy-start.1 = (bf16[2,1024]{1,0:T(2,128)(2,1)S(1)}, bf16[2,1024]{1,0:T(2,128)(2,1)}, u32[]{:S(2)}) copy-start(bf16[2,1024]{1,0:T(2,128)(2,1)} %param.11) | copy-start | bytes 12292
  83.9 16.7 %collective-permute-start.8 = (bf16[128,1024]{1,0:T(8,128)(2,1)S(1)}, bf16[128,1024]{1,0:T(8,128)(2,1)S(1)}, u32[]{:S(2)}, u32[]{:S(2)}) collective-permute-start(bf16[128,1024]{1,0:T(8,128)(2,1)S(1)} %get-tuple-element.29), channel_id=1, source_target_pairs={{0,6},{1,7},{2,4},{3,5},{4,2},{5,3},{6,0},{7,1},{8,14},{9,15},{10,... | collective-permute-start | bytes 786440 | tf_op jit(solution)/shard_map/ppermute | solution.py:108
  100.9 14.5 %collective-permute-start.15 = (bf16[128,1024]{1,0:T(8,128)(2,1)S(1)}, bf16[128,1024]{1,0:T(8,128)(2,1)S(1)}, u32[]{:S(2)}, u32[]{:S(2)}) collective-permute-start(bf16[128,1024]{1,0:T(8,128)(2,1)S(1)} %get-tuple-element.41), channel_id=1, source_target_pairs={{1,8},{3,10},{5,12},{7,14},{8,0},{10,2},{12,4},{14,6},{17,24},{19,... | collective-permute-start | bytes 786440 | tf_op jit(solution)/shard_map/ppermute | solution.py:108
  102.2 13.2 %collective-permute-start.16 = (bf16[128,1024]{1,0:T(8,128)(2,1)S(1)}, bf16[128,1024]{1,0:T(8,128)(2,1)S(1)}, u32[]{:S(2)}, u32[]{:S(2)}) collective-permute-start(bf16[128,1024]{1,0:T(8,128)(2,1)S(1)} %get-tuple-element.40), channel_id=1, source_target_pairs={{1,9},{3,11},{5,13},{7,15},{8,1},{10,3},{12,5},{14,7},{17,25},{19,... | collective-permute-start | bytes 786440 | tf_op jit(solution)/shard_map/ppermute | solution.py:108
  102.9 12.6 %collective-permute-start.14 = (bf16[128,1024]{1,0:T(8,128)(2,1)S(1)}, bf16[128,1024]{1,0:T(8,128)(2,1)S(1)}, u32[]{:S(2)}, u32[]{:S(2)}) collective-permute-start(bf16[128,1024]{1,0:T(8,128)(2,1)S(1)} %get-tuple-element.39), channel_id=1, source_target_pairs={{0,1},{2,3},{4,5},{6,7},{9,8},{11,10},{13,12},{15,14},{16,17},{18,... | collective-permute-start | bytes 786440 | tf_op jit(solution)/shard_map/ppermute | solution.py:108

commit v3 on v2

--- a/solution.py
+++ b/solution.py
@@ -110,18 +110,39 @@
     )
 
 
-def basis_body(block_count, accumulate, square, narrow, *refs):
+def basis_body(block_count, accumulate, square, narrow, load, *refs):
     refs = list(refs)
-    refs.pop(0)
+    which = refs.pop(0)
     blocks = [refs.pop(0) for _ in range(block_count)]
     features = refs.pop(0) if square else None
     gate_ref, up_ref = refs.pop(0), refs.pop(0)
     before = refs.pop(0) if accumulate else None
+    source = refs.pop(0) if load else None
     total = refs.pop(0)
     narrow_ref = refs.pop(0) if narrow else None
     square_ref = refs.pop(0) if square else None
+    loaded = refs.pop(0) if load else None
     lhs = refs.pop(0)
+    arrived = refs.pop(0) if load else None
     tile, block = pl.program_id(0), pl.program_id(1)
+
+    def copies():
+        cols = loaded.shape[1] // load
+        for at in range(load):
+            begin = pl.multiple_of(which[block_count + at] * cols, 128)
+            yield pltpu.make_async_copy(
+                source.at[:, pl.ds(begin, cols)],
+                loaded.at[:, at * cols : (at + 1) * cols],
+                arrived.at[at],
+            )
+
+    if load:
+
+        @pl.when((tile == 0) & (block == 0))
+        def _():
+            for copy in copies():
+                copy.start()
+
     states_at = features.shape[1] - SMALL if square else blocks[0].shape[0] - SMALL
 
     for index, ref in enumerate(blocks):
@@ -168,9 +189,16 @@
         def _():
             narrow_ref[...] = total[...].astype(jnp.bfloat16)
 
+    if load:
+
+        @pl.when((tile == pl.num_programs(0) - 1) & (block == block_count - 1))
+        def _():
+            for copy in copies():
+                copy.wait()
+
 
 def basis_products(
-    blocks, which, features, gate_weight, up_weight, before, columns, square, narrow, tile
+    blocks, which, features, gate_weight, up_weight, before, columns, square, narrow, tile, load=None
 ):
     count = len(blocks)
     m, k = blocks[0].shape
@@ -188,6 +216,9 @@
     if before is not None:
         specs.append(pl.BlockSpec((2, m, tile), lambda j, b, s: (0, 0, base + j)))
         operands.append(before)
+    if load is not None:
+        specs.append(pl.BlockSpec(memory_space=pl.ANY))
+        operands.append(load[0])
     part = pl.BlockSpec((2, m, tile), lambda j, b, s: (0, 0, j))
     outs = [jax.ShapeDtypeStruct((2, m, width), jnp.float32)]
     out_specs = [part]
@@ -197,18 +228,25 @@
     if square:
         outs.append(jax.ShapeDtypeStruct((features.shape[0], 128), jnp.float32))
         out_specs.append(whole(features.shape[0], 128))
+    scratch = [pltpu.VMEM((count, m, k), jnp.bfloat16)]
+    loads = 0
+    if load is not None:
+        loads = which.shape[0] - count
+        outs.append(jax.ShapeDtypeStruct((load[0].shape[0], loads * load[1]), jnp.bfloat16))
+        out_specs.append(pl.BlockSpec(memory_space=pltpu.VMEM))
+        scratch.append(pltpu.SemaphoreType.DMA((loads,)))
     return pl.pallas_call(
-        functools.partial(basis_body, count, before is not None, square, narrow),
+        functools.partial(basis_body, count, before is not None, square, narrow, loads),
         out_shape=outs,
         grid_spec=pltpu.PrefetchScalarGridSpec(
             num_scalar_prefetch=1,
             grid=(tiles, count),
             in_specs=specs,
             out_specs=out_specs,
-            scratch_shapes=[pltpu.VMEM((count, m, k), jnp.bfloat16)],
+            scratch_shapes=scratch,
         ),
         compiler_params=pltpu.CompilerParams(
-            dimension_semantics=("arbitrary", "arbitrary"), vmem_limit_bytes=32 * MIB
+            dimension_semantics=("arbitrary", "arbitrary"), vmem_limit_bytes=16 * MIB
         ),
         cost_estimate=pl.CostEstimate(
             flops=4 * m * k * width * count,
@@ -245,41 +283,55 @@
     )(own, other, features, square_own, square_other)
 
 
-def down_body(count, which, *refs):
-    hidden = refs[:count]
-    weight, *outs = refs[count:]
-    total = None
-    at = 0
-    for ref in hidden:
-        depth = ref.shape[1]
-        term = jnp.dot(ref[...], weight[at : at + depth, :], preferred_element_type=jnp.float32)
-        total = term if total is None else total + term
-        at += depth
-    rows = total.shape[0] // 2
-    for part in range(2):
-        outs[part][...] = total[part * rows : (part + 1) * rows].astype(jnp.bfloat16)
-
-
-def down_products(hidden, down_weight, which, width, tile):
+def down_body(places, cols, hidden, weights, outs):
+    half = hidden[0].shape[0] // 2
+    tile = 512
+    for rows, which, block, targets in places:
+        low, high = rows[0] * half, rows[-1] * half + half
+        for j in range(cols // tile):
+            at = block * cols + j * tile
+            total = None
+            depth_at = 0
+            for ref in hidden:
+                depth = ref.shape[1]
+                term = jnp.dot(
+                    ref[low:high, :],
+                    weights[which][depth_at : depth_at + depth, at : at + tile],
+                    preferred_element_type=jnp.float32,
+                )
+                total = term if total is None else total + term
+                depth_at += depth
+            total = total.astype(jnp.bfloat16)
+            for index, (out, column) in enumerate(targets):
+                to = column + j * tile
+                outs[out][:, to : to + tile] = total[index * half : (index + 1) * half]
+
+
+def down_products(hidden, weights, cols, places, widths, copies=()):
     rows = hidden[0].shape[0]
-    depth = down_weight.shape[0]
-    tiles = width // tile
-    half = pl.BlockSpec((rows // 2, tile), lambda j, s: (0, j))
+    depth = weights[0].shape[0]
+    flops = sum(len(r) * rows * depth * cols for r, *_ in places)
+    vmem = pl.BlockSpec(memory_space=pltpu.VMEM)
+    counts = (len(hidden), len(weights), len(copies))
+
+    def body(*refs):
+        groups, at = [], 0
+        for count in counts:
+            groups.append(refs[at : at + count])
+            at += count
+        outs = refs[at:]
+        down_body(places, cols, groups[0], groups[1], outs)
+        for source, (_, out) in zip(groups[2], copies):
+            outs[out][:, : source.shape[1]] = source[...]
+
     return pl.pallas_call(
-        functools.partial(down_body, len(hidden)),
-        out_shape=[jax.ShapeDtypeStruct((rows // 2, width), jnp.bfloat16)] * 2,
-        grid_spec=pltpu.PrefetchScalarGridSpec(
-            num_scalar_prefetch=1,
-            grid=(tiles,),
-            in_specs=[pl.BlockSpec(h.shape, lambda j, s: (0, 0)) for h in hidden]
-            + [pl.BlockSpec((depth, tile), lambda j, s: (0, s[0] * tiles + j))],
-            out_specs=[half, half],
-        ),
-        compiler_params=pltpu.CompilerParams(vmem_limit_bytes=32 * MIB),
-        cost_estimate=pl.CostEstimate(
-            flops=2 * rows * depth * width, bytes_accessed=2 * depth * width, transcendentals=0
-        ),
-    )(which, *hidden, down_weight)
+        body,
+        out_shape=[jax.ShapeDtypeStruct((rows // 2, width), jnp.bfloat16) for width in widths],
+        in_specs=[vmem] * sum(counts),
+        out_specs=[vmem] * len(widths),
+        compiler_params=pltpu.CompilerParams(vmem_limit_bytes=12 * MIB),
+        cost_estimate=pl.CostEstimate(flops=flops // 16, bytes_accessed=0, transcendentals=0),
+    )(*hidden, *weights, *[c[0] for c in copies])
 
 
 def local_blocks(
@@ -354,13 +406,18 @@
     features = jnp.concatenate([features, onehot], axis=1)
 
     index = lambda *ks: jnp.stack([place ^ k for k in ks]).astype(jnp.int32)
+    gate_weight, up_weight, down_weight = (
+        pltpu.with_memory_space_constraint(weight, pltpu.HBM)
+        for weight in (gate_weight, up_weight, down_weight)
+    )
     weights = (gate_weight, up_weight)
     tile = 512
-    basis, square0 = basis_products(
-        [block], index(0), features, *weights, None, (0, units), True, False, tile
-    )
-    basis, square2 = basis_products(
-        [near[2]], index(2), features, *weights, basis, (0, units), True, False, tile
+    load = (down_weight, cols)
+    basis, square0, down_first = basis_products(
+        [block], index(0, 3, 1), features, *weights, None, (0, units), True, False, tile, load
+    )
+    basis, square2, down_second = basis_products(
+        [near[2]], index(2, 2, 0), features, *weights, basis, (0, units), True, False, tile, load
     )
     cut = units // 2
     rest = [near[1], near[3]]
@@ -379,16 +436,39 @@
         for own, other in ((own_a, other_a), (own_b, other_b))
     ]
 
-    partial = {
-        k: down_products(hidden, down_weight, index(k), cols, 256) for k in (3, 1, 2, 0)
-    }
-    sums = []
-    for part in range(2):
-        total = partial[0][part].astype(f32)
-        for k in (3, 1, 2):
-            got = send(partial[k][part], [((t, d), (t ^ k, d)) for t, d in every])
-            total = total + got.astype(f32)
-        sums.append(total.astype(bf16))
+    both, lower, upper = (0, 1), (0,), (1,)
+    step = lambda array, k: send(array, [((t, d), (t ^ k, d)) for t, d in every])
+    x_pair, diagonal_upper = down_products(
+        hidden,
+        [down_first],
+        cols,
+        [(both, 0, 0, [(0, 0), (1, 0)]), (lower, 0, 1, [(0, cols)])],
+        [2 * cols, cols],
+    )
+    got_x = step(x_pair, 1)
+    (z_pair,) = down_products(
+        hidden,
+        [down_second],
+        cols,
+        [(upper, 0, 0, [(0, cols)])],
+        [2 * cols],
+        [(diagonal_upper, 0)],
+    )
+    got_z = step(z_pair, 2)
+    z_lower, x_upper, own_lower, own_upper = down_products(
+        hidden,
+        [down_first, down_second],
+        cols,
+        [(lower, 1, 0, [(0, 0)]), (upper, 0, 1, [(1, 0)]), (both, 1, 1, [(2, 0), (3, 0)])],
+        [cols] * 4,
+    )
+    add = lambda *parts: sum(part.astype(f32) for part in parts).astype(bf16)
+    got_lower = step(add(z_lower, got_x[:, :cols]), 2)
+    got_upper = step(add(x_upper, got_z[:, :cols]), 1)
+    sums = [
+        add(own_lower, got_x[:, cols:], got_lower),
+        add(own_upper, got_z[:, cols:], got_upper),
+    ]
     far = [
         send(sums[part], [((t, 1 - t // 4), (t ^ 4, part)) for t in range(TP)])
         for part in range(2)
@@ -415,8 +495,8 @@
             jnp.sum(wide_out * (head_gain * value_weight), axis=1),
         ]
     )
-    totals = lax.all_to_all(jnp.broadcast_to(totals, (TP, 2, rows)), "tp", 0, 0)
-    totals = jnp.sum(totals, axis=0)
+    for k in (1, 2, 4):
+        totals = totals + step(totals, k)
     values = totals[1] * lax.rsqrt(totals[0] / full_width + epsilon)
     return (
         output_local.reshape(states, cands, cols),

time: 128 us -> 125 us (0.977)
  blocking collectives: 9.94 us -> 0 us
  starting transfers between devices: 25.8 us -> 32 us
  local copies, waits for them, and re-layouts: 2.24 us -> 6.81 us
  Pallas kernels: 54 us -> 51.6 us
    pallas_call x4 -> x3, Pallas kernels: 18.9 us -> 7 us  [down_products(): pl.pallas_call(body, out_shape=[jax.ShapeDtypeStruct((rows // 2, width),...]
    all_to_all x1 -> x0, blocking collectives: 9.94 us -> none  [local_blocks(): totals = lax.all_to_all(jnp.broadcast_to(totals, (TP, 2, rows)), 'tp', 0, 0)]
    pallas_call x4, Pallas kernels: 32.4 us -> 41.9 us  [basis_products(): pl.pallas_call(functools.partial(basis_body, count, before is not None, s...]
    ppermute x17 -> x18, starting transfers between devices: 25.8 us -> 32 us  [send(): lax.ppermute(array, ('tp', 'dp'), [(2 * st + sd, 2 * dt + dd) for (st, sd...]
    unnamed x8 -> x12, local copies, waits for them, and re-layouts: 0.02 us -> 4.6 us
    ppermute x17 -> x18, waiting for transfers between devices: 29.4 us -> 28.4 us  [send(): lax.ppermute(array, ('tp', 'dp'), [(2 * st + sd, 2 * dt + dd) for (st, sd...]
  transfers between devices with their start and end apart: 17 -> 18, of which waited for: 8 -> 10; matrix products, arithmetic and copies ran while one was open for 2% -> 2% of each run, Pallas kernels for 31% -> 28%
where the time goes in v3:
time: 125 us
  Pallas kernels  51.6 us (41%)
  starting transfers between devices  32 us (26%)
  waiting for transfers between devices  28.4 us (23%)
  local copies, waits for them, and re-layouts  6.81 us (5%)
  other arithmetic  4.55 us (4%)
    pallas_call x4, Pallas kernels, basis_products(): pl.pallas_call(functools.partial(basis_body, count, before is not None, s...  41.9 us
    ppermute x18, starting transfers between devices, send(): lax.ppermute(array, ('tp', 'dp'), [(2 * st + sd, 2 * dt + dd) for (st, sd...  32 us
    ppermute x18, waiting for transfers between devices, send(): lax.ppermute(array, ('tp', 'dp'), [(2 * st + sd, 2 * dt + dd) for (st, sd...  28.4 us
    pallas_call x3, Pallas kernels, down_products(): pl.pallas_call(body, out_shape=[jax.ShapeDtypeStruct((rows // 2, width),...  7 us
    unnamed x12, local copies, waits for them, and re-layouts  4.6 us
    pallas_call x2, Pallas kernels, hidden_units(): pl.pallas_call(functools.partial(hidden_body, width), out_shape=jax.Shape...  2.67 us
  transfers between devices with their start and end apart: 18, of which 10 were waited for; matrix products, arithmetic and copies ran while one was open for 2% of the time, Pallas kernels for 28%

profile of v3, /device:TPU:0, one launch (start us, length us, event | category | flops | bytes accessed | tf_op | source)
XLA Modules:
  0.0 124.6 jit_solution(5577606756364091641)
XLA Ops:
  3.1 4.1 %collective-permute-start = (bf16[80,1024]{1,0:T(8,128)(2,1)S(1)}, bf16[80,1024]{1,0:T(8,128)(2,1)S(1)}, u32[]{:S(2)}, u32[]{:S(2)}) collective-permute-start(bf16[80,1024]{1,0:T(8,128)(2,1)S(1)} %concatenate.17), channel_id=1, source_target_pairs={{0,8},{2,10},{4,12},{6,14},{9,1},{11,3},{13,5},{15,7},{1,0},{3,2},... | collective-permute-start | bytes 491528 | tf_op jit(solution)/shard_map/ppermute | solution.py:108
  8.3 2.2 %collective-permute-done = bf16[80,1024]{1,0:T(8,128)(2,1)S(1)} collective-permute-done((bf16[80,1024]{1,0:T(8,128)(2,1)S(1)}, bf16[80,1024]{1,0:T(8,128)(2,1)S(1)}, u32[]{:S(2)}, u32[]{:S(2)}) %collective-permute-start) | collective-permute-done | bytes 163872 | tf_op jit(solution)/shard_map/ppermute | solution.py:108
  10.8 1.6 %collective-permute-start.2 = (bf16[144,1024]{1,0:T(8,128)(2,1)S(1)}, bf16[144,1024]{1,0:T(8,128)(2,1)S(1)}, u32[]{:S(2)}, u32[]{:S(2)}) collective-permute-start(bf16[144,1024]{1,0:T(8,128)(2,1)S(1)} %concatenate.20.refs_1_), channel_id=1, source_target_pairs={{0,2},{1,3},{2,0},{3,1},{4,6},{5,7},{6,4},{7,5},{8,10},{9,11},{10,... | collective-permute-start | bytes 884744 | tf_op jit(solution)/shard_map/ppermute | solution.py:108
  12.4 6.2 %collective-permute-start.3 = (bf16[144,1024]{1,0:T(8,128)(2,1)S(1)}, bf16[144,1024]{1,0:T(8,128)(2,1)S(1)}, u32[]{:S(2)}, u32[]{:S(2)}) collective-permute-start(bf16[144,1024]{1,0:T(8,128)(2,1)S(1)} %concatenate.20.refs_1_), channel_id=1, source_target_pairs={{0,6},{1,7},{2,4},{3,5},{4,2},{5,3},{6,0},{7,1},{8,14},{9,15},{10,... | collective-permute-start | bytes 884744 | tf_op jit(solution)/shard_map/ppermute | solution.py:108
  18.9 1.3 %fusion.9 = bf16[256,128]{1,0:T(8,128)(2,1)S(1)} fusion(s32[128]{0:T(128)S(1)} %iota_add_fusion, s32[256]{0:T(256)S(1)} %add.125, f32[128]{0:T(128)} %param.14, f32[128]{0:T(128)} %param.13), kind=kLoop, calls=%fused_computation.26 | loop fusion | flops 393216 | bytes 68096 | tf_op jit(solution)/shard_map/convert_element_type | solution.py:19
  20.2 10.9 %shard_map.122 = (f32[2,144,3072]{2,1,0:T(8,128)S(1)}, f32[256,128]{1,0:T(8,128)S(1)}, bf16[3072,2048]{1,0:T(8,128)(2,1)S(1)}) custom-call(s32[3]{0:T(128)S(1)} %pad_add_fusion.2.refs_0_, bf16[144,1024]{1,0:T(8,128)(2,1)S(1)} %concatenate.20.refs_1_, bf16[256,144]{1,0:T(8,128)(2,1)S(1)} %pad_maximum_fusion.refs_2_.refs_3_.features, ...), custom_call_target="tpu_custom_call" | custom-call | flops 1811939328 | bytes 12582912 | tf_op jit(solution)/shard_map/pallas_call | solution.py:238
  31.2 1.0 collective-permute-done.4.refs_1_
  32.2 11.0 %shard_map.123 = (f32[2,144,3072]{2,1,0:T(8,128)S(1)}, f32[256,128]{1,0:T(8,128)S(1)}, bf16[3072,2048]{1,0:T(8,128)(2,1)S(1)}) custom-call(s32[3]{0:T(128)S(1)} %pad_add_fusion.1.refs_0_, bf16[144,1024]{1,0:T(8,128)(2,1)S(1)} %collective-permute-done.4.refs_1_, bf16[256,144]{1,0:T(8,128)(2,1)S(1)} %pad_maximum_fusion.refs_2_.refs_3_.features, ...), custom_call_target="tpu_custom_call" | custom-call | flops 1811939328 | bytes 12582912 | tf_op jit(solution)/shard_map/pallas_call | solution.py:238
  43.2 11.7 %shard_map.124 = (f32[2,144,1536]{2,1,0:T(8,128)S(1)}, bf16[2,144,1536]{2,1,0:T(8,128)(2,1)S(1)}, f32[256,128]{1,0:T(8,128)S(1)}) custom-call(s32[2]{0:T(128)S(1)} %pad_add_fusion.refs_0_, bf16[144,1024]{1,0:T(8,128)(2,1)S(1)} %collective-permute-done.2.refs_1_, bf16[144,1024]{1,0:T(8,128)(2,1)S(1)} %collective-permute-done.3.refs_2_, ...), custom_call_target="tpu_custom_call" | custom-call | flops 1811939328 | bytes 12582912 | tf_op jit(solution)/shard_map/pallas_call | solution.py:238
  55.0 8.3 %shard_map.126 = (f32[2,144,1536]{2,1,0:T(8,128)S(1)}, bf16[2,144,1536]{2,1,0:T(8,128)(2,1)S(1)}) custom-call(s32[2]{0:T(128)S(1)} %pad_add_fusion.refs_0_, bf16[144,1024]{1,0:T(8,128)(2,1)S(1)} %collective-permute-done.2.refs_1_, bf16[144,1024]{1,0:T(8,128)(2,1)S(1)} %collective-permute-done.3.refs_2_, bf16[4096,3072]{1,0:T(8,128)(2,1)} %refs_3_.5, ...), custom_call_target="tpu_custom_call" | custom-call | flops 1811939328 | bytes 12582912 | tf_op jit(solution)/shard_map/pallas_call | solution.py:238
  64.0 2.1 %collective-permute-done.6.square_other = f32[256,128]{1,0:T(8,128)S(1)} collective-permute-done((f32[256,128]{1,0:T(8,128)S(1)}, f32[256,128]{1,0:T(8,128)S(1)}, u32[]{:S(2)}, u32[]{:S(2)}) %collective-permute-start.6) | collective-permute-done | bytes 131104 | tf_op jit(solution)/shard_map/ppermute | solution.py:108
  66.1 1.3 %shard_map.125.refs_0_ = bf16[256,1536]{1,0:T(8,128)(2,1)S(1)} custom-call(f32[2,144,1536]{2,1,0:T(8,128)S(1)} %get-tuple-element.21.own, bf16[2,144,1536]{2,1,0:T(8,128)(2,1)S(1)} %collective-permute-done.5.other, bf16[256,144]{1,0:T(8,128)(2,1)S(1)} %pad_maximum_fusion.refs_2_.refs_3_.features, f32[256,128]{1,0:T(8,128)S(1)} %add_add_fusion.square_own, ...), custom_call_target="tpu_custom_call" | custom-call | flops 226492416 | bytes 2654208 | tf_op jit(solution)/shard_map/pallas_call | solution.py:273
  67.5 1.3 %shard_map.127.refs_1_ = bf16[256,1536]{1,0:T(8,128)(2,1)S(1)} custom-call(f32[2,144,1536]{2,1,0:T(8,128)S(1)} %get-tuple-element.26.own, bf16[2,144,1536]{2,1,0:T(8,128)(2,1)S(1)} %collective-permute-done.7.other, bf16[256,144]{1,0:T(8,128)(2,1)S(1)} %pad_maximum_fusion.refs_2_.refs_3_.features, f32[256,128]{1,0:T(8,128)S(1)} %add_add_fusion.square_own, ...), custom_call_target="tpu_custom_call" | custom-call | flops 226492416 | bytes 2654208 | tf_op jit(solution)/shard_map/pallas_call | solution.py:273
  68.8 2.6 %shard_map.129 = (bf16[128,2048]{1,0:T(8,128)(2,1)S(1)}, bf16[128,1024]{1,0:T(8,128)(2,1)S(1)}) custom-call(bf16[256,1536]{1,0:T(8,128)(2,1)S(1)} %shard_map.125.refs_0_, bf16[256,1536]{1,0:T(8,128)(2,1)S(1)} %shard_map.127.refs_1_, bf16[3072,2048]{1,0:T(8,128)(2,1)S(1)} %get-tuple-element.28.refs_2_), custom_call_target="tpu_custom_call" | custom-call | flops 150994944 | tf_op jit(solution)/shard_map/pallas_call | solution.py:327
  71.4 1.0 shard_map.130
  72.4 1.7 %collective-permute-start.10 = (bf16[128,2048]{1,0:T(8,128)(2,1)S(1)}, bf16[128,2048]{1,0:T(8,128)(2,1)S(1)}, u32[]{:S(2)}, u32[]{:S(2)}) collective-permute-start(bf16[128,2048]{1,0:T(8,128)(2,1)S(1)} %shard_map.130), channel_id=1, source_target_pairs={{0,4},{1,5},{2,6},{3,7},{4,0},{5,1},{6,2},{7,3},{8,12},{9,13},{10,... | collective-permute-start | bytes 1572872 | tf_op jit(solution)/shard_map/ppermute | solution.py:108
  74.2 1.4 %collective-permute-start.8 = (bf16[128,2048]{1,0:T(8,128)(2,1)S(1)}, bf16[128,2048]{1,0:T(8,128)(2,1)S(1)}, u32[]{:S(2)}, u32[]{:S(2)}) collective-permute-start(bf16[128,2048]{1,0:T(8,128)(2,1)S(1)} %get-tuple-element.31), channel_id=1, source_target_pairs={{0,2},{1,3},{2,0},{3,1},{4,6},{5,7},{6,4},{7,5},{8,10},{9,11},{10,... | collective-permute-start | bytes 1572872 | tf_op jit(solution)/shard_map/ppermute | solution.py:108
  75.6 4.6 %copy-done.2 = bf16[3072,2048]{1,0:T(8,128)(2,1)S(1)} copy-done((bf16[3072,2048]{1,0:T(8,128)(2,1)S(1)}, bf16[3072,2048]{1,0:T(8,128)(2,1)}, u32[]{:S(2)}) %copy-start.2) | copy-done | bytes 12582936
  80.2 3.4 %shard_map.128 = (bf16[128,1024]{1,0:T(8,128)(2,1)S(1)}, bf16[128,1024]{1,0:T(8,128)(2,1)S(1)}, bf16[128,1024]{1,0:T(8,128)(2,1)S(1)}, bf16[128,1024]{1,0:T(8,128)(2,1)S(1)}) custom-call(bf16[256,1536]{1,0:T(8,128)(2,1)S(1)} %shard_map.125.refs_0_, bf16[256,1536]{1,0:T(8,128)(2,1)S(1)} %shard_map.127.refs_1_, ...), custom_call_target="tpu_custom_call" | custom-call | flops 201326592 | tf_op jit(solution)/shard_map/pallas_call | solution.py:327
  83.6 3.1 %collective-permute-done.10 = bf16[128,2048]{1,0:T(8,128)(2,1)S(1)} collective-permute-done((bf16[128,2048]{1,0:T(8,128)(2,1)S(1)}, bf16[128,2048]{1,0:T(8,128)(2,1)S(1)}, u32[]{:S(2)}, u32[]{:S(2)}) %collective-permute-start.10) | collective-permute-done | bytes 524320 | tf_op jit(solution)/shard_map/ppermute | solution.py:108
  86.8 1.4 %collective-permute-start.11 = (bf16[128,1024]{1,0:T(8,128)(2,1)S(1)}, bf16[128,1024]{1,0:T(8,128)(2,1)S(1)}, u32[]{:S(2)}, u32[]{:S(2)}) collective-permute-start(bf16[128,1024]{1,0:T(8,128)(2,1)S(1)} %add_convert_fusion.2), channel_id=1, source_target_pairs={{0,2},{1,3},{2,0},{3,1},{4,6},{5,7},{6,4},{7,5},{8,10},{9,11},{10,... | collective-permute-start | bytes 786440 | tf_op jit(solution)/shard_map/ppermute | solution.py:108
  88.3 1.8 %collective-permute-start.9 = (bf16[128,1024]{1,0:T(8,128)(2,1)S(1)}, bf16[128,1024]{1,0:T(8,128)(2,1)S(1)}, u32[]{:S(2)}, u32[]{:S(2)}) collective-permute-start(bf16[128,1024]{1,0:T(8,128)(2,1)S(1)} %add_convert_fusion.4), channel_id=1, source_target_pairs={{0,4},{1,5},{2,6},{3,7},{4,0},{5,1},{6,2},{7,3},{8,12},{9,13},{10,... | collective-permute-start | bytes 786440 | tf_op jit(solution)/shard_map/ppermute | solution.py:108
  90.1 4.5 %collective-permute-done.11 = bf16[128,1024]{1,0:T(8,128)(2,1)S(1)} collective-permute-done((bf16[128,1024]{1,0:T(8,128)(2,1)S(1)}, bf16[128,1024]{1,0:T(8,128)(2,1)S(1)}, u32[]{:S(2)}, u32[]{:S(2)}) %collective-permute-start.11) | collective-permute-done | bytes 262176 | tf_op jit(solution)/shard_map/ppermute | solution.py:108
  94.6 1.5 %collective-permute-done.9 = bf16[128,1024]{1,0:T(8,128)(2,1)S(1)} collective-permute-done((bf16[128,1024]{1,0:T(8,128)(2,1)S(1)}, bf16[128,1024]{1,0:T(8,128)(2,1)S(1)}, u32[]{:S(2)}, u32[]{:S(2)}) %collective-permute-start.9) | collective-permute-done | bytes 262176 | tf_op jit(solution)/shard_map/ppermute | solution.py:108
  96.4 1.3 %collective-permute-start.13 = (bf16[128,1024]{1,0:T(8,128)(2,1)S(1)}, bf16[128,1024]{1,0:T(8,128)(2,1)S(1)}, u32[]{:S(2)}, u32[]{:S(2)}) collective-permute-start(bf16[128,1024]{1,0:T(8,128)(2,1)S(1)} %get-tuple-element.41), channel_id=1, source_target_pairs={{1,8},{3,10},{5,12},{7,14},{8,0},{10,2},{12,4},{14,6},{17,24},{19,... | collective-permute-start | bytes 786440 | tf_op jit(solution)/shard_map/ppermute | solution.py:108
  98.3 6.7 %collective-permute-start.12 = (bf16[128,1024]{1,0:T(8,128)(2,1)S(1)}, bf16[128,1024]{1,0:T(8,128)(2,1)S(1)}, u32[]{:S(2)}, u32[]{:S(2)}) collective-permute-start(bf16[128,1024]{1,0:T(8,128)(2,1)S(1)} %get-tuple-element.39), channel_id=1, source_target_pairs={{0,1},{2,3},{4,5},{6,7},{9,8},{11,10},{13,12},{15,14},{16,17},{18,... | collective-permute-start | bytes 786440 | tf_op jit(solution)/shard_map/ppermute | solution.py:108
  105.4 5.8 %collective-permute-done.13 = bf16[128,1024]{1,0:T(8,128)(2,1)S(1)} collective-permute-done((bf16[128,1024]{1,0:T(8,128)(2,1)S(1)}, bf16[128,1024]{1,0:T(8,128)(2,1)S(1)}, u32[]{:S(2)}, u32[]{:S(2)}) %collective-permute-start.13) | collective-permute-done | bytes 262176 | tf_op jit(solution)/shard_map/ppermute | solution.py:108
  112.1 1.1 collective-permute-start.15
  113.2 2.5 %collective-permute-done.15 = f32[2,128]{1,0:T(2,128)S(1)} collective-permute-done((f32[2,128]{1,0:T(2,128)S(1)}, f32[2,128]{1,0:T(2,128)S(1)}, u32[]{:S(2)}, u32[]{:S(2)}) %collective-permute-start.15) | collective-permute-done | bytes 1056 | tf_op jit(solution)/shard_map/ppermute | solution.py:108
  115.8 3.6 %collective-permute-done.16 = f32[2,128]{1,0:T(2,128)S(1)} collective-permute-done((f32[2,128]{1,0:T(2,128)S(1)}, f32[2,128]{1,0:T(2,128)S(1)}, u32[]{:S(2)}, u32[]{:S(2)}) %collective-permute-start.16) | collective-permute-done | bytes 1056 | tf_op jit(solution)/shard_map/ppermute | solution.py:108
  119.4 2.4 %collective-permute-start.17 = (f32[2,128]{1,0:T(2,128)S(1)}, f32[2,128]{1,0:T(2,128)S(1)}, u32[]{:S(2)}, u32[]{:S(2)}) collective-permute-start(f32[2,128]{1,0:T(2,128)S(1)} %fusion.22), channel_id=1, source_target_pairs={{0,8},{1,9},{2,10},{3,11},{4,12},{5,13},{6,14},{7,15},{8,0},{9,1},... | collective-permute-start | bytes 3080 | tf_op jit(solution)/shard_map/ppermute | solution.py:108
  121.8 2.1 %collective-permute-done.17 = f32[2,128]{1,0:T(2,128)S(1)} collective-permute-done((f32[2,128]{1,0:T(2,128)S(1)}, f32[2,128]{1,0:T(2,128)S(1)}, u32[]{:S(2)}, u32[]{:S(2)}) %collective-permute-start.17) | collective-permute-done | bytes 1056 | tf_op jit(solution)/shard_map/ppermute | solution.py:108
  (70 shorter events, 7.9 us)
Async XLA Ops:
  0.6 1.6 %copy-start = (bf16[128,1024]{1,0:T(8,128)(2,1)S(1)}, bf16[128,1024]{1,0:T(8,128)(2,1)}, u32[]{:S(2)}) copy-start(bf16[128,1024]{1,0:T(8,128)(2,1)} %param.15) | copy-start | bytes 786436
  3.1 7.4 %collective-permute-start = (bf16[80,1024]{1,0:T(8,128)(2,1)S(1)}, bf16[80,1024]{1,0:T(8,128)(2,1)S(1)}, u32[]{:S(2)}, u32[]{:S(2)}) collective-permute-start(bf16[80,1024]{1,0:T(8,128)(2,1)S(1)} %concatenate.17), channel_id=1, source_target_pairs={{0,8},{2,10},{4,12},{6,14},{9,1},{11,3},{13,5},{15,7},{1,0},{3,2},... | collective-permute-start | bytes 491528 | tf_op jit(solution)/shard_map/ppermute | solution.py:108
  7.2 3.3 %collective-permute-start.1 = (bf16[80,1024]{1,0:T(8,128)(2,1)S(1)}, bf16[80,1024]{1,0:T(8,128)(2,1)S(1)}, u32[]{:S(2)}, u32[]{:S(2)}) collective-permute-start(bf16[80,1024]{1,0:T(8,128)(2,1)S(1)} %concatenate.17), channel_id=1, source_target_pairs={{1,8},{3,10},{5,12},{7,14},{8,1},{10,3},{12,5},{14,7},{17,24},{19,... | collective-permute-start | bytes 491528 | tf_op jit(solution)/shard_map/ppermute | solution.py:108
  10.8 32.4 %collective-permute-start.2 = (bf16[144,1024]{1,0:T(8,128)(2,1)S(1)}, bf16[144,1024]{1,0:T(8,128)(2,1)S(1)}, u32[]{:S(2)}, u32[]{:S(2)}) collective-permute-start(bf16[144,1024]{1,0:T(8,128)(2,1)S(1)} %concatenate.20.refs_1_), channel_id=1, source_target_pairs={{0,2},{1,3},{2,0},{3,1},{4,6},{5,7},{6,4},{7,5},{8,10},{9,11},{10,... | collective-permute-start | bytes 884744 | tf_op jit(solution)/shard_map/ppermute | solution.py:108
  12.4 30.8 %collective-permute-start.3 = (bf16[144,1024]{1,0:T(8,128)(2,1)S(1)}, bf16[144,1024]{1,0:T(8,128)(2,1)S(1)}, u32[]{:S(2)}, u32[]{:S(2)}) collective-permute-start(bf16[144,1024]{1,0:T(8,128)(2,1)S(1)} %concatenate.20.refs_1_), channel_id=1, source_target_pairs={{0,6},{1,7},{2,4},{3,5},{4,2},{5,3},{6,0},{7,1},{8,14},{9,15},{10,... | collective-permute-start | bytes 884744 | tf_op jit(solution)/shard_map/ppermute | solution.py:108
  18.6 13.6 %collective-permute-start.4 = (bf16[144,1024]{1,0:T(8,128)(2,1)S(1)}, bf16[144,1024]{1,0:T(8,128)(2,1)S(1)}, u32[]{:S(2)}, u32[]{:S(2)}) collective-permute-start(bf16[144,1024]{1,0:T(8,128)(2,1)S(1)} %concatenate.20.refs_1_), channel_id=1, source_target_pairs={{0,4},{1,5},{2,6},{3,7},{4,0},{5,1},{6,2},{7,3},{8,12},{9,13},{10,... | collective-permute-start | bytes 884744 | tf_op jit(solution)/shard_map/ppermute | solution.py:108
  43.2 28.2 %copy-start.1 = (bf16[3072,2048]{1,0:T(8,128)(2,1)}, bf16[3072,2048]{1,0:T(8,128)(2,1)S(1)}, u32[]{:S(2)}) copy-start(bf16[3072,2048]{1,0:T(8,128)(2,1)S(1)} %get-tuple-element.29.refs_3_.refs_2_) | copy-start | bytes 37748740
  54.9 11.2 %collective-permute-start.5 = (bf16[2,144,1536]{2,1,0:T(8,128)(2,1)S(1)}, bf16[2,144,1536]{2,1,0:T(8,128)(2,1)S(1)}, u32[]{:S(2)}, u32[]{:S(2)}) collective-permute-start(bf16[2,144,1536]{2,1,0:T(8,128)(2,1)S(1)} %get-tuple-element.22), channel_id=1, source_target_pairs={{0,1},{1,0},{2,3},{3,2},{4,5},{5,4},{6,7},{7,6},{8,9},{9,8},{10,11... | collective-permute-start | bytes 2654216 | tf_op jit(solution)/shard_map/ppermute | solution.py:108
  63.3 4.1 %collective-permute-start.7 = (bf16[2,144,1536]{2,1,0:T(8,128)(2,1)S(1)}, bf16[2,144,1536]{2,1,0:T(8,128)(2,1)S(1)}, u32[]{:S(2)}, u32[]{:S(2)}) collective-permute-start(bf16[2,144,1536]{2,1,0:T(8,128)(2,1)S(1)} %get-tuple-element.27), channel_id=1, source_target_pairs={{0,1},{1,0},{2,3},{3,2},{4,5},{5,4},{6,7},{7,6},{8,9},{9,8},{10,11... | collective-permute-start | bytes 2654216 | tf_op jit(solution)/shard_map/ppermute | solution.py:108
  63.9 2.2 %collective-permute-start.6 = (f32[256,128]{1,0:T(8,128)S(1)}, f32[256,128]{1,0:T(8,128)S(1)}, u32[]{:S(2)}, u32[]{:S(2)}) collective-permute-start(f32[256,128]{1,0:T(8,128)S(1)} %add_add_fusion.square_own), channel_id=1, source_target_pairs={{0,1},{1,0},{2,3},{3,2},{4,5},{5,4},{6,7},{7,6},{8,9},{9,8},{10,11... | collective-permute-start | bytes 393224 | tf_op jit(solution)/shard_map/ppermute | solution.py:108
  72.4 14.3 %collective-permute-start.10 = (bf16[128,2048]{1,0:T(8,128)(2,1)S(1)}, bf16[128,2048]{1,0:T(8,128)(2,1)S(1)}, u32[]{:S(2)}, u32[]{:S(2)}) collective-permute-start(bf16[128,2048]{1,0:T(8,128)(2,1)S(1)} %shard_map.130), channel_id=1, source_target_pairs={{0,4},{1,5},{2,6},{3,7},{4,0},{5,1},{6,2},{7,3},{8,12},{9,13},{10,... | collective-permute-start | bytes 1572872 | tf_op jit(solution)/shard_map/ppermute | solution.py:108
  74.2 14.0 %collective-permute-start.8 = (bf16[128,2048]{1,0:T(8,128)(2,1)S(1)}, bf16[128,2048]{1,0:T(8,128)(2,1)S(1)}, u32[]{:S(2)}, u32[]{:S(2)}) collective-permute-start(bf16[128,2048]{1,0:T(8,128)(2,1)S(1)} %get-tuple-element.31), channel_id=1, source_target_pairs={{0,2},{1,3},{2,0},{3,1},{4,6},{5,7},{6,4},{7,5},{8,10},{9,11},{10,... | collective-permute-start | bytes 1572872 | tf_op jit(solution)/shard_map/ppermute | solution.py:108
  75.6 4.6 %copy-start.2 = (bf16[3072,2048]{1,0:T(8,128)(2,1)S(1)}, bf16[3072,2048]{1,0:T(8,128)(2,1)}, u32[]{:S(2)}) copy-start(bf16[3072,2048]{1,0:T(8,128)(2,1)} %copy-done.1) | copy-start | bytes 37748740
  80.2 24.9 %copy-start.4 = (f32[1024]{0:T(1024)S(1)}, f32[1024]{0:T(1024)}, u32[]{:S(2)}) copy-start(f32[1024]{0:T(1024)} %param.20) | copy-start | bytes 12292
  80.2 24.9 %copy-start.5 = (f32[1024]{0:T(1024)S(1)}, f32[1024]{0:T(1024)}, u32[]{:S(2)}) copy-start(f32[1024]{0:T(1024)} %param.21) | copy-start | bytes 12292
  80.2 24.9 %copy-start.3 = (bf16[2,1024]{1,0:T(2,128)(2,1)S(1)}, bf16[2,1024]{1,0:T(2,128)(2,1)}, u32[]{:S(2)}) copy-start(bf16[2,1024]{1,0:T(2,128)(2,1)} %param.11) | copy-start | bytes 12292
  86.8 7.8 %collective-permute-start.11 = (bf16[128,1024]{1,0:T(8,128)(2,1)S(1)}, bf16[128,1024]{1,0:T(8,128)(2,1)S(1)}, u32[]{:S(2)}, u32[]{:S(2)}) collective-permute-start(bf16[128,1024]{1,0:T(8,128)(2,1)S(1)} %add_convert_fusion.2), channel_id=1, source_target_pairs={{0,2},{1,3},{2,0},{3,1},{4,6},{5,7},{6,4},{7,5},{8,10},{9,11},{10,... | collective-permute-start | bytes 786440 | tf_op jit(solution)/shard_map/ppermute | solution.py:108
  88.3 7.8 %collective-permute-start.9 = (bf16[128,1024]{1,0:T(8,128)(2,1)S(1)}, bf16[128,1024]{1,0:T(8,128)(2,1)S(1)}, u32[]{:S(2)}, u32[]{:S(2)}) collective-permute-start(bf16[128,1024]{1,0:T(8,128)(2,1)S(1)} %add_convert_fusion.4), channel_id=1, source_target_pairs={{0,4},{1,5},{2,6},{3,7},{4,0},{5,1},{6,2},{7,3},{8,12},{9,13},{10,... | collective-permute-start | bytes 786440 | tf_op jit(solution)/shard_map/ppermute | solution.py:108
  96.4 14.8 %collective-permute-start.13 = (bf16[128,1024]{1,0:T(8,128)(2,1)S(1)}, bf16[128,1024]{1,0:T(8,128)(2,1)S(1)}, u32[]{:S(2)}, u32[]{:S(2)}) collective-permute-start(bf16[128,1024]{1,0:T(8,128)(2,1)S(1)} %get-tuple-element.41), channel_id=1, source_target_pairs={{1,8},{3,10},{5,12},{7,14},{8,0},{10,2},{12,4},{14,6},{17,24},{19,... | collective-permute-start | bytes 786440 | tf_op jit(solution)/shard_map/ppermute | solution.py:108
  97.7 13.5 %collective-permute-start.14 = (bf16[128,1024]{1,0:T(8,128)(2,1)S(1)}, bf16[128,1024]{1,0:T(8,128)(2,1)S(1)}, u32[]{:S(2)}, u32[]{:S(2)}) collective-permute-start(bf16[128,1024]{1,0:T(8,128)(2,1)S(1)} %get-tuple-element.40), channel_id=1, source_target_pairs={{1,9},{3,11},{5,13},{7,15},{8,1},{10,3},{12,5},{14,7},{17,25},{19,... | collective-permute-start | bytes 786440 | tf_op jit(solution)/shard_map/ppermute | solution.py:108
  98.3 12.8 %collective-permute-start.12 = (bf16[128,1024]{1,0:T(8,128)(2,1)S(1)}, bf16[128,1024]{1,0:T(8,128)(2,1)S(1)}, u32[]{:S(2)}, u32[]{:S(2)}) collective-permute-start(bf16[128,1024]{1,0:T(8,128)(2,1)S(1)} %get-tuple-element.39), channel_id=1, source_target_pairs={{0,1},{2,3},{4,5},{6,7},{9,8},{11,10},{13,12},{15,14},{16,17},{18,... | collective-permute-start | bytes 786440 | tf_op jit(solution)/shard_map/ppermute | solution.py:108
  112.1 3.6 %collective-permute-start.15 = (f32[2,128]{1,0:T(2,128)S(1)}, f32[2,128]{1,0:T(2,128)S(1)}, u32[]{:S(2)}, u32[]{:S(2)}) collective-permute-start(f32[2,128]{1,0:T(2,128)S(1)} %pad_maximum_fusion.2), channel_id=1, source_target_pairs={{0,2},{1,3},{2,0},{3,1},{4,6},{5,7},{6,4},{7,5},{8,10},{9,11},{10,... | collective-permute-start | bytes 3080 | tf_op jit(solution)/shard_map/ppermute | solution.py:108
  115.8 3.6 %collective-permute-start.16 = (f32[2,128]{1,0:T(2,128)S(1)}, f32[2,128]{1,0:T(2,128)S(1)}, u32[]{:S(2)}, u32[]{:S(2)}) collective-permute-start(f32[2,128]{1,0:T(2,128)S(1)} %fusion.20), channel_id=1, source_target_pairs={{0,4},{1,5},{2,6},{3,7},{4,0},{5,1},{6,2},{7,3},{8,12},{9,13},{10,... | collective-permute-start | bytes 3080 | tf_op jit(solution)/shard_map/ppermute | solution.py:108
  119.4 4.5 %collective-permute-start.17 = (f32[2,128]{1,0:T(2,128)S(1)}, f32[2,128]{1,0:T(2,128)S(1)}, u32[]{:S(2)}, u32[]{:S(2)}) collective-permute-start(f32[2,128]{1,0:T(2,128)S(1)} %fusion.22), channel_id=1, source_target_pairs={{0,8},{1,9},{2,10},{3,11},{4,12},{5,13},{6,14},{7,15},{8,0},{9,1},... | collective-permute-start | bytes 3080 | tf_op jit(solution)/shard_map/ppermute | solution.py:108

commit v4 on v0

--- a/solution.py
+++ b/solution.py
@@ -1,8 +1,11 @@
+import functools
 import math
 
 import jax
 import jax.numpy as jnp
 from jax import lax
+from jax.experimental import pallas as pl
+from jax.experimental.pallas import tpu as pltpu
 from jax.sharding import PartitionSpec as P
 
 epsilon = 1e-05
@@ -22,7 +25,7 @@
     return jnp.sum(wide_out * (head_gain * value_weight), axis=1) * scale
 
 
-def local(
+def local_gathered(
     state_hidden,
     action_seeds,
     action_mean,
@@ -96,7 +99,407 @@
     )
 
 
+TP = 8
+SMALL = 16
+MIB = 1024 * 1024
+
+
+def send(array, pairs):
+    return lax.ppermute(
+        array, ("tp", "dp"), [(2 * st + sd, 2 * dt + dd) for (st, sd), (dt, dd) in pairs]
+    )
+
+
+SPLIT = 4
+
+
+def copies_of(which, loads, sources, targets, arrived):
+    made = []
+    for at, (kind, size) in enumerate(loads):
+        source, target = sources[at], targets[at]
+        part = target.shape[0] // SPLIT
+        for cut in range(SPLIT):
+            rows = pl.ds(cut * part, part)
+            if kind == "rows":
+                begin = pl.multiple_of(which[at] * size + cut * part, 16)
+                view = source.at[pl.ds(begin, part), :]
+            else:
+                view = source.at[rows, pl.ds(pl.multiple_of(which[at] * size, 128), size)]
+            made.append(
+                pltpu.make_async_copy(view, target.at[rows, :], arrived.at[at * SPLIT + cut])
+            )
+    return made
+
+
+def stage(which, loads, ins, outs, compute, scratch=(), limit=6, flops=0):
+    vmem = pl.BlockSpec(memory_space=pltpu.VMEM)
+    n, count = len(loads), len(ins)
+    kinds = [(kind, size) for kind, size, _ in loads]
+    shapes = list(outs)
+    for kind, size, array in loads:
+        shape = (size, array.shape[1]) if kind == "rows" else (array.shape[0], size)
+        shapes.append(jax.ShapeDtypeStruct(shape, array.dtype))
+
+    def body(which_ref, *refs):
+        sources, inputs = refs[:n], refs[n : n + count]
+        results = refs[n + count : n + count + len(outs)]
+        targets = refs[n + count + len(outs) : n + count + len(shapes)]
+        extra = refs[n + count + len(shapes) :]
+        made = copies_of(which_ref, kinds, sources, targets, extra[0]) if n else []
+        for copy in made:
+            copy.start()
+        if compute is not None:
+            compute(inputs, results, extra[1:] if n else extra)
+        for copy in made:
+            copy.wait()
+
+    loaded = sum(2 * math.prod(shape.shape) for shape in shapes[len(outs) :])
+    return pl.pallas_call(
+        body,
+        out_shape=shapes,
+        in_specs=[pl.BlockSpec(memory_space=pltpu.SMEM)]
+        + [pl.BlockSpec(memory_space=pl.ANY)] * n
+        + [vmem] * count,
+        out_specs=[vmem] * len(shapes),
+        scratch_shapes=([pltpu.SemaphoreType.DMA((n * SPLIT,))] if n else []) + list(scratch),
+        compiler_params=pltpu.CompilerParams(vmem_limit_bytes=limit * MIB),
+        cost_estimate=pl.CostEstimate(
+            flops=flops, bytes_accessed=loaded, transcendentals=0
+        ),
+    )(which, *[array for _, _, array in loads], *ins)
+
+
+def basis_stage(which, loads, blocks, held, before, columns, features, squared, narrow):
+    m, k = blocks[0].shape
+    start, stop = columns
+    width = stop - start
+    tile = 512
+    count = len(blocks)
+    ins = list(blocks) + [part for pair in held for part in pair]
+    if before is not None:
+        ins.append(before)
+    ins += list(squared) + ([features] if squared else [])
+    outs = [jax.ShapeDtypeStruct((2, m, width), jnp.float32)]
+    if narrow:
+        outs.append(jax.ShapeDtypeStruct((2, m, width), jnp.bfloat16))
+    if squared:
+        outs.append(jax.ShapeDtypeStruct((features.shape[0], 128), jnp.float32))
+
+    def compute(inputs, results, extra):
+        refs = list(inputs)
+        lhs = extra[0]
+        rows = [refs.pop(0) for _ in range(count)]
+        weights = [(refs.pop(0), refs.pop(0)) for _ in range(count)]
+        old = refs.pop(0) if before is not None else None
+        for index, ref in enumerate(rows):
+            gain = ref[m - SMALL + 4 : m - SMALL + 5, :].astype(jnp.float32)
+            lhs[index] = (ref[...].astype(jnp.float32) * gain).astype(jnp.bfloat16)
+
+        @pl.loop(0, width // tile)
+        def _(j):
+            at = pl.ds(pl.multiple_of(start + j * tile, tile), tile)
+            to = pl.ds(pl.multiple_of(j * tile, tile), tile)
+            for side in range(2):
+                total = old[side, :, at] if old is not None else None
+                for index in range(count):
+                    term = jnp.dot(
+                        lhs[index],
+                        weights[index][side][:, at],
+                        preferred_element_type=jnp.float32,
+                    )
+                    total = term if total is None else total + term
+                results[0][side, :, to] = total
+                if narrow:
+                    results[1][side, :, to] = total.astype(jnp.bfloat16)
+
+        if squared:
+            feature_rows = refs.pop()
+            part = None
+            for ref in refs:
+                wide = jnp.dot(feature_rows[...], ref[...], preferred_element_type=jnp.float32)
+                wide = wide.astype(jnp.bfloat16).astype(jnp.float32)
+                wide = wide * wide
+                for at in range(0, k, 128):
+                    piece = wide[:, at : at + 128]
+                    part = piece if part is None else part + piece
+            results[-1][...] = part
+
+    return stage(
+        which,
+        loads,
+        ins,
+        outs,
+        compute,
+        [pltpu.VMEM((count, m, k), jnp.bfloat16)],
+        flops=4 * m * k * width * count,
+    )
+
+
+def hidden_stage(which, loads, own, other, features, square_own, square_other, width):
+    _, m, units = own.shape
+    rows = features.shape[0]
+    tile = 512
+
+    def compute(inputs, results, extra):
+        own, other, features, square_own, square_other = inputs
+        squares = jnp.sum(square_own[...] + square_other[...], axis=1, keepdims=True)
+        scale = lax.rsqrt(squares / width + epsilon)
+
+        @pl.loop(0, units // tile)
+        def _(j):
+            at = pl.ds(pl.multiple_of(j * tile, tile), tile)
+            sums = []
+            for side in range(2):
+                basis = own[side, :, at] + other[side, :, at].astype(jnp.float32)
+                sums.append(
+                    scale
+                    * jnp.dot(
+                        features[...],
+                        basis.astype(jnp.bfloat16),
+                        preferred_element_type=jnp.float32,
+                    )
+                )
+            gate, up = sums
+            results[0][:, at] = (gate / (1.0 + jnp.exp(-gate)) * up).astype(jnp.bfloat16)
+
+    return stage(
+        which,
+        loads,
+        [own, other, features, square_own, square_other],
+        [jax.ShapeDtypeStruct((rows, units), jnp.bfloat16)],
+        compute,
+        flops=4 * m * rows * units,
+    )
+
+
+def down_body(places, cols, hidden, weights, outs):
+    half = hidden[0].shape[0] // 2
+    tile = 512
+    for rows, which, targets in places:
+        low, high = rows[0] * half, rows[-1] * half + half
+        for j in range(cols // tile):
+            at = j * tile
+            total = None
+            depth_at = 0
+            for ref in hidden:
+                depth = ref.shape[1]
+                term = jnp.dot(
+                    ref[low:high, :],
+                    weights[which][depth_at : depth_at + depth, at : at + tile],
+                    preferred_element_type=jnp.float32,
+                )
+                total = term if total is None else total + term
+                depth_at += depth
+            total = total.astype(jnp.bfloat16)
+            for index, (out, column) in enumerate(targets):
+                to = column + j * tile
+                outs[out][:, to : to + tile] = total[index * half : (index + 1) * half]
+
+
+def down_products(hidden, weights, cols, places, widths, copies=()):
+    rows = hidden[0].shape[0]
+    depth = weights[0].shape[0]
+    flops = sum(len(r) * rows * depth * cols for r, *_ in places)
+    vmem = pl.BlockSpec(memory_space=pltpu.VMEM)
+    counts = (len(hidden), len(weights), len(copies))
+
+    def body(*refs):
+        groups, at = [], 0
+        for count in counts:
+            groups.append(refs[at : at + count])
+            at += count
+        outs = refs[at:]
+        down_body(places, cols, groups[0], groups[1], outs)
+        for source, (_, out) in zip(groups[2], copies):
+            outs[out][:, : source.shape[1]] = source[...]
+
+    return pl.pallas_call(
+        body,
+        out_shape=[jax.ShapeDtypeStruct((rows // 2, width), jnp.bfloat16) for width in widths],
+        in_specs=[vmem] * sum(counts),
+        out_specs=[vmem] * len(widths),
+        compiler_params=pltpu.CompilerParams(vmem_limit_bytes=6 * MIB),
+        cost_estimate=pl.CostEstimate(flops=flops // 16, bytes_accessed=0, transcendentals=0),
+    )(*hidden, *weights, *[c[0] for c in copies])
+
+
+def local_blocks(
+    state_hidden,
+    action_seeds,
+    action_mean,
+    action_spread,
+    action_weight,
+    norm_gain,
+    gate_weight,
+    up_weight,
+    down_weight,
+    head_gain,
+    value_weight,
+):
+    f32, bf16 = jnp.float32, jnp.bfloat16
+    states, cands = action_seeds.shape
+    rows = states * cands
+    act, cols = action_weight.shape
+    half = act // 2
+    units = gate_weight.shape[1]
+    full_width = gate_weight.shape[0] * 2
+    tp, dp = lax.axis_index("tp"), lax.axis_index("dp")
+    home = tp // 4 == dp
+    place = tp % 4
+    every = [(t, d) for t in range(TP) for d in range(2)]
+    swap_core = [((t, d), (t, 1 - d)) for t, d in every]
+
+    head = head_gain * value_weight
+    seeds = jnp.concatenate([action_seeds // 256, action_seeds % 256]).astype(bf16)
+    seeds_row = jnp.pad(seeds.reshape(1, -1), ((0, 0), (0, cols - seeds.size)))
+    small = jnp.concatenate([state_hidden, seeds_row, jnp.zeros((5, cols), bf16)])
+    small, head = lax.optimization_barrier((small, head))
+    other_small = send(small, swap_core)
+    low = jnp.where(dp == 0, small, other_small)
+    high = jnp.where(dp == 0, other_small, small)
+    own_block = jnp.concatenate(
+        [
+            action_weight,
+            low[:states],
+            high[:states],
+            norm_gain.astype(bf16)[None],
+            jnp.zeros((SMALL - 2 * states - 1, cols), bf16),
+        ]
+    )
+
+    far_block = send(own_block, [((t, t // 4), (t ^ 4, t // 4)) for t in range(TP)])
+    near_home = {
+        k: send(own_block, [((t, t // 4), (t ^ k, t // 4)) for t in range(TP)]) for k in (2, 1, 3)
+    }
+    block = jnp.where(home, own_block, far_block)
+    near = {}
+    for k in (2, 1, 3):
+        got = send(block, [((t, 1 - t // 4), (t ^ k, 1 - t // 4)) for t in range(TP)])
+        near[k] = jnp.where(home, near_home[k], got)
+
+    all_seeds = jnp.concatenate(
+        [part[states, : seeds.size].reshape(2, states, cands) for part in (low, high)],
+        axis=1,
+    ).astype(jnp.int32)
+    all_seeds = all_seeds[0] * 256 + all_seeds[1]
+    features = action_features(all_seeds, action_mean, action_spread).reshape(2 * rows, act)
+    row_state = jnp.arange(2 * rows) // cands
+    onehot = (row_state[:, None] == jnp.arange(SMALL)[None]).astype(bf16)
+    features = jnp.concatenate([features, onehot], axis=1)
+    own_features = lax.dynamic_slice(features, (dp * rows, 0), (rows, act))
+    embedded = jnp.dot(own_features, action_weight, preferred_element_type=f32)
+    inputs_local = (
+        (state_hidden.astype(f32)[:, None, :] + embedded.reshape(states, cands, cols))
+        .reshape(rows, cols)
+        .astype(bf16)
+    )
+
+    gate_weight, up_weight, down_weight = (
+        pltpu.with_memory_space_constraint(weight, pltpu.HBM)
+        for weight in (gate_weight, up_weight, down_weight)
+    )
+    index = lambda *ks: jnp.stack([place ^ k for k in ks]).astype(jnp.int32)
+    pair = [("rows", cols, gate_weight), ("rows", cols, up_weight)]
+    column = [("cols", cols, down_weight)]
+    held = stage(index(0, 0), pair, [], [], None)
+    basis, *held = basis_stage(
+        index(2, 2), pair, [block], [held], None, (0, units), features, [], False
+    )
+    basis, *held = basis_stage(
+        index(1, 1), pair, [near[2]], [held], basis, (0, units), features, [], False
+    )
+    basis, square, *held = basis_stage(
+        index(3, 3),
+        pair,
+        [near[1]],
+        [held],
+        basis,
+        (0, units),
+        features,
+        [block, near[2], near[1]],
+        False,
+    )
+    cut = units // 2
+    none = index(0)
+    own_a, narrow_a, square_last = basis_stage(
+        none, [], [near[3]], [held], basis, (0, cut), features, [near[3]], True
+    )
+    other_a = send(narrow_a, swap_core)
+    square = square + square_last
+    other_square = send(square, swap_core)
+    own_b, narrow_b = basis_stage(
+        none, [], [near[3]], [held], basis, (cut, units), features, [], True
+    )
+    other_b = send(narrow_b, swap_core)
+    down_first = stage(index(3, 1), column * 2, [], [], None)
+    hidden_a, down_z = hidden_stage(
+        index(2), column, own_a, other_a, features, square, other_square, full_width
+    )
+    hidden_b, down_own = hidden_stage(
+        index(0), column, own_b, other_b, features, square, other_square, full_width
+    )
+    hidden_a, inputs_local, head = lax.optimization_barrier((hidden_a, inputs_local, head))
+    hidden = [hidden_a, hidden_b]
+
+    both, lower, upper = (0, 1), (0,), (1,)
+    step = lambda array, k: send(array, [((t, d), (t ^ k, d)) for t, d in every])
+    x_pair, diagonal_upper = down_products(
+        hidden,
+        down_first,
+        cols,
+        [(both, 0, [(0, 0), (1, 0)]), (lower, 1, [(0, cols)])],
+        [2 * cols, cols],
+    )
+    got_x = step(x_pair, 1)
+    (z_pair,) = down_products(
+        hidden,
+        [down_z],
+        cols,
+        [(upper, 0, [(0, cols)])],
+        [2 * cols],
+        [(diagonal_upper, 0)],
+    )
+    got_z = step(z_pair, 2)
+    z_lower, x_upper, own_lower, own_upper = down_products(
+        hidden,
+        [down_z, down_first[1], down_own],
+        cols,
+        [(lower, 0, [(0, 0)]), (upper, 1, [(1, 0)]), (both, 2, [(2, 0), (3, 0)])],
+        [cols] * 4,
+    )
+    add = lambda *parts: sum(part.astype(f32) for part in parts).astype(bf16)
+    got_lower = step(add(z_lower, got_x[:, :cols]), 2)
+    got_upper = step(add(x_upper, got_z[:, :cols]), 1)
+    sums = [
+        add(own_lower, got_x[:, cols:], got_lower),
+        add(own_upper, got_z[:, cols:], got_upper),
+    ]
+    swapped = send(jnp.where(dp == 0, sums[1], sums[0]), swap_core)
+    stays = jnp.where(dp == 0, sums[0], sums[1])
+    got_far = step(jnp.where(home, swapped, stays), 4)
+    kept = jnp.where(home, stays, swapped)
+
+    summed = kept.astype(f32) + got_far.astype(f32)
+    output_local = (inputs_local.astype(f32) + summed).astype(bf16)
+
+    wide_out = output_local.astype(f32)
+    totals = jnp.stack(
+        [
+            jnp.sum(wide_out * wide_out, axis=1),
+            jnp.sum(wide_out * head, axis=1),
+        ]
+    )
+    for k in (1, 2, 4):
+        totals = totals + step(totals, k)
+    values = totals[1] * lax.rsqrt(totals[0] / full_width + epsilon)
+    return (
+        output_local.reshape(states, cands, cols),
+        values.reshape(states, cands),
+    )
+
+
 def solution(mesh):
+    local = local_blocks if mesh.shape["tp"] == TP and mesh.shape["dp"] == 2 else local_gathered
     return jax.shard_map(
         local,
         mesh=mesh,

time: 462 us -> 138 us (0.30)
  waiting for transfers between devices: 281 us -> 38.3 us
  blocking collectives: 80.4 us -> 0 us
  matrix products: 77.7 us -> 0.22 us
  Pallas kernels: 0 us -> 45.3 us
  starting transfers between devices: 0.24 us -> 34.5 us
  between operations: 14.2 us -> 1.04 us
  local copies, waits for them, and re-layouts: 0.9 us -> 12.3 us
    all_gather x5 -> x0, waiting for transfers between devices: 190 us -> none  [the longest x1 71.1 us: local(): lax.all_gather(gate_weight, 'dp', axis=0, tiled=True)]
    reduce_scatter x1 -> x0, waiting for transfers between devices: 89.7 us -> none  [local(): lax.psum_scatter(partial_terms, 'tp', scatter_dimension=1, tiled=True)]
    all_gather x3 -> x0, blocking collectives: 80.4 us -> none  [the longest x1 27.9 us: local(): lax.all_gather(norm_gain.astype(jnp.bfloat16), 'tp', axis=0, tiled=True)]
    dot_general x4 -> x1, matrix products: 77.7 us -> 0.22 us  [local_blocks(): embedded = jnp.dot(own_features, action_weight, preferred_element_type=f32)]
    pallas_call x0 -> x12, Pallas kernels: none -> 45.3 us  [the longest x9 38.2 us: stage(): pl.pallas_call(body, out_shape=shapes, in_specs=[pl.BlockSpec(memory_spac...]
    ppermute x0 -> x20, waiting for transfers between devices: none -> 38.3 us  [send(): lax.ppermute(array, ('tp', 'dp'), [(2 * st + sd, 2 * dt + dd) for (st, sd...]
    ppermute x0 -> x20, starting transfers between devices: none -> 34.5 us  [send(): lax.ppermute(array, ('tp', 'dp'), [(2 * st + sd, 2 * dt + dd) for (st, sd...]
    unnamed x14 -> x20, local copies, waits for them, and re-layouts: 0.25 us -> 10.8 us
  transfers between devices with their start and end apart: 6 -> 20, of which waited for: 5 -> 9; matrix products, arithmetic and copies ran while one was open for 13% -> 2% of each run, Pallas kernels for 0% -> 26%
where the time goes in v4:
time: 138 us; the launch traced here: 137 us
  Pallas kernels  45.3 us (33%)
  waiting for transfers between devices  38.3 us (28%)
  starting transfers between devices  34.5 us (25%)
  local copies, waits for them, and re-layouts  12.3 us (9%)
  other arithmetic  5.6 us (4%)
    ppermute x20, waiting for transfers between devices, send(): lax.ppermute(array, ('tp', 'dp'), [(2 * st + sd, 2 * dt + dd) for (st, sd...  38.3 us
    pallas_call x9, Pallas kernels, stage(): pl.pallas_call(body, out_shape=shapes, in_specs=[pl.BlockSpec(memory_spac...  38.2 us
    ppermute x20, starting transfers between devices, send(): lax.ppermute(array, ('tp', 'dp'), [(2 * st + sd, 2 * dt + dd) for (st, sd...  34.5 us
    unnamed x20, local copies, waits for them, and re-layouts  10.8 us
    pallas_call x3, Pallas kernels, down_products(): pl.pallas_call(body, out_shape=[jax.ShapeDtypeStruct((rows // 2, width),...  7.01 us
  transfers between devices with their start and end apart: 20, of which 9 were waited for; matrix products, arithmetic and copies ran while one was open for 2% of the time, Pallas kernels for 26%

profile of v4, /device:TPU:0, one launch (start us, length us, event | category | flops | bytes accessed | tf_op | source)
XLA Modules:
  0.0 137.2 jit_solution(17283462136962720692)
XLA Ops:
  4.6 5.2 %shard_map.122 = (bf16[1024,3072]{1,0:T(8,128)(2,1)S(1)}, bf16[1024,3072]{1,0:T(8,128)(2,1)S(1)}) custom-call(s32[2]{0:T(128)S(1)} %pad_add_fusion.3.which_ref, bf16[4096,3072]{1,0:T(8,128)(2,1)} %refs_0_.10, bf16[4096,3072]{1,0:T(8,128)(2,1)} %refs_1_.8), custom_call_target="tpu_custom_call" | custom-call | bytes 12582912 | tf_op jit(solution)/shard_map/pallas_call | solution.py:157
  9.8 2.6 %copy-done = bf16[1024,3072]{1,0:T(8,128)(2,1)} copy-done((bf16[1024,3072]{1,0:T(8,128)(2,1)}, bf16[1024,3072]{1,0:T(8,128)(2,1)S(1)}, u32[]{:S(2)}) %copy-start) | copy-done | bytes 6291480
  12.5 2.6 %copy-done.2 = bf16[1024,3072]{1,0:T(8,128)(2,1)} copy-done((bf16[1024,3072]{1,0:T(8,128)(2,1)}, bf16[1024,3072]{1,0:T(8,128)(2,1)S(1)}, u32[]{:S(2)}) %copy-start.2) | copy-done | bytes 6291480
  15.4 5.6 %collective-permute-start.2 = (bf16[144,1024]{1,0:T(8,128)(2,1)S(1)}, bf16[144,1024]{1,0:T(8,128)(2,1)S(1)}, u32[]{:S(2)}, u32[]{:S(2)}) collective-permute-start(bf16[144,1024]{1,0:T(8,128)(2,1)S(1)} %concatenate.18), channel_id=1, source_target_pairs={{0,8},{2,10},{4,12},{6,14},{9,1},{11,3},{13,5},{15,7},{16,24},{18,... | collective-permute-start | bytes 884744 | tf_op jit(solution)/shard_map/ppermute | solution.py:108
  21.0 3.5 %collective-permute-start.6 = (bf16[144,1024]{1,0:T(8,128)(2,1)S(1)}, bf16[144,1024]{1,0:T(8,128)(2,1)S(1)}, u32[]{:S(2)}, u32[]{:S(2)}) collective-permute-start(bf16[144,1024]{1,0:T(8,128)(2,1)S(1)} %concatenate.18), channel_id=1, source_target_pairs={{0,4},{2,6},{4,0},{6,2},{9,13},{11,15},{13,9},{15,11},{16,20},{18,... | collective-permute-start | bytes 884744 | tf_op jit(solution)/shard_map/ppermute | solution.py:108
  24.5 3.4 %collective-permute-start.4 = (bf16[144,1024]{1,0:T(8,128)(2,1)S(1)}, bf16[144,1024]{1,0:T(8,128)(2,1)S(1)}, u32[]{:S(2)}, u32[]{:S(2)}) collective-permute-start(bf16[144,1024]{1,0:T(8,128)(2,1)S(1)} %concatenate.18), channel_id=1, source_target_pairs={{0,2},{2,0},{4,6},{6,4},{9,11},{11,9},{13,15},{15,13},{16,18},{18,... | collective-permute-start | bytes 884744 | tf_op jit(solution)/shard_map/ppermute | solution.py:108
  27.9 2.3 %collective-permute-start.1 = (bf16[144,1024]{1,0:T(8,128)(2,1)S(1)}, bf16[144,1024]{1,0:T(8,128)(2,1)S(1)}, u32[]{:S(2)}, u32[]{:S(2)}) collective-permute-start(bf16[144,1024]{1,0:T(8,128)(2,1)S(1)} %concatenate.18), channel_id=1, source_target_pairs={{0,6},{2,4},{4,2},{6,0},{9,15},{11,13},{13,11},{15,9},{16,22},{18,... | collective-permute-start | bytes 884744 | tf_op jit(solution)/shard_map/ppermute | solution.py:108
  32.6 2.8 %copy-done.1 = bf16[1024,3072]{1,0:T(8,128)(2,1)S(1)} copy-done((bf16[1024,3072]{1,0:T(8,128)(2,1)S(1)}, bf16[1024,3072]{1,0:T(8,128)(2,1)}, u32[]{:S(2)}) %copy-start.1) | copy-done | bytes 6291480
  35.4 2.8 %copy-done.3 = bf16[1024,3072]{1,0:T(8,128)(2,1)S(1)} copy-done((bf16[1024,3072]{1,0:T(8,128)(2,1)S(1)}, bf16[1024,3072]{1,0:T(8,128)(2,1)}, u32[]{:S(2)}) %copy-start.3) | copy-done | bytes 6291480
  38.2 5.2 %shard_map.123 = (f32[2,144,3072]{2,1,0:T(8,128)S(1)}, bf16[1024,3072]{1,0:T(8,128)(2,1)S(1)}, bf16[1024,3072]{1,0:T(8,128)(2,1)S(1)}) custom-call(s32[2]{0:T(128)S(1)} %pad_add_fusion.2.which_ref, bf16[4096,3072]{1,0:T(8,128)(2,1)} %refs_0_.10, bf16[4096,3072]{1,0:T(8,128)(2,1)} %refs_1_.8, bf16[144,1024]{1,0:T(8,128)(2,1)S(1)} %broadcast_select_fusion.3.refs_2_.refs_6_, ...), custom_call_target="tpu_custom_call" | custom-call | flops 1811939328 | bytes 12582912 | tf_op jit(solution)/shard_map/pallas_call | solution.py:157
  44.4 5.3 %shard_map.124 = (f32[2,144,3072]{2,1,0:T(8,128)S(1)}, bf16[1024,3072]{1,0:T(8,128)(2,1)S(1)}, bf16[1024,3072]{1,0:T(8,128)(2,1)S(1)}) custom-call(s32[2]{0:T(128)S(1)} %pad_add_fusion.1.which_ref, bf16[4096,3072]{1,0:T(8,128)(2,1)} %refs_0_.10, bf16[4096,3072]{1,0:T(8,128)(2,1)} %refs_1_.8, bf16[144,1024]{1,0:T(8,128)(2,1)S(1)} %broadcast_select_fusion.refs_2_.refs_7_, ...), custom_call_target="tpu_custom_call" | custom-call | flops 1811939328 | bytes 12582912 | tf_op jit(solution)/shard_map/pallas_call | solution.py:157
  49.7 5.3 %shard_map.125 = (f32[2,144,3072]{2,1,0:T(8,128)S(1)}, f32[256,128]{1,0:T(8,128)S(1)}, bf16[1024,3072]{1,0:T(8,128)(2,1)S(1)}, bf16[1024,3072]{1,0:T(8,128)(2,1)S(1)}) custom-call(s32[2]{0:T(128)S(1)} %pad_add_fusion.which_ref, bf16[4096,3072]{1,0:T(8,128)(2,1)} %refs_0_.10, bf16[4096,3072]{1,0:T(8,128)(2,1)} %refs_1_.8, ...), custom_call_target="tpu_custom_call" | custom-call | flops 1811939328 | bytes 12582912 | tf_op jit(solution)/shard_map/pallas_call | solution.py:157
  55.0 2.5 %shard_map.126 = (f32[2,144,1536]{2,1,0:T(8,128)S(1)}, bf16[2,144,1536]{2,1,0:T(8,128)(2,1)}, f32[256,128]{1,0:T(8,128)S(1)}) custom-call(s32[1]{0:T(128)} %bitcast.1.which_ref, bf16[144,1024]{1,0:T(8,128)(2,1)S(1)} %broadcast_select_fusion.2.refs_0_.refs_4_, bf16[1024,3072]{1,0:T(8,128)(2,1)S(1)} %get-tuple-element.45.refs_1_, ...), custom_call_target="tpu_custom_call" | custom-call | flops 905969664 | tf_op jit(solution)/shard_map/pallas_call | solution.py:157
  57.5 4.2 %collective-permute-start.8 = (bf16[2,144,1536]{2,1,0:T(8,128)(2,1)}, bf16[2,144,1536]{2,1,0:T(8,128)(2,1)}, u32[]{:S(2)}, u32[]{:S(2)}) collective-permute-start(bf16[2,144,1536]{2,1,0:T(8,128)(2,1)} %get-tuple-element.49), channel_id=1, source_target_pairs={{0,1},{1,0},{2,3},{3,2},{4,5},{5,4},{6,7},{7,6},{8,9},{9,8},{10,11... | collective-permute-start | bytes 2654216 | tf_op jit(solution)/shard_map/ppermute | solution.py:108
  61.7 2.5 %shard_map.128 = (f32[2,144,1536]{2,1,0:T(8,128)S(1)}, bf16[2,144,1536]{2,1,0:T(8,128)(2,1)}) custom-call(s32[1]{0:T(128)} %bitcast.1.which_ref, bf16[144,1024]{1,0:T(8,128)(2,1)S(1)} %broadcast_select_fusion.2.refs_0_.refs_4_, bf16[1024,3072]{1,0:T(8,128)(2,1)S(1)} %get-tuple-element.45.refs_1_, bf16[1024,3072]{1,0:T(8,128)(2,1)S(1)} %get-tuple-element.46.refs_2_, ...), custom_call_target="tpu_custom_call" | custom-call | flops 905969664 | tf_op jit(solution)/shard_map/pallas_call | solution.py:157
  64.2 5.3 %shard_map.130 = (bf16[3072,1024]{1,0:T(8,128)(2,1)S(1)}, bf16[3072,1024]{1,0:T(8,128)(2,1)S(1)}) custom-call(s32[2]{0:T(128)S(1)} %pad_add_fusion.4.which_ref, bf16[3072,4096]{1,0:T(8,128)(2,1)} %refs_1_.9, bf16[3072,4096]{1,0:T(8,128)(2,1)} %refs_1_.9), custom_call_target="tpu_custom_call" | custom-call | bytes 12582912 | tf_op jit(solution)/shard_map/pallas_call | solution.py:157
  71.1 4.1 %shard_map.127 = (bf16[256,1536]{1,0:T(8,128)(2,1)S(1)}, bf16[3072,1024]{1,0:T(8,128)(2,1)S(1)}) custom-call(s32[1]{0:T(128)} %bitcast.which_ref, bf16[3072,4096]{1,0:T(8,128)(2,1)} %refs_1_.9, f32[2,144,1536]{2,1,0:T(8,128)S(1)} %copy-done.5, bf16[2,144,1536]{2,1,0:T(8,128)(2,1)} %collective-permute-done.8.refs_2_, ...), custom_call_target="tpu_custom_call" | custom-call | flops 226492416 | bytes 6291456 | tf_op jit(solution)/shard_map/pallas_call | solution.py:157
  75.2 2.9 %shard_map.129 = (bf16[256,1536]{1,0:T(8,128)(2,1)S(1)}, bf16[3072,1024]{1,0:T(8,128)(2,1)S(1)}) custom-call(s32[1]{0:T(128)} %bitcast.1.which_ref, bf16[3072,4096]{1,0:T(8,128)(2,1)} %refs_1_.9, f32[2,144,1536]{2,1,0:T(8,128)S(1)} %get-tuple-element.56.refs_1_, bf16[2,144,1536]{2,1,0:T(8,128)(2,1)S(1)} %collective-permute-done.10.refs_2_, ...), custom_call_target="tpu_custom_call" | custom-call | flops 226492416 | bytes 6291456 | tf_op jit(solution)/shard_map/pallas_call | solution.py:157
  78.1 2.6 %shard_map.132 = (bf16[128,2048]{1,0:T(8,128)(2,1)S(1)}, bf16[128,1024]{1,0:T(8,128)(2,1)S(1)}) custom-call(bf16[256,1536]{1,0:T(8,128)(2,1)S(1)} %get-tuple-element.55.refs_0_, bf16[256,1536]{1,0:T(8,128)(2,1)S(1)} %get-tuple-element.58.refs_1_, bf16[3072,1024]{1,0:T(8,128)(2,1)S(1)} %get-tuple-element.63.refs_2_, ...), custom_call_target="tpu_custom_call" | custom-call | flops 150994944 | tf_op jit(solution)/shard_map/pallas_call | solution.py:316
  82.3 1.5 %collective-permute-start.11 = (bf16[128,2048]{1,0:T(8,128)(2,1)S(1)}, bf16[128,2048]{1,0:T(8,128)(2,1)S(1)}, u32[]{:S(2)}, u32[]{:S(2)}) collective-permute-start(bf16[128,2048]{1,0:T(8,128)(2,1)S(1)} %get-tuple-element.64), channel_id=1, source_target_pairs={{0,2},{1,3},{2,0},{3,1},{4,6},{5,7},{6,4},{7,5},{8,10},{9,11},{10,... | collective-permute-start | bytes 1572872 | tf_op jit(solution)/shard_map/ppermute | solution.py:108
  83.8 3.4 %shard_map.131 = (bf16[128,1024]{1,0:T(8,128)(2,1)S(1)}, bf16[128,1024]{1,0:T(8,128)(2,1)S(1)}, bf16[128,1024]{1,0:T(8,128)(2,1)S(1)}, bf16[128,1024]{1,0:T(8,128)(2,1)S(1)}) custom-call(bf16[256,1536]{1,0:T(8,128)(2,1)S(1)} %get-tuple-element.55.refs_0_, bf16[256,1536]{1,0:T(8,128)(2,1)S(1)} %get-tuple-element.58.refs_1_, ...), custom_call_target="tpu_custom_call" | custom-call | flops 201326592 | tf_op jit(solution)/shard_map/pallas_call | solution.py:316
  87.2 8.7 %collective-permute-done.13 = bf16[128,2048]{1,0:T(8,128)(2,1)S(1)} collective-permute-done((bf16[128,2048]{1,0:T(8,128)(2,1)S(1)}, bf16[128,2048]{1,0:T(8,128)(2,1)S(1)}, u32[]{:S(2)}, u32[]{:S(2)}) %collective-permute-start.13) | collective-permute-done | bytes 524320 | tf_op jit(solution)/shard_map/ppermute | solution.py:108
  96.0 1.8 %collective-permute-start.14 = (bf16[128,1024]{1,0:T(8,128)(2,1)S(1)}, bf16[128,1024]{1,0:T(8,128)(2,1)S(1)}, u32[]{:S(2)}, u32[]{:S(2)}) collective-permute-start(bf16[128,1024]{1,0:T(8,128)(2,1)S(1)} %add_convert_fusion.2), channel_id=1, source_target_pairs={{0,2},{1,3},{2,0},{3,1},{4,6},{5,7},{6,4},{7,5},{8,10},{9,11},{10,... | collective-permute-start | bytes 786440 | tf_op jit(solution)/shard_map/ppermute | solution.py:108
  98.2 5.6 %collective-permute-done.14 = bf16[128,1024]{1,0:T(8,128)(2,1)S(1)} collective-permute-done((bf16[128,1024]{1,0:T(8,128)(2,1)S(1)}, bf16[128,1024]{1,0:T(8,128)(2,1)S(1)}, u32[]{:S(2)}, u32[]{:S(2)}) %collective-permute-start.14) | collective-permute-done | bytes 262176 | tf_op jit(solution)/shard_map/ppermute | solution.py:108
  103.9 1.6 %collective-permute-done.12 = bf16[128,1024]{1,0:T(8,128)(2,1)S(1)} collective-permute-done((bf16[128,1024]{1,0:T(8,128)(2,1)S(1)}, bf16[128,1024]{1,0:T(8,128)(2,1)S(1)}, u32[]{:S(2)}, u32[]{:S(2)}) %collective-permute-start.12) | collective-permute-done | bytes 262176 | tf_op jit(solution)/shard_map/ppermute | solution.py:108
  105.8 1.5 %collective-permute-done.15 = bf16[128,1024]{1,0:T(8,128)(2,1)S(1)} collective-permute-done((bf16[128,1024]{1,0:T(8,128)(2,1)S(1)}, bf16[128,1024]{1,0:T(8,128)(2,1)S(1)}, u32[]{:S(2)}, u32[]{:S(2)}) %collective-permute-start.15) | collective-permute-done | bytes 262176 | tf_op jit(solution)/shard_map/ppermute | solution.py:108
  107.4 4.1 %collective-permute-start.16 = (bf16[128,1024]{1,0:T(8,128)(2,1)S(1)}, bf16[128,1024]{1,0:T(8,128)(2,1)S(1)}, u32[]{:S(2)}, u32[]{:S(2)}) collective-permute-start(bf16[128,1024]{1,0:T(8,128)(2,1)S(1)} %broadcast_select_fusion.6), channel_id=1, source_target_pairs={{0,8},{1,9},{2,10},{3,11},{4,12},{5,13},{6,14},{7,15},{8,0},{9,1},... | collective-permute-start | bytes 786440 | tf_op jit(solution)/shard_map/ppermute | solution.py:108
  111.5 12.2 %collective-permute-done.16 = bf16[128,1024]{1,0:T(8,128)(2,1)S(1)} collective-permute-done((bf16[128,1024]{1,0:T(8,128)(2,1)S(1)}, bf16[128,1024]{1,0:T(8,128)(2,1)S(1)}, u32[]{:S(2)}, u32[]{:S(2)}) %collective-permute-start.16) | collective-permute-done | bytes 262176 | tf_op jit(solution)/shard_map/ppermute | solution.py:108
  125.7 2.6 %collective-permute-done.17 = f32[2,128]{1,0:T(2,128)S(1)} collective-permute-done((f32[2,128]{1,0:T(2,128)S(1)}, f32[2,128]{1,0:T(2,128)S(1)}, u32[]{:S(2)}, u32[]{:S(2)}) %collective-permute-start.17) | collective-permute-done | bytes 1056 | tf_op jit(solution)/shard_map/ppermute | solution.py:108
  129.1 2.9 %collective-permute-done.18 = f32[2,128]{1,0:T(2,128)S(1)} collective-permute-done((f32[2,128]{1,0:T(2,128)S(1)}, f32[2,128]{1,0:T(2,128)S(1)}, u32[]{:S(2)}, u32[]{:S(2)}) %collective-permute-start.18) | collective-permute-done | bytes 1056 | tf_op jit(solution)/shard_map/ppermute | solution.py:108
  132.0 2.1 %collective-permute-start.19 = (f32[2,128]{1,0:T(2,128)S(1)}, f32[2,128]{1,0:T(2,128)S(1)}, u32[]{:S(2)}, u32[]{:S(2)}) collective-permute-start(f32[2,128]{1,0:T(2,128)S(1)} %fusion.25), channel_id=1, source_target_pairs={{0,8},{1,9},{2,10},{3,11},{4,12},{5,13},{6,14},{7,15},{8,0},{9,1},... | collective-permute-start | bytes 3080 | tf_op jit(solution)/shard_map/ppermute | solution.py:108
  134.1 2.4 %collective-permute-done.19 = f32[2,128]{1,0:T(2,128)S(1)} collective-permute-done((f32[2,128]{1,0:T(2,128)S(1)}, f32[2,128]{1,0:T(2,128)S(1)}, u32[]{:S(2)}, u32[]{:S(2)}) %collective-permute-start.19) | collective-permute-done | bytes 1056 | tf_op jit(solution)/shard_map/ppermute | solution.py:108
  (88 shorter events, 15.1 us)
Async XLA Ops:
  3.0 12.1 %collective-permute-start = (bf16[8,1024]{1,0:T(8,128)(2,1)S(1)}, bf16[8,1024]{1,0:T(8,128)(2,1)S(1)}, u32[]{:S(2)}, u32[]{:S(2)}) collective-permute-start(bf16[8,1024]{1,0:T(8,128)(2,1)S(1)} %fusion.18), channel_id=1, source_target_pairs={{0,1},{1,0},{2,3},{3,2},{4,5},{5,4},{6,7},{7,6},{8,9},{9,8},{10,11... | collective-permute-start | bytes 49160 | tf_op jit(solution)/shard_map/ppermute | solution.py:108
  4.5 10.6 %copy-start.6 = (bf16[128,1024]{1,0:T(8,128)(2,1)S(1)}, bf16[128,1024]{1,0:T(8,128)(2,1)}, u32[]{:S(2)}) copy-start(bf16[128,1024]{1,0:T(8,128)(2,1)} %param.15) | copy-start | bytes 786436
  4.5 26.7 %copy-start.8 = (f32[128]{0:T(128)S(1)}, f32[128]{0:T(128)}, u32[]{:S(2)}) copy-start(f32[128]{0:T(128)} %param.14) | copy-start | bytes 1540
  4.6 26.7 %copy-start.9 = (f32[128]{0:T(128)S(1)}, f32[128]{0:T(128)}, u32[]{:S(2)}) copy-start(f32[128]{0:T(128)} %param.13) | copy-start | bytes 1540
  9.8 2.6 %copy-start = (bf16[1024,3072]{1,0:T(8,128)(2,1)}, bf16[1024,3072]{1,0:T(8,128)(2,1)S(1)}, u32[]{:S(2)}) copy-start(bf16[1024,3072]{1,0:T(8,128)(2,1)S(1)} %get-tuple-element.37.refs_3_) | copy-start | bytes 18874372
  12.5 2.6 %copy-start.2 = (bf16[1024,3072]{1,0:T(8,128)(2,1)}, bf16[1024,3072]{1,0:T(8,128)(2,1)S(1)}, u32[]{:S(2)}) copy-start(bf16[1024,3072]{1,0:T(8,128)(2,1)S(1)} %get-tuple-element.38.refs_4_) | copy-start | bytes 18874372
  15.4 15.1 %collective-permute-start.2 = (bf16[144,1024]{1,0:T(8,128)(2,1)S(1)}, bf16[144,1024]{1,0:T(8,128)(2,1)S(1)}, u32[]{:S(2)}, u32[]{:S(2)}) collective-permute-start(bf16[144,1024]{1,0:T(8,128)(2,1)S(1)} %concatenate.18), channel_id=1, source_target_pairs={{0,8},{2,10},{4,12},{6,14},{9,1},{11,3},{13,5},{15,7},{16,24},{18,... | collective-permute-start | bytes 884744 | tf_op jit(solution)/shard_map/ppermute | solution.py:108
  21.0 22.4 %collective-permute-start.6 = (bf16[144,1024]{1,0:T(8,128)(2,1)S(1)}, bf16[144,1024]{1,0:T(8,128)(2,1)S(1)}, u32[]{:S(2)}, u32[]{:S(2)}) collective-permute-start(bf16[144,1024]{1,0:T(8,128)(2,1)S(1)} %concatenate.18), channel_id=1, source_target_pairs={{0,4},{2,6},{4,0},{6,2},{9,13},{11,15},{13,9},{15,11},{16,20},{18,... | collective-permute-start | bytes 884744 | tf_op jit(solution)/shard_map/ppermute | solution.py:108
  24.5 19.9 %collective-permute-start.4 = (bf16[144,1024]{1,0:T(8,128)(2,1)S(1)}, bf16[144,1024]{1,0:T(8,128)(2,1)S(1)}, u32[]{:S(2)}, u32[]{:S(2)}) collective-permute-start(bf16[144,1024]{1,0:T(8,128)(2,1)S(1)} %concatenate.18), channel_id=1, source_target_pairs={{0,2},{2,0},{4,6},{6,4},{9,11},{11,9},{13,15},{15,13},{16,18},{18,... | collective-permute-start | bytes 884744 | tf_op jit(solution)/shard_map/ppermute | solution.py:108
  27.9 27.0 %collective-permute-start.1 = (bf16[144,1024]{1,0:T(8,128)(2,1)S(1)}, bf16[144,1024]{1,0:T(8,128)(2,1)S(1)}, u32[]{:S(2)}, u32[]{:S(2)}) collective-permute-start(bf16[144,1024]{1,0:T(8,128)(2,1)S(1)} %concatenate.18), channel_id=1, source_target_pairs={{0,6},{2,4},{4,2},{6,0},{9,15},{11,13},{13,11},{15,9},{16,22},{18,... | collective-permute-start | bytes 884744 | tf_op jit(solution)/shard_map/ppermute | solution.py:108
  30.6 13.7 %collective-permute-start.7 = (bf16[144,1024]{1,0:T(8,128)(2,1)S(1)}, bf16[144,1024]{1,0:T(8,128)(2,1)S(1)}, u32[]{:S(2)}, u32[]{:S(2)}) collective-permute-start(bf16[144,1024]{1,0:T(8,128)(2,1)S(1)} %broadcast_select_fusion.3.refs_2_.refs_6_), channel_id=1, source_target_pairs={{1,5},{3,7},{5,1},{7,3},{8,12},{10,14},{12,8},{14,10},{17,21},{19,... | collective-permute-start | bytes 884744 | tf_op jit(solution)/shard_map/ppermute | solution.py:108
  31.9 12.5 %collective-permute-start.5 = (bf16[144,1024]{1,0:T(8,128)(2,1)S(1)}, bf16[144,1024]{1,0:T(8,128)(2,1)S(1)}, u32[]{:S(2)}, u32[]{:S(2)}) collective-permute-start(bf16[144,1024]{1,0:T(8,128)(2,1)S(1)} %broadcast_select_fusion.3.refs_2_.refs_6_), channel_id=1, source_target_pairs={{1,3},{3,1},{5,7},{7,5},{8,10},{10,8},{12,14},{14,12},{17,19},{19,... | collective-permute-start | bytes 884744 | tf_op jit(solution)/shard_map/ppermute | solution.py:108
  32.6 2.8 %copy-start.1 = (bf16[1024,3072]{1,0:T(8,128)(2,1)S(1)}, bf16[1024,3072]{1,0:T(8,128)(2,1)}, u32[]{:S(2)}) copy-start(bf16[1024,3072]{1,0:T(8,128)(2,1)} %copy-done) | copy-start | bytes 18874372
  35.4 2.8 %copy-start.3 = (bf16[1024,3072]{1,0:T(8,128)(2,1)S(1)}, bf16[1024,3072]{1,0:T(8,128)(2,1)}, u32[]{:S(2)}) copy-start(bf16[1024,3072]{1,0:T(8,128)(2,1)} %copy-done.2) | copy-start | bytes 18874372
  43.4 11.5 %collective-permute-start.3 = (bf16[144,1024]{1,0:T(8,128)(2,1)S(1)}, bf16[144,1024]{1,0:T(8,128)(2,1)S(1)}, u32[]{:S(2)}, u32[]{:S(2)}) collective-permute-start(bf16[144,1024]{1,0:T(8,128)(2,1)S(1)} %broadcast_select_fusion.3.refs_2_.refs_6_), channel_id=1, source_target_pairs={{1,7},{3,5},{5,3},{7,1},{8,14},{10,12},{12,10},{14,8},{17,23},{19,... | collective-permute-start | bytes 884744 | tf_op jit(solution)/shard_map/ppermute | solution.py:108
  57.5 6.6 %copy-start.4 = (f32[2,144,1536]{2,1,0:T(8,128)}, f32[2,144,1536]{2,1,0:T(8,128)S(1)}, u32[]{:S(2)}) copy-start(f32[2,144,1536]{2,1,0:T(8,128)S(1)} %get-tuple-element.48.refs_1_) | copy-start | bytes 5308420
  57.5 13.6 %collective-permute-start.8 = (bf16[2,144,1536]{2,1,0:T(8,128)(2,1)}, bf16[2,144,1536]{2,1,0:T(8,128)(2,1)}, u32[]{:S(2)}, u32[]{:S(2)}) collective-permute-start(bf16[2,144,1536]{2,1,0:T(8,128)(2,1)} %get-tuple-element.49), channel_id=1, source_target_pairs={{0,1},{1,0},{2,3},{3,2},{4,5},{5,4},{6,7},{7,6},{8,9},{9,8},{10,11... | collective-permute-start | bytes 2654216 | tf_op jit(solution)/shard_map/ppermute | solution.py:108
  64.1 11.0 %collective-permute-start.10 = (bf16[2,144,1536]{2,1,0:T(8,128)(2,1)}, bf16[2,144,1536]{2,1,0:T(8,128)(2,1)S(1)}, u32[]{:S(2)}, u32[]{:S(2)}) collective-permute-start(bf16[2,144,1536]{2,1,0:T(8,128)(2,1)} %get-tuple-element.57), channel_id=1, source_target_pairs={{0,1},{1,0},{2,3},{3,2},{4,5},{5,4},{6,7},{7,6},{8,9},{9,8},{10,11... | collective-permute-start | bytes 2654216 | tf_op jit(solution)/shard_map/ppermute | solution.py:108
  64.2 5.9 %copy-start.7 = (bf16[2,1024]{1,0:T(2,128)(2,1)S(1)}, bf16[2,1024]{1,0:T(2,128)(2,1)}, u32[]{:S(2)}) copy-start(bf16[2,1024]{1,0:T(2,128)(2,1)} %param.11) | copy-start | bytes 12292
  64.2 6.9 %copy-start.5 = (f32[2,144,1536]{2,1,0:T(8,128)S(1)}, f32[2,144,1536]{2,1,0:T(8,128)}, u32[]{:S(2)}) copy-start(f32[2,144,1536]{2,1,0:T(8,128)} %copy-done.4) | copy-start | bytes 5308420
  69.6 1.6 %collective-permute-start.9 = (f32[256,128]{1,0:T(8,128)S(1)}, f32[256,128]{1,0:T(8,128)S(1)}, u32[]{:S(2)}, u32[]{:S(2)}) collective-permute-start(f32[256,128]{1,0:T(8,128)S(1)} %add.122.refs_4_), channel_id=1, source_target_pairs={{0,1},{1,0},{2,3},{3,2},{4,5},{5,4},{6,7},{7,6},{8,9},{9,8},{10,11... | collective-permute-start | bytes 393224 | tf_op jit(solution)/shard_map/ppermute | solution.py:108
  81.7 14.3 %collective-permute-start.13 = (bf16[128,2048]{1,0:T(8,128)(2,1)S(1)}, bf16[128,2048]{1,0:T(8,128)(2,1)S(1)}, u32[]{:S(2)}, u32[]{:S(2)}) collective-permute-start(bf16[128,2048]{1,0:T(8,128)(2,1)S(1)} %shard_map.133), channel_id=1, source_target_pairs={{0,4},{1,5},{2,6},{3,7},{4,0},{5,1},{6,2},{7,3},{8,12},{9,13},{10,... | collective-permute-start | bytes 1572872 | tf_op jit(solution)/shard_map/ppermute | solution.py:108
  82.3 15.5 %collective-permute-start.11 = (bf16[128,2048]{1,0:T(8,128)(2,1)S(1)}, bf16[128,2048]{1,0:T(8,128)(2,1)S(1)}, u32[]{:S(2)}, u32[]{:S(2)}) collective-permute-start(bf16[128,2048]{1,0:T(8,128)(2,1)S(1)} %get-tuple-element.64), channel_id=1, source_target_pairs={{0,2},{1,3},{2,0},{3,1},{4,6},{5,7},{6,4},{7,5},{8,10},{9,11},{10,... | collective-permute-start | bytes 1572872 | tf_op jit(solution)/shard_map/ppermute | solution.py:108
  96.0 7.8 %collective-permute-start.14 = (bf16[128,1024]{1,0:T(8,128)(2,1)S(1)}, bf16[128,1024]{1,0:T(8,128)(2,1)S(1)}, u32[]{:S(2)}, u32[]{:S(2)}) collective-permute-start(bf16[128,1024]{1,0:T(8,128)(2,1)S(1)} %add_convert_fusion.2), channel_id=1, source_target_pairs={{0,2},{1,3},{2,0},{3,1},{4,6},{5,7},{6,4},{7,5},{8,10},{9,11},{10,... | collective-permute-start | bytes 786440 | tf_op jit(solution)/shard_map/ppermute | solution.py:108
  97.9 7.5 %collective-permute-start.12 = (bf16[128,1024]{1,0:T(8,128)(2,1)S(1)}, bf16[128,1024]{1,0:T(8,128)(2,1)S(1)}, u32[]{:S(2)}, u32[]{:S(2)}) collective-permute-start(bf16[128,1024]{1,0:T(8,128)(2,1)S(1)} %add_convert_fusion.4), channel_id=1, source_target_pairs={{0,4},{1,5},{2,6},{3,7},{4,0},{5,1},{6,2},{7,3},{8,12},{9,13},{10,... | collective-permute-start | bytes 786440 | tf_op jit(solution)/shard_map/ppermute | solution.py:108
  105.7 1.6 %collective-permute-start.15 = (bf16[128,1024]{1,0:T(8,128)(2,1)S(1)}, bf16[128,1024]{1,0:T(8,128)(2,1)S(1)}, u32[]{:S(2)}, u32[]{:S(2)}) collective-permute-start(bf16[128,1024]{1,0:T(8,128)(2,1)S(1)} %get-tuple-element.73), channel_id=1, source_target_pairs={{0,1},{1,0},{2,3},{3,2},{4,5},{5,4},{6,7},{7,6},{8,9},{9,8},{10,11... | collective-permute-start | bytes 786440 | tf_op jit(solution)/shard_map/ppermute | solution.py:108
  107.4 16.4 %collective-permute-start.16 = (bf16[128,1024]{1,0:T(8,128)(2,1)S(1)}, bf16[128,1024]{1,0:T(8,128)(2,1)S(1)}, u32[]{:S(2)}, u32[]{:S(2)}) collective-permute-start(bf16[128,1024]{1,0:T(8,128)(2,1)S(1)} %broadcast_select_fusion.6), channel_id=1, source_target_pairs={{0,8},{1,9},{2,10},{3,11},{4,12},{5,13},{6,14},{7,15},{8,0},{9,1},... | collective-permute-start | bytes 786440 | tf_op jit(solution)/shard_map/ppermute | solution.py:108
  124.7 3.6 %collective-permute-start.17 = (f32[2,128]{1,0:T(2,128)S(1)}, f32[2,128]{1,0:T(2,128)S(1)}, u32[]{:S(2)}, u32[]{:S(2)}) collective-permute-start(f32[2,128]{1,0:T(2,128)S(1)} %pad_maximum_fusion.2), channel_id=1, source_target_pairs={{0,2},{1,3},{2,0},{3,1},{4,6},{5,7},{6,4},{7,5},{8,10},{9,11},{10,... | collective-permute-start | bytes 3080 | tf_op jit(solution)/shard_map/ppermute | solution.py:108
  128.3 3.6 %collective-permute-start.18 = (f32[2,128]{1,0:T(2,128)S(1)}, f32[2,128]{1,0:T(2,128)S(1)}, u32[]{:S(2)}, u32[]{:S(2)}) collective-permute-start(f32[2,128]{1,0:T(2,128)S(1)} %fusion.23), channel_id=1, source_target_pairs={{0,4},{1,5},{2,6},{3,7},{4,0},{5,1},{6,2},{7,3},{8,12},{9,13},{10,... | collective-permute-start | bytes 3080 | tf_op jit(solution)/shard_map/ppermute | solution.py:108
  132.0 4.5 %collective-permute-start.19 = (f32[2,128]{1,0:T(2,128)S(1)}, f32[2,128]{1,0:T(2,128)S(1)}, u32[]{:S(2)}, u32[]{:S(2)}) collective-permute-start(f32[2,128]{1,0:T(2,128)S(1)} %fusion.25), channel_id=1, source_target_pairs={{0,8},{1,9},{2,10},{3,11},{4,12},{5,13},{6,14},{7,15},{8,0},{9,1},... | collective-permute-start | bytes 3080 | tf_op jit(solution)/shard_map/ppermute | solution.py:108

commit v5 on v4

--- a/solution.py
+++ b/solution.py
@@ -115,16 +115,16 @@
 
 def copies_of(which, loads, sources, targets, arrived):
     made = []
-    for at, (kind, size) in enumerate(loads):
+    for at, (kind, size, place) in enumerate(loads):
         source, target = sources[at], targets[at]
         part = target.shape[0] // SPLIT
         for cut in range(SPLIT):
             rows = pl.ds(cut * part, part)
             if kind == "rows":
-                begin = pl.multiple_of(which[at] * size + cut * part, 16)
+                begin = pl.multiple_of(which[place] * size + cut * part, 16)
                 view = source.at[pl.ds(begin, part), :]
             else:
-                view = source.at[rows, pl.ds(pl.multiple_of(which[at] * size, 128), size)]
+                view = source.at[rows, pl.ds(pl.multiple_of(which[place] * size, 128), size)]
             made.append(
                 pltpu.make_async_copy(view, target.at[rows, :], arrived.at[at * SPLIT + cut])
             )
@@ -134,9 +134,9 @@
 def stage(which, loads, ins, outs, compute, scratch=(), limit=6, flops=0):
     vmem = pl.BlockSpec(memory_space=pltpu.VMEM)
     n, count = len(loads), len(ins)
-    kinds = [(kind, size) for kind, size, _ in loads]
+    kinds = [load[:3] for load in loads]
     shapes = list(outs)
-    for kind, size, array in loads:
+    for kind, size, _, array in loads:
         shape = (size, array.shape[1]) if kind == "rows" else (array.shape[0], size)
         shapes.append(jax.ShapeDtypeStruct(shape, array.dtype))
 
@@ -166,7 +166,7 @@
         cost_estimate=pl.CostEstimate(
             flops=flops, bytes_accessed=loaded, transcendentals=0
         ),
-    )(which, *[array for _, _, array in loads], *ins)
+    )(which, *[load[3] for load in loads], *ins)
 
 
 def basis_stage(which, loads, blocks, held, before, columns, features, squared, narrow):
@@ -321,6 +321,88 @@
         compiler_params=pltpu.CompilerParams(vmem_limit_bytes=6 * MIB),
         cost_estimate=pl.CostEstimate(flops=flops // 16, bytes_accessed=0, transcendentals=0),
     )(*hidden, *weights, *[c[0] for c in copies])
+
+
+def piece_body(flags, weight, states, gain, seeds, piece, rows):
+    half = weight.shape[0] // 2
+    count = states.shape[0]
+    piece[:half, :] = weight[pl.ds(pl.multiple_of(flags[4] * half, 16), half), :]
+    rows[...] = jnp.zeros_like(rows)
+    rows[:count, :] = states[...].astype(jnp.float32)
+    rows[count : count + 1, :] = gain[...].reshape(1, -1)
+    high = lax.shift_right_logical(seeds[...], 8)
+    low = seeds[...] - high * 256
+    width = seeds.shape[1]
+    rows[count + 1 : 2 * count + 1, :width] = high.astype(jnp.float32)
+    rows[2 * count + 1 : 3 * count + 1, :width] = low.astype(jnp.float32)
+    piece[half:, :] = rows[...].astype(jnp.bfloat16)
+
+
+def block_body(count, cands, flags, piece, first, second, weight, states, mean, spread, gain, value,
+               block, features, inputs, head, rows):
+    f32, bf16 = jnp.float32, jnp.bfloat16
+    half = weight.shape[0] // 2
+    act = weight.shape[0]
+    lower, home = flags[4] == 0, flags[5] == 1
+    same = jnp.where(home, piece[...], first[...])
+    other = jnp.where(home, first[...], second[...])
+    low = jnp.where(lower, same, other)
+    high = jnp.where(lower, other, same)
+    block[:half, :] = low[:half]
+    block[half:act, :] = high[:half]
+    parts = [low[half:].astype(f32), high[half:].astype(f32)]
+    rows[...] = jnp.zeros_like(rows)
+    for index, part in enumerate(parts):
+        rows[index * count : (index + 1) * count, :] = part[:count]
+    rows[2 * count : 2 * count + 1, :] = parts[0][count : count + 1]
+    block[act:, :] = rows[...].astype(bf16)
+
+    harmonic = (lax.broadcasted_iota(jnp.int32, (cands, act), 1) + 1).astype(f32)
+    diagonal = lax.broadcasted_iota(jnp.int32, (cands, cands), 0) == lax.broadcasted_iota(
+        jnp.int32, (cands, cands), 1
+    )
+    states_at = lax.broadcasted_iota(jnp.int32, (cands, SMALL), 1)
+    made = []
+    for state in range(2 * count):
+        part, at = parts[state // count], state % count
+        seed = (
+            part[count + 1 + at : count + 2 + at, :cands] * 256.0
+            + part[2 * count + 1 + at : 2 * count + 2 + at, :cands]
+        )
+        column = jnp.sum(jnp.where(diagonal, seed, 0.0), axis=1, keepdims=True)
+        product = column * harmonic
+        rest = product - modulus * jnp.floor(product * (1.0 / modulus))
+        rest = jnp.where(rest < 0.0, rest + modulus, rest)
+        rest = jnp.where(rest >= modulus, rest - modulus, rest)
+        wave = jnp.cos(rest * (2.0 * math.pi / modulus))
+        value_rows = (mean[...].reshape(1, -1) + spread[...].reshape(1, -1) * wave).astype(bf16)
+        made.append(value_rows)
+        to = slice(state * cands, (state + 1) * cands)
+        features[to, :act] = value_rows
+        features[to, act:] = (states_at == state).astype(f32).astype(bf16)
+    for at in range(count):
+        own = jnp.where(lower, made[at], made[count + at])
+        wide = jnp.dot(own, weight[...], preferred_element_type=f32)
+        wide = wide + states[at : at + 1, :].astype(f32)
+        inputs[at * cands : (at + 1) * cands, :] = wide.astype(bf16)
+    head[...] = (gain[...] * value[...]).reshape(1, -1)
+
+
+def whole_call(body, outs, scratch, after, *operands):
+    whole = lambda array: pl.BlockSpec(array.shape, lambda i: (0,) * len(array.shape))
+    count = len(after)
+    return pl.pallas_call(
+        lambda *refs: body(refs[count], *refs[count + 1 :]),
+        out_shape=outs,
+        grid=(1,),
+        in_specs=[pl.BlockSpec(memory_space=pl.ANY)] * count
+        + [pl.BlockSpec(memory_space=pltpu.SMEM)]
+        + [whole(array) for array in operands[1:]],
+        out_specs=[whole(array) for array in outs],
+        scratch_shapes=scratch,
+        compiler_params=pltpu.CompilerParams(vmem_limit_bytes=6 * MIB),
+        cost_estimate=pl.CostEstimate(flops=1000000, bytes_accessed=1000000, transcendentals=0),
+    )(*after, *operands)
 
 
 def local_blocks(
@@ -349,100 +431,97 @@
     every = [(t, d) for t in range(TP) for d in range(2)]
     swap_core = [((t, d), (t, 1 - d)) for t, d in every]
 
-    head = head_gain * value_weight
-    seeds = jnp.concatenate([action_seeds // 256, action_seeds % 256]).astype(bf16)
-    seeds_row = jnp.pad(seeds.reshape(1, -1), ((0, 0), (0, cols - seeds.size)))
-    small = jnp.concatenate([state_hidden, seeds_row, jnp.zeros((5, cols), bf16)])
-    small, head = lax.optimization_barrier((small, head))
-    other_small = send(small, swap_core)
-    low = jnp.where(dp == 0, small, other_small)
-    high = jnp.where(dp == 0, other_small, small)
-    own_block = jnp.concatenate(
-        [
-            action_weight,
-            low[:states],
-            high[:states],
-            norm_gain.astype(bf16)[None],
-            jnp.zeros((SMALL - 2 * states - 1, cols), bf16),
-        ]
-    )
-
-    far_block = send(own_block, [((t, t // 4), (t ^ 4, t // 4)) for t in range(TP)])
-    near_home = {
-        k: send(own_block, [((t, t // 4), (t ^ k, t // 4)) for t in range(TP)]) for k in (2, 1, 3)
-    }
-    block = jnp.where(home, own_block, far_block)
-    near = {}
-    for k in (2, 1, 3):
-        got = send(block, [((t, 1 - t // 4), (t ^ k, 1 - t // 4)) for t in range(TP)])
-        near[k] = jnp.where(home, near_home[k], got)
-
-    all_seeds = jnp.concatenate(
-        [part[states, : seeds.size].reshape(2, states, cands) for part in (low, high)],
-        axis=1,
-    ).astype(jnp.int32)
-    all_seeds = all_seeds[0] * 256 + all_seeds[1]
-    features = action_features(all_seeds, action_mean, action_spread).reshape(2 * rows, act)
-    row_state = jnp.arange(2 * rows) // cands
-    onehot = (row_state[:, None] == jnp.arange(SMALL)[None]).astype(bf16)
-    features = jnp.concatenate([features, onehot], axis=1)
-    own_features = lax.dynamic_slice(features, (dp * rows, 0), (rows, act))
-    embedded = jnp.dot(own_features, action_weight, preferred_element_type=f32)
-    inputs_local = (
-        (state_hidden.astype(f32)[:, None, :] + embedded.reshape(states, cands, cols))
-        .reshape(rows, cols)
-        .astype(bf16)
-    )
+    flags = jnp.stack([place, place ^ 1, place ^ 2, place ^ 3, dp, home.astype(jnp.int32)])
+    flags = flags.astype(jnp.int32)
+    out = jax.ShapeDtypeStruct
+    (piece,) = whole_call(
+        piece_body,
+        [out((half + SMALL, cols), bf16)],
+        [pltpu.VMEM((SMALL, cols), f32)],
+        [],
+        flags,
+        *[
+            pltpu.with_memory_space_constraint(array, pltpu.HBM)
+            for array in (action_weight, state_hidden, norm_gain, action_seeds)
+        ],
+    )
+
+    first = send(
+        piece,
+        [((t, t // 4), (t ^ 4, t // 4)) for t in range(TP)]
+        + [((t, 1 - t // 4), (t, t // 4)) for t in range(TP)],
+    )
+    second = send(piece, [((t, 1 - t // 4), (t ^ 4, t // 4)) for t in range(TP)])
 
     gate_weight, up_weight, down_weight = (
         pltpu.with_memory_space_constraint(weight, pltpu.HBM)
         for weight in (gate_weight, up_weight, down_weight)
     )
-    index = lambda *ks: jnp.stack([place ^ k for k in ks]).astype(jnp.int32)
-    pair = [("rows", cols, gate_weight), ("rows", cols, up_weight)]
-    column = [("cols", cols, down_weight)]
-    held = stage(index(0, 0), pair, [], [], None)
-    basis, *held = basis_stage(
-        index(2, 2), pair, [block], [held], None, (0, units), features, [], False
-    )
-    basis, *held = basis_stage(
-        index(1, 1), pair, [near[2]], [held], basis, (0, units), features, [], False
-    )
+    pair = lambda k: [("rows", cols, k, gate_weight), ("rows", cols, k, up_weight)]
+    column = lambda k: ("cols", cols, k, down_weight)
+    held = stage(flags, pair(0), [], [], None)
+
+    block, features, inputs_local, head = whole_call(
+        functools.partial(block_body, states, cands),
+        [
+            out((act + SMALL, cols), bf16),
+            out((2 * rows, act + SMALL), bf16),
+            out((rows, cols), bf16),
+            out((1, cols), f32),
+        ],
+        [pltpu.VMEM((SMALL, cols), f32)],
+        held,
+        flags,
+        piece,
+        first,
+        second,
+        action_weight,
+        state_hidden,
+        action_mean,
+        action_spread,
+        head_gain,
+        value_weight,
+    )
+
+    step = lambda array, k: send(array, [((t, d), (t ^ k, d)) for t, d in every])
+    near = {k: step(block, k) for k in (2, 1, 3)}
+
+    basis, *later = basis_stage(
+        flags, pair(2) + pair(1), [block], [held], None, (0, units), features, [], False
+    )
+    near_two = [near[2], near[1]]
     basis, square, *held = basis_stage(
-        index(3, 3),
-        pair,
-        [near[1]],
-        [held],
+        flags,
+        pair(3),
+        near_two,
+        [later[:2], later[2:]],
         basis,
         (0, units),
         features,
-        [block, near[2], near[1]],
+        [block] + near_two,
         False,
     )
     cut = units // 2
-    none = index(0)
     own_a, narrow_a, square_last = basis_stage(
-        none, [], [near[3]], [held], basis, (0, cut), features, [near[3]], True
+        flags, [], [near[3]], [held], basis, (0, cut), features, [near[3]], True
     )
     other_a = send(narrow_a, swap_core)
     square = square + square_last
     other_square = send(square, swap_core)
     own_b, narrow_b = basis_stage(
-        none, [], [near[3]], [held], basis, (cut, units), features, [], True
+        flags, [], [near[3]], [held], basis, (cut, units), features, [], True
     )
     other_b = send(narrow_b, swap_core)
-    down_first = stage(index(3, 1), column * 2, [], [], None)
+    down_first = stage(flags, [column(3), column(1)], [], [], None)
     hidden_a, down_z = hidden_stage(
-        index(2), column, own_a, other_a, features, square, other_square, full_width
+        flags, [column(2)], own_a, other_a, features, square, other_square, full_width
     )
     hidden_b, down_own = hidden_stage(
-        index(0), column, own_b, other_b, features, square, other_square, full_width
-    )
-    hidden_a, inputs_local, head = lax.optimization_barrier((hidden_a, inputs_local, head))
+        flags, [column(0)], own_b, other_b, features, square, other_square, full_width
+    )
     hidden = [hidden_a, hidden_b]
 
     both, lower, upper = (0, 1), (0,), (1,)
-    step = lambda array, k: send(array, [((t, d), (t ^ k, d)) for t, d in every])
     x_pair, diagonal_upper = down_products(
         hidden,
         down_first,
@@ -474,12 +553,15 @@
         add(own_lower, got_x[:, cols:], got_lower),
         add(own_upper, got_z[:, cols:], got_upper),
     ]
-    swapped = send(jnp.where(dp == 0, sums[1], sums[0]), swap_core)
-    stays = jnp.where(dp == 0, sums[0], sums[1])
-    got_far = step(jnp.where(home, swapped, stays), 4)
-    kept = jnp.where(home, stays, swapped)
-
-    summed = kept.astype(f32) + got_far.astype(f32)
+    far = [
+        send(sums[part], [((t, 1 - t // 4), (t ^ 4, part)) for t in range(TP)])
+        for part in range(2)
+    ]
+    crossed = send(
+        jnp.where(dp == 0, sums[1], sums[0]), [((t, t // 4), (t, 1 - t // 4)) for t in range(TP)]
+    )
+    mine = jnp.where(home, jnp.where(dp == 0, sums[0], sums[1]), crossed).astype(f32)
+    summed = mine + jnp.where(dp == 0, far[0], far[1]).astype(f32)
     output_local = (inputs_local.astype(f32) + summed).astype(bf16)
 
     wide_out = output_local.astype(f32)

time: 138 us -> 113 us (0.82)
  starting transfers between devices: 34.5 us -> 19.9 us
  local copies, waits for them, and re-layouts: 12.3 us -> 0.77 us
  waiting for transfers between devices: 38.3 us -> 43 us
  other arithmetic: 5.6 us -> 1.46 us
    ppermute x20 -> x18, starting transfers between devices: 34.5 us -> 19.9 us  [send(): lax.ppermute(array, ('tp', 'dp'), [(2 * st + sd, 2 * dt + dd) for (st, sd...]
    unnamed x20 -> x12, local copies, waits for them, and re-layouts: 10.8 us -> 0.04 us
    ppermute x20 -> x18, waiting for transfers between devices: 38.3 us -> 43 us  [send(): lax.ppermute(array, ('tp', 'dp'), [(2 * st + sd, 2 * dt + dd) for (st, sd...]
    pallas_call x0 -> x2, Pallas kernels: none -> 2.34 us  [whole_call(): pl.pallas_call(lambda *refs: body(refs[count], *refs[count + 1:]), out_sh...]
    convert_element_type x4 -> x0, other arithmetic: 1.39 us -> none  [the longest x1 0.69 us: local_blocks(): norm_gain.astype(bf16)[None]]
    pallas_call x9 -> x8, Pallas kernels: 38.2 us -> 37 us  [stage(): pl.pallas_call(body, out_shape=shapes, in_specs=[pl.BlockSpec(memory_spac...]
  transfers between devices with their start and end apart: 20 -> 18, of which waited for: 9 -> 9; matrix products, arithmetic and copies ran while one was open for 2% -> 0% of each run, Pallas kernels for 26% -> 32%
where the time goes in v5:
time: 113 us; the launch traced here: 112 us
  Pallas kernels  46.3 us (41%)
  waiting for transfers between devices  43 us (38%)
  starting transfers between devices  19.9 us (18%)
  other arithmetic  1.46 us (1%)
    ppermute x18, waiting for transfers between devices, send(): lax.ppermute(array, ('tp', 'dp'), [(2 * st + sd, 2 * dt + dd) for (st, sd...  43 us
    pallas_call x8, Pallas kernels, stage(): pl.pallas_call(body, out_shape=shapes, in_specs=[pl.BlockSpec(memory_spac...  37 us
    ppermute x18, starting transfers between devices, send(): lax.ppermute(array, ('tp', 'dp'), [(2 * st + sd, 2 * dt + dd) for (st, sd...  19.9 us
    pallas_call x3, Pallas kernels, down_products(): pl.pallas_call(body, out_shape=[jax.ShapeDtypeStruct((rows // 2, width),...  7 us
    pallas_call x2, Pallas kernels, whole_call(): pl.pallas_call(lambda *refs: body(refs[count], *refs[count + 1:]), out_sh...  2.34 us
  transfers between devices with their start and end apart: 18, of which 9 were waited for; matrix products, arithmetic and copies ran while one was open for 0% of the time, Pallas kernels for 32%

profile of v5, /device:TPU:0, one launch (start us, length us, event | category | flops | bytes accessed | tf_op | source)
XLA Modules:
  0.0 112.4 jit_solution(5618704874277646378)
XLA Ops:
  0.7 1.0 shard_map.123.refs_3_
  1.8 4.1 %collective-permute-start = (bf16[80,1024]{1,0:T(8,128)(2,1)S(1)}, bf16[80,1024]{1,0:T(8,128)(2,1)S(1)}, u32[]{:S(2)}, u32[]{:S(2)}) collective-permute-start(bf16[80,1024]{1,0:T(8,128)(2,1)S(1)} %shard_map.123.refs_3_), channel_id=1, source_target_pairs={{0,8},{2,10},{4,12},{6,14},{9,1},{11,3},{13,5},{15,7},{1,0},{3,2},... | collective-permute-start | bytes 491528 | tf_op jit(solution)/shard_map/ppermute | solution.py:108
  6.6 5.2 %shard_map.122 = (bf16[1024,3072]{1,0:T(8,128)(2,1)S(1)}, bf16[1024,3072]{1,0:T(8,128)(2,1)S(1)}) custom-call(s32[6]{0:T(128)S(1)} %stack.40.which_ref.refs_0_.refs_2_, bf16[4096,3072]{1,0:T(8,128)(2,1)} %refs_0_.8, bf16[4096,3072]{1,0:T(8,128)(2,1)} %refs_1_.8), custom_call_target="tpu_custom_call" | custom-call | bytes 12582912 | tf_op jit(solution)/shard_map/pallas_call | solution.py:157
  11.9 1.3 %shard_map.124 = (bf16[144,1024]{1,0:T(8,128)(2,1)S(1)}, bf16[256,144]{1,0:T(8,128)(2,1)S(1)}, bf16[128,1024]{1,0:T(8,128)(2,1)S(1)}, f32[1,1024]{1,0:T(1,128)S(1)}) custom-call(bf16[1024,3072]{1,0:T(8,128)(2,1)S(1)} %get-tuple-element.34.refs_0_.refs_5_, bf16[1024,3072]{1,0:T(8,128)(2,1)S(1)} %get-tuple-element.35.refs_1_.refs_6_, ...), custom_call_target="tpu_custom_call" | custom-call | flops 1000000 | bytes 1000000 | tf_op jit(solution)/shard_map/pallas_call | solution.py:394
  13.3 3.6 %collective-permute-start.3 = (bf16[144,1024]{1,0:T(8,128)(2,1)S(1)}, bf16[144,1024]{1,0:T(8,128)(2,1)S(1)}, u32[]{:S(2)}, u32[]{:S(2)}) collective-permute-start(bf16[144,1024]{1,0:T(8,128)(2,1)S(1)} %get-tuple-element.37.refs_4_.refs_9_), channel_id=1, source_target_pairs={{0,4},{1,5},{2,6},{3,7},{4,0},{5,1},{6,2},{7,3},{8,12},{9,13},{10,... | collective-permute-start | bytes 884744 | tf_op jit(solution)/shard_map/ppermute | solution.py:108
  16.8 1.5 %collective-permute-start.4 = (bf16[144,1024]{1,0:T(8,128)(2,1)S(1)}, bf16[144,1024]{1,0:T(8,128)(2,1)S(1)}, u32[]{:S(2)}, u32[]{:S(2)}) collective-permute-start(bf16[144,1024]{1,0:T(8,128)(2,1)S(1)} %get-tuple-element.37.refs_4_.refs_9_), channel_id=1, source_target_pairs={{0,2},{1,3},{2,0},{3,1},{4,6},{5,7},{6,4},{7,5},{8,10},{9,11},{10,... | collective-permute-start | bytes 884744 | tf_op jit(solution)/shard_map/ppermute | solution.py:108
  18.4 8.9 %shard_map.125 = (f32[2,144,3072]{2,1,0:T(8,128)S(1)}, bf16[1024,3072]{1,0:T(8,128)(2,1)S(1)}, bf16[1024,3072]{1,0:T(8,128)(2,1)S(1)}, bf16[1024,3072]{1,0:T(8,128)(2,1)S(1)}, bf16[1024,3072]{1,0:T(8,128)(2,1)S(1)}) custom-call(s32[6]{0:T(128)S(1)} %stack.40.which_ref.refs_0_.refs_2_, bf16[4096,3072]{1,0:T(8,128)(2,1)} %refs_0_.8, ...), custom_call_target="tpu_custom_call" | custom-call | flops 1811939328 | bytes 25165824 | tf_op jit(solution)/shard_map/pallas_call | solution.py:157
  27.3 4.8 %collective-permute-done.4.refs_3_.refs_11_ = bf16[144,1024]{1,0:T(8,128)(2,1)S(1)} collective-permute-done((bf16[144,1024]{1,0:T(8,128)(2,1)S(1)}, bf16[144,1024]{1,0:T(8,128)(2,1)S(1)}, u32[]{:S(2)}, u32[]{:S(2)}) %collective-permute-start.4) | collective-permute-done | bytes 294944 | tf_op jit(solution)/shard_map/ppermute | solution.py:108
  32.1 6.2 %shard_map.126 = (f32[2,144,3072]{2,1,0:T(8,128)S(1)}, f32[256,128]{1,0:T(8,128)S(1)}, bf16[1024,3072]{1,0:T(8,128)(2,1)S(1)}, bf16[1024,3072]{1,0:T(8,128)(2,1)S(1)}) custom-call(s32[6]{0:T(128)S(1)} %stack.40.which_ref.refs_0_.refs_2_, bf16[4096,3072]{1,0:T(8,128)(2,1)} %refs_0_.8, bf16[4096,3072]{1,0:T(8,128)(2,1)} %refs_1_.8, ...), custom_call_target="tpu_custom_call" | custom-call | flops 3623878656 | bytes 12582912 | tf_op jit(solution)/shard_map/pallas_call | solution.py:157
  38.3 2.1 %shard_map.129 = (f32[2,144,1536]{2,1,0:T(8,128)S(1)}, bf16[2,144,1536]{2,1,0:T(8,128)(2,1)S(1)}) custom-call(s32[6]{0:T(128)S(1)} %stack.40.which_ref.refs_0_.refs_2_, bf16[144,1024]{1,0:T(8,128)(2,1)S(1)} %collective-permute-done.2.refs_0_.refs_4_, bf16[1024,3072]{1,0:T(8,128)(2,1)S(1)} %get-tuple-element.44.refs_1_, ...), custom_call_target="tpu_custom_call" | custom-call | flops 905969664 | tf_op jit(solution)/shard_map/pallas_call | solution.py:157
  40.5 2.4 %shard_map.127 = (f32[2,144,1536]{2,1,0:T(8,128)S(1)}, bf16[2,144,1536]{2,1,0:T(8,128)(2,1)S(1)}, f32[256,128]{1,0:T(8,128)S(1)}) custom-call(s32[6]{0:T(128)S(1)} %stack.40.which_ref.refs_0_.refs_2_, bf16[144,1024]{1,0:T(8,128)(2,1)S(1)} %collective-permute-done.2.refs_0_.refs_4_, bf16[1024,3072]{1,0:T(8,128)(2,1)S(1)} %get-tuple-element.44.refs_1_, ...), custom_call_target="tpu_custom_call" | custom-call | flops 905969664 | tf_op jit(solution)/shard_map/pallas_call | solution.py:157
  43.5 5.3 %shard_map.131 = (bf16[3072,1024]{1,0:T(8,128)(2,1)S(1)}, bf16[3072,1024]{1,0:T(8,128)(2,1)S(1)}) custom-call(s32[6]{0:T(128)S(1)} %stack.40.which_ref.refs_0_.refs_2_, bf16[3072,4096]{1,0:T(8,128)(2,1)} %refs_1_.9, bf16[3072,4096]{1,0:T(8,128)(2,1)} %refs_1_.9), custom_call_target="tpu_custom_call" | custom-call | bytes 12582912 | tf_op jit(solution)/shard_map/pallas_call | solution.py:157
  48.9 3.4 %shard_map.130 = (bf16[256,1536]{1,0:T(8,128)(2,1)S(1)}, bf16[3072,1024]{1,0:T(8,128)(2,1)S(1)}) custom-call(s32[6]{0:T(128)S(1)} %stack.40.which_ref.refs_0_.refs_2_, bf16[3072,4096]{1,0:T(8,128)(2,1)} %refs_1_.9, f32[2,144,1536]{2,1,0:T(8,128)S(1)} %get-tuple-element.52.refs_1_, bf16[2,144,1536]{2,1,0:T(8,128)(2,1)S(1)} %collective-permute-done.7.refs_2_, ...), custom_call_target="tpu_custom_call" | custom-call | flops 226492416 | bytes 6291456 | tf_op jit(solution)/shard_map/pallas_call | solution.py:157
  52.3 3.4 %shard_map.128 = (bf16[256,1536]{1,0:T(8,128)(2,1)S(1)}, bf16[3072,1024]{1,0:T(8,128)(2,1)S(1)}) custom-call(s32[6]{0:T(128)S(1)} %stack.40.which_ref.refs_0_.refs_2_, bf16[3072,4096]{1,0:T(8,128)(2,1)} %refs_1_.9, f32[2,144,1536]{2,1,0:T(8,128)S(1)} %get-tuple-element.47.refs_1_, bf16[2,144,1536]{2,1,0:T(8,128)(2,1)S(1)} %collective-permute-done.5.refs_2_, ...), custom_call_target="tpu_custom_call" | custom-call | flops 226492416 | bytes 6291456 | tf_op jit(solution)/shard_map/pallas_call | solution.py:157
  55.8 2.6 %shard_map.133 = (bf16[128,2048]{1,0:T(8,128)(2,1)S(1)}, bf16[128,1024]{1,0:T(8,128)(2,1)S(1)}) custom-call(bf16[256,1536]{1,0:T(8,128)(2,1)S(1)} %get-tuple-element.51.refs_0_, bf16[256,1536]{1,0:T(8,128)(2,1)S(1)} %get-tuple-element.54.refs_1_, bf16[3072,1024]{1,0:T(8,128)(2,1)S(1)} %get-tuple-element.59.refs_2_, ...), custom_call_target="tpu_custom_call" | custom-call | flops 150994944 | tf_op jit(solution)/shard_map/pallas_call | solution.py:316
  58.4 1.6 %collective-permute-start.8 = (bf16[128,2048]{1,0:T(8,128)(2,1)S(1)}, bf16[128,2048]{1,0:T(8,128)(2,1)S(1)}, u32[]{:S(2)}, u32[]{:S(2)}) collective-permute-start(bf16[128,2048]{1,0:T(8,128)(2,1)S(1)} %get-tuple-element.60), channel_id=1, source_target_pairs={{0,2},{1,3},{2,0},{3,1},{4,6},{5,7},{6,4},{7,5},{8,10},{9,11},{10,... | collective-permute-start | bytes 1572872 | tf_op jit(solution)/shard_map/ppermute | solution.py:108
  59.9 1.0 shard_map.134
  61.3 3.4 %shard_map.132 = (bf16[128,1024]{1,0:T(8,128)(2,1)S(1)}, bf16[128,1024]{1,0:T(8,128)(2,1)S(1)}, bf16[128,1024]{1,0:T(8,128)(2,1)S(1)}, bf16[128,1024]{1,0:T(8,128)(2,1)S(1)}) custom-call(bf16[256,1536]{1,0:T(8,128)(2,1)S(1)} %get-tuple-element.51.refs_0_, bf16[256,1536]{1,0:T(8,128)(2,1)S(1)} %get-tuple-element.54.refs_1_, ...), custom_call_target="tpu_custom_call" | custom-call | flops 201326592 | tf_op jit(solution)/shard_map/pallas_call | solution.py:316
  64.8 8.0 %collective-permute-done.8 = bf16[128,2048]{1,0:T(8,128)(2,1)S(1)} collective-permute-done((bf16[128,2048]{1,0:T(8,128)(2,1)S(1)}, bf16[128,2048]{1,0:T(8,128)(2,1)S(1)}, u32[]{:S(2)}, u32[]{:S(2)}) %collective-permute-start.8) | collective-permute-done | bytes 524320 | tf_op jit(solution)/shard_map/ppermute | solution.py:108
  73.0 2.0 %collective-permute-done.10 = bf16[128,2048]{1,0:T(8,128)(2,1)S(1)} collective-permute-done((bf16[128,2048]{1,0:T(8,128)(2,1)S(1)}, bf16[128,2048]{1,0:T(8,128)(2,1)S(1)}, u32[]{:S(2)}, u32[]{:S(2)}) %collective-permute-start.10) | collective-permute-done | bytes 524320 | tf_op jit(solution)/shard_map/ppermute | solution.py:108
  75.7 5.1 %collective-permute-done.9 = bf16[128,1024]{1,0:T(8,128)(2,1)S(1)} collective-permute-done((bf16[128,1024]{1,0:T(8,128)(2,1)S(1)}, bf16[128,1024]{1,0:T(8,128)(2,1)S(1)}, u32[]{:S(2)}, u32[]{:S(2)}) %collective-permute-start.9) | collective-permute-done | bytes 262176 | tf_op jit(solution)/shard_map/ppermute | solution.py:108
  80.8 2.0 %collective-permute-done.11 = bf16[128,1024]{1,0:T(8,128)(2,1)S(1)} collective-permute-done((bf16[128,1024]{1,0:T(8,128)(2,1)S(1)}, bf16[128,1024]{1,0:T(8,128)(2,1)S(1)}, u32[]{:S(2)}, u32[]{:S(2)}) %collective-permute-start.11) | collective-permute-done | bytes 262176 | tf_op jit(solution)/shard_map/ppermute | solution.py:108
  83.1 1.3 %collective-permute-start.12 = (bf16[128,1024]{1,0:T(8,128)(2,1)S(1)}, bf16[128,1024]{1,0:T(8,128)(2,1)S(1)}, u32[]{:S(2)}, u32[]{:S(2)}) collective-permute-start(bf16[128,1024]{1,0:T(8,128)(2,1)S(1)} %get-tuple-element.69), channel_id=1, source_target_pairs={{0,1},{2,3},{4,5},{6,7},{9,8},{11,10},{13,12},{15,14},{16,17},{18,... | collective-permute-start | bytes 786440 | tf_op jit(solution)/shard_map/ppermute | solution.py:108
  84.4 1.3 %collective-permute-start.13 = (bf16[128,1024]{1,0:T(8,128)(2,1)S(1)}, bf16[128,1024]{1,0:T(8,128)(2,1)S(1)}, u32[]{:S(2)}, u32[]{:S(2)}) collective-permute-start(bf16[128,1024]{1,0:T(8,128)(2,1)S(1)} %get-tuple-element.71), channel_id=1, source_target_pairs={{1,8},{3,10},{5,12},{7,14},{8,0},{10,2},{12,4},{14,6},{17,24},{19,... | collective-permute-start | bytes 786440 | tf_op jit(solution)/shard_map/ppermute | solution.py:108
  85.7 0.7 collective-permute-start.14
  86.4 12.6 %collective-permute-done.13 = bf16[128,1024]{1,0:T(8,128)(2,1)S(1)} collective-permute-done((bf16[128,1024]{1,0:T(8,128)(2,1)S(1)}, bf16[128,1024]{1,0:T(8,128)(2,1)S(1)}, u32[]{:S(2)}, u32[]{:S(2)}) %collective-permute-start.13) | collective-permute-done | bytes 262176 | tf_op jit(solution)/shard_map/ppermute | solution.py:108
  99.0 1.0 fusion
  99.9 0.8 collective-permute-start.15
  100.7 2.8 %collective-permute-done.15 = f32[2,128]{1,0:T(2,128)S(1)} collective-permute-done((f32[2,128]{1,0:T(2,128)S(1)}, f32[2,128]{1,0:T(2,128)S(1)}, u32[]{:S(2)}, u32[]{:S(2)}) %collective-permute-start.15) | collective-permute-done | bytes 1056 | tf_op jit(solution)/shard_map/ppermute | solution.py:108
  103.7 3.6 %collective-permute-done.16 = f32[2,128]{1,0:T(2,128)S(1)} collective-permute-done((f32[2,128]{1,0:T(2,128)S(1)}, f32[2,128]{1,0:T(2,128)S(1)}, u32[]{:S(2)}, u32[]{:S(2)}) %collective-permute-start.16) | collective-permute-done | bytes 1056 | tf_op jit(solution)/shard_map/ppermute | solution.py:108
  107.2 2.4 %collective-permute-start.17 = (f32[2,128]{1,0:T(2,128)S(1)}, f32[2,128]{1,0:T(2,128)S(1)}, u32[]{:S(2)}, u32[]{:S(2)}) collective-permute-start(f32[2,128]{1,0:T(2,128)S(1)} %fusion.3), channel_id=1, source_target_pairs={{0,8},{1,9},{2,10},{3,11},{4,12},{5,13},{6,14},{7,15},{8,0},{9,1},... | collective-permute-start | bytes 3080 | tf_op jit(solution)/shard_map/ppermute | solution.py:108
  109.6 2.1 %collective-permute-done.17 = f32[2,128]{1,0:T(2,128)S(1)} collective-permute-done((f32[2,128]{1,0:T(2,128)S(1)}, f32[2,128]{1,0:T(2,128)S(1)}, u32[]{:S(2)}, u32[]{:S(2)}) %collective-permute-start.17) | collective-permute-done | bytes 1056 | tf_op jit(solution)/shard_map/ppermute | solution.py:108
  (41 shorter events, 4.0 us)
Async XLA Ops:
  1.7 10.1 %copy-start = (bf16[128,1024]{1,0:T(8,128)(2,1)S(1)}, bf16[128,1024]{1,0:T(8,128)(2,1)}, u32[]{:S(2)}) copy-start(bf16[128,1024]{1,0:T(8,128)(2,1)} %refs_6_.1) | copy-start | bytes 786436
  1.8 10.1 %copy-start.1 = (bf16[2,1024]{1,0:T(2,128)(2,1)S(1)}, bf16[2,1024]{1,0:T(2,128)(2,1)}, u32[]{:S(2)}) copy-start(bf16[2,1024]{1,0:T(2,128)(2,1)} %refs_7_.1) | copy-start | bytes 12292
  1.8 10.1 %copy-start.2 = (f32[1024]{0:T(1024)S(1)}, f32[1024]{0:T(1024)}, u32[]{:S(2)}) copy-start(f32[1024]{0:T(1024)} %refs_10_.1) | copy-start | bytes 12292
  1.8 10.1 %copy-start.3 = (f32[1024]{0:T(1024)S(1)}, f32[1024]{0:T(1024)}, u32[]{:S(2)}) copy-start(f32[1024]{0:T(1024)} %refs_11_.1) | copy-start | bytes 12292
  1.8 10.1 %copy-start.4 = (f32[128]{0:T(128)S(1)}, f32[128]{0:T(128)}, u32[]{:S(2)}) copy-start(f32[128]{0:T(128)} %refs_8_.1) | copy-start | bytes 1540
  1.8 10.1 %copy-start.5 = (f32[128]{0:T(128)S(1)}, f32[128]{0:T(128)}, u32[]{:S(2)}) copy-start(f32[128]{0:T(128)} %refs_9_.1) | copy-start | bytes 1540
  1.8 10.0 %collective-permute-start = (bf16[80,1024]{1,0:T(8,128)(2,1)S(1)}, bf16[80,1024]{1,0:T(8,128)(2,1)S(1)}, u32[]{:S(2)}, u32[]{:S(2)}) collective-permute-start(bf16[80,1024]{1,0:T(8,128)(2,1)S(1)} %shard_map.123.refs_3_), channel_id=1, source_target_pairs={{0,8},{2,10},{4,12},{6,14},{9,1},{11,3},{13,5},{15,7},{1,0},{3,2},... | collective-permute-start | bytes 491528 | tf_op jit(solution)/shard_map/ppermute | solution.py:108
  5.9 5.9 %collective-permute-start.1 = (bf16[80,1024]{1,0:T(8,128)(2,1)S(1)}, bf16[80,1024]{1,0:T(8,128)(2,1)S(1)}, u32[]{:S(2)}, u32[]{:S(2)}) collective-permute-start(bf16[80,1024]{1,0:T(8,128)(2,1)S(1)} %shard_map.123.refs_3_), channel_id=1, source_target_pairs={{1,8},{3,10},{5,12},{7,14},{8,1},{10,3},{12,5},{14,7},{17,24},{19,... | collective-permute-start | bytes 491528 | tf_op jit(solution)/shard_map/ppermute | solution.py:108
  13.3 14.0 %collective-permute-start.3 = (bf16[144,1024]{1,0:T(8,128)(2,1)S(1)}, bf16[144,1024]{1,0:T(8,128)(2,1)S(1)}, u32[]{:S(2)}, u32[]{:S(2)}) collective-permute-start(bf16[144,1024]{1,0:T(8,128)(2,1)S(1)} %get-tuple-element.37.refs_4_.refs_9_), channel_id=1, source_target_pairs={{0,4},{1,5},{2,6},{3,7},{4,0},{5,1},{6,2},{7,3},{8,12},{9,13},{10,... | collective-permute-start | bytes 884744 | tf_op jit(solution)/shard_map/ppermute | solution.py:108
  16.8 15.3 %collective-permute-start.4 = (bf16[144,1024]{1,0:T(8,128)(2,1)S(1)}, bf16[144,1024]{1,0:T(8,128)(2,1)S(1)}, u32[]{:S(2)}, u32[]{:S(2)}) collective-permute-start(bf16[144,1024]{1,0:T(8,128)(2,1)S(1)} %get-tuple-element.37.refs_4_.refs_9_), channel_id=1, source_target_pairs={{0,2},{1,3},{2,0},{3,1},{4,6},{5,7},{6,4},{7,5},{8,10},{9,11},{10,... | collective-permute-start | bytes 884744 | tf_op jit(solution)/shard_map/ppermute | solution.py:108
  18.3 20.0 %collective-permute-start.2 = (bf16[144,1024]{1,0:T(8,128)(2,1)S(1)}, bf16[144,1024]{1,0:T(8,128)(2,1)S(1)}, u32[]{:S(2)}, u32[]{:S(2)}) collective-permute-start(bf16[144,1024]{1,0:T(8,128)(2,1)S(1)} %get-tuple-element.37.refs_4_.refs_9_), channel_id=1, source_target_pairs={{0,6},{1,7},{2,4},{3,5},{4,2},{5,3},{6,0},{7,1},{8,14},{9,15},{10,... | collective-permute-start | bytes 884744 | tf_op jit(solution)/shard_map/ppermute | solution.py:108
  40.4 8.4 %collective-permute-start.7 = (bf16[2,144,1536]{2,1,0:T(8,128)(2,1)S(1)}, bf16[2,144,1536]{2,1,0:T(8,128)(2,1)S(1)}, u32[]{:S(2)}, u32[]{:S(2)}) collective-permute-start(bf16[2,144,1536]{2,1,0:T(8,128)(2,1)S(1)} %get-tuple-element.53), channel_id=1, source_target_pairs={{0,1},{1,0},{2,3},{3,2},{4,5},{5,4},{6,7},{7,6},{8,9},{9,8},{10,11... | collective-permute-start | bytes 2654216 | tf_op jit(solution)/shard_map/ppermute | solution.py:108
  42.9 9.4 %collective-permute-start.5 = (bf16[2,144,1536]{2,1,0:T(8,128)(2,1)S(1)}, bf16[2,144,1536]{2,1,0:T(8,128)(2,1)S(1)}, u32[]{:S(2)}, u32[]{:S(2)}) collective-permute-start(bf16[2,144,1536]{2,1,0:T(8,128)(2,1)S(1)} %get-tuple-element.48), channel_id=1, source_target_pairs={{0,1},{1,0},{2,3},{3,2},{4,5},{5,4},{6,7},{7,6},{8,9},{9,8},{10,11... | collective-permute-start | bytes 2654216 | tf_op jit(solution)/shard_map/ppermute | solution.py:108
  43.5 5.4 %collective-permute-start.6 = (f32[256,128]{1,0:T(8,128)S(1)}, f32[256,128]{1,0:T(8,128)S(1)}, u32[]{:S(2)}, u32[]{:S(2)}) collective-permute-start(f32[256,128]{1,0:T(8,128)S(1)} %add.50.refs_4_), channel_id=1, source_target_pairs={{0,1},{1,0},{2,3},{3,2},{4,5},{5,4},{6,7},{7,6},{8,9},{9,8},{10,11... | collective-permute-start | bytes 393224 | tf_op jit(solution)/shard_map/ppermute | solution.py:108
  58.4 14.4 %collective-permute-start.8 = (bf16[128,2048]{1,0:T(8,128)(2,1)S(1)}, bf16[128,2048]{1,0:T(8,128)(2,1)S(1)}, u32[]{:S(2)}, u32[]{:S(2)}) collective-permute-start(bf16[128,2048]{1,0:T(8,128)(2,1)S(1)} %get-tuple-element.60), channel_id=1, source_target_pairs={{0,2},{1,3},{2,0},{3,1},{4,6},{5,7},{6,4},{7,5},{8,10},{9,11},{10,... | collective-permute-start | bytes 1572872 | tf_op jit(solution)/shard_map/ppermute | solution.py:108
  60.9 14.1 %collective-permute-start.10 = (bf16[128,2048]{1,0:T(8,128)(2,1)S(1)}, bf16[128,2048]{1,0:T(8,128)(2,1)S(1)}, u32[]{:S(2)}, u32[]{:S(2)}) collective-permute-start(bf16[128,2048]{1,0:T(8,128)(2,1)S(1)} %shard_map.134), channel_id=1, source_target_pairs={{0,4},{1,5},{2,6},{3,7},{4,0},{5,1},{6,2},{7,3},{8,12},{9,13},{10,... | collective-permute-start | bytes 1572872 | tf_op jit(solution)/shard_map/ppermute | solution.py:108
  72.8 8.0 %collective-permute-start.9 = (bf16[128,1024]{1,0:T(8,128)(2,1)S(1)}, bf16[128,1024]{1,0:T(8,128)(2,1)S(1)}, u32[]{:S(2)}, u32[]{:S(2)}) collective-permute-start(bf16[128,1024]{1,0:T(8,128)(2,1)S(1)} %add_convert_fusion.4), channel_id=1, source_target_pairs={{0,4},{1,5},{2,6},{3,7},{4,0},{5,1},{6,2},{7,3},{8,12},{9,13},{10,... | collective-permute-start | bytes 786440 | tf_op jit(solution)/shard_map/ppermute | solution.py:108
  75.1 7.7 %collective-permute-start.11 = (bf16[128,1024]{1,0:T(8,128)(2,1)S(1)}, bf16[128,1024]{1,0:T(8,128)(2,1)S(1)}, u32[]{:S(2)}, u32[]{:S(2)}) collective-permute-start(bf16[128,1024]{1,0:T(8,128)(2,1)S(1)} %add_convert_fusion.2), channel_id=1, source_target_pairs={{0,2},{1,3},{2,0},{3,1},{4,6},{5,7},{6,4},{7,5},{8,10},{9,11},{10,... | collective-permute-start | bytes 786440 | tf_op jit(solution)/shard_map/ppermute | solution.py:108
  83.1 3.3 %collective-permute-start.12 = (bf16[128,1024]{1,0:T(8,128)(2,1)S(1)}, bf16[128,1024]{1,0:T(8,128)(2,1)S(1)}, u32[]{:S(2)}, u32[]{:S(2)}) collective-permute-start(bf16[128,1024]{1,0:T(8,128)(2,1)S(1)} %get-tuple-element.69), channel_id=1, source_target_pairs={{0,1},{2,3},{4,5},{6,7},{9,8},{11,10},{13,12},{15,14},{16,17},{18,... | collective-permute-start | bytes 786440 | tf_op jit(solution)/shard_map/ppermute | solution.py:108
  84.4 14.6 %collective-permute-start.13 = (bf16[128,1024]{1,0:T(8,128)(2,1)S(1)}, bf16[128,1024]{1,0:T(8,128)(2,1)S(1)}, u32[]{:S(2)}, u32[]{:S(2)}) collective-permute-start(bf16[128,1024]{1,0:T(8,128)(2,1)S(1)} %get-tuple-element.71), channel_id=1, source_target_pairs={{1,8},{3,10},{5,12},{7,14},{8,0},{10,2},{12,4},{14,6},{17,24},{19,... | collective-permute-start | bytes 786440 | tf_op jit(solution)/shard_map/ppermute | solution.py:108
  85.7 13.3 %collective-permute-start.14 = (bf16[128,1024]{1,0:T(8,128)(2,1)S(1)}, bf16[128,1024]{1,0:T(8,128)(2,1)S(1)}, u32[]{:S(2)}, u32[]{:S(2)}) collective-permute-start(bf16[128,1024]{1,0:T(8,128)(2,1)S(1)} %get-tuple-element.70), channel_id=1, source_target_pairs={{1,9},{3,11},{5,13},{7,15},{8,1},{10,3},{12,5},{14,7},{17,25},{19,... | collective-permute-start | bytes 786440 | tf_op jit(solution)/shard_map/ppermute | solution.py:108
  99.9 3.6 %collective-permute-start.15 = (f32[2,128]{1,0:T(2,128)S(1)}, f32[2,128]{1,0:T(2,128)S(1)}, u32[]{:S(2)}, u32[]{:S(2)}) collective-permute-start(f32[2,128]{1,0:T(2,128)S(1)} %pad_maximum_fusion), channel_id=1, source_target_pairs={{0,2},{1,3},{2,0},{3,1},{4,6},{5,7},{6,4},{7,5},{8,10},{9,11},{10,... | collective-permute-start | bytes 3080 | tf_op jit(solution)/shard_map/ppermute | solution.py:108
  103.6 3.6 %collective-permute-start.16 = (f32[2,128]{1,0:T(2,128)S(1)}, f32[2,128]{1,0:T(2,128)S(1)}, u32[]{:S(2)}, u32[]{:S(2)}) collective-permute-start(f32[2,128]{1,0:T(2,128)S(1)} %fusion.2), channel_id=1, source_target_pairs={{0,4},{1,5},{2,6},{3,7},{4,0},{5,1},{6,2},{7,3},{8,12},{9,13},{10,... | collective-permute-start | bytes 3080 | tf_op jit(solution)/shard_map/ppermute | solution.py:108
  107.2 4.5 %collective-permute-start.17 = (f32[2,128]{1,0:T(2,128)S(1)}, f32[2,128]{1,0:T(2,128)S(1)}, u32[]{:S(2)}, u32[]{:S(2)}) collective-permute-start(f32[2,128]{1,0:T(2,128)S(1)} %fusion.3), channel_id=1, source_target_pairs={{0,8},{1,9},{2,10},{3,11},{4,12},{5,13},{6,14},{7,15},{8,0},{9,1},... | collective-permute-start | bytes 3080 | tf_op jit(solution)/shard_map/ppermute | solution.py:108

commit v6 on v5

--- a/solution.py
+++ b/solution.py
@@ -110,7 +110,7 @@
     )
 
 
-SPLIT = 4
+SPLIT = 8
 
 
 def copies_of(which, loads, sources, targets, arrived):
@@ -131,7 +131,7 @@
     return made
 
 
-def stage(which, loads, ins, outs, compute, scratch=(), limit=6, flops=0):
+def stage(which, loads, ins, outs, compute, scratch=(), limit=3, flops=0, alias=None):
     vmem = pl.BlockSpec(memory_space=pltpu.VMEM)
     n, count = len(loads), len(ins)
     kinds = [load[:3] for load in loads]
@@ -162,6 +162,7 @@
         + [vmem] * count,
         out_specs=[vmem] * len(shapes),
         scratch_shapes=([pltpu.SemaphoreType.DMA((n * SPLIT,))] if n else []) + list(scratch),
+        input_output_aliases={} if alias is None else {1 + n + alias: 0},
         compiler_params=pltpu.CompilerParams(vmem_limit_bytes=limit * MIB),
         cost_estimate=pl.CostEstimate(
             flops=flops, bytes_accessed=loaded, transcendentals=0
@@ -169,60 +170,79 @@
     )(which, *[load[3] for load in loads], *ins)
 
 
-def basis_stage(which, loads, blocks, held, before, columns, features, squared, narrow):
-    m, k = blocks[0].shape
+def to_row(column):
+    size = column.shape[0]
+    rows = lax.broadcasted_iota(jnp.int32, (size, size), 0)
+    cols = lax.broadcasted_iota(jnp.int32, (size, size), 1)
+    return jnp.sum(jnp.where(rows == cols, column, 0.0), axis=0, keepdims=True)
+
+
+def to_column(row):
+    size = row.shape[1]
+    rows = lax.broadcasted_iota(jnp.int32, (size, size), 0)
+    cols = lax.broadcasted_iota(jnp.int32, (size, size), 1)
+    return jnp.sum(jnp.where(rows == cols, row, 0.0), axis=1, keepdims=True)
+
+
+def basis_stage(
+    which, loads, block, held, before, columns, features, squares, narrow, keep=()
+):
+    m, k = block.shape
     start, stop = columns
     width = stop - start
     tile = 512
-    count = len(blocks)
-    ins = list(blocks) + [part for pair in held for part in pair]
-    if before is not None:
-        ins.append(before)
-    ins += list(squared) + ([features] if squared else [])
+    ins = [block, *held] + ([] if before is None else [before])
+    summed = squares is not None
+    if summed:
+        ins += [features] + squares
+        rows = features.shape[0]
+    ins += list(keep)
     outs = [jax.ShapeDtypeStruct((2, m, width), jnp.float32)]
     if narrow:
         outs.append(jax.ShapeDtypeStruct((2, m, width), jnp.bfloat16))
-    if squared:
-        outs.append(jax.ShapeDtypeStruct((features.shape[0], 128), jnp.float32))
+    if summed:
+        outs.append(jax.ShapeDtypeStruct((rows, 128), jnp.float32))
 
     def compute(inputs, results, extra):
-        refs = list(inputs)
+        ref, *weights = inputs[:3]
+        rest = list(inputs[3 : len(inputs) - len(keep)])
         lhs = extra[0]
-        rows = [refs.pop(0) for _ in range(count)]
-        weights = [(refs.pop(0), refs.pop(0)) for _ in range(count)]
-        old = refs.pop(0) if before is not None else None
-        for index, ref in enumerate(rows):
-            gain = ref[m - SMALL + 4 : m - SMALL + 5, :].astype(jnp.float32)
-            lhs[index] = (ref[...].astype(jnp.float32) * gain).astype(jnp.bfloat16)
+        old = rest.pop(0) if before is not None else None
+        gain = ref[m - SMALL + 4 : m - SMALL + 5, :].astype(jnp.float32)
+        lhs[...] = (ref[...].astype(jnp.float32) * gain).astype(jnp.bfloat16)
 
         @pl.loop(0, width // tile)
         def _(j):
             at = pl.ds(pl.multiple_of(start + j * tile, tile), tile)
             to = pl.ds(pl.multiple_of(j * tile, tile), tile)
             for side in range(2):
-                total = old[side, :, at] if old is not None else None
-                for index in range(count):
-                    term = jnp.dot(
-                        lhs[index],
-                        weights[index][side][:, at],
-                        preferred_element_type=jnp.float32,
-                    )
-                    total = term if total is None else total + term
+                total = jnp.dot(lhs[...], weights[side][:, at], preferred_element_type=jnp.float32)
+                if old is not None:
+                    total = old[side, :, at] + total
                 results[0][side, :, to] = total
                 if narrow:
                     results[1][side, :, to] = total.astype(jnp.bfloat16)
 
-        if squared:
-            feature_rows = refs.pop()
-            part = None
-            for ref in refs:
-                wide = jnp.dot(feature_rows[...], ref[...], preferred_element_type=jnp.float32)
-                wide = wide.astype(jnp.bfloat16).astype(jnp.float32)
-                wide = wide * wide
-                for at in range(0, k, 128):
-                    piece = wide[:, at : at + 128]
-                    part = piece if part is None else part + piece
-            results[-1][...] = part
+        if summed:
+            feature_rows, *parts = rest
+            wide = jnp.dot(feature_rows[...], ref[...], preferred_element_type=jnp.float32)
+            wide = wide.astype(jnp.bfloat16).astype(jnp.float32)
+            wide = wide * wide
+            total = None
+            for at in range(0, k, 128):
+                piece = wide[:, at : at + 128]
+                total = piece if total is None else total + piece
+            for part in parts:
+                total = total + part[...]
+            results[-1][...] = total
+            if narrow:
+                row = to_row(jnp.sum(total, axis=1, keepdims=True))
+                high = row.astype(jnp.bfloat16).astype(jnp.float32)
+                last = results[1][0, m - SMALL :, :rows].astype(jnp.float32)
+                line = lax.broadcasted_iota(jnp.int32, last.shape, 0)
+                last = jnp.where(line == SMALL - 2, high, last)
+                last = jnp.where(line == SMALL - 1, row - high, last)
+                results[1][0, m - SMALL :, :rows] = last.astype(jnp.bfloat16)
 
     return stage(
         which,
@@ -230,20 +250,31 @@
         ins,
         outs,
         compute,
-        [pltpu.VMEM((count, m, k), jnp.bfloat16)],
-        flops=4 * m * k * width * count,
-    )
-
-
-def hidden_stage(which, loads, own, other, features, square_own, square_other, width):
+        [pltpu.VMEM((m, k), jnp.bfloat16)],
+        flops=4 * m * k * width,
+        alias=None if before is None or narrow else 3,
+    )
+
+
+def hidden_stage(which, loads, own, other, features, square, scale, width):
     _, m, units = own.shape
     rows = features.shape[0]
     tile = 512
+    first = scale is None
+    outs = [jax.ShapeDtypeStruct((rows, units), jnp.bfloat16)]
+    if first:
+        outs.append(jax.ShapeDtypeStruct((rows, 128), jnp.float32))
 
     def compute(inputs, results, extra):
-        own, other, features, square_own, square_other = inputs
-        squares = jnp.sum(square_own[...] + square_other[...], axis=1, keepdims=True)
-        scale = lax.rsqrt(squares / width + epsilon)
+        own, other, features, last = inputs
+        if first:
+            lines = other[0, m - SMALL :, :rows].astype(jnp.float32)
+            row = lines[SMALL - 2 : SMALL - 1] + lines[SMALL - 1 :]
+            squares = jnp.sum(last[...], axis=1, keepdims=True) + to_column(row)
+            factor = lax.rsqrt(squares / width + epsilon)
+            results[1][...] = jnp.broadcast_to(factor, results[1].shape)
+        else:
+            factor = last[:, :1]
 
         @pl.loop(0, units // tile)
         def _(j):
@@ -252,7 +283,7 @@
             for side in range(2):
                 basis = own[side, :, at] + other[side, :, at].astype(jnp.float32)
                 sums.append(
-                    scale
+                    factor
                     * jnp.dot(
                         features[...],
                         basis.astype(jnp.bfloat16),
@@ -265,8 +296,8 @@
     return stage(
         which,
         loads,
-        [own, other, features, square_own, square_other],
-        [jax.ShapeDtypeStruct((rows, units), jnp.bfloat16)],
+        [own, other, features, square if first else scale],
+        outs,
         compute,
         flops=4 * m * rows * units,
     )
@@ -486,45 +517,37 @@
     step = lambda array, k: send(array, [((t, d), (t ^ k, d)) for t, d in every])
     near = {k: step(block, k) for k in (2, 1, 3)}
 
-    basis, *later = basis_stage(
-        flags, pair(2) + pair(1), [block], [held], None, (0, units), features, [], False
-    )
-    near_two = [near[2], near[1]]
-    basis, square, *held = basis_stage(
-        flags,
-        pair(3),
-        near_two,
-        [later[:2], later[2:]],
-        basis,
-        (0, units),
-        features,
-        [block] + near_two,
-        False,
+    span = (0, units)
+    basis, square, *later = basis_stage(
+        flags, pair(2), block, held, None, span, features, [], False
+    )
+    basis, square, *later = basis_stage(
+        flags, pair(1), near[2], later, basis, span, features, [square], False
+    )
+    basis, square, *last = basis_stage(
+        flags, pair(3), near[1], later, basis, span, features, [square], False
     )
     cut = units // 2
-    own_a, narrow_a, square_last = basis_stage(
-        flags, [], [near[3]], [held], basis, (0, cut), features, [near[3]], True
+    own_a, narrow_a, square, down_diagonal = basis_stage(
+        flags, [column(3)], near[3], last, basis, (0, cut), features, [square], True
     )
     other_a = send(narrow_a, swap_core)
-    square = square + square_last
-    other_square = send(square, swap_core)
-    own_b, narrow_b = basis_stage(
-        flags, [], [near[3]], [held], basis, (cut, units), features, [], True
+    own_b, narrow_b, down_x = basis_stage(
+        flags, [column(1)], near[3], last, basis, (cut, units), features, None, True
     )
     other_b = send(narrow_b, swap_core)
-    down_first = stage(flags, [column(3), column(1)], [], [], None)
-    hidden_a, down_z = hidden_stage(
-        flags, [column(2)], own_a, other_a, features, square, other_square, full_width
+    hidden_a, scale, down_z = hidden_stage(
+        flags, [column(2)], own_a, other_a, features, square, None, full_width
     )
     hidden_b, down_own = hidden_stage(
-        flags, [column(0)], own_b, other_b, features, square, other_square, full_width
+        flags, [column(0)], own_b, other_b, features, None, scale, full_width
     )
     hidden = [hidden_a, hidden_b]
 
     both, lower, upper = (0, 1), (0,), (1,)
     x_pair, diagonal_upper = down_products(
         hidden,
-        down_first,
+        [down_diagonal, down_x],
         cols,
         [(both, 0, [(0, 0), (1, 0)]), (lower, 1, [(0, cols)])],
         [2 * cols, cols],
@@ -541,7 +564,7 @@
     got_z = step(z_pair, 2)
     z_lower, x_upper, own_lower, own_upper = down_products(
         hidden,
-        [down_z, down_first[1], down_own],
+        [down_z, down_x, down_own],
         cols,
         [(lower, 0, [(0, 0)]), (upper, 1, [(1, 0)]), (both, 2, [(2, 0), (3, 0)])],
         [cols] * 4,
@@ -550,8 +573,8 @@
     got_lower = step(add(z_lower, got_x[:, :cols]), 2)
     got_upper = step(add(x_upper, got_z[:, :cols]), 1)
     sums = [
-        add(own_lower, got_x[:, cols:], got_lower),
-        add(own_upper, got_z[:, cols:], got_upper),
+        lax.optimization_barrier(add(own_lower, got_x[:, cols:], got_lower)),
+        lax.optimization_barrier(add(own_upper, got_z[:, cols:], got_upper)),
     ]
     far = [
         send(sums[part], [((t, 1 - t // 4), (t ^ 4, part)) for t in range(TP)])

time: 113 us -> 106 us (0.938)
  waiting for transfers between devices: 43 us -> 27.7 us
  starting transfers between devices: 19.9 us -> 30.1 us
  Pallas kernels: 46.3 us -> 44.5 us
    ppermute x18 -> x17, waiting for transfers between devices: 43 us -> 27.7 us  [send(): lax.ppermute(array, ('tp', 'dp'), [(2 * st + sd, 2 * dt + dd) for (st, sd...]
    ppermute x18 -> x17, starting transfers between devices: 19.9 us -> 30.1 us  [send(): lax.ppermute(array, ('tp', 'dp'), [(2 * st + sd, 2 * dt + dd) for (st, sd...]
    pallas_call x8, Pallas kernels: 37 us -> 34.9 us  [stage(): pl.pallas_call(body, out_shape=shapes, in_specs=[pl.BlockSpec(memory_spac...]
  transfers between devices with their start and end apart: 18 -> 17, of which waited for: 9 -> 10; matrix products, arithmetic and copies ran while one was open for 0% -> 0% of each run, Pallas kernels for 32% -> 31%
where the time goes in v6:
time: 106 us; the launch traced here: 105 us
  Pallas kernels  44.5 us (42%)
  starting transfers between devices  30.1 us (28%)
  waiting for transfers between devices  27.7 us (26%)
  other arithmetic  1.44 us (1%)
    pallas_call x8, Pallas kernels, stage(): pl.pallas_call(body, out_shape=shapes, in_specs=[pl.BlockSpec(memory_spac...  34.9 us
    ppermute x17, starting transfers between devices, send(): lax.ppermute(array, ('tp', 'dp'), [(2 * st + sd, 2 * dt + dd) for (st, sd...  30.1 us
    ppermute x17, waiting for transfers between devices, send(): lax.ppermute(array, ('tp', 'dp'), [(2 * st + sd, 2 * dt + dd) for (st, sd...  27.7 us
    pallas_call x3, Pallas kernels, down_products(): pl.pallas_call(body, out_shape=[jax.ShapeDtypeStruct((rows // 2, width),...  7.29 us
    pallas_call x2, Pallas kernels, whole_call(): pl.pallas_call(lambda *refs: body(refs[count], *refs[count + 1:]), out_sh...  2.34 us
  transfers between devices with their start and end apart: 17, of which 10 were waited for; matrix products, arithmetic and copies ran while one was open for 0% of the time, Pallas kernels for 31%

profile of v6, /device:TPU:0, one launch (start us, length us, event | category | flops | bytes accessed | tf_op | source)
XLA Modules:
  0.0 105.5 jit_solution(15469682496708484548)
XLA Ops:
  0.7 1.0 shard_map.123.refs_3_
  2.6 5.3 %collective-permute-start = (bf16[80,1024]{1,0:T(8,128)(2,1)S(1)}, bf16[80,1024]{1,0:T(8,128)(2,1)S(1)}, u32[]{:S(2)}, u32[]{:S(2)}) collective-permute-start(bf16[80,1024]{1,0:T(8,128)(2,1)S(1)} %shard_map.123.refs_3_), channel_id=1, source_target_pairs={{0,8},{2,10},{4,12},{6,14},{9,1},{11,3},{13,5},{15,7},{1,0},{3,2},... | collective-permute-start | bytes 491528 | tf_op jit(solution)/shard_map/ppermute | solution.py:108
  8.0 5.3 %shard_map.122 = (bf16[1024,3072]{1,0:T(8,128)(2,1)S(1)}, bf16[1024,3072]{1,0:T(8,128)(2,1)S(1)}) custom-call(s32[6]{0:T(128)S(1)} %stack.40.which_ref.refs_0_.refs_2_, bf16[4096,3072]{1,0:T(8,128)(2,1)} %refs_0_.11, bf16[4096,3072]{1,0:T(8,128)(2,1)} %refs_1_.9), custom_call_target="tpu_custom_call" | custom-call | bytes 12582912 | tf_op jit(solution)/shard_map/pallas_call | solution.py:157
  13.3 1.3 %shard_map.124 = (bf16[144,1024]{1,0:T(8,128)(2,1)S(1)}, bf16[256,144]{1,0:T(8,128)(2,1)S(1)}, bf16[128,1024]{1,0:T(8,128)(2,1)S(1)}, f32[1,1024]{1,0:T(1,128)S(1)}) custom-call(bf16[1024,3072]{1,0:T(8,128)(2,1)S(1)} %get-tuple-element.38.refs_0_.refs_3_, bf16[1024,3072]{1,0:T(8,128)(2,1)S(1)} %get-tuple-element.39.refs_1_.refs_4_, ...), custom_call_target="tpu_custom_call" | custom-call | flops 1000000 | bytes 1000000 | tf_op jit(solution)/shard_map/pallas_call | solution.py:425
  14.7 3.6 %collective-permute-start.4 = (bf16[144,1024]{1,0:T(8,128)(2,1)S(1)}, bf16[144,1024]{1,0:T(8,128)(2,1)S(1)}, u32[]{:S(2)}, u32[]{:S(2)}) collective-permute-start(bf16[144,1024]{1,0:T(8,128)(2,1)S(1)} %get-tuple-element.41.refs_2_), channel_id=1, source_target_pairs={{0,4},{1,5},{2,6},{3,7},{4,0},{5,1},{6,2},{7,3},{8,12},{9,13},{10,... | collective-permute-start | bytes 884744 | tf_op jit(solution)/shard_map/ppermute | solution.py:108
  18.3 1.5 %collective-permute-start.3 = (bf16[144,1024]{1,0:T(8,128)(2,1)S(1)}, bf16[144,1024]{1,0:T(8,128)(2,1)S(1)}, u32[]{:S(2)}, u32[]{:S(2)}) collective-permute-start(bf16[144,1024]{1,0:T(8,128)(2,1)S(1)} %get-tuple-element.41.refs_2_), channel_id=1, source_target_pairs={{0,2},{1,3},{2,0},{3,1},{4,6},{5,7},{6,4},{7,5},{8,10},{9,11},{10,... | collective-permute-start | bytes 884744 | tf_op jit(solution)/shard_map/ppermute | solution.py:108
  19.9 5.3 %shard_map.125 = (f32[2,144,3072]{2,1,0:T(8,128)S(1)}, f32[256,128]{1,0:T(8,128)S(1)}, bf16[1024,3072]{1,0:T(8,128)(2,1)S(1)}, bf16[1024,3072]{1,0:T(8,128)(2,1)S(1)}) custom-call(s32[6]{0:T(128)S(1)} %stack.40.which_ref.refs_0_.refs_2_, bf16[4096,3072]{1,0:T(8,128)(2,1)} %refs_0_.11, bf16[4096,3072]{1,0:T(8,128)(2,1)} %refs_1_.9, ...), custom_call_target="tpu_custom_call" | custom-call | flops 1811939328 | bytes 12582912 | tf_op jit(solution)/shard_map/pallas_call | solution.py:157
  25.8 5.3 %shard_map.126 = (f32[2,144,3072]{2,1,0:T(8,128)S(1)}, f32[256,128]{1,0:T(8,128)S(1)}, bf16[1024,3072]{1,0:T(8,128)(2,1)S(1)}, bf16[1024,3072]{1,0:T(8,128)(2,1)S(1)}) custom-call(s32[6]{0:T(128)S(1)} %stack.40.which_ref.refs_0_.refs_2_, bf16[4096,3072]{1,0:T(8,128)(2,1)} %refs_0_.11, bf16[4096,3072]{1,0:T(8,128)(2,1)} %refs_1_.9, ...), custom_call_target="tpu_custom_call", output_to_operand_aliasing={{0}: (6, {})} | custom-call | flops 1811939328 | bytes 12582912 | tf_op jit(solution)/shard_map/pallas_call | solution.py:157
  31.2 1.2 %collective-permute-done.3.refs_2_ = bf16[144,1024]{1,0:T(8,128)(2,1)S(1)} collective-permute-done((bf16[144,1024]{1,0:T(8,128)(2,1)S(1)}, bf16[144,1024]{1,0:T(8,128)(2,1)S(1)}, u32[]{:S(2)}, u32[]{:S(2)}) %collective-permute-start.3) | collective-permute-done | bytes 294944 | tf_op jit(solution)/shard_map/ppermute | solution.py:108
  32.3 5.3 %shard_map.127 = (f32[2,144,3072]{2,1,0:T(8,128)S(1)}, f32[256,128]{1,0:T(8,128)S(1)}, bf16[1024,3072]{1,0:T(8,128)(2,1)S(1)}, bf16[1024,3072]{1,0:T(8,128)(2,1)S(1)}) custom-call(s32[6]{0:T(128)S(1)} %stack.40.which_ref.refs_0_.refs_2_, bf16[4096,3072]{1,0:T(8,128)(2,1)} %refs_0_.11, bf16[4096,3072]{1,0:T(8,128)(2,1)} %refs_1_.9, ...), custom_call_target="tpu_custom_call", output_to_operand_aliasing={{0}: (6, {})} | custom-call | flops 1811939328 | bytes 12582912 | tf_op jit(solution)/shard_map/pallas_call | solution.py:157
  37.6 3.4 %shard_map.128 = (f32[2,144,1536]{2,1,0:T(8,128)S(1)}, bf16[2,144,1536]{2,1,0:T(8,128)(2,1)S(1)}, f32[256,128]{1,0:T(8,128)S(1)}, bf16[3072,1024]{1,0:T(8,128)(2,1)S(1)}) custom-call(s32[6]{0:T(128)S(1)} %stack.40.which_ref.refs_0_.refs_2_, bf16[3072,4096]{1,0:T(8,128)(2,1)} %refs_0_.15, bf16[144,1024]{1,0:T(8,128)(2,1)S(1)} %collective-permute-done.2.refs_1_, ...), custom_call_target="tpu_custom_call" | custom-call | flops 905969664 | bytes 6291456 | tf_op jit(solution)/shard_map/pallas_call | solution.py:157
  41.1 3.4 %shard_map.130 = (f32[2,144,1536]{2,1,0:T(8,128)S(1)}, bf16[2,144,1536]{2,1,0:T(8,128)(2,1)S(1)}, bf16[3072,1024]{1,0:T(8,128)(2,1)S(1)}) custom-call(s32[6]{0:T(128)S(1)} %stack.40.which_ref.refs_0_.refs_2_, bf16[3072,4096]{1,0:T(8,128)(2,1)} %refs_0_.15, bf16[144,1024]{1,0:T(8,128)(2,1)S(1)} %collective-permute-done.2.refs_1_, ...), custom_call_target="tpu_custom_call" | custom-call | flops 905969664 | bytes 6291456 | tf_op jit(solution)/shard_map/pallas_call | solution.py:157
  45.1 3.4 %shard_map.129 = (bf16[256,1536]{1,0:T(8,128)(2,1)S(1)}, f32[256,128]{1,0:T(8,128)S(1)}, bf16[3072,1024]{1,0:T(8,128)(2,1)S(1)}) custom-call(s32[6]{0:T(128)S(1)} %stack.40.which_ref.refs_0_.refs_2_, bf16[3072,4096]{1,0:T(8,128)(2,1)} %refs_0_.15, f32[2,144,1536]{2,1,0:T(8,128)S(1)} %get-tuple-element.55.refs_1_, ...), custom_call_target="tpu_custom_call" | custom-call | flops 226492416 | bytes 6291456 | tf_op jit(solution)/shard_map/pallas_call | solution.py:157
  48.6 3.4 %shard_map.131 = (bf16[256,1536]{1,0:T(8,128)(2,1)S(1)}, bf16[3072,1024]{1,0:T(8,128)(2,1)S(1)}) custom-call(s32[6]{0:T(128)S(1)} %stack.40.which_ref.refs_0_.refs_2_, bf16[3072,4096]{1,0:T(8,128)(2,1)} %refs_0_.15, f32[2,144,1536]{2,1,0:T(8,128)S(1)} %get-tuple-element.59.refs_1_, bf16[2,144,1536]{2,1,0:T(8,128)(2,1)S(1)} %collective-permute-done.6.refs_2_, ...), custom_call_target="tpu_custom_call" | custom-call | flops 226492416 | bytes 6291456 | tf_op jit(solution)/shard_map/pallas_call | solution.py:157
  52.0 2.8 %shard_map.133 = (bf16[128,2048]{1,0:T(8,128)(2,1)S(1)}, bf16[128,1024]{1,0:T(8,128)(2,1)S(1)}) custom-call(bf16[256,1536]{1,0:T(8,128)(2,1)S(1)} %get-tuple-element.58.refs_0_, bf16[256,1536]{1,0:T(8,128)(2,1)S(1)} %get-tuple-element.62.refs_1_, bf16[3072,1024]{1,0:T(8,128)(2,1)S(1)} %get-tuple-element.67.refs_2_, ...), custom_call_target="tpu_custom_call" | custom-call | flops 150994944 | tf_op jit(solution)/shard_map/pallas_call | solution.py:347
  54.8 2.6 %collective-permute-start.7 = (bf16[128,2048]{1,0:T(8,128)(2,1)S(1)}, bf16[128,2048]{1,0:T(8,128)(2,1)S(1)}, u32[]{:S(2)}, u32[]{:S(2)}) collective-permute-start(bf16[128,2048]{1,0:T(8,128)(2,1)S(1)} %get-tuple-element.68), channel_id=1, source_target_pairs={{0,2},{1,3},{2,0},{3,1},{4,6},{5,7},{6,4},{7,5},{8,10},{9,11},{10,... | collective-permute-start | bytes 1572872 | tf_op jit(solution)/shard_map/ppermute | solution.py:108
  57.4 1.0 shard_map.134
  58.4 1.2 %collective-permute-start.9 = (bf16[128,2048]{1,0:T(8,128)(2,1)S(1)}, bf16[128,2048]{1,0:T(8,128)(2,1)S(1)}, u32[]{:S(2)}, u32[]{:S(2)}) collective-permute-start(bf16[128,2048]{1,0:T(8,128)(2,1)S(1)} %shard_map.134), channel_id=1, source_target_pairs={{0,4},{1,5},{2,6},{3,7},{4,0},{5,1},{6,2},{7,3},{8,12},{9,13},{10,... | collective-permute-start | bytes 1572872 | tf_op jit(solution)/shard_map/ppermute | solution.py:108
  59.6 3.5 %shard_map.132 = (bf16[128,1024]{1,0:T(8,128)(2,1)S(1)}, bf16[128,1024]{1,0:T(8,128)(2,1)S(1)}, bf16[128,1024]{1,0:T(8,128)(2,1)S(1)}, bf16[128,1024]{1,0:T(8,128)(2,1)S(1)}) custom-call(bf16[256,1536]{1,0:T(8,128)(2,1)S(1)} %get-tuple-element.58.refs_0_, bf16[256,1536]{1,0:T(8,128)(2,1)S(1)} %get-tuple-element.62.refs_1_, ...), custom_call_target="tpu_custom_call" | custom-call | flops 201326592 | tf_op jit(solution)/shard_map/pallas_call | solution.py:347
  63.1 6.3 %collective-permute-done.7 = bf16[128,2048]{1,0:T(8,128)(2,1)S(1)} collective-permute-done((bf16[128,2048]{1,0:T(8,128)(2,1)S(1)}, bf16[128,2048]{1,0:T(8,128)(2,1)S(1)}, u32[]{:S(2)}, u32[]{:S(2)}) %collective-permute-start.7) | collective-permute-done | bytes 524320 | tf_op jit(solution)/shard_map/ppermute | solution.py:108
  69.6 1.3 %collective-permute-start.8 = (bf16[128,1024]{1,0:T(8,128)(2,1)S(1)}, bf16[128,1024]{1,0:T(8,128)(2,1)S(1)}, u32[]{:S(2)}, u32[]{:S(2)}) collective-permute-start(bf16[128,1024]{1,0:T(8,128)(2,1)S(1)} %add_convert_fusion.4), channel_id=1, source_target_pairs={{0,4},{1,5},{2,6},{3,7},{4,0},{5,1},{6,2},{7,3},{8,12},{9,13},{10,... | collective-permute-start | bytes 786440 | tf_op jit(solution)/shard_map/ppermute | solution.py:108
  70.9 1.4 %collective-permute-done.9 = bf16[128,2048]{1,0:T(8,128)(2,1)S(1)} collective-permute-done((bf16[128,2048]{1,0:T(8,128)(2,1)S(1)}, bf16[128,2048]{1,0:T(8,128)(2,1)S(1)}, u32[]{:S(2)}, u32[]{:S(2)}) %collective-permute-start.9) | collective-permute-done | bytes 524320 | tf_op jit(solution)/shard_map/ppermute | solution.py:108
  72.8 4.9 %collective-permute-done.8 = bf16[128,1024]{1,0:T(8,128)(2,1)S(1)} collective-permute-done((bf16[128,1024]{1,0:T(8,128)(2,1)S(1)}, bf16[128,1024]{1,0:T(8,128)(2,1)S(1)}, u32[]{:S(2)}, u32[]{:S(2)}) %collective-permute-start.8) | collective-permute-done | bytes 262176 | tf_op jit(solution)/shard_map/ppermute | solution.py:108
  77.7 1.3 %collective-permute-start.12 = (bf16[128,1024]{1,0:T(8,128)(2,1)S(1)}, bf16[128,1024]{1,0:T(8,128)(2,1)S(1)}, u32[]{:S(2)}, u32[]{:S(2)}) collective-permute-start(bf16[128,1024]{1,0:T(8,128)(2,1)S(1)} %add_convert_fusion.3), channel_id=1, source_target_pairs={{1,8},{3,10},{5,12},{7,14},{8,0},{10,2},{12,4},{14,6},{17,24},{19,... | collective-permute-start | bytes 786440 | tf_op jit(solution)/shard_map/ppermute | solution.py:108
  79.4 4.1 %collective-permute-start.11 = (bf16[128,1024]{1,0:T(8,128)(2,1)S(1)}, bf16[128,1024]{1,0:T(8,128)(2,1)S(1)}, u32[]{:S(2)}, u32[]{:S(2)}) collective-permute-start(bf16[128,1024]{1,0:T(8,128)(2,1)S(1)} %broadcast_select_fusion), channel_id=1, source_target_pairs={{0,1},{2,3},{4,5},{6,7},{9,8},{11,10},{13,12},{15,14},{16,17},{18,... | collective-permute-start | bytes 786440 | tf_op jit(solution)/shard_map/ppermute | solution.py:108
  84.2 5.6 %collective-permute-done.12 = bf16[128,1024]{1,0:T(8,128)(2,1)S(1)} collective-permute-done((bf16[128,1024]{1,0:T(8,128)(2,1)S(1)}, bf16[128,1024]{1,0:T(8,128)(2,1)S(1)}, u32[]{:S(2)}, u32[]{:S(2)}) %collective-permute-start.12) | collective-permute-done | bytes 262176 | tf_op jit(solution)/shard_map/ppermute | solution.py:108
  89.7 1.0 fusion
  90.7 1.2 %collective-permute-start.14 = (f32[2,128]{1,0:T(2,128)S(1)}, f32[2,128]{1,0:T(2,128)S(1)}, u32[]{:S(2)}, u32[]{:S(2)}) collective-permute-start(f32[2,128]{1,0:T(2,128)S(1)} %pad_maximum_fusion), channel_id=1, source_target_pairs={{0,2},{1,3},{2,0},{3,1},{4,6},{5,7},{6,4},{7,5},{8,10},{9,11},{10,... | collective-permute-start | bytes 3080 | tf_op jit(solution)/shard_map/ppermute | solution.py:108
  91.9 2.5 %collective-permute-done.14 = f32[2,128]{1,0:T(2,128)S(1)} collective-permute-done((f32[2,128]{1,0:T(2,128)S(1)}, f32[2,128]{1,0:T(2,128)S(1)}, u32[]{:S(2)}, u32[]{:S(2)}) %collective-permute-start.14) | collective-permute-done | bytes 1056 | tf_op jit(solution)/shard_map/ppermute | solution.py:108
  94.4 3.6 %collective-permute-done.15 = f32[2,128]{1,0:T(2,128)S(1)} collective-permute-done((f32[2,128]{1,0:T(2,128)S(1)}, f32[2,128]{1,0:T(2,128)S(1)}, u32[]{:S(2)}, u32[]{:S(2)}) %collective-permute-start.15) | collective-permute-done | bytes 1056 | tf_op jit(solution)/shard_map/ppermute | solution.py:108
  98.0 5.2 %collective-permute-start.16 = (f32[2,128]{1,0:T(2,128)S(1)}, f32[2,128]{1,0:T(2,128)S(1)}, u32[]{:S(2)}, u32[]{:S(2)}) collective-permute-start(f32[2,128]{1,0:T(2,128)S(1)} %fusion.3), channel_id=1, source_target_pairs={{0,8},{1,9},{2,10},{3,11},{4,12},{5,13},{6,14},{7,15},{8,0},{9,1},... | collective-permute-start | bytes 3080 | tf_op jit(solution)/shard_map/ppermute | solution.py:108
  103.2 1.5 %collective-permute-done.16 = f32[2,128]{1,0:T(2,128)S(1)} collective-permute-done((f32[2,128]{1,0:T(2,128)S(1)}, f32[2,128]{1,0:T(2,128)S(1)}, u32[]{:S(2)}, u32[]{:S(2)}) %collective-permute-start.16) | collective-permute-done | bytes 1056 | tf_op jit(solution)/shard_map/ppermute | solution.py:108
  (40 shorter events, 4.8 us)
Async XLA Ops:
  1.7 11.5 %copy-start = (bf16[128,1024]{1,0:T(8,128)(2,1)S(1)}, bf16[128,1024]{1,0:T(8,128)(2,1)}, u32[]{:S(2)}) copy-start(bf16[128,1024]{1,0:T(8,128)(2,1)} %refs_6_.1) | copy-start | bytes 786436
  1.8 11.5 %copy-start.1 = (bf16[2,1024]{1,0:T(2,128)(2,1)S(1)}, bf16[2,1024]{1,0:T(2,128)(2,1)}, u32[]{:S(2)}) copy-start(bf16[2,1024]{1,0:T(2,128)(2,1)} %refs_7_.1) | copy-start | bytes 12292
  1.8 11.5 %copy-start.2 = (f32[1024]{0:T(1024)S(1)}, f32[1024]{0:T(1024)}, u32[]{:S(2)}) copy-start(f32[1024]{0:T(1024)} %refs_10_.1) | copy-start | bytes 12292
  1.8 11.5 %copy-start.3 = (f32[1024]{0:T(1024)S(1)}, f32[1024]{0:T(1024)}, u32[]{:S(2)}) copy-start(f32[1024]{0:T(1024)} %refs_11_.1) | copy-start | bytes 12292
  1.8 11.5 %copy-start.4 = (f32[128]{0:T(128)S(1)}, f32[128]{0:T(128)}, u32[]{:S(2)}) copy-start(f32[128]{0:T(128)} %refs_8_.1) | copy-start | bytes 1540
  1.8 11.5 %copy-start.5 = (f32[128]{0:T(128)S(1)}, f32[128]{0:T(128)}, u32[]{:S(2)}) copy-start(f32[128]{0:T(128)} %refs_9_.1) | copy-start | bytes 1540
  1.8 11.4 %collective-permute-start.1 = (bf16[80,1024]{1,0:T(8,128)(2,1)S(1)}, bf16[80,1024]{1,0:T(8,128)(2,1)S(1)}, u32[]{:S(2)}, u32[]{:S(2)}) collective-permute-start(bf16[80,1024]{1,0:T(8,128)(2,1)S(1)} %shard_map.123.refs_3_), channel_id=1, source_target_pairs={{1,8},{3,10},{5,12},{7,14},{8,1},{10,3},{12,5},{14,7},{17,24},{19,... | collective-permute-start | bytes 491528 | tf_op jit(solution)/shard_map/ppermute | solution.py:108
  2.6 10.6 %collective-permute-start = (bf16[80,1024]{1,0:T(8,128)(2,1)S(1)}, bf16[80,1024]{1,0:T(8,128)(2,1)S(1)}, u32[]{:S(2)}, u32[]{:S(2)}) collective-permute-start(bf16[80,1024]{1,0:T(8,128)(2,1)S(1)} %shard_map.123.refs_3_), channel_id=1, source_target_pairs={{0,8},{2,10},{4,12},{6,14},{9,1},{11,3},{13,5},{15,7},{1,0},{3,2},... | collective-permute-start | bytes 491528 | tf_op jit(solution)/shard_map/ppermute | solution.py:108
  14.7 11.1 %collective-permute-start.4 = (bf16[144,1024]{1,0:T(8,128)(2,1)S(1)}, bf16[144,1024]{1,0:T(8,128)(2,1)S(1)}, u32[]{:S(2)}, u32[]{:S(2)}) collective-permute-start(bf16[144,1024]{1,0:T(8,128)(2,1)S(1)} %get-tuple-element.41.refs_2_), channel_id=1, source_target_pairs={{0,4},{1,5},{2,6},{3,7},{4,0},{5,1},{6,2},{7,3},{8,12},{9,13},{10,... | collective-permute-start | bytes 884744 | tf_op jit(solution)/shard_map/ppermute | solution.py:108
  18.3 14.0 %collective-permute-start.3 = (bf16[144,1024]{1,0:T(8,128)(2,1)S(1)}, bf16[144,1024]{1,0:T(8,128)(2,1)S(1)}, u32[]{:S(2)}, u32[]{:S(2)}) collective-permute-start(bf16[144,1024]{1,0:T(8,128)(2,1)S(1)} %get-tuple-element.41.refs_2_), channel_id=1, source_target_pairs={{0,2},{1,3},{2,0},{3,1},{4,6},{5,7},{6,4},{7,5},{8,10},{9,11},{10,... | collective-permute-start | bytes 884744 | tf_op jit(solution)/shard_map/ppermute | solution.py:108
  19.8 17.8 %collective-permute-start.2 = (bf16[144,1024]{1,0:T(8,128)(2,1)S(1)}, bf16[144,1024]{1,0:T(8,128)(2,1)S(1)}, u32[]{:S(2)}, u32[]{:S(2)}) collective-permute-start(bf16[144,1024]{1,0:T(8,128)(2,1)S(1)} %get-tuple-element.41.refs_2_), channel_id=1, source_target_pairs={{0,6},{1,7},{2,4},{3,5},{4,2},{5,3},{6,0},{7,1},{8,14},{9,15},{10,... | collective-permute-start | bytes 884744 | tf_op jit(solution)/shard_map/ppermute | solution.py:108
  41.1 4.1 %collective-permute-start.5 = (bf16[2,144,1536]{2,1,0:T(8,128)(2,1)S(1)}, bf16[2,144,1536]{2,1,0:T(8,128)(2,1)S(1)}, u32[]{:S(2)}, u32[]{:S(2)}) collective-permute-start(bf16[2,144,1536]{2,1,0:T(8,128)(2,1)S(1)} %get-tuple-element.56), channel_id=1, source_target_pairs={{0,1},{1,0},{2,3},{3,2},{4,5},{5,4},{6,7},{7,6},{8,9},{9,8},{10,11... | collective-permute-start | bytes 2654216 | tf_op jit(solution)/shard_map/ppermute | solution.py:108
  44.6 4.0 %collective-permute-start.6 = (bf16[2,144,1536]{2,1,0:T(8,128)(2,1)S(1)}, bf16[2,144,1536]{2,1,0:T(8,128)(2,1)S(1)}, u32[]{:S(2)}, u32[]{:S(2)}) collective-permute-start(bf16[2,144,1536]{2,1,0:T(8,128)(2,1)S(1)} %get-tuple-element.60), channel_id=1, source_target_pairs={{0,1},{1,0},{2,3},{3,2},{4,5},{5,4},{6,7},{7,6},{8,9},{9,8},{10,11... | collective-permute-start | bytes 2654216 | tf_op jit(solution)/shard_map/ppermute | solution.py:108
  54.8 14.7 %collective-permute-start.7 = (bf16[128,2048]{1,0:T(8,128)(2,1)S(1)}, bf16[128,2048]{1,0:T(8,128)(2,1)S(1)}, u32[]{:S(2)}, u32[]{:S(2)}) collective-permute-start(bf16[128,2048]{1,0:T(8,128)(2,1)S(1)} %get-tuple-element.68), channel_id=1, source_target_pairs={{0,2},{1,3},{2,0},{3,1},{4,6},{5,7},{6,4},{7,5},{8,10},{9,11},{10,... | collective-permute-start | bytes 1572872 | tf_op jit(solution)/shard_map/ppermute | solution.py:108
  58.4 13.9 %collective-permute-start.9 = (bf16[128,2048]{1,0:T(8,128)(2,1)S(1)}, bf16[128,2048]{1,0:T(8,128)(2,1)S(1)}, u32[]{:S(2)}, u32[]{:S(2)}) collective-permute-start(bf16[128,2048]{1,0:T(8,128)(2,1)S(1)} %shard_map.134), channel_id=1, source_target_pairs={{0,4},{1,5},{2,6},{3,7},{4,0},{5,1},{6,2},{7,3},{8,12},{9,13},{10,... | collective-permute-start | bytes 1572872 | tf_op jit(solution)/shard_map/ppermute | solution.py:108
  69.6 8.1 %collective-permute-start.8 = (bf16[128,1024]{1,0:T(8,128)(2,1)S(1)}, bf16[128,1024]{1,0:T(8,128)(2,1)S(1)}, u32[]{:S(2)}, u32[]{:S(2)}) collective-permute-start(bf16[128,1024]{1,0:T(8,128)(2,1)S(1)} %add_convert_fusion.4), channel_id=1, source_target_pairs={{0,4},{1,5},{2,6},{3,7},{4,0},{5,1},{6,2},{7,3},{8,12},{9,13},{10,... | collective-permute-start | bytes 786440 | tf_op jit(solution)/shard_map/ppermute | solution.py:108
  72.3 6.9 %collective-permute-start.10 = (bf16[128,1024]{1,0:T(8,128)(2,1)S(1)}, bf16[128,1024]{1,0:T(8,128)(2,1)S(1)}, u32[]{:S(2)}, u32[]{:S(2)}) collective-permute-start(bf16[128,1024]{1,0:T(8,128)(2,1)S(1)} %add_convert_fusion.2), channel_id=1, source_target_pairs={{0,2},{1,3},{2,0},{3,1},{4,6},{5,7},{6,4},{7,5},{8,10},{9,11},{10,... | collective-permute-start | bytes 786440 | tf_op jit(solution)/shard_map/ppermute | solution.py:108
  77.7 12.0 %collective-permute-start.12 = (bf16[128,1024]{1,0:T(8,128)(2,1)S(1)}, bf16[128,1024]{1,0:T(8,128)(2,1)S(1)}, u32[]{:S(2)}, u32[]{:S(2)}) collective-permute-start(bf16[128,1024]{1,0:T(8,128)(2,1)S(1)} %add_convert_fusion.3), channel_id=1, source_target_pairs={{1,8},{3,10},{5,12},{7,14},{8,0},{10,2},{12,4},{14,6},{17,24},{19,... | collective-permute-start | bytes 786440 | tf_op jit(solution)/shard_map/ppermute | solution.py:108
  79.4 10.4 %collective-permute-start.11 = (bf16[128,1024]{1,0:T(8,128)(2,1)S(1)}, bf16[128,1024]{1,0:T(8,128)(2,1)S(1)}, u32[]{:S(2)}, u32[]{:S(2)}) collective-permute-start(bf16[128,1024]{1,0:T(8,128)(2,1)S(1)} %broadcast_select_fusion), channel_id=1, source_target_pairs={{0,1},{2,3},{4,5},{6,7},{9,8},{11,10},{13,12},{15,14},{16,17},{18,... | collective-permute-start | bytes 786440 | tf_op jit(solution)/shard_map/ppermute | solution.py:108
  83.5 6.2 %collective-permute-start.13 = (bf16[128,1024]{1,0:T(8,128)(2,1)S(1)}, bf16[128,1024]{1,0:T(8,128)(2,1)S(1)}, u32[]{:S(2)}, u32[]{:S(2)}) collective-permute-start(bf16[128,1024]{1,0:T(8,128)(2,1)S(1)} %add_convert_fusion.1), channel_id=1, source_target_pairs={{1,9},{3,11},{5,13},{7,15},{8,1},{10,3},{12,5},{14,7},{17,25},{19,... | collective-permute-start | bytes 786440 | tf_op jit(solution)/shard_map/ppermute | solution.py:108
  90.7 3.6 %collective-permute-start.14 = (f32[2,128]{1,0:T(2,128)S(1)}, f32[2,128]{1,0:T(2,128)S(1)}, u32[]{:S(2)}, u32[]{:S(2)}) collective-permute-start(f32[2,128]{1,0:T(2,128)S(1)} %pad_maximum_fusion), channel_id=1, source_target_pairs={{0,2},{1,3},{2,0},{3,1},{4,6},{5,7},{6,4},{7,5},{8,10},{9,11},{10,... | collective-permute-start | bytes 3080 | tf_op jit(solution)/shard_map/ppermute | solution.py:108
  94.4 3.6 %collective-permute-start.15 = (f32[2,128]{1,0:T(2,128)S(1)}, f32[2,128]{1,0:T(2,128)S(1)}, u32[]{:S(2)}, u32[]{:S(2)}) collective-permute-start(f32[2,128]{1,0:T(2,128)S(1)} %fusion.2), channel_id=1, source_target_pairs={{0,4},{1,5},{2,6},{3,7},{4,0},{5,1},{6,2},{7,3},{8,12},{9,13},{10,... | collective-permute-start | bytes 3080 | tf_op jit(solution)/shard_map/ppermute | solution.py:108
  98.0 6.8 %collective-permute-start.16 = (f32[2,128]{1,0:T(2,128)S(1)}, f32[2,128]{1,0:T(2,128)S(1)}, u32[]{:S(2)}, u32[]{:S(2)}) collective-permute-start(f32[2,128]{1,0:T(2,128)S(1)} %fusion.3), channel_id=1, source_target_pairs={{0,8},{1,9},{2,10},{3,11},{4,12},{5,13},{6,14},{7,15},{8,0},{9,1},... | collective-permute-start | bytes 3080 | tf_op jit(solution)/shard_map/ppermute | solution.py:108

commit v7 on v6

--- a/solution.py
+++ b/solution.py
@@ -113,39 +113,42 @@
 SPLIT = 8
 
 
-def copies_of(which, loads, sources, targets, arrived):
-    made = []
-    for at, (kind, size, place) in enumerate(loads):
-        source, target = sources[at], targets[at]
-        part = target.shape[0] // SPLIT
-        for cut in range(SPLIT):
-            rows = pl.ds(cut * part, part)
-            if kind == "rows":
-                begin = pl.multiple_of(which[place] * size + cut * part, 16)
-                view = source.at[pl.ds(begin, part), :]
-            else:
-                view = source.at[rows, pl.ds(pl.multiple_of(which[place] * size, 128), size)]
-            made.append(
-                pltpu.make_async_copy(view, target.at[rows, :], arrived.at[at * SPLIT + cut])
-            )
-    return made
-
-
-def stage(which, loads, ins, outs, compute, scratch=(), limit=3, flops=0, alias=None):
+def stage(which, loads, ins, outs, compute, scratch=(), limit=6, flops=0, alias=None):
     vmem = pl.BlockSpec(memory_space=pltpu.VMEM)
-    n, count = len(loads), len(ins)
-    kinds = [load[:3] for load in loads]
-    shapes = list(outs)
-    for kind, size, _, array in loads:
-        shape = (size, array.shape[1]) if kind == "rows" else (array.shape[0], size)
+    count = len(ins)
+    shapes, sources, flat = list(outs), [], []
+    for kind, parts in loads:
+        array, total = parts[0][0], sum(part[4] for part in parts)
+        shape = (total, array.shape[1]) if kind == "rows" else (array.shape[0], total)
         shapes.append(jax.ShapeDtypeStruct(shape, array.dtype))
+        sources += [part[0] for part in parts]
+        flat.append((kind, parts))
+    n = len(sources)
 
     def body(which_ref, *refs):
-        sources, inputs = refs[:n], refs[n : n + count]
+        inputs = refs[n : n + count]
         results = refs[n + count : n + count + len(outs)]
         targets = refs[n + count + len(outs) : n + count + len(shapes)]
         extra = refs[n + count + len(shapes) :]
-        made = copies_of(which_ref, kinds, sources, targets, extra[0]) if n else []
+        made, at = [], 0
+        for (kind, parts), target in zip(flat, targets):
+            filled = 0
+            for _, place, unit, offset, size in parts:
+                block = which_ref[place] * unit + offset
+                length = size if kind == "rows" else target.shape[0]
+                piece = length // SPLIT
+                for cut in range(SPLIT):
+                    if kind == "rows":
+                        begin = pl.multiple_of(block + cut * piece, 16)
+                        view = refs[at].at[pl.ds(begin, piece), :]
+                        to = target.at[pl.ds(filled + cut * piece, piece), :]
+                    else:
+                        rows = pl.ds(cut * piece, piece)
+                        view = refs[at].at[rows, pl.ds(pl.multiple_of(block, 128), size)]
+                        to = target.at[rows, pl.ds(filled, size)]
+                    made.append(pltpu.make_async_copy(view, to, extra[0].at[len(made)]))
+                filled += size
+                at += 1
         for copy in made:
             copy.start()
         if compute is not None:
@@ -164,10 +167,8 @@
         scratch_shapes=([pltpu.SemaphoreType.DMA((n * SPLIT,))] if n else []) + list(scratch),
         input_output_aliases={} if alias is None else {1 + n + alias: 0},
         compiler_params=pltpu.CompilerParams(vmem_limit_bytes=limit * MIB),
-        cost_estimate=pl.CostEstimate(
-            flops=flops, bytes_accessed=loaded, transcendentals=0
-        ),
-    )(which, *[load[3] for load in loads], *ins)
+        cost_estimate=pl.CostEstimate(flops=flops, bytes_accessed=loaded, transcendentals=0),
+    )(which, *sources, *ins)
 
 
 def to_row(column):
@@ -184,19 +185,17 @@
     return jnp.sum(jnp.where(rows == cols, row, 0.0), axis=1, keepdims=True)
 
 
-def basis_stage(
-    which, loads, block, held, before, columns, features, squares, narrow, keep=()
-):
-    m, k = block.shape
+def basis_stage(which, loads, blocks, held, before, columns, features, squares, narrow):
+    m, k = blocks[0].shape
+    count = len(blocks)
     start, stop = columns
     width = stop - start
     tile = 512
-    ins = [block, *held] + ([] if before is None else [before])
+    ins = [*blocks, *held] + ([] if before is None else [before])
     summed = squares is not None
     if summed:
         ins += [features] + squares
         rows = features.shape[0]
-    ins += list(keep)
     outs = [jax.ShapeDtypeStruct((2, m, width), jnp.float32)]
     if narrow:
         outs.append(jax.ShapeDtypeStruct((2, m, width), jnp.bfloat16))
@@ -204,34 +203,41 @@
         outs.append(jax.ShapeDtypeStruct((rows, 128), jnp.float32))
 
     def compute(inputs, results, extra):
-        ref, *weights = inputs[:3]
-        rest = list(inputs[3 : len(inputs) - len(keep)])
+        refs, weights = inputs[:count], inputs[count : 3 * count]
+        rest = list(inputs[3 * count :])
         lhs = extra[0]
         old = rest.pop(0) if before is not None else None
-        gain = ref[m - SMALL + 4 : m - SMALL + 5, :].astype(jnp.float32)
-        lhs[...] = (ref[...].astype(jnp.float32) * gain).astype(jnp.bfloat16)
+        for index, ref in enumerate(refs):
+            gain = ref[m - SMALL + 4 : m - SMALL + 5, :].astype(jnp.float32)
+            lhs[index] = (ref[...].astype(jnp.float32) * gain).astype(jnp.bfloat16)
 
         @pl.loop(0, width // tile)
         def _(j):
             at = pl.ds(pl.multiple_of(start + j * tile, tile), tile)
             to = pl.ds(pl.multiple_of(j * tile, tile), tile)
             for side in range(2):
-                total = jnp.dot(lhs[...], weights[side][:, at], preferred_element_type=jnp.float32)
-                if old is not None:
-                    total = old[side, :, at] + total
+                total = old[side, :, at] if old is not None else None
+                for index in range(count):
+                    term = jnp.dot(
+                        lhs[index],
+                        weights[2 * index + side][:, at],
+                        preferred_element_type=jnp.float32,
+                    )
+                    total = term if total is None else total + term
                 results[0][side, :, to] = total
                 if narrow:
                     results[1][side, :, to] = total.astype(jnp.bfloat16)
 
         if summed:
             feature_rows, *parts = rest
-            wide = jnp.dot(feature_rows[...], ref[...], preferred_element_type=jnp.float32)
-            wide = wide.astype(jnp.bfloat16).astype(jnp.float32)
-            wide = wide * wide
             total = None
-            for at in range(0, k, 128):
-                piece = wide[:, at : at + 128]
-                total = piece if total is None else total + piece
+            for ref in refs:
+                wide = jnp.dot(feature_rows[...], ref[...], preferred_element_type=jnp.float32)
+                wide = wide.astype(jnp.bfloat16).astype(jnp.float32)
+                wide = wide * wide
+                for at in range(0, k, 128):
+                    piece = wide[:, at : at + 128]
+                    total = piece if total is None else total + piece
             for part in parts:
                 total = total + part[...]
             results[-1][...] = total
@@ -250,9 +256,9 @@
         ins,
         outs,
         compute,
-        [pltpu.VMEM((m, k), jnp.bfloat16)],
-        flops=4 * m * k * width,
-        alias=None if before is None or narrow else 3,
+        [pltpu.VMEM((count, m, k), jnp.bfloat16)],
+        flops=4 * m * k * width * count,
+        alias=None,
     )
 
 
@@ -306,10 +312,9 @@
 def down_body(places, cols, hidden, weights, outs):
     half = hidden[0].shape[0] // 2
     tile = 512
-    for rows, which, targets in places:
+    for rows, tiles, targets in places:
         low, high = rows[0] * half, rows[-1] * half + half
-        for j in range(cols // tile):
-            at = j * tile
+        for j, (which, at) in enumerate(tiles):
             total = None
             depth_at = 0
             for ref in hidden:
@@ -488,8 +493,9 @@
         pltpu.with_memory_space_constraint(weight, pltpu.HBM)
         for weight in (gate_weight, up_weight, down_weight)
     )
-    pair = lambda k: [("rows", cols, k, gate_weight), ("rows", cols, k, up_weight)]
-    column = lambda k: ("cols", cols, k, down_weight)
+    pair = lambda k: [("rows", [(w, k, cols, 0, cols)]) for w in (gate_weight, up_weight)]
+    column = lambda k: ("cols", [(down_weight, k, cols, 0, cols)])
+    tile = cols // 2
     held = stage(flags, pair(0), [], [], None)
 
     block, features, inputs_local, head = whole_call(
@@ -515,25 +521,24 @@
     )
 
     step = lambda array, k: send(array, [((t, d), (t ^ k, d)) for t, d in every])
-    near = {k: step(block, k) for k in (2, 1, 3)}
+    near = {k: step(block, k) for k in (2, 1)}
 
     span = (0, units)
     basis, square, *later = basis_stage(
-        flags, pair(2), block, held, None, span, features, [], False
-    )
-    basis, square, *later = basis_stage(
-        flags, pair(1), near[2], later, basis, span, features, [square], False
-    )
+        flags, pair(2) + pair(1), [block], held, None, span, features, [], False
+    )
+    late_block, square = lax.optimization_barrier((block, square))
+    near[3] = step(late_block, 3)
     basis, square, *last = basis_stage(
-        flags, pair(3), near[1], later, basis, span, features, [square], False
+        flags, pair(3), [near[2], near[1]], later, basis, span, features, [square], False
     )
     cut = units // 2
     own_a, narrow_a, square, down_diagonal = basis_stage(
-        flags, [column(3)], near[3], last, basis, (0, cut), features, [square], True
+        flags, [column(3)], [near[3]], last, basis, (0, cut), features, [square], True
     )
     other_a = send(narrow_a, swap_core)
     own_b, narrow_b, down_x = basis_stage(
-        flags, [column(1)], near[3], last, basis, (cut, units), features, None, True
+        flags, [column(1)], [near[3]], last, basis, (cut, units), features, None, True
     )
     other_b = send(narrow_b, swap_core)
     hidden_a, scale, down_z = hidden_stage(
@@ -549,7 +554,10 @@
         hidden,
         [down_diagonal, down_x],
         cols,
-        [(both, 0, [(0, 0), (1, 0)]), (lower, 1, [(0, cols)])],
+        [
+            (both, [(0, 0), (0, tile)], [(0, 0), (1, 0)]),
+            (lower, [(1, 0), (1, tile)], [(0, cols)]),
+        ],
         [2 * cols, cols],
     )
     got_x = step(x_pair, 1)
@@ -557,7 +565,7 @@
         hidden,
         [down_z],
         cols,
-        [(upper, 0, [(0, cols)])],
+        [(upper, [(0, 0), (0, tile)], [(0, cols)])],
         [2 * cols],
         [(diagonal_upper, 0)],
     )
@@ -566,7 +574,11 @@
         hidden,
         [down_z, down_x, down_own],
         cols,
-        [(lower, 0, [(0, 0)]), (upper, 1, [(1, 0)]), (both, 2, [(2, 0), (3, 0)])],
+        [
+            (lower, [(0, 0), (0, tile)], [(0, 0)]),
+            (upper, [(1, 0), (1, tile)], [(1, 0)]),
+            (both, [(2, 0), (2, tile)], [(2, 0), (3, 0)]),
+        ],
         [cols] * 4,
     )
     add = lambda *parts: sum(part.astype(f32) for part in parts).astype(bf16)
@@ -576,15 +588,17 @@
         lax.optimization_barrier(add(own_lower, got_x[:, cols:], got_lower)),
         lax.optimization_barrier(add(own_upper, got_z[:, cols:], got_upper)),
     ]
-    far = [
-        send(sums[part], [((t, 1 - t // 4), (t ^ 4, part)) for t in range(TP)])
-        for part in range(2)
-    ]
-    crossed = send(
-        jnp.where(dp == 0, sums[1], sums[0]), [((t, t // 4), (t, 1 - t // 4)) for t in range(TP)]
-    )
-    mine = jnp.where(home, jnp.where(dp == 0, sums[0], sums[1]), crossed).astype(f32)
-    summed = mine + jnp.where(dp == 0, far[0], far[1]).astype(f32)
+    far = []
+    for part in range(2):
+        pairs = [((t, 1 - t // 4), (t ^ 4, part)) for t in range(TP)]
+        pairs += [((t, part), (t, 1 - part)) for t in range(TP) if t // 4 == part]
+        far.append(send(jnp.where(home, sums[1 - part], sums[part]), pairs))
+    mine = jnp.where(
+        home,
+        jnp.where(dp == 0, sums[0], sums[1]),
+        jnp.where(dp == 0, far[1], far[0]),
+    )
+    summed = mine.astype(f32) + jnp.where(dp == 0, far[0], far[1]).astype(f32)
     output_local = (inputs_local.astype(f32) + summed).astype(bf16)
 
     wide_out = output_local.astype(f32)

time: 106 us -> 109 us (1.028)
  waiting for transfers between devices: 27.7 us -> 38.9 us
  starting transfers between devices: 30.1 us -> 21.9 us
    ppermute x17 -> x16, waiting for transfers between devices: 27.7 us -> 38.9 us  [send(): lax.ppermute(array, ('tp', 'dp'), [(2 * st + sd, 2 * dt + dd) for (st, sd...]
    ppermute x17 -> x16, starting transfers between devices: 30.1 us -> 21.9 us  [send(): lax.ppermute(array, ('tp', 'dp'), [(2 * st + sd, 2 * dt + dd) for (st, sd...]
    pallas_call x8 -> x7, Pallas kernels: 34.9 us -> 34.1 us  [stage(): pl.pallas_call(body, out_shape=shapes, in_specs=[pl.BlockSpec(memory_spac...]
  transfers between devices with their start and end apart: 17 -> 16, of which waited for: 10 -> 8; matrix products, arithmetic and copies ran while one was open for 0% -> 0% of each run, Pallas kernels for 31% -> 29%
where the time goes in v7:
time: 109 us
  Pallas kernels  43.9 us (40%)
  waiting for transfers between devices  38.9 us (36%)
  starting transfers between devices  21.9 us (20%)
  local copies, waits for them, and re-layouts  1.48 us (1%)
  other arithmetic  1.44 us (1%)
    ppermute x16, waiting for transfers between devices, send(): lax.ppermute(array, ('tp', 'dp'), [(2 * st + sd, 2 * dt + dd) for (st, sd...  38.9 us
    pallas_call x7, Pallas kernels, stage(): pl.pallas_call(body, out_shape=shapes, in_specs=[pl.BlockSpec(memory_spac...  34.1 us
    ppermute x16, starting transfers between devices, send(): lax.ppermute(array, ('tp', 'dp'), [(2 * st + sd, 2 * dt + dd) for (st, sd...  21.9 us
    pallas_call x3, Pallas kernels, down_products(): pl.pallas_call(body, out_shape=[jax.ShapeDtypeStruct((rows // 2, width),...  7.44 us
    pallas_call x2, Pallas kernels, whole_call(): pl.pallas_call(lambda *refs: body(refs[count], *refs[count + 1:]), out_sh...  2.34 us
  transfers between devices with their start and end apart: 16, of which 8 were waited for; matrix products, arithmetic and copies ran while one was open for 0% of the time, Pallas kernels for 29%

profile of v7, /device:TPU:0, one launch (start us, length us, event | category | flops | bytes accessed | tf_op | source)
XLA Modules:
  0.0 108.6 jit_solution(12167658196635476108)
XLA Ops:
  0.7 1.0 shard_map.123.refs_3_
  1.8 0.8 collective-permute-start.1
  2.6 5.3 %collective-permute-start = (bf16[80,1024]{1,0:T(8,128)(2,1)S(1)}, bf16[80,1024]{1,0:T(8,128)(2,1)S(1)}, u32[]{:S(2)}, u32[]{:S(2)}) collective-permute-start(bf16[80,1024]{1,0:T(8,128)(2,1)S(1)} %shard_map.123.refs_3_), channel_id=1, source_target_pairs={{0,8},{2,10},{4,12},{6,14},{9,1},{11,3},{13,5},{15,7},{1,0},{3,2},... | collective-permute-start | bytes 491528 | tf_op jit(solution)/shard_map/ppermute | solution.py:108
  8.0 5.3 %shard_map.122 = (bf16[1024,3072]{1,0:T(8,128)(2,1)S(1)}, bf16[1024,3072]{1,0:T(8,128)(2,1)S(1)}) custom-call(s32[6]{0:T(128)S(1)} %stack.40.which_ref.refs_0_.refs_2_, bf16[4096,3072]{1,0:T(8,128)(2,1)} %refs_0_.9, bf16[4096,3072]{1,0:T(8,128)(2,1)} %refs_1_.7), custom_call_target="tpu_custom_call" | custom-call | bytes 12582912 | tf_op jit(solution)/shard_map/pallas_call | solution.py:160
  13.3 1.3 %shard_map.124 = (bf16[144,1024]{1,0:T(8,128)(2,1)S(1)}, bf16[256,144]{1,0:T(8,128)(2,1)S(1)}, bf16[128,1024]{1,0:T(8,128)(2,1)S(1)}, f32[1,1024]{1,0:T(1,128)S(1)}) custom-call(bf16[1024,3072]{1,0:T(8,128)(2,1)S(1)} %get-tuple-element.38.refs_0_.refs_5_, bf16[1024,3072]{1,0:T(8,128)(2,1)S(1)} %get-tuple-element.39.refs_1_.refs_6_, ...), custom_call_target="tpu_custom_call" | custom-call | flops 1000000 | bytes 1000000 | tf_op jit(solution)/shard_map/pallas_call | solution.py:430
  14.7 0.7 copy-done.3
  15.4 1.6 %collective-permute-start.4 = (bf16[144,1024]{1,0:T(8,128)(2,1)S(1)}, bf16[144,1024]{1,0:T(8,128)(2,1)S(1)}, u32[]{:S(2)}, u32[]{:S(2)}) collective-permute-start(bf16[144,1024]{1,0:T(8,128)(2,1)S(1)} %get-tuple-element.44.refs_4_), channel_id=1, source_target_pairs={{0,2},{1,3},{2,0},{3,1},{4,6},{5,7},{6,4},{7,5},{8,10},{9,11},{10,... | collective-permute-start | bytes 884744 | tf_op jit(solution)/shard_map/ppermute | solution.py:108
  17.0 3.5 %collective-permute-start.3 = (bf16[144,1024]{1,0:T(8,128)(2,1)S(1)}, bf16[144,1024]{1,0:T(8,128)(2,1)S(1)}, u32[]{:S(2)}, u32[]{:S(2)}) collective-permute-start(bf16[144,1024]{1,0:T(8,128)(2,1)S(1)} %get-tuple-element.44.refs_4_), channel_id=1, source_target_pairs={{0,4},{1,5},{2,6},{3,7},{4,0},{5,1},{6,2},{7,3},{8,12},{9,13},{10,... | collective-permute-start | bytes 884744 | tf_op jit(solution)/shard_map/ppermute | solution.py:108
  20.5 9.0 %shard_map.125 = (f32[2,144,3072]{2,1,0:T(8,128)S(1)}, f32[256,128]{1,0:T(8,128)S(1)}, bf16[1024,3072]{1,0:T(8,128)(2,1)S(1)}, bf16[1024,3072]{1,0:T(8,128)(2,1)...) custom-call(s32[6]{0:T(128)S(1)} %stack.40.which_ref.refs_0_.refs_2_, bf16[4096,3072]{1,0:T(8,128)(2,1)} %refs_0_.9, ...), custom_call_target="tpu_custom_call" | custom-call | flops 1811939328 | bytes 25165824 | tf_op jit(solution)/shard_map/pallas_call | solution.py:160
  29.6 6.1 %shard_map.126 = (f32[2,144,3072]{2,1,0:T(8,128)S(1)}, f32[256,128]{1,0:T(8,128)S(1)}, bf16[1024,3072]{1,0:T(8,128)(2,1)S(1)}, bf16[1024,3072]{1,0:T(8,128)(2,1)S(1)}) custom-call(s32[6]{0:T(128)S(1)} %stack.40.which_ref.refs_0_.refs_2_, bf16[4096,3072]{1,0:T(8,128)(2,1)} %refs_0_.9, bf16[4096,3072]{1,0:T(8,128)(2,1)} %refs_1_.7, ...), custom_call_target="tpu_custom_call" | custom-call | flops 3623878656 | bytes 12582912 | tf_op jit(solution)/shard_map/pallas_call | solution.py:160
  35.7 3.1 %collective-permute-done.2.refs_1_ = bf16[144,1024]{1,0:T(8,128)(2,1)S(1)} collective-permute-done((bf16[144,1024]{1,0:T(8,128)(2,1)S(1)}, bf16[144,1024]{1,0:T(8,128)(2,1)S(1)}, u32[]{:S(2)}, u32[]{:S(2)}) %collective-permute-start.2) | collective-permute-done | bytes 294944 | tf_op jit(solution)/shard_map/ppermute | solution.py:108
  38.8 3.4 %shard_map.127 = (f32[2,144,1536]{2,1,0:T(8,128)S(1)}, bf16[2,144,1536]{2,1,0:T(8,128)(2,1)S(1)}, f32[256,128]{1,0:T(8,128)S(1)}, bf16[3072,1024]{1,0:T(8,128)(2,1)S(1)}) custom-call(s32[6]{0:T(128)S(1)} %stack.40.which_ref.refs_0_.refs_2_, bf16[3072,4096]{1,0:T(8,128)(2,1)} %refs_0_.13, bf16[144,1024]{1,0:T(8,128)(2,1)S(1)} %collective-permute-done.2.refs_1_, ...), custom_call_target="tpu_custom_call" | custom-call | flops 905969664 | bytes 6291456 | tf_op jit(solution)/shard_map/pallas_call | solution.py:160
  42.4 3.4 %shard_map.129 = (f32[2,144,1536]{2,1,0:T(8,128)S(1)}, bf16[2,144,1536]{2,1,0:T(8,128)(2,1)S(1)}, bf16[3072,1024]{1,0:T(8,128)(2,1)S(1)}) custom-call(s32[6]{0:T(128)S(1)} %stack.40.which_ref.refs_0_.refs_2_, bf16[3072,4096]{1,0:T(8,128)(2,1)} %refs_0_.13, bf16[144,1024]{1,0:T(8,128)(2,1)S(1)} %collective-permute-done.2.refs_1_, ...), custom_call_target="tpu_custom_call" | custom-call | flops 905969664 | bytes 6291456 | tf_op jit(solution)/shard_map/pallas_call | solution.py:160
  46.4 3.4 %shard_map.128 = (bf16[256,1536]{1,0:T(8,128)(2,1)S(1)}, f32[256,128]{1,0:T(8,128)S(1)}, bf16[3072,1024]{1,0:T(8,128)(2,1)S(1)}) custom-call(s32[6]{0:T(128)S(1)} %stack.40.which_ref.refs_0_.refs_2_, bf16[3072,4096]{1,0:T(8,128)(2,1)} %refs_0_.13, f32[2,144,1536]{2,1,0:T(8,128)S(1)} %get-tuple-element.55.refs_1_, ...), custom_call_target="tpu_custom_call" | custom-call | flops 226492416 | bytes 6291456 | tf_op jit(solution)/shard_map/pallas_call | solution.py:160
  49.8 3.4 %shard_map.130 = (bf16[256,1536]{1,0:T(8,128)(2,1)S(1)}, bf16[3072,1024]{1,0:T(8,128)(2,1)S(1)}) custom-call(s32[6]{0:T(128)S(1)} %stack.40.which_ref.refs_0_.refs_2_, bf16[3072,4096]{1,0:T(8,128)(2,1)} %refs_0_.13, f32[2,144,1536]{2,1,0:T(8,128)S(1)} %get-tuple-element.59.refs_1_, bf16[2,144,1536]{2,1,0:T(8,128)(2,1)S(1)} %collective-permute-done.6.refs_2_, ...), custom_call_target="tpu_custom_call" | custom-call | flops 226492416 | bytes 6291456 | tf_op jit(solution)/shard_map/pallas_call | solution.py:160
  53.2 2.7 %shard_map.132 = (bf16[128,2048]{1,0:T(8,128)(2,1)S(1)}, bf16[128,1024]{1,0:T(8,128)(2,1)S(1)}) custom-call(bf16[256,1536]{1,0:T(8,128)(2,1)S(1)} %get-tuple-element.58.refs_0_, bf16[256,1536]{1,0:T(8,128)(2,1)S(1)} %get-tuple-element.62.refs_1_, bf16[3072,1024]{1,0:T(8,128)(2,1)S(1)} %get-tuple-element.67.refs_2_, ...), custom_call_target="tpu_custom_call" | custom-call | flops 150994944 | tf_op jit(solution)/shard_map/pallas_call | solution.py:352
  56.6 1.1 shard_map.133
  57.7 1.4 %collective-permute-start.9 = (bf16[128,2048]{1,0:T(8,128)(2,1)S(1)}, bf16[128,2048]{1,0:T(8,128)(2,1)S(1)}, u32[]{:S(2)}, u32[]{:S(2)}) collective-permute-start(bf16[128,2048]{1,0:T(8,128)(2,1)S(1)} %shard_map.133), channel_id=1, source_target_pairs={{0,4},{1,5},{2,6},{3,7},{4,0},{5,1},{6,2},{7,3},{8,12},{9,13},{10,... | collective-permute-start | bytes 1572872 | tf_op jit(solution)/shard_map/ppermute | solution.py:108
  59.1 3.7 %shard_map.131 = (bf16[128,1024]{1,0:T(8,128)(2,1)S(1)}, bf16[128,1024]{1,0:T(8,128)(2,1)S(1)}, bf16[128,1024]{1,0:T(8,128)(2,1)S(1)}, bf16[128,1024]{1,0:T(8,128)(2,1)S(1)}) custom-call(bf16[256,1536]{1,0:T(8,128)(2,1)S(1)} %get-tuple-element.58.refs_0_, bf16[256,1536]{1,0:T(8,128)(2,1)S(1)} %get-tuple-element.62.refs_1_, ...), custom_call_target="tpu_custom_call" | custom-call | flops 201326592 | tf_op jit(solution)/shard_map/pallas_call | solution.py:352
  62.7 7.1 %collective-permute-done.7 = bf16[128,2048]{1,0:T(8,128)(2,1)S(1)} collective-permute-done((bf16[128,2048]{1,0:T(8,128)(2,1)S(1)}, bf16[128,2048]{1,0:T(8,128)(2,1)S(1)}, u32[]{:S(2)}, u32[]{:S(2)}) %collective-permute-start.7) | collective-permute-done | bytes 524320 | tf_op jit(solution)/shard_map/ppermute | solution.py:108
  69.9 1.5 %collective-permute-start.8 = (bf16[128,1024]{1,0:T(8,128)(2,1)S(1)}, bf16[128,1024]{1,0:T(8,128)(2,1)S(1)}, u32[]{:S(2)}, u32[]{:S(2)}) collective-permute-start(bf16[128,1024]{1,0:T(8,128)(2,1)S(1)} %add_convert_fusion.4), channel_id=1, source_target_pairs={{0,4},{1,5},{2,6},{3,7},{4,0},{5,1},{6,2},{7,3},{8,12},{9,13},{10,... | collective-permute-start | bytes 786440 | tf_op jit(solution)/shard_map/ppermute | solution.py:108
  71.5 1.7 %collective-permute-start.10 = (bf16[128,1024]{1,0:T(8,128)(2,1)S(1)}, bf16[128,1024]{1,0:T(8,128)(2,1)S(1)}, u32[]{:S(2)}, u32[]{:S(2)}) collective-permute-start(bf16[128,1024]{1,0:T(8,128)(2,1)S(1)} %add_convert_fusion.2), channel_id=1, source_target_pairs={{0,2},{1,3},{2,0},{3,1},{4,6},{5,7},{6,4},{7,5},{8,10},{9,11},{10,... | collective-permute-start | bytes 786440 | tf_op jit(solution)/shard_map/ppermute | solution.py:108
  73.2 4.2 %collective-permute-done.8 = bf16[128,1024]{1,0:T(8,128)(2,1)S(1)} collective-permute-done((bf16[128,1024]{1,0:T(8,128)(2,1)S(1)}, bf16[128,1024]{1,0:T(8,128)(2,1)S(1)}, u32[]{:S(2)}, u32[]{:S(2)}) %collective-permute-start.8) | collective-permute-done | bytes 262176 | tf_op jit(solution)/shard_map/ppermute | solution.py:108
  77.5 1.1 %collective-permute-done.10 = bf16[128,1024]{1,0:T(8,128)(2,1)S(1)} collective-permute-done((bf16[128,1024]{1,0:T(8,128)(2,1)S(1)}, bf16[128,1024]{1,0:T(8,128)(2,1)S(1)}, u32[]{:S(2)}, u32[]{:S(2)}) %collective-permute-start.10) | collective-permute-done | bytes 262176 | tf_op jit(solution)/shard_map/ppermute | solution.py:108
  78.9 0.7 collective-permute-start.11
  79.5 2.3 %collective-permute-start.12 = (bf16[128,1024]{1,0:T(8,128)(2,1)S(1)}, bf16[128,1024]{1,0:T(8,128)(2,1)S(1)}, u32[]{:S(2)}, u32[]{:S(2)}) collective-permute-start(bf16[128,1024]{1,0:T(8,128)(2,1)S(1)} %get-tuple-element.78), channel_id=1, source_target_pairs={{1,8},{3,10},{5,12},{7,14},{8,0},{10,2},{12,4},{14,6},{0,1},{2,3},... | collective-permute-start | bytes 786440 | tf_op jit(solution)/shard_map/ppermute | solution.py:108
  81.9 13.2 %collective-permute-done.12 = bf16[128,1024]{1,0:T(8,128)(2,1)S(1)} collective-permute-done((bf16[128,1024]{1,0:T(8,128)(2,1)S(1)}, bf16[128,1024]{1,0:T(8,128)(2,1)S(1)}, u32[]{:S(2)}, u32[]{:S(2)}) %collective-permute-start.12) | collective-permute-done | bytes 262176 | tf_op jit(solution)/shard_map/ppermute | solution.py:108
  95.1 1.0 fusion
  96.1 1.5 %collective-permute-start.13 = (f32[2,128]{1,0:T(2,128)S(1)}, f32[2,128]{1,0:T(2,128)S(1)}, u32[]{:S(2)}, u32[]{:S(2)}) collective-permute-start(f32[2,128]{1,0:T(2,128)S(1)} %pad_maximum_fusion), channel_id=1, source_target_pairs={{0,2},{1,3},{2,0},{3,1},{4,6},{5,7},{6,4},{7,5},{8,10},{9,11},{10,... | collective-permute-start | bytes 3080 | tf_op jit(solution)/shard_map/ppermute | solution.py:108
  97.6 2.1 %collective-permute-done.13 = f32[2,128]{1,0:T(2,128)S(1)} collective-permute-done((f32[2,128]{1,0:T(2,128)S(1)}, f32[2,128]{1,0:T(2,128)S(1)}, u32[]{:S(2)}, u32[]{:S(2)}) %collective-permute-start.13) | collective-permute-done | bytes 1056 | tf_op jit(solution)/shard_map/ppermute | solution.py:108
  99.8 3.6 %collective-permute-done.14 = f32[2,128]{1,0:T(2,128)S(1)} collective-permute-done((f32[2,128]{1,0:T(2,128)S(1)}, f32[2,128]{1,0:T(2,128)S(1)}, u32[]{:S(2)}, u32[]{:S(2)}) %collective-permute-start.14) | collective-permute-done | bytes 1056 | tf_op jit(solution)/shard_map/ppermute | solution.py:108
  103.4 4.5 %collective-permute-done.15 = f32[2,128]{1,0:T(2,128)S(1)} collective-permute-done((f32[2,128]{1,0:T(2,128)S(1)}, f32[2,128]{1,0:T(2,128)S(1)}, u32[]{:S(2)}, u32[]{:S(2)}) %collective-permute-start.15) | collective-permute-done | bytes 1056 | tf_op jit(solution)/shard_map/ppermute | solution.py:108
  (45 shorter events, 2.8 us)
Async XLA Ops:
  1.7 11.5 %copy-start.2 = (bf16[128,1024]{1,0:T(8,128)(2,1)S(1)}, bf16[128,1024]{1,0:T(8,128)(2,1)}, u32[]{:S(2)}) copy-start(bf16[128,1024]{1,0:T(8,128)(2,1)} %refs_6_.1) | copy-start | bytes 786436
  1.8 11.5 %copy-start.5 = (bf16[2,1024]{1,0:T(2,128)(2,1)S(1)}, bf16[2,1024]{1,0:T(2,128)(2,1)}, u32[]{:S(2)}) copy-start(bf16[2,1024]{1,0:T(2,128)(2,1)} %refs_7_.1) | copy-start | bytes 12292
  1.8 11.5 %copy-start.6 = (f32[1024]{0:T(1024)S(1)}, f32[1024]{0:T(1024)}, u32[]{:S(2)}) copy-start(f32[1024]{0:T(1024)} %refs_10_.1) | copy-start | bytes 12292
  1.8 11.5 %copy-start.7 = (f32[1024]{0:T(1024)S(1)}, f32[1024]{0:T(1024)}, u32[]{:S(2)}) copy-start(f32[1024]{0:T(1024)} %refs_11_.1) | copy-start | bytes 12292
  1.8 11.5 %copy-start.8 = (f32[128]{0:T(128)S(1)}, f32[128]{0:T(128)}, u32[]{:S(2)}) copy-start(f32[128]{0:T(128)} %refs_8_.1) | copy-start | bytes 1540
  1.8 11.5 %copy-start.9 = (f32[128]{0:T(128)S(1)}, f32[128]{0:T(128)}, u32[]{:S(2)}) copy-start(f32[128]{0:T(128)} %refs_9_.1) | copy-start | bytes 1540
  1.8 11.4 %collective-permute-start.1 = (bf16[80,1024]{1,0:T(8,128)(2,1)S(1)}, bf16[80,1024]{1,0:T(8,128)(2,1)S(1)}, u32[]{:S(2)}, u32[]{:S(2)}) collective-permute-start(bf16[80,1024]{1,0:T(8,128)(2,1)S(1)} %shard_map.123.refs_3_), channel_id=1, source_target_pairs={{1,8},{3,10},{5,12},{7,14},{8,1},{10,3},{12,5},{14,7},{17,24},{19,... | collective-permute-start | bytes 491528 | tf_op jit(solution)/shard_map/ppermute | solution.py:108
  2.6 10.6 %collective-permute-start = (bf16[80,1024]{1,0:T(8,128)(2,1)S(1)}, bf16[80,1024]{1,0:T(8,128)(2,1)S(1)}, u32[]{:S(2)}, u32[]{:S(2)}) collective-permute-start(bf16[80,1024]{1,0:T(8,128)(2,1)S(1)} %shard_map.123.refs_3_), channel_id=1, source_target_pairs={{0,8},{2,10},{4,12},{6,14},{9,1},{11,3},{13,5},{15,7},{1,0},{3,2},... | collective-permute-start | bytes 491528 | tf_op jit(solution)/shard_map/ppermute | solution.py:108
  14.7 0.7 copy-start.3
  15.4 23.5 %copy-start = (bf16[256,144]{1,0:T(8,128)(2,1)}, bf16[256,144]{1,0:T(8,128)(2,1)S(1)}, u32[]{:S(2)}) copy-start(bf16[256,144]{1,0:T(8,128)(2,1)S(1)} %get-tuple-element.42.refs_7_.refs_9_.refs_5_.refs_3_) | copy-start | bytes 221188
  15.4 14.2 %collective-permute-start.4 = (bf16[144,1024]{1,0:T(8,128)(2,1)S(1)}, bf16[144,1024]{1,0:T(8,128)(2,1)S(1)}, u32[]{:S(2)}, u32[]{:S(2)}) collective-permute-start(bf16[144,1024]{1,0:T(8,128)(2,1)S(1)} %get-tuple-element.44.refs_4_), channel_id=1, source_target_pairs={{0,2},{1,3},{2,0},{3,1},{4,6},{5,7},{6,4},{7,5},{8,10},{9,11},{10,... | collective-permute-start | bytes 884744 | tf_op jit(solution)/shard_map/ppermute | solution.py:108
  17.0 12.6 %collective-permute-start.3 = (bf16[144,1024]{1,0:T(8,128)(2,1)S(1)}, bf16[144,1024]{1,0:T(8,128)(2,1)S(1)}, u32[]{:S(2)}, u32[]{:S(2)}) collective-permute-start(bf16[144,1024]{1,0:T(8,128)(2,1)S(1)} %get-tuple-element.44.refs_4_), channel_id=1, source_target_pairs={{0,4},{1,5},{2,6},{3,7},{4,0},{5,1},{6,2},{7,3},{8,12},{9,13},{10,... | collective-permute-start | bytes 884744 | tf_op jit(solution)/shard_map/ppermute | solution.py:108
  29.5 9.4 %collective-permute-start.2 = (bf16[144,1024]{1,0:T(8,128)(2,1)S(1)}, bf16[144,1024]{1,0:T(8,128)(2,1)S(1)}, u32[]{:S(2)}, u32[]{:S(2)}) collective-permute-start(bf16[144,1024]{1,0:T(8,128)(2,1)S(1)} %get-tuple-element.44.refs_4_), channel_id=1, source_target_pairs={{0,6},{1,7},{2,4},{3,5},{4,2},{5,3},{6,0},{7,1},{8,14},{9,15},{10,... | collective-permute-start | bytes 884744 | tf_op jit(solution)/shard_map/ppermute | solution.py:108
  42.3 4.1 %copy-start.1 = (bf16[256,144]{1,0:T(8,128)(2,1)S(1)}, bf16[256,144]{1,0:T(8,128)(2,1)}, u32[]{:S(2)}) copy-start(bf16[256,144]{1,0:T(8,128)(2,1)} %copy-done) | copy-start | bytes 221188
  42.3 4.1 %collective-permute-start.5 = (bf16[2,144,1536]{2,1,0:T(8,128)(2,1)S(1)}, bf16[2,144,1536]{2,1,0:T(8,128)(2,1)S(1)}, u32[]{:S(2)}, u32[]{:S(2)}) collective-permute-start(bf16[2,144,1536]{2,1,0:T(8,128)(2,1)S(1)} %get-tuple-element.56), channel_id=1, source_target_pairs={{0,1},{1,0},{2,3},{3,2},{4,5},{5,4},{6,7},{7,6},{8,9},{9,8},{10,11... | collective-permute-start | bytes 2654216 | tf_op jit(solution)/shard_map/ppermute | solution.py:108
  45.8 4.0 %collective-permute-start.6 = (bf16[2,144,1536]{2,1,0:T(8,128)(2,1)S(1)}, bf16[2,144,1536]{2,1,0:T(8,128)(2,1)S(1)}, u32[]{:S(2)}, u32[]{:S(2)}) collective-permute-start(bf16[2,144,1536]{2,1,0:T(8,128)(2,1)S(1)} %get-tuple-element.60), channel_id=1, source_target_pairs={{0,1},{1,0},{2,3},{3,2},{4,5},{5,4},{6,7},{7,6},{8,9},{9,8},{10,11... | collective-permute-start | bytes 2654216 | tf_op jit(solution)/shard_map/ppermute | solution.py:108
  56.0 13.9 %collective-permute-start.7 = (bf16[128,2048]{1,0:T(8,128)(2,1)S(1)}, bf16[128,2048]{1,0:T(8,128)(2,1)S(1)}, u32[]{:S(2)}, u32[]{:S(2)}) collective-permute-start(bf16[128,2048]{1,0:T(8,128)(2,1)S(1)} %get-tuple-element.68), channel_id=1, source_target_pairs={{0,2},{1,3},{2,0},{3,1},{4,6},{5,7},{6,4},{7,5},{8,10},{9,11},{10,... | collective-permute-start | bytes 1572872 | tf_op jit(solution)/shard_map/ppermute | solution.py:108
  57.7 13.8 %collective-permute-start.9 = (bf16[128,2048]{1,0:T(8,128)(2,1)S(1)}, bf16[128,2048]{1,0:T(8,128)(2,1)S(1)}, u32[]{:S(2)}, u32[]{:S(2)}) collective-permute-start(bf16[128,2048]{1,0:T(8,128)(2,1)S(1)} %shard_map.133), channel_id=1, source_target_pairs={{0,4},{1,5},{2,6},{3,7},{4,0},{5,1},{6,2},{7,3},{8,12},{9,13},{10,... | collective-permute-start | bytes 1572872 | tf_op jit(solution)/shard_map/ppermute | solution.py:108
  59.1 36.0 %copy-start.4 = (bf16[128,1024]{1,0:T(8,128)(2,1)S(1)}, bf16[128,1024]{1,0:T(8,128)(2,1)}, u32[]{:S(2)}) copy-start(bf16[128,1024]{1,0:T(8,128)(2,1)} %copy-done.3) | copy-start | bytes 786436
  69.9 7.5 %collective-permute-start.8 = (bf16[128,1024]{1,0:T(8,128)(2,1)S(1)}, bf16[128,1024]{1,0:T(8,128)(2,1)S(1)}, u32[]{:S(2)}, u32[]{:S(2)}) collective-permute-start(bf16[128,1024]{1,0:T(8,128)(2,1)S(1)} %add_convert_fusion.4), channel_id=1, source_target_pairs={{0,4},{1,5},{2,6},{3,7},{4,0},{5,1},{6,2},{7,3},{8,12},{9,13},{10,... | collective-permute-start | bytes 786440 | tf_op jit(solution)/shard_map/ppermute | solution.py:108
  71.5 7.2 %collective-permute-start.10 = (bf16[128,1024]{1,0:T(8,128)(2,1)S(1)}, bf16[128,1024]{1,0:T(8,128)(2,1)S(1)}, u32[]{:S(2)}, u32[]{:S(2)}) collective-permute-start(bf16[128,1024]{1,0:T(8,128)(2,1)S(1)} %add_convert_fusion.2), channel_id=1, source_target_pairs={{0,2},{1,3},{2,0},{3,1},{4,6},{5,7},{6,4},{7,5},{8,10},{9,11},{10,... | collective-permute-start | bytes 786440 | tf_op jit(solution)/shard_map/ppermute | solution.py:108
  78.9 3.0 %collective-permute-start.11 = (bf16[128,1024]{1,0:T(8,128)(2,1)S(1)}, bf16[128,1024]{1,0:T(8,128)(2,1)S(1)}, u32[]{:S(2)}, u32[]{:S(2)}) collective-permute-start(bf16[128,1024]{1,0:T(8,128)(2,1)S(1)} %get-tuple-element.77), channel_id=1, source_target_pairs={{1,9},{3,11},{5,13},{7,15},{8,1},{10,3},{12,5},{14,7},{9,8},{11,10... | collective-permute-start | bytes 786440 | tf_op jit(solution)/shard_map/ppermute | solution.py:108
  79.5 15.5 %collective-permute-start.12 = (bf16[128,1024]{1,0:T(8,128)(2,1)S(1)}, bf16[128,1024]{1,0:T(8,128)(2,1)S(1)}, u32[]{:S(2)}, u32[]{:S(2)}) collective-permute-start(bf16[128,1024]{1,0:T(8,128)(2,1)S(1)} %get-tuple-element.78), channel_id=1, source_target_pairs={{1,8},{3,10},{5,12},{7,14},{8,0},{10,2},{12,4},{14,6},{0,1},{2,3},... | collective-permute-start | bytes 786440 | tf_op jit(solution)/shard_map/ppermute | solution.py:108
  96.1 3.6 %collective-permute-start.13 = (f32[2,128]{1,0:T(2,128)S(1)}, f32[2,128]{1,0:T(2,128)S(1)}, u32[]{:S(2)}, u32[]{:S(2)}) collective-permute-start(f32[2,128]{1,0:T(2,128)S(1)} %pad_maximum_fusion), channel_id=1, source_target_pairs={{0,2},{1,3},{2,0},{3,1},{4,6},{5,7},{6,4},{7,5},{8,10},{9,11},{10,... | collective-permute-start | bytes 3080 | tf_op jit(solution)/shard_map/ppermute | solution.py:108
  99.7 3.6 %collective-permute-start.14 = (f32[2,128]{1,0:T(2,128)S(1)}, f32[2,128]{1,0:T(2,128)S(1)}, u32[]{:S(2)}, u32[]{:S(2)}) collective-permute-start(f32[2,128]{1,0:T(2,128)S(1)} %fusion.2), channel_id=1, source_target_pairs={{0,4},{1,5},{2,6},{3,7},{4,0},{5,1},{6,2},{7,3},{8,12},{9,13},{10,... | collective-permute-start | bytes 3080 | tf_op jit(solution)/shard_map/ppermute | solution.py:108
  103.3 4.5 %collective-permute-start.15 = (f32[2,128]{1,0:T(2,128)S(1)}, f32[2,128]{1,0:T(2,128)S(1)}, u32[]{:S(2)}, u32[]{:S(2)}) collective-permute-start(f32[2,128]{1,0:T(2,128)S(1)} %fusion.3), channel_id=1, source_target_pairs={{0,8},{1,9},{2,10},{3,11},{4,12},{5,13},{6,14},{7,15},{8,0},{9,1},... | collective-permute-start | bytes 3080 | tf_op jit(solution)/shard_map/ppermute | solution.py:108

commit v8 on v7

--- a/solution.py
+++ b/solution.py
@@ -113,7 +113,7 @@
 SPLIT = 8
 
 
-def stage(which, loads, ins, outs, compute, scratch=(), limit=6, flops=0, alias=None):
+def stage(which, loads, ins, outs, compute, scratch=(), limit=3, flops=0, alias=None, manual=False):
     vmem = pl.BlockSpec(memory_space=pltpu.VMEM)
     count = len(ins)
     shapes, sources, flat = list(outs), [], []
@@ -151,10 +151,19 @@
                 at += 1
         for copy in made:
             copy.start()
-        if compute is not None:
+        waited = []
+
+        def wait():
+            if not waited:
+                waited.append(True)
+                for copy in made:
+                    copy.wait()
+
+        if manual:
+            compute(inputs, results, extra, list(targets), wait)
+        elif compute is not None:
             compute(inputs, results, extra[1:] if n else extra)
-        for copy in made:
-            copy.wait()
+        wait()
 
     loaded = sum(2 * math.prod(shape.shape) for shape in shapes[len(outs) :])
     return pl.pallas_call(
@@ -258,7 +267,7 @@
         compute,
         [pltpu.VMEM((count, m, k), jnp.bfloat16)],
         flops=4 * m * k * width * count,
-        alias=None,
+        alias=None if before is None or narrow else 3 * count,
     )
 
 
@@ -309,54 +318,51 @@
     )
 
 
-def down_body(places, cols, hidden, weights, outs):
-    half = hidden[0].shape[0] // 2
-    tile = 512
-    for rows, tiles, targets in places:
-        low, high = rows[0] * half, rows[-1] * half + half
-        for j, (which, at) in enumerate(tiles):
-            total = None
-            depth_at = 0
-            for ref in hidden:
-                depth = ref.shape[1]
-                term = jnp.dot(
-                    ref[low:high, :],
-                    weights[which][depth_at : depth_at + depth, at : at + tile],
-                    preferred_element_type=jnp.float32,
-                )
-                total = term if total is None else total + term
-                depth_at += depth
-            total = total.astype(jnp.bfloat16)
-            for index, (out, column) in enumerate(targets):
-                to = column + j * tile
-                outs[out][:, to : to + tile] = total[index * half : (index + 1) * half]
-
-
-def down_products(hidden, weights, cols, places, widths, copies=()):
+def down_stage(which, loads, hidden, weights, tile, places, widths, copies=()):
     rows = hidden[0].shape[0]
     depth = weights[0].shape[0]
-    flops = sum(len(r) * rows * depth * cols for r, *_ in places)
-    vmem = pl.BlockSpec(memory_space=pltpu.VMEM)
-    counts = (len(hidden), len(weights), len(copies))
-
-    def body(*refs):
-        groups, at = [], 0
-        for count in counts:
-            groups.append(refs[at : at + count])
-            at += count
-        outs = refs[at:]
-        down_body(places, cols, groups[0], groups[1], outs)
-        for source, (_, out) in zip(groups[2], copies):
-            outs[out][:, : source.shape[1]] = source[...]
-
-    return pl.pallas_call(
-        body,
-        out_shape=[jax.ShapeDtypeStruct((rows // 2, width), jnp.bfloat16) for width in widths],
-        in_specs=[vmem] * sum(counts),
-        out_specs=[vmem] * len(widths),
-        compiler_params=pltpu.CompilerParams(vmem_limit_bytes=6 * MIB),
-        cost_estimate=pl.CostEstimate(flops=flops // 16, bytes_accessed=0, transcendentals=0),
-    )(*hidden, *weights, *[c[0] for c in copies])
+    half = rows // 2
+    flops = sum(2 * len(r) * half * depth * tile * len(tiles) for r, tiles, _ in places)
+    counts = (len(hidden), len(weights))
+
+    def compute(inputs, results, extra, loaded, wait):
+        hidden = inputs[: counts[0]]
+        weights = list(inputs[counts[0] : sum(counts)])
+        sources = inputs[sum(counts) :]
+        for parts, tiles, targets in places:
+            low, high = parts[0] * half, parts[-1] * half + half
+            for j, (index, at) in enumerate(tiles):
+                if index == len(weights):
+                    wait()
+                    weights += loaded
+                total = None
+                depth_at = 0
+                for ref in hidden:
+                    size = ref.shape[1]
+                    term = jnp.dot(
+                        ref[low:high, :],
+                        weights[index][depth_at : depth_at + size, at : at + tile],
+                        preferred_element_type=jnp.float32,
+                    )
+                    total = term if total is None else total + term
+                    depth_at += size
+                total = total.astype(jnp.bfloat16)
+                for part, (out, column) in enumerate(targets):
+                    to = column + j * tile
+                    results[out][:, to : to + tile] = total[part * half : (part + 1) * half]
+        for source, (_, out) in zip(sources, copies):
+            results[out][:, : source.shape[1]] = source[...]
+
+    return stage(
+        which,
+        loads,
+        [*hidden, *weights, *[copy[0] for copy in copies]],
+        [jax.ShapeDtypeStruct((half, width), jnp.bfloat16) for width in widths],
+        compute,
+        limit=6,
+        flops=flops // 16,
+        manual=True,
+    )
 
 
 def piece_body(flags, weight, states, gain, seeds, piece, rows):
@@ -521,39 +527,40 @@
     )
 
     step = lambda array, k: send(array, [((t, d), (t ^ k, d)) for t, d in every])
-    near = {k: step(block, k) for k in (2, 1)}
+    near = {k: step(block, k) for k in (2, 1, 3)}
 
     span = (0, units)
-    basis, square, *later = basis_stage(
-        flags, pair(2) + pair(1), [block], held, None, span, features, [], False
-    )
-    late_block, square = lax.optimization_barrier((block, square))
-    near[3] = step(late_block, 3)
-    basis, square, *last = basis_stage(
-        flags, pair(3), [near[2], near[1]], later, basis, span, features, [square], False
+    basis, square, *held = basis_stage(
+        flags, pair(2), [block], held, None, span, features, [], False
+    )
+    basis, square, *held = basis_stage(
+        flags, pair(1), [near[2]], held, basis, span, features, [square], False
+    )
+    basis, square, *held = basis_stage(
+        flags, pair(3), [near[1]], held, basis, span, features, [square], False
     )
     cut = units // 2
     own_a, narrow_a, square, down_diagonal = basis_stage(
-        flags, [column(3)], [near[3]], last, basis, (0, cut), features, [square], True
+        flags, [column(3)], [near[3]], held, basis, (0, cut), features, [square], True
     )
     other_a = send(narrow_a, swap_core)
     own_b, narrow_b, down_x = basis_stage(
-        flags, [column(1)], [near[3]], last, basis, (cut, units), features, None, True
+        flags, [column(1)], [near[3]], held, basis, (cut, units), features, None, True
     )
     other_b = send(narrow_b, swap_core)
-    hidden_a, scale, down_z = hidden_stage(
-        flags, [column(2)], own_a, other_a, features, square, None, full_width
-    )
-    hidden_b, down_own = hidden_stage(
-        flags, [column(0)], own_b, other_b, features, None, scale, full_width
-    )
+    hidden_a, scale = hidden_stage(
+        flags, [], own_a, other_a, features, square, None, full_width
+    )
+    (hidden_b,) = hidden_stage(flags, [], own_b, other_b, features, None, scale, full_width)
     hidden = [hidden_a, hidden_b]
 
     both, lower, upper = (0, 1), (0,), (1,)
-    x_pair, diagonal_upper = down_products(
+    x_pair, diagonal_upper, down_z = down_stage(
+        flags,
+        [column(2)],
         hidden,
         [down_diagonal, down_x],
-        cols,
+        tile,
         [
             (both, [(0, 0), (0, tile)], [(0, 0), (1, 0)]),
             (lower, [(1, 0), (1, tile)], [(0, cols)]),
@@ -561,19 +568,23 @@
         [2 * cols, cols],
     )
     got_x = step(x_pair, 1)
-    (z_pair,) = down_products(
+    (z_pair,) = down_stage(
+        flags,
+        [],
         hidden,
         [down_z],
-        cols,
+        tile,
         [(upper, [(0, 0), (0, tile)], [(0, cols)])],
         [2 * cols],
         [(diagonal_upper, 0)],
     )
     got_z = step(z_pair, 2)
-    z_lower, x_upper, own_lower, own_upper = down_products(
+    z_lower, x_upper, own_lower, own_upper, _ = down_stage(
+        flags,
+        [column(0)],
         hidden,
-        [down_z, down_x, down_own],
-        cols,
+        [down_z, down_x],
+        tile,
         [
             (lower, [(0, 0), (0, tile)], [(0, 0)]),
             (upper, [(1, 0), (1, tile)], [(1, 0)]),
@@ -588,17 +599,15 @@
         lax.optimization_barrier(add(own_lower, got_x[:, cols:], got_lower)),
         lax.optimization_barrier(add(own_upper, got_z[:, cols:], got_upper)),
     ]
-    far = []
-    for part in range(2):
-        pairs = [((t, 1 - t // 4), (t ^ 4, part)) for t in range(TP)]
-        pairs += [((t, part), (t, 1 - part)) for t in range(TP) if t // 4 == part]
-        far.append(send(jnp.where(home, sums[1 - part], sums[part]), pairs))
-    mine = jnp.where(
-        home,
-        jnp.where(dp == 0, sums[0], sums[1]),
-        jnp.where(dp == 0, far[1], far[0]),
-    )
-    summed = mine.astype(f32) + jnp.where(dp == 0, far[0], far[1]).astype(f32)
+    far = [
+        send(sums[part], [((t, 1 - t // 4), (t ^ 4, part)) for t in range(TP)])
+        for part in range(2)
+    ]
+    crossed = send(
+        jnp.where(dp == 0, sums[1], sums[0]), [((t, t // 4), (t, 1 - t // 4)) for t in range(TP)]
+    )
+    mine = jnp.where(home, jnp.where(dp == 0, sums[0], sums[1]), crossed).astype(f32)
+    summed = mine + jnp.where(dp == 0, far[0], far[1]).astype(f32)
     output_local = (inputs_local.astype(f32) + summed).astype(bf16)
 
     wide_out = output_local.astype(f32)

time: 109 us -> 106 us (0.972)
  waiting for transfers between devices: 38.9 us -> 28.4 us
  starting transfers between devices: 21.9 us -> 26.2 us
  Pallas kernels: 43.9 us -> 47.7 us
    pallas_call x7 -> x11, Pallas kernels: 34.1 us -> 45.4 us  [stage(): pl.pallas_call(body, out_shape=shapes, in_specs=[pl.BlockSpec(memory_spac...]
    ppermute x16 -> x17, waiting for transfers between devices: 38.9 us -> 28.4 us  [send(): lax.ppermute(array, ('tp', 'dp'), [(2 * st + sd, 2 * dt + dd) for (st, sd...]
    pallas_call x3 -> x0, Pallas kernels: 7.44 us -> none  [down_products(): pl.pallas_call(body, out_shape=[jax.ShapeDtypeStruct((rows // 2, width),...]
    ppermute x16 -> x17, starting transfers between devices: 21.9 us -> 26.2 us  [send(): lax.ppermute(array, ('tp', 'dp'), [(2 * st + sd, 2 * dt + dd) for (st, sd...]
  transfers between devices with their start and end apart: 16 -> 17, of which waited for: 8 -> 10; matrix products, arithmetic and copies ran while one was open for 0% -> 0% of each run, Pallas kernels for 29% -> 33%
where the time goes in v8:
time: 106 us; the launch traced here: 105 us
  Pallas kernels  47.7 us (45%)
  waiting for transfers between devices  28.4 us (27%)
  starting transfers between devices  26.2 us (25%)
  other arithmetic  1.44 us (1%)
    pallas_call x11, Pallas kernels, stage(): pl.pallas_call(body, out_shape=shapes, in_specs=[pl.BlockSpec(memory_spac...  45.4 us
    ppermute x17, waiting for transfers between devices, send(): lax.ppermute(array, ('tp', 'dp'), [(2 * st + sd, 2 * dt + dd) for (st, sd...  28.4 us
    ppermute x17, starting transfers between devices, send(): lax.ppermute(array, ('tp', 'dp'), [(2 * st + sd, 2 * dt + dd) for (st, sd...  26.2 us
    pallas_call x2, Pallas kernels, whole_call(): pl.pallas_call(lambda *refs: body(refs[count], *refs[count + 1:]), out_sh...  2.34 us
  transfers between devices with their start and end apart: 17, of which 10 were waited for; matrix products, arithmetic and copies ran while one was open for 0% of the time, Pallas kernels for 33%

profile of v8, /device:TPU:0, one launch (start us, length us, event | category | flops | bytes accessed | tf_op | source)
XLA Modules:
  0.0 105.4 jit_solution(12445070320208967192)
XLA Ops:
  0.7 1.0 shard_map.123.refs_3_
  1.8 4.1 %collective-permute-start = (bf16[80,1024]{1,0:T(8,128)(2,1)S(1)}, bf16[80,1024]{1,0:T(8,128)(2,1)S(1)}, u32[]{:S(2)}, u32[]{:S(2)}) collective-permute-start(bf16[80,1024]{1,0:T(8,128)(2,1)S(1)} %shard_map.123.refs_3_), channel_id=1, source_target_pairs={{0,8},{2,10},{4,12},{6,14},{9,1},{11,3},{13,5},{15,7},{1,0},{3,2},... | collective-permute-start | bytes 491528 | tf_op jit(solution)/shard_map/ppermute | solution.py:108
  6.6 5.3 %shard_map.122 = (bf16[1024,3072]{1,0:T(8,128)(2,1)S(1)}, bf16[1024,3072]{1,0:T(8,128)(2,1)S(1)}) custom-call(s32[6]{0:T(128)S(1)} %stack.40.which_ref.refs_0_.refs_2_, bf16[4096,3072]{1,0:T(8,128)(2,1)} %refs_0_.11, bf16[4096,3072]{1,0:T(8,128)(2,1)} %refs_1_.9), custom_call_target="tpu_custom_call" | custom-call | bytes 12582912 | tf_op jit(solution)/shard_map/pallas_call | solution.py:169
  11.9 1.3 %shard_map.124 = (bf16[144,1024]{1,0:T(8,128)(2,1)S(1)}, bf16[256,144]{1,0:T(8,128)(2,1)S(1)}, bf16[128,1024]{1,0:T(8,128)(2,1)S(1)}, f32[1,1024]{1,0:T(1,128)S(1)}) custom-call(bf16[1024,3072]{1,0:T(8,128)(2,1)S(1)} %get-tuple-element.36.refs_0_.refs_3_, bf16[1024,3072]{1,0:T(8,128)(2,1)S(1)} %get-tuple-element.37.refs_1_.refs_4_, ...), custom_call_target="tpu_custom_call" | custom-call | flops 1000000 | bytes 1000000 | tf_op jit(solution)/shard_map/pallas_call | solution.py:436
  13.3 3.5 %collective-permute-start.4 = (bf16[144,1024]{1,0:T(8,128)(2,1)S(1)}, bf16[144,1024]{1,0:T(8,128)(2,1)S(1)}, u32[]{:S(2)}, u32[]{:S(2)}) collective-permute-start(bf16[144,1024]{1,0:T(8,128)(2,1)S(1)} %get-tuple-element.39.refs_2_), channel_id=1, source_target_pairs={{0,4},{1,5},{2,6},{3,7},{4,0},{5,1},{6,2},{7,3},{8,12},{9,13},{10,... | collective-permute-start | bytes 884744 | tf_op jit(solution)/shard_map/ppermute | solution.py:108
  16.8 1.0 collective-permute-start.2
  18.4 5.3 %shard_map.125 = (f32[2,144,3072]{2,1,0:T(8,128)S(1)}, f32[256,128]{1,0:T(8,128)S(1)}, bf16[1024,3072]{1,0:T(8,128)(2,1)S(1)}, bf16[1024,3072]{1,0:T(8,128)(2,1)S(1)}) custom-call(s32[6]{0:T(128)S(1)} %stack.40.which_ref.refs_0_.refs_2_, bf16[4096,3072]{1,0:T(8,128)(2,1)} %refs_0_.11, bf16[4096,3072]{1,0:T(8,128)(2,1)} %refs_1_.9, ...), custom_call_target="tpu_custom_call" | custom-call | flops 1811939328 | bytes 12582912 | tf_op jit(solution)/shard_map/pallas_call | solution.py:169
  23.7 1.0 collective-permute-done.4.refs_2_
  24.6 5.3 %shard_map.126 = (f32[2,144,3072]{2,1,0:T(8,128)S(1)}, f32[256,128]{1,0:T(8,128)S(1)}, bf16[1024,3072]{1,0:T(8,128)(2,1)S(1)}, bf16[1024,3072]{1,0:T(8,128)(2,1)S(1)}) custom-call(s32[6]{0:T(128)S(1)} %stack.40.which_ref.refs_0_.refs_2_, bf16[4096,3072]{1,0:T(8,128)(2,1)} %refs_0_.11, bf16[4096,3072]{1,0:T(8,128)(2,1)} %refs_1_.9, ...), custom_call_target="tpu_custom_call", output_to_operand_aliasing={{0}: (6, {})} | custom-call | flops 1811939328 | bytes 12582912 | tf_op jit(solution)/shard_map/pallas_call | solution.py:169
  30.0 3.1 %collective-permute-done.3.refs_2_ = bf16[144,1024]{1,0:T(8,128)(2,1)S(1)} collective-permute-done((bf16[144,1024]{1,0:T(8,128)(2,1)S(1)}, bf16[144,1024]{1,0:T(8,128)(2,1)S(1)}, u32[]{:S(2)}, u32[]{:S(2)}) %collective-permute-start.3) | collective-permute-done | bytes 294944 | tf_op jit(solution)/shard_map/ppermute | solution.py:108
  33.1 5.3 %shard_map.127 = (f32[2,144,3072]{2,1,0:T(8,128)S(1)}, f32[256,128]{1,0:T(8,128)S(1)}, bf16[1024,3072]{1,0:T(8,128)(2,1)S(1)}, bf16[1024,3072]{1,0:T(8,128)(2,1)S(1)}) custom-call(s32[6]{0:T(128)S(1)} %stack.40.which_ref.refs_0_.refs_2_, bf16[4096,3072]{1,0:T(8,128)(2,1)} %refs_0_.11, bf16[4096,3072]{1,0:T(8,128)(2,1)} %refs_1_.9, ...), custom_call_target="tpu_custom_call", output_to_operand_aliasing={{0}: (6, {})} | custom-call | flops 1811939328 | bytes 12582912 | tf_op jit(solution)/shard_map/pallas_call | solution.py:169
  38.4 3.4 %shard_map.128 = (f32[2,144,1536]{2,1,0:T(8,128)S(1)}, bf16[2,144,1536]{2,1,0:T(8,128)(2,1)S(1)}, f32[256,128]{1,0:T(8,128)S(1)}, bf16[3072,1024]{1,0:T(8,128)(2,1)S(1)}) custom-call(s32[6]{0:T(128)S(1)} %stack.40.which_ref.refs_0_.refs_2_, bf16[3072,4096]{1,0:T(8,128)(2,1)} %refs_0_.15, bf16[144,1024]{1,0:T(8,128)(2,1)S(1)} %collective-permute-done.2.refs_1_, ...), custom_call_target="tpu_custom_call" | custom-call | flops 905969664 | bytes 6291456 | tf_op jit(solution)/shard_map/pallas_call | solution.py:169
  41.9 3.4 %shard_map.130 = (f32[2,144,1536]{2,1,0:T(8,128)S(1)}, bf16[2,144,1536]{2,1,0:T(8,128)(2,1)S(1)}, bf16[3072,1024]{1,0:T(8,128)(2,1)S(1)}) custom-call(s32[6]{0:T(128)S(1)} %stack.40.which_ref.refs_0_.refs_2_, bf16[3072,4096]{1,0:T(8,128)(2,1)} %refs_0_.15, bf16[144,1024]{1,0:T(8,128)(2,1)S(1)} %collective-permute-done.2.refs_1_, ...), custom_call_target="tpu_custom_call" | custom-call | flops 905969664 | bytes 6291456 | tf_op jit(solution)/shard_map/pallas_call | solution.py:169
  45.9 1.7 %shard_map.129 = (bf16[256,1536]{1,0:T(8,128)(2,1)S(1)}, f32[256,128]{1,0:T(8,128)S(1)}) custom-call(s32[6]{0:T(128)S(1)} %stack.40.which_ref.refs_0_.refs_2_, f32[2,144,1536]{2,1,0:T(8,128)S(1)} %get-tuple-element.53.refs_0_, bf16[2,144,1536]{2,1,0:T(8,128)(2,1)S(1)} %collective-permute-done.5.refs_1_, ...), custom_call_target="tpu_custom_call" | custom-call | flops 226492416 | tf_op jit(solution)/shard_map/pallas_call | solution.py:169
  48.0 1.6 %shard_map.131.refs_2_.refs_1_ = bf16[256,1536]{1,0:T(8,128)(2,1)S(1)} custom-call(s32[6]{0:T(128)S(1)} %stack.40.which_ref.refs_0_.refs_2_, f32[2,144,1536]{2,1,0:T(8,128)S(1)} %get-tuple-element.57.refs_0_, bf16[2,144,1536]{2,1,0:T(8,128)(2,1)S(1)} %collective-permute-done.6.refs_1_, bf16[256,144]{1,0:T(8,128)(2,1)S(1)} %get-tuple-element.40.refs_5_.refs_6_.refs_2_, ...), custom_call_target="tpu_custom_call" | custom-call | flops 226492416 | tf_op jit(solution)/shard_map/pallas_call | solution.py:169
  49.6 5.3 %shard_map.132 = (bf16[128,2048]{1,0:T(8,128)(2,1)S(1)}, bf16[128,1024]{1,0:T(8,128)(2,1)S(1)}, bf16[3072,1024]{1,0:T(8,128)(2,1)S(1)}) custom-call(s32[6]{0:T(128)S(1)} %stack.40.which_ref.refs_0_.refs_2_, bf16[3072,4096]{1,0:T(8,128)(2,1)} %refs_0_.15, bf16[256,1536]{1,0:T(8,128)(2,1)S(1)} %get-tuple-element.56.refs_1_.refs_0_, ...), custom_call_target="tpu_custom_call" | custom-call | flops 150994944 | bytes 6291456 | tf_op jit(solution)/shard_map/pallas_call | solution.py:169
  55.5 1.5 %shard_map.134 = bf16[128,2048]{1,0:T(8,128)(2,1)S(1)} custom-call(s32[6]{0:T(128)S(1)} %stack.40.which_ref.refs_0_.refs_2_, bf16[256,1536]{1,0:T(8,128)(2,1)S(1)} %get-tuple-element.56.refs_1_.refs_0_, bf16[256,1536]{1,0:T(8,128)(2,1)S(1)} %shard_map.131.refs_2_.refs_1_, bf16[3072,1024]{1,0:T(8,128)(2,1)S(1)} %get-tuple-element.62.refs_3_.refs_2_, ...), custom_call_target="tpu_custom_call" | custom-call | flops 50331648 | tf_op jit(solution)/shard_map/pallas_call | solution.py:169
  57.0 1.7 %collective-permute-start.9 = (bf16[128,2048]{1,0:T(8,128)(2,1)S(1)}, bf16[128,2048]{1,0:T(8,128)(2,1)S(1)}, u32[]{:S(2)}, u32[]{:S(2)}) collective-permute-start(bf16[128,2048]{1,0:T(8,128)(2,1)S(1)} %shard_map.134), channel_id=1, source_target_pairs={{0,4},{1,5},{2,6},{3,7},{4,0},{5,1},{6,2},{7,3},{8,12},{9,13},{10,... | collective-permute-start | bytes 1572872 | tf_op jit(solution)/shard_map/ppermute | solution.py:108
  58.7 7.3 %shard_map.133 = (bf16[128,1024]{1,0:T(8,128)(2,1)S(1)}, bf16[128,1024]{1,0:T(8,128)(2,1)S(1)}, bf16[128,1024]{1,0:T(8,128)(2,1)S(1)}, bf16[128,1024]{1,0:T(8,128)(2,1)S(1)}, bf16[3072,1024]{1,0:T(8,128)(2,1)}) custom-call(s32[6]{0:T(128)S(1)} %stack.40.which_ref.refs_0_.refs_2_, bf16[3072,4096]{1,0:T(8,128)(2,1)} %refs_0_.15, ...), custom_call_target="tpu_custom_call" | custom-call | flops 201326592 | bytes 6291456 | tf_op jit(solution)/shard_map/pallas_call | solution.py:169
  66.0 3.1 %collective-permute-done.7 = bf16[128,2048]{1,0:T(8,128)(2,1)S(1)} collective-permute-done((bf16[128,2048]{1,0:T(8,128)(2,1)S(1)}, bf16[128,2048]{1,0:T(8,128)(2,1)S(1)}, u32[]{:S(2)}, u32[]{:S(2)}) %collective-permute-start.7) | collective-permute-done | bytes 524320 | tf_op jit(solution)/shard_map/ppermute | solution.py:108
  69.2 1.8 %collective-permute-start.8 = (bf16[128,1024]{1,0:T(8,128)(2,1)S(1)}, bf16[128,1024]{1,0:T(8,128)(2,1)S(1)}, u32[]{:S(2)}, u32[]{:S(2)}) collective-permute-start(bf16[128,1024]{1,0:T(8,128)(2,1)S(1)} %add_convert_fusion.4), channel_id=1, source_target_pairs={{0,4},{1,5},{2,6},{3,7},{4,0},{5,1},{6,2},{7,3},{8,12},{9,13},{10,... | collective-permute-start | bytes 786440 | tf_op jit(solution)/shard_map/ppermute | solution.py:108
  71.1 2.0 %collective-permute-start.10 = (bf16[128,1024]{1,0:T(8,128)(2,1)S(1)}, bf16[128,1024]{1,0:T(8,128)(2,1)S(1)}, u32[]{:S(2)}, u32[]{:S(2)}) collective-permute-start(bf16[128,1024]{1,0:T(8,128)(2,1)S(1)} %add_convert_fusion.2), channel_id=1, source_target_pairs={{0,2},{1,3},{2,0},{3,1},{4,6},{5,7},{6,4},{7,5},{8,10},{9,11},{10,... | collective-permute-start | bytes 786440 | tf_op jit(solution)/shard_map/ppermute | solution.py:108
  73.0 4.0 %collective-permute-done.8 = bf16[128,1024]{1,0:T(8,128)(2,1)S(1)} collective-permute-done((bf16[128,1024]{1,0:T(8,128)(2,1)S(1)}, bf16[128,1024]{1,0:T(8,128)(2,1)S(1)}, u32[]{:S(2)}, u32[]{:S(2)}) %collective-permute-start.8) | collective-permute-done | bytes 262176 | tf_op jit(solution)/shard_map/ppermute | solution.py:108
  77.2 1.3 %collective-permute-start.12 = (bf16[128,1024]{1,0:T(8,128)(2,1)S(1)}, bf16[128,1024]{1,0:T(8,128)(2,1)S(1)}, u32[]{:S(2)}, u32[]{:S(2)}) collective-permute-start(bf16[128,1024]{1,0:T(8,128)(2,1)S(1)} %add_convert_fusion.3), channel_id=1, source_target_pairs={{1,8},{3,10},{5,12},{7,14},{8,0},{10,2},{12,4},{14,6},{17,24},{19,... | collective-permute-start | bytes 786440 | tf_op jit(solution)/shard_map/ppermute | solution.py:108
  79.5 4.0 %collective-permute-start.11 = (bf16[128,1024]{1,0:T(8,128)(2,1)S(1)}, bf16[128,1024]{1,0:T(8,128)(2,1)S(1)}, u32[]{:S(2)}, u32[]{:S(2)}) collective-permute-start(bf16[128,1024]{1,0:T(8,128)(2,1)S(1)} %broadcast_select_fusion), channel_id=1, source_target_pairs={{0,1},{2,3},{4,5},{6,7},{9,8},{11,10},{13,12},{15,14},{16,17},{18,... | collective-permute-start | bytes 786440 | tf_op jit(solution)/shard_map/ppermute | solution.py:108
  83.5 8.5 %collective-permute-done.12 = bf16[128,1024]{1,0:T(8,128)(2,1)S(1)} collective-permute-done((bf16[128,1024]{1,0:T(8,128)(2,1)S(1)}, bf16[128,1024]{1,0:T(8,128)(2,1)S(1)}, u32[]{:S(2)}, u32[]{:S(2)}) %collective-permute-start.12) | collective-permute-done | bytes 262176 | tf_op jit(solution)/shard_map/ppermute | solution.py:108
  91.9 1.0 fusion
  92.9 1.1 %collective-permute-start.14 = (f32[2,128]{1,0:T(2,128)S(1)}, f32[2,128]{1,0:T(2,128)S(1)}, u32[]{:S(2)}, u32[]{:S(2)}) collective-permute-start(f32[2,128]{1,0:T(2,128)S(1)} %pad_maximum_fusion), channel_id=1, source_target_pairs={{0,2},{1,3},{2,0},{3,1},{4,6},{5,7},{6,4},{7,5},{8,10},{9,11},{10,... | collective-permute-start | bytes 3080 | tf_op jit(solution)/shard_map/ppermute | solution.py:108
  94.0 2.5 %collective-permute-done.14 = f32[2,128]{1,0:T(2,128)S(1)} collective-permute-done((f32[2,128]{1,0:T(2,128)S(1)}, f32[2,128]{1,0:T(2,128)S(1)}, u32[]{:S(2)}, u32[]{:S(2)}) %collective-permute-start.14) | collective-permute-done | bytes 1056 | tf_op jit(solution)/shard_map/ppermute | solution.py:108
  96.6 3.6 %collective-permute-done.15 = f32[2,128]{1,0:T(2,128)S(1)} collective-permute-done((f32[2,128]{1,0:T(2,128)S(1)}, f32[2,128]{1,0:T(2,128)S(1)}, u32[]{:S(2)}, u32[]{:S(2)}) %collective-permute-start.15) | collective-permute-done | bytes 1056 | tf_op jit(solution)/shard_map/ppermute | solution.py:108
  100.2 2.4 %collective-permute-start.16 = (f32[2,128]{1,0:T(2,128)S(1)}, f32[2,128]{1,0:T(2,128)S(1)}, u32[]{:S(2)}, u32[]{:S(2)}) collective-permute-start(f32[2,128]{1,0:T(2,128)S(1)} %fusion.3), channel_id=1, source_target_pairs={{0,8},{1,9},{2,10},{3,11},{4,12},{5,13},{6,14},{7,15},{8,0},{9,1},... | collective-permute-start | bytes 3080 | tf_op jit(solution)/shard_map/ppermute | solution.py:108
  102.6 2.1 %collective-permute-done.16 = f32[2,128]{1,0:T(2,128)S(1)} collective-permute-done((f32[2,128]{1,0:T(2,128)S(1)}, f32[2,128]{1,0:T(2,128)S(1)}, u32[]{:S(2)}, u32[]{:S(2)}) %collective-permute-start.16) | collective-permute-done | bytes 1056 | tf_op jit(solution)/shard_map/ppermute | solution.py:108
  (40 shorter events, 4.9 us)
Async XLA Ops:
  1.7 10.1 %copy-start = (bf16[128,1024]{1,0:T(8,128)(2,1)S(1)}, bf16[128,1024]{1,0:T(8,128)(2,1)}, u32[]{:S(2)}) copy-start(bf16[128,1024]{1,0:T(8,128)(2,1)} %refs_6_.1) | copy-start | bytes 786436
  1.8 10.1 %copy-start.1 = (bf16[2,1024]{1,0:T(2,128)(2,1)S(1)}, bf16[2,1024]{1,0:T(2,128)(2,1)}, u32[]{:S(2)}) copy-start(bf16[2,1024]{1,0:T(2,128)(2,1)} %refs_7_.1) | copy-start | bytes 12292
  1.8 10.1 %copy-start.2 = (f32[1024]{0:T(1024)S(1)}, f32[1024]{0:T(1024)}, u32[]{:S(2)}) copy-start(f32[1024]{0:T(1024)} %refs_10_.1) | copy-start | bytes 12292
  1.8 10.1 %copy-start.3 = (f32[1024]{0:T(1024)S(1)}, f32[1024]{0:T(1024)}, u32[]{:S(2)}) copy-start(f32[1024]{0:T(1024)} %refs_11_.1) | copy-start | bytes 12292
  1.8 10.1 %copy-start.4 = (f32[128]{0:T(128)S(1)}, f32[128]{0:T(128)}, u32[]{:S(2)}) copy-start(f32[128]{0:T(128)} %refs_8_.1) | copy-start | bytes 1540
  1.8 10.1 %copy-start.5 = (f32[128]{0:T(128)S(1)}, f32[128]{0:T(128)}, u32[]{:S(2)}) copy-start(f32[128]{0:T(128)} %refs_9_.1) | copy-start | bytes 1540
  1.8 10.0 %collective-permute-start = (bf16[80,1024]{1,0:T(8,128)(2,1)S(1)}, bf16[80,1024]{1,0:T(8,128)(2,1)S(1)}, u32[]{:S(2)}, u32[]{:S(2)}) collective-permute-start(bf16[80,1024]{1,0:T(8,128)(2,1)S(1)} %shard_map.123.refs_3_), channel_id=1, source_target_pairs={{0,8},{2,10},{4,12},{6,14},{9,1},{11,3},{13,5},{15,7},{1,0},{3,2},... | collective-permute-start | bytes 491528 | tf_op jit(solution)/shard_map/ppermute | solution.py:108
  5.9 6.0 %collective-permute-start.1 = (bf16[80,1024]{1,0:T(8,128)(2,1)S(1)}, bf16[80,1024]{1,0:T(8,128)(2,1)S(1)}, u32[]{:S(2)}, u32[]{:S(2)}) collective-permute-start(bf16[80,1024]{1,0:T(8,128)(2,1)S(1)} %shard_map.123.refs_3_), channel_id=1, source_target_pairs={{1,8},{3,10},{5,12},{7,14},{8,1},{10,3},{12,5},{14,7},{17,24},{19,... | collective-permute-start | bytes 491528 | tf_op jit(solution)/shard_map/ppermute | solution.py:108
  13.3 11.3 %collective-permute-start.4 = (bf16[144,1024]{1,0:T(8,128)(2,1)S(1)}, bf16[144,1024]{1,0:T(8,128)(2,1)S(1)}, u32[]{:S(2)}, u32[]{:S(2)}) collective-permute-start(bf16[144,1024]{1,0:T(8,128)(2,1)S(1)} %get-tuple-element.39.refs_2_), channel_id=1, source_target_pairs={{0,4},{1,5},{2,6},{3,7},{4,0},{5,1},{6,2},{7,3},{8,12},{9,13},{10,... | collective-permute-start | bytes 884744 | tf_op jit(solution)/shard_map/ppermute | solution.py:108
  16.8 21.5 %collective-permute-start.2 = (bf16[144,1024]{1,0:T(8,128)(2,1)S(1)}, bf16[144,1024]{1,0:T(8,128)(2,1)S(1)}, u32[]{:S(2)}, u32[]{:S(2)}) collective-permute-start(bf16[144,1024]{1,0:T(8,128)(2,1)S(1)} %get-tuple-element.39.refs_2_), channel_id=1, source_target_pairs={{0,6},{1,7},{2,4},{3,5},{4,2},{5,3},{6,0},{7,1},{8,14},{9,15},{10,... | collective-permute-start | bytes 884744 | tf_op jit(solution)/shard_map/ppermute | solution.py:108
  17.9 15.3 %collective-permute-start.3 = (bf16[144,1024]{1,0:T(8,128)(2,1)S(1)}, bf16[144,1024]{1,0:T(8,128)(2,1)S(1)}, u32[]{:S(2)}, u32[]{:S(2)}) collective-permute-start(bf16[144,1024]{1,0:T(8,128)(2,1)S(1)} %get-tuple-element.39.refs_2_), channel_id=1, source_target_pairs={{0,2},{1,3},{2,0},{3,1},{4,6},{5,7},{6,4},{7,5},{8,10},{9,11},{10,... | collective-permute-start | bytes 884744 | tf_op jit(solution)/shard_map/ppermute | solution.py:108
  41.8 4.1 %collective-permute-start.5 = (bf16[2,144,1536]{2,1,0:T(8,128)(2,1)S(1)}, bf16[2,144,1536]{2,1,0:T(8,128)(2,1)S(1)}, u32[]{:S(2)}, u32[]{:S(2)}) collective-permute-start(bf16[2,144,1536]{2,1,0:T(8,128)(2,1)S(1)} %get-tuple-element.54), channel_id=1, source_target_pairs={{0,1},{1,0},{2,3},{3,2},{4,5},{5,4},{6,7},{7,6},{8,9},{9,8},{10,11... | collective-permute-start | bytes 2654216 | tf_op jit(solution)/shard_map/ppermute | solution.py:108
  45.3 2.6 %collective-permute-start.6 = (bf16[2,144,1536]{2,1,0:T(8,128)(2,1)S(1)}, bf16[2,144,1536]{2,1,0:T(8,128)(2,1)S(1)}, u32[]{:S(2)}, u32[]{:S(2)}) collective-permute-start(bf16[2,144,1536]{2,1,0:T(8,128)(2,1)S(1)} %get-tuple-element.58), channel_id=1, source_target_pairs={{0,1},{1,0},{2,3},{3,2},{4,5},{5,4},{6,7},{7,6},{8,9},{9,8},{10,11... | collective-permute-start | bytes 2654216 | tf_op jit(solution)/shard_map/ppermute | solution.py:108
  54.8 14.3 %collective-permute-start.7 = (bf16[128,2048]{1,0:T(8,128)(2,1)S(1)}, bf16[128,2048]{1,0:T(8,128)(2,1)S(1)}, u32[]{:S(2)}, u32[]{:S(2)}) collective-permute-start(bf16[128,2048]{1,0:T(8,128)(2,1)S(1)} %get-tuple-element.64), channel_id=1, source_target_pairs={{0,2},{1,3},{2,0},{3,1},{4,6},{5,7},{6,4},{7,5},{8,10},{9,11},{10,... | collective-permute-start | bytes 1572872 | tf_op jit(solution)/shard_map/ppermute | solution.py:108
  57.0 14.0 %collective-permute-start.9 = (bf16[128,2048]{1,0:T(8,128)(2,1)S(1)}, bf16[128,2048]{1,0:T(8,128)(2,1)S(1)}, u32[]{:S(2)}, u32[]{:S(2)}) collective-permute-start(bf16[128,2048]{1,0:T(8,128)(2,1)S(1)} %shard_map.134), channel_id=1, source_target_pairs={{0,4},{1,5},{2,6},{3,7},{4,0},{5,1},{6,2},{7,3},{8,12},{9,13},{10,... | collective-permute-start | bytes 1572872 | tf_op jit(solution)/shard_map/ppermute | solution.py:108
  69.2 7.8 %collective-permute-start.8 = (bf16[128,1024]{1,0:T(8,128)(2,1)S(1)}, bf16[128,1024]{1,0:T(8,128)(2,1)S(1)}, u32[]{:S(2)}, u32[]{:S(2)}) collective-permute-start(bf16[128,1024]{1,0:T(8,128)(2,1)S(1)} %add_convert_fusion.4), channel_id=1, source_target_pairs={{0,4},{1,5},{2,6},{3,7},{4,0},{5,1},{6,2},{7,3},{8,12},{9,13},{10,... | collective-permute-start | bytes 786440 | tf_op jit(solution)/shard_map/ppermute | solution.py:108
  71.1 7.6 %collective-permute-start.10 = (bf16[128,1024]{1,0:T(8,128)(2,1)S(1)}, bf16[128,1024]{1,0:T(8,128)(2,1)S(1)}, u32[]{:S(2)}, u32[]{:S(2)}) collective-permute-start(bf16[128,1024]{1,0:T(8,128)(2,1)S(1)} %add_convert_fusion.2), channel_id=1, source_target_pairs={{0,2},{1,3},{2,0},{3,1},{4,6},{5,7},{6,4},{7,5},{8,10},{9,11},{10,... | collective-permute-start | bytes 786440 | tf_op jit(solution)/shard_map/ppermute | solution.py:108
  77.2 14.8 %collective-permute-start.12 = (bf16[128,1024]{1,0:T(8,128)(2,1)S(1)}, bf16[128,1024]{1,0:T(8,128)(2,1)S(1)}, u32[]{:S(2)}, u32[]{:S(2)}) collective-permute-start(bf16[128,1024]{1,0:T(8,128)(2,1)S(1)} %add_convert_fusion.3), channel_id=1, source_target_pairs={{1,8},{3,10},{5,12},{7,14},{8,0},{10,2},{12,4},{14,6},{17,24},{19,... | collective-permute-start | bytes 786440 | tf_op jit(solution)/shard_map/ppermute | solution.py:108
  78.7 13.2 %collective-permute-start.13 = (bf16[128,1024]{1,0:T(8,128)(2,1)S(1)}, bf16[128,1024]{1,0:T(8,128)(2,1)S(1)}, u32[]{:S(2)}, u32[]{:S(2)}) collective-permute-start(bf16[128,1024]{1,0:T(8,128)(2,1)S(1)} %add_convert_fusion.1), channel_id=1, source_target_pairs={{1,9},{3,11},{5,13},{7,15},{8,1},{10,3},{12,5},{14,7},{17,25},{19,... | collective-permute-start | bytes 786440 | tf_op jit(solution)/shard_map/ppermute | solution.py:108
  79.5 12.5 %collective-permute-start.11 = (bf16[128,1024]{1,0:T(8,128)(2,1)S(1)}, bf16[128,1024]{1,0:T(8,128)(2,1)S(1)}, u32[]{:S(2)}, u32[]{:S(2)}) collective-permute-start(bf16[128,1024]{1,0:T(8,128)(2,1)S(1)} %broadcast_select_fusion), channel_id=1, source_target_pairs={{0,1},{2,3},{4,5},{6,7},{9,8},{11,10},{13,12},{15,14},{16,17},{18,... | collective-permute-start | bytes 786440 | tf_op jit(solution)/shard_map/ppermute | solution.py:108
  92.9 3.6 %collective-permute-start.14 = (f32[2,128]{1,0:T(2,128)S(1)}, f32[2,128]{1,0:T(2,128)S(1)}, u32[]{:S(2)}, u32[]{:S(2)}) collective-permute-start(f32[2,128]{1,0:T(2,128)S(1)} %pad_maximum_fusion), channel_id=1, source_target_pairs={{0,2},{1,3},{2,0},{3,1},{4,6},{5,7},{6,4},{7,5},{8,10},{9,11},{10,... | collective-permute-start | bytes 3080 | tf_op jit(solution)/shard_map/ppermute | solution.py:108
  96.6 3.6 %collective-permute-start.15 = (f32[2,128]{1,0:T(2,128)S(1)}, f32[2,128]{1,0:T(2,128)S(1)}, u32[]{:S(2)}, u32[]{:S(2)}) collective-permute-start(f32[2,128]{1,0:T(2,128)S(1)} %fusion.2), channel_id=1, source_target_pairs={{0,4},{1,5},{2,6},{3,7},{4,0},{5,1},{6,2},{7,3},{8,12},{9,13},{10,... | collective-permute-start | bytes 3080 | tf_op jit(solution)/shard_map/ppermute | solution.py:108
  100.2 4.5 %collective-permute-start.16 = (f32[2,128]{1,0:T(2,128)S(1)}, f32[2,128]{1,0:T(2,128)S(1)}, u32[]{:S(2)}, u32[]{:S(2)}) collective-permute-start(f32[2,128]{1,0:T(2,128)S(1)} %fusion.3), channel_id=1, source_target_pairs={{0,8},{1,9},{2,10},{3,11},{4,12},{5,13},{6,14},{7,15},{8,0},{9,1},... | collective-permute-start | bytes 3080 | tf_op jit(solution)/shard_map/ppermute | solution.py:108

commit v9 on v8

--- a/solution.py
+++ b/solution.py
@@ -113,7 +113,16 @@
 SPLIT = 8
 
 
-def stage(which, loads, ins, outs, compute, scratch=(), limit=3, flops=0, alias=None, manual=False):
+def near_place(k):
+    place = lax.rem(lax.axis_index("tp"), 4)
+    if k == 1:
+        return place + 1 - 2 * lax.rem(place, 2)
+    if k == 2:
+        return lax.rem(place + 2, 4)
+    return place if k == 0 else 3 - place
+
+
+def stage(loads, ins, outs, compute, scratch=(), limit=3, flops=0, alias=None, manual=False):
     vmem = pl.BlockSpec(memory_space=pltpu.VMEM)
     count = len(ins)
     shapes, sources, flat = list(outs), [], []
@@ -125,7 +134,7 @@
         flat.append((kind, parts))
     n = len(sources)
 
-    def body(which_ref, *refs):
+    def body(*refs):
         inputs = refs[n : n + count]
         results = refs[n + count : n + count + len(outs)]
         targets = refs[n + count + len(outs) : n + count + len(shapes)]
@@ -134,7 +143,7 @@
         for (kind, parts), target in zip(flat, targets):
             filled = 0
             for _, place, unit, offset, size in parts:
-                block = which_ref[place] * unit + offset
+                block = near_place(place) * unit + offset
                 length = size if kind == "rows" else target.shape[0]
                 piece = length // SPLIT
                 for cut in range(SPLIT):
@@ -169,15 +178,13 @@
     return pl.pallas_call(
         body,
         out_shape=shapes,
-        in_specs=[pl.BlockSpec(memory_space=pltpu.SMEM)]
-        + [pl.BlockSpec(memory_space=pl.ANY)] * n
-        + [vmem] * count,
+        in_specs=[pl.BlockSpec(memory_space=pl.ANY)] * n + [vmem] * count,
         out_specs=[vmem] * len(shapes),
         scratch_shapes=([pltpu.SemaphoreType.DMA((n * SPLIT,))] if n else []) + list(scratch),
-        input_output_aliases={} if alias is None else {1 + n + alias: 0},
+        input_output_aliases={} if alias is None else {n + alias: 0},
         compiler_params=pltpu.CompilerParams(vmem_limit_bytes=limit * MIB),
         cost_estimate=pl.CostEstimate(flops=flops, bytes_accessed=loaded, transcendentals=0),
-    )(which, *sources, *ins)
+    )(*sources, *ins)
 
 
 def to_row(column):
@@ -194,7 +201,7 @@
     return jnp.sum(jnp.where(rows == cols, row, 0.0), axis=1, keepdims=True)
 
 
-def basis_stage(which, loads, blocks, held, before, columns, features, squares, narrow):
+def basis_stage(loads, blocks, held, before, columns, features, squares, narrow):
     m, k = blocks[0].shape
     count = len(blocks)
     start, stop = columns
@@ -260,7 +267,6 @@
                 results[1][0, m - SMALL :, :rows] = last.astype(jnp.bfloat16)
 
     return stage(
-        which,
         loads,
         ins,
         outs,
@@ -271,7 +277,7 @@
     )
 
 
-def hidden_stage(which, loads, own, other, features, square, scale, width):
+def hidden_stage(loads, own, other, features, square, scale, width):
     _, m, units = own.shape
     rows = features.shape[0]
     tile = 512
@@ -309,7 +315,6 @@
             results[0][:, at] = (gate / (1.0 + jnp.exp(-gate)) * up).astype(jnp.bfloat16)
 
     return stage(
-        which,
         loads,
         [own, other, features, square if first else scale],
         outs,
@@ -318,7 +323,7 @@
     )
 
 
-def down_stage(which, loads, hidden, weights, tile, places, widths, copies=()):
+def down_stage(loads, hidden, weights, tile, places, widths, copies=()):
     rows = hidden[0].shape[0]
     depth = weights[0].shape[0]
     half = rows // 2
@@ -354,7 +359,6 @@
             results[out][:, : source.shape[1]] = source[...]
 
     return stage(
-        which,
         loads,
         [*hidden, *weights, *[copy[0] for copy in copies]],
         [jax.ShapeDtypeStruct((half, width), jnp.bfloat16) for width in widths],
@@ -365,10 +369,10 @@
     )
 
 
-def piece_body(flags, weight, states, gain, seeds, piece, rows):
+def piece_body(weight, states, gain, seeds, piece, rows):
     half = weight.shape[0] // 2
     count = states.shape[0]
-    piece[:half, :] = weight[pl.ds(pl.multiple_of(flags[4] * half, 16), half), :]
+    piece[:half, :] = weight[pl.ds(pl.multiple_of(lax.axis_index("dp") * half, 16), half), :]
     rows[...] = jnp.zeros_like(rows)
     rows[:count, :] = states[...].astype(jnp.float32)
     rows[count : count + 1, :] = gain[...].reshape(1, -1)
@@ -380,12 +384,14 @@
     piece[half:, :] = rows[...].astype(jnp.bfloat16)
 
 
-def block_body(count, cands, flags, piece, first, second, weight, states, mean, spread, gain, value,
+def block_body(count, cands, piece, first, second, weight, states, mean, spread, gain, value,
                block, features, inputs, head, rows):
     f32, bf16 = jnp.float32, jnp.bfloat16
     half = weight.shape[0] // 2
     act = weight.shape[0]
-    lower, home = flags[4] == 0, flags[5] == 1
+    core = lax.axis_index("dp")
+    lower = core == 0
+    home = lax.div(lax.axis_index("tp"), 4) == core
     same = jnp.where(home, piece[...], first[...])
     other = jnp.where(home, first[...], second[...])
     low = jnp.where(lower, same, other)
@@ -434,12 +440,11 @@
     whole = lambda array: pl.BlockSpec(array.shape, lambda i: (0,) * len(array.shape))
     count = len(after)
     return pl.pallas_call(
-        lambda *refs: body(refs[count], *refs[count + 1 :]),
+        lambda *refs: body(*refs[count:]),
         out_shape=outs,
         grid=(1,),
         in_specs=[pl.BlockSpec(memory_space=pl.ANY)] * count
-        + [pl.BlockSpec(memory_space=pltpu.SMEM)]
-        + [whole(array) for array in operands[1:]],
+        + [whole(array) for array in operands],
         out_specs=[whole(array) for array in outs],
         scratch_shapes=scratch,
         compiler_params=pltpu.CompilerParams(vmem_limit_bytes=6 * MIB),
@@ -469,19 +474,15 @@
     full_width = gate_weight.shape[0] * 2
     tp, dp = lax.axis_index("tp"), lax.axis_index("dp")
     home = tp // 4 == dp
-    place = tp % 4
     every = [(t, d) for t in range(TP) for d in range(2)]
     swap_core = [((t, d), (t, 1 - d)) for t, d in every]
 
-    flags = jnp.stack([place, place ^ 1, place ^ 2, place ^ 3, dp, home.astype(jnp.int32)])
-    flags = flags.astype(jnp.int32)
     out = jax.ShapeDtypeStruct
     (piece,) = whole_call(
         piece_body,
         [out((half + SMALL, cols), bf16)],
         [pltpu.VMEM((SMALL, cols), f32)],
         [],
-        flags,
         *[
             pltpu.with_memory_space_constraint(array, pltpu.HBM)
             for array in (action_weight, state_hidden, norm_gain, action_seeds)
@@ -502,7 +503,7 @@
     pair = lambda k: [("rows", [(w, k, cols, 0, cols)]) for w in (gate_weight, up_weight)]
     column = lambda k: ("cols", [(down_weight, k, cols, 0, cols)])
     tile = cols // 2
-    held = stage(flags, pair(0), [], [], None)
+    held = stage(pair(0), [], [], None)
 
     block, features, inputs_local, head = whole_call(
         functools.partial(block_body, states, cands),
@@ -514,7 +515,6 @@
         ],
         [pltpu.VMEM((SMALL, cols), f32)],
         held,
-        flags,
         piece,
         first,
         second,
@@ -531,33 +531,32 @@
 
     span = (0, units)
     basis, square, *held = basis_stage(
-        flags, pair(2), [block], held, None, span, features, [], False
+        pair(2), [block], held, None, span, features, [], False
     )
     basis, square, *held = basis_stage(
-        flags, pair(1), [near[2]], held, basis, span, features, [square], False
+        pair(1), [near[2]], held, basis, span, features, [square], False
     )
     basis, square, *held = basis_stage(
-        flags, pair(3), [near[1]], held, basis, span, features, [square], False
+        pair(3), [near[1]], held, basis, span, features, [square], False
     )
     cut = units // 2
     own_a, narrow_a, square, down_diagonal = basis_stage(
-        flags, [column(3)], [near[3]], held, basis, (0, cut), features, [square], True
+        [column(3)], [near[3]], held, basis, (0, cut), features, [square], True
     )
     other_a = send(narrow_a, swap_core)
     own_b, narrow_b, down_x = basis_stage(
-        flags, [column(1)], [near[3]], held, basis, (cut, units), features, None, True
+        [column(1)], [near[3]], held, basis, (cut, units), features, None, True
     )
     other_b = send(narrow_b, swap_core)
-    hidden_a, scale = hidden_stage(
-        flags, [], own_a, other_a, features, square, None, full_width
-    )
-    (hidden_b,) = hidden_stage(flags, [], own_b, other_b, features, None, scale, full_width)
+    hidden_a, scale, down_z = hidden_stage(
+        [column(2)], own_a, other_a, features, square, None, full_width
+    )
+    (hidden_b,) = hidden_stage([], own_b, other_b, features, None, scale, full_width)
     hidden = [hidden_a, hidden_b]
 
     both, lower, upper = (0, 1), (0,), (1,)
-    x_pair, diagonal_upper, down_z = down_stage(
-        flags,
-        [column(2)],
+    x_pair, diagonal_upper = down_stage(
+        [],
         hidden,
         [down_diagonal, down_x],
         tile,
@@ -569,7 +568,6 @@
     )
     got_x = step(x_pair, 1)
     (z_pair,) = down_stage(
-        flags,
         [],
         hidden,
         [down_z],
@@ -580,7 +578,6 @@
     )
     got_z = step(z_pair, 2)
     z_lower, x_upper, own_lower, own_upper, _ = down_stage(
-        flags,
         [column(0)],
         hidden,
         [down_z, down_x],

time: 106 us -> 102 us (0.962)
  Pallas kernels: 47.7 us -> 41.3 us
  waiting for transfers between devices: 28.4 us -> 32.1 us
    pallas_call x11, Pallas kernels: 45.4 us -> 39.5 us  [stage(): pl.pallas_call(body, out_shape=shapes, in_specs=[pl.BlockSpec(memory_spac...]
    ppermute x17, waiting for transfers between devices: 28.4 us -> 32.1 us  [send(): lax.ppermute(array, ('tp', 'dp'), [(2 * st + sd, 2 * dt + dd) for (st, sd...]
  transfers between devices with their start and end apart: 17 -> 17, of which waited for: 10 -> 9; matrix products, arithmetic and copies ran while one was open for 0% -> 0% of each run, Pallas kernels for 33% -> 31%
where the time goes in v9:
time: 102 us
  Pallas kernels  41.3 us (40%)
  waiting for transfers between devices  32.1 us (31%)
  starting transfers between devices  25.5 us (25%)
  other arithmetic  1.44 us (1%)
    pallas_call x11, Pallas kernels, stage(): pl.pallas_call(body, out_shape=shapes, in_specs=[pl.BlockSpec(memory_spac...  39.5 us
    ppermute x17, waiting for transfers between devices, send(): lax.ppermute(array, ('tp', 'dp'), [(2 * st + sd, 2 * dt + dd) for (st, sd...  32.1 us
    ppermute x17, starting transfers between devices, send(): lax.ppermute(array, ('tp', 'dp'), [(2 * st + sd, 2 * dt + dd) for (st, sd...  25.5 us
  transfers between devices with their start and end apart: 17, of which 9 were waited for; matrix products, arithmetic and copies ran while one was open for 0% of the time, Pallas kernels for 31%

profile of v9, /device:TPU:0, one launch (start us, length us, event | category | flops | bytes accessed | tf_op | source)
XLA Modules:
  0.0 102.0 jit_solution(16750567616021511348)
XLA Ops:
  0.6 1.0 shard_map.123.refs_2_
  1.7 0.8 collective-permute-start.1
  2.5 5.3 %collective-permute-start = (bf16[80,1024]{1,0:T(8,128)(2,1)S(1)}, bf16[80,1024]{1,0:T(8,128)(2,1)S(1)}, u32[]{:S(2)}, u32[]{:S(2)}) collective-permute-start(bf16[80,1024]{1,0:T(8,128)(2,1)S(1)} %shard_map.123.refs_2_), channel_id=1, source_target_pairs={{0,8},{2,10},{4,12},{6,14},{9,1},{11,3},{13,5},{15,7},{1,0},{3,2},... | collective-permute-start | bytes 491528 | tf_op jit(solution)/shard_map/ppermute | solution.py:108
  7.9 4.7 %shard_map.122 = (bf16[1024,3072]{1,0:T(8,128)(2,1)S(1)}, bf16[1024,3072]{1,0:T(8,128)(2,1)S(1)}) custom-call(bf16[4096,3072]{1,0:T(8,128)(2,1)} %refs_0_.13, bf16[4096,3072]{1,0:T(8,128)(2,1)} %refs_1_.9), custom_call_target="tpu_custom_call" | custom-call | bytes 12582912 | tf_op jit(solution)/shard_map/pallas_call | solution.py:178
  13.5 4.2 %collective-permute-start.4 = (bf16[144,1024]{1,0:T(8,128)(2,1)S(1)}, bf16[144,1024]{1,0:T(8,128)(2,1)S(1)}, u32[]{:S(2)}, u32[]{:S(2)}) collective-permute-start(bf16[144,1024]{1,0:T(8,128)(2,1)S(1)} %get-tuple-element.39.refs_2_), channel_id=1, source_target_pairs={{0,4},{1,5},{2,6},{3,7},{4,0},{5,1},{6,2},{7,3},{8,12},{9,13},{10,... | collective-permute-start | bytes 884744 | tf_op jit(solution)/shard_map/ppermute | solution.py:108
  17.7 1.5 %collective-permute-start.3 = (bf16[144,1024]{1,0:T(8,128)(2,1)S(1)}, bf16[144,1024]{1,0:T(8,128)(2,1)S(1)}, u32[]{:S(2)}, u32[]{:S(2)}) collective-permute-start(bf16[144,1024]{1,0:T(8,128)(2,1)S(1)} %get-tuple-element.39.refs_2_), channel_id=1, source_target_pairs={{0,2},{1,3},{2,0},{3,1},{4,6},{5,7},{6,4},{7,5},{8,10},{9,11},{10,... | collective-permute-start | bytes 884744 | tf_op jit(solution)/shard_map/ppermute | solution.py:108
  19.2 4.7 %shard_map.125 = (f32[2,144,3072]{2,1,0:T(8,128)S(1)}, f32[256,128]{1,0:T(8,128)S(1)}, bf16[1024,3072]{1,0:T(8,128)(2,1)S(1)}, bf16[1024,3072]{1,0:T(8,128)(2,1)S(1)}) custom-call(bf16[4096,3072]{1,0:T(8,128)(2,1)} %refs_0_.13, bf16[4096,3072]{1,0:T(8,128)(2,1)} %refs_1_.9, bf16[144,1024]{1,0:T(8,128)(2,1)S(1)} %get-tuple-element.39.refs_2_, ...), custom_call_target="tpu_custom_call" | custom-call | flops 1811939328 | bytes 12582912 | tf_op jit(solution)/shard_map/pallas_call | solution.py:178
  24.0 1.2 %collective-permute-done.4.refs_2_ = bf16[144,1024]{1,0:T(8,128)(2,1)S(1)} collective-permute-done((bf16[144,1024]{1,0:T(8,128)(2,1)S(1)}, bf16[144,1024]{1,0:T(8,128)(2,1)S(1)}, u32[]{:S(2)}, u32[]{:S(2)}) %collective-permute-start.4) | collective-permute-done | bytes 294944 | tf_op jit(solution)/shard_map/ppermute | solution.py:108
  25.2 4.8 %shard_map.126 = (f32[2,144,3072]{2,1,0:T(8,128)S(1)}, f32[256,128]{1,0:T(8,128)S(1)}, bf16[1024,3072]{1,0:T(8,128)(2,1)S(1)}, bf16[1024,3072]{1,0:T(8,128)(2,1)S(1)}) custom-call(bf16[4096,3072]{1,0:T(8,128)(2,1)} %refs_0_.13, bf16[4096,3072]{1,0:T(8,128)(2,1)} %refs_1_.9, ...), custom_call_target="tpu_custom_call", output_to_operand_aliasing={{0}: (5, {})} | custom-call | flops 1811939328 | bytes 12582912 | tf_op jit(solution)/shard_map/pallas_call | solution.py:178
  30.0 1.7 %collective-permute-done.3.refs_2_ = bf16[144,1024]{1,0:T(8,128)(2,1)S(1)} collective-permute-done((bf16[144,1024]{1,0:T(8,128)(2,1)S(1)}, bf16[144,1024]{1,0:T(8,128)(2,1)S(1)}, u32[]{:S(2)}, u32[]{:S(2)}) %collective-permute-start.3) | collective-permute-done | bytes 294944 | tf_op jit(solution)/shard_map/ppermute | solution.py:108
  31.7 4.7 %shard_map.127 = (f32[2,144,3072]{2,1,0:T(8,128)S(1)}, f32[256,128]{1,0:T(8,128)S(1)}, bf16[1024,3072]{1,0:T(8,128)(2,1)S(1)}, bf16[1024,3072]{1,0:T(8,128)(2,1)S(1)}) custom-call(bf16[4096,3072]{1,0:T(8,128)(2,1)} %refs_0_.13, bf16[4096,3072]{1,0:T(8,128)(2,1)} %refs_1_.9, ...), custom_call_target="tpu_custom_call", output_to_operand_aliasing={{0}: (5, {})} | custom-call | flops 1811939328 | bytes 12582912 | tf_op jit(solution)/shard_map/pallas_call | solution.py:178
  36.4 2.9 %shard_map.128 = (f32[2,144,1536]{2,1,0:T(8,128)S(1)}, bf16[2,144,1536]{2,1,0:T(8,128)(2,1)S(1)}, f32[256,128]{1,0:T(8,128)S(1)}, bf16[3072,1024]{1,0:T(8,128)(2,1)S(1)}) custom-call(bf16[3072,4096]{1,0:T(8,128)(2,1)} %refs_0_.17, bf16[144,1024]{1,0:T(8,128)(2,1)S(1)} %collective-permute-done.2.refs_1_, bf16[1024,3072]{1,0:T(8,128)(2,1)S(1)} %get-tuple-element.49.refs_2_, ...), custom_call_target="tpu_custom_call" | custom-call | flops 905969664 | bytes 6291456 | tf_op jit(solution)/shard_map/pallas_call | solution.py:178
  39.4 2.9 %shard_map.130 = (f32[2,144,1536]{2,1,0:T(8,128)S(1)}, bf16[2,144,1536]{2,1,0:T(8,128)(2,1)S(1)}, bf16[3072,1024]{1,0:T(8,128)(2,1)S(1)}) custom-call(bf16[3072,4096]{1,0:T(8,128)(2,1)} %refs_0_.17, bf16[144,1024]{1,0:T(8,128)(2,1)S(1)} %collective-permute-done.2.refs_1_, bf16[1024,3072]{1,0:T(8,128)(2,1)S(1)} %get-tuple-element.49.refs_2_, ...), custom_call_target="tpu_custom_call" | custom-call | flops 905969664 | bytes 6291456 | tf_op jit(solution)/shard_map/pallas_call | solution.py:178
  42.9 2.9 %shard_map.129 = (bf16[256,1536]{1,0:T(8,128)(2,1)S(1)}, f32[256,128]{1,0:T(8,128)S(1)}, bf16[3072,1024]{1,0:T(8,128)(2,1)S(1)}) custom-call(bf16[3072,4096]{1,0:T(8,128)(2,1)} %refs_0_.17, f32[2,144,1536]{2,1,0:T(8,128)S(1)} %get-tuple-element.53.refs_1_, bf16[2,144,1536]{2,1,0:T(8,128)(2,1)S(1)} %collective-permute-done.5.refs_2_, ...), custom_call_target="tpu_custom_call" | custom-call | flops 226492416 | bytes 6291456 | tf_op jit(solution)/shard_map/pallas_call | solution.py:178
  45.8 1.1 %shard_map.131.refs_2_.refs_1_ = bf16[256,1536]{1,0:T(8,128)(2,1)S(1)} custom-call(f32[2,144,1536]{2,1,0:T(8,128)S(1)} %get-tuple-element.57.refs_0_, bf16[2,144,1536]{2,1,0:T(8,128)(2,1)S(1)} %collective-permute-done.6.refs_1_, bf16[256,144]{1,0:T(8,128)(2,1)S(1)} %get-tuple-element.40.refs_5_.refs_6_.refs_3_.refs_2_, f32[256,128]{1,0:T(8,128)S(1)} %get-tuple-element.59.refs_3_), custom_call_target="tpu_custom_call" | custom-call | flops 226492416 | tf_op jit(solution)/shard_map/pallas_call | solution.py:178
  46.9 2.6 %shard_map.133 = (bf16[128,2048]{1,0:T(8,128)(2,1)S(1)}, bf16[128,1024]{1,0:T(8,128)(2,1)S(1)}) custom-call(bf16[256,1536]{1,0:T(8,128)(2,1)S(1)} %get-tuple-element.56.refs_1_.refs_0_, bf16[256,1536]{1,0:T(8,128)(2,1)S(1)} %shard_map.131.refs_2_.refs_1_, bf16[3072,1024]{1,0:T(8,128)(2,1)S(1)} %get-tuple-element.63.refs_2_, ...), custom_call_target="tpu_custom_call" | custom-call | flops 150994944 | tf_op jit(solution)/shard_map/pallas_call | solution.py:178
  49.5 1.0 shard_map.134
  50.5 1.3 %collective-permute-start.9 = (bf16[128,2048]{1,0:T(8,128)(2,1)S(1)}, bf16[128,2048]{1,0:T(8,128)(2,1)S(1)}, u32[]{:S(2)}, u32[]{:S(2)}) collective-permute-start(bf16[128,2048]{1,0:T(8,128)(2,1)S(1)} %shard_map.134), channel_id=1, source_target_pairs={{0,4},{1,5},{2,6},{3,7},{4,0},{5,1},{6,2},{7,3},{8,12},{9,13},{10,... | collective-permute-start | bytes 1572872 | tf_op jit(solution)/shard_map/ppermute | solution.py:108
  51.8 2.4 %collective-permute-start.7 = (bf16[128,2048]{1,0:T(8,128)(2,1)S(1)}, bf16[128,2048]{1,0:T(8,128)(2,1)S(1)}, u32[]{:S(2)}, u32[]{:S(2)}) collective-permute-start(bf16[128,2048]{1,0:T(8,128)(2,1)S(1)} %get-tuple-element.64), channel_id=1, source_target_pairs={{0,2},{1,3},{2,0},{3,1},{4,6},{5,7},{6,4},{7,5},{8,10},{9,11},{10,... | collective-permute-start | bytes 1572872 | tf_op jit(solution)/shard_map/ppermute | solution.py:108
  54.2 7.2 %shard_map.132 = (bf16[128,1024]{1,0:T(8,128)(2,1)S(1)}, bf16[128,1024]{1,0:T(8,128)(2,1)S(1)}, bf16[128,1024]{1,0:T(8,128)(2,1)S(1)}, bf16[128,1024]{1,0:T(8,128)(2,1)S(1)}, bf16[3072,1024]{1,0:T(8,128)(2,1)}) custom-call(bf16[3072,4096]{1,0:T(8,128)(2,1)} %refs_0_.17, bf16[256,1536]{1,0:T(8,128)(2,1)S(1)} %get-tuple-element.56.refs_1_.refs_0_, ...), custom_call_target="tpu_custom_call" | custom-call | flops 201326592 | bytes 6291456 | tf_op jit(solution)/shard_map/pallas_call | solution.py:178
  61.4 3.0 %collective-permute-done.9 = bf16[128,2048]{1,0:T(8,128)(2,1)S(1)} collective-permute-done((bf16[128,2048]{1,0:T(8,128)(2,1)S(1)}, bf16[128,2048]{1,0:T(8,128)(2,1)S(1)}, u32[]{:S(2)}, u32[]{:S(2)}) %collective-permute-start.9) | collective-permute-done | bytes 524320 | tf_op jit(solution)/shard_map/ppermute | solution.py:108
  64.5 2.6 %collective-permute-start.10 = (bf16[128,1024]{1,0:T(8,128)(2,1)S(1)}, bf16[128,1024]{1,0:T(8,128)(2,1)S(1)}, u32[]{:S(2)}, u32[]{:S(2)}) collective-permute-start(bf16[128,1024]{1,0:T(8,128)(2,1)S(1)} %add_convert_fusion.2), channel_id=1, source_target_pairs={{0,2},{1,3},{2,0},{3,1},{4,6},{5,7},{6,4},{7,5},{8,10},{9,11},{10,... | collective-permute-start | bytes 786440 | tf_op jit(solution)/shard_map/ppermute | solution.py:108
  67.1 1.3 %collective-permute-start.8 = (bf16[128,1024]{1,0:T(8,128)(2,1)S(1)}, bf16[128,1024]{1,0:T(8,128)(2,1)S(1)}, u32[]{:S(2)}, u32[]{:S(2)}) collective-permute-start(bf16[128,1024]{1,0:T(8,128)(2,1)S(1)} %add_convert_fusion.4), channel_id=1, source_target_pairs={{0,4},{1,5},{2,6},{3,7},{4,0},{5,1},{6,2},{7,3},{8,12},{9,13},{10,... | collective-permute-start | bytes 786440 | tf_op jit(solution)/shard_map/ppermute | solution.py:108
  68.4 4.2 %collective-permute-done.10 = bf16[128,1024]{1,0:T(8,128)(2,1)S(1)} collective-permute-done((bf16[128,1024]{1,0:T(8,128)(2,1)S(1)}, bf16[128,1024]{1,0:T(8,128)(2,1)S(1)}, u32[]{:S(2)}, u32[]{:S(2)}) %collective-permute-start.10) | collective-permute-done | bytes 262176 | tf_op jit(solution)/shard_map/ppermute | solution.py:108
  74.4 1.7 %collective-permute-start.11 = (bf16[128,1024]{1,0:T(8,128)(2,1)S(1)}, bf16[128,1024]{1,0:T(8,128)(2,1)S(1)}, u32[]{:S(2)}, u32[]{:S(2)}) collective-permute-start(bf16[128,1024]{1,0:T(8,128)(2,1)S(1)} %broadcast_select_fusion), channel_id=1, source_target_pairs={{0,1},{2,3},{4,5},{6,7},{9,8},{11,10},{13,12},{15,14},{16,17},{18,... | collective-permute-start | bytes 786440 | tf_op jit(solution)/shard_map/ppermute | solution.py:108
  76.2 1.3 %collective-permute-start.12 = (bf16[128,1024]{1,0:T(8,128)(2,1)S(1)}, bf16[128,1024]{1,0:T(8,128)(2,1)S(1)}, u32[]{:S(2)}, u32[]{:S(2)}) collective-permute-start(bf16[128,1024]{1,0:T(8,128)(2,1)S(1)} %add_convert_fusion.3), channel_id=1, source_target_pairs={{1,8},{3,10},{5,12},{7,14},{8,0},{10,2},{12,4},{14,6},{17,24},{19,... | collective-permute-start | bytes 786440 | tf_op jit(solution)/shard_map/ppermute | solution.py:108
  77.5 11.0 %collective-permute-done.12 = bf16[128,1024]{1,0:T(8,128)(2,1)S(1)} collective-permute-done((bf16[128,1024]{1,0:T(8,128)(2,1)S(1)}, bf16[128,1024]{1,0:T(8,128)(2,1)S(1)}, u32[]{:S(2)}, u32[]{:S(2)}) %collective-permute-start.12) | collective-permute-done | bytes 262176 | tf_op jit(solution)/shard_map/ppermute | solution.py:108
  88.5 1.0 fusion
  89.5 1.5 %collective-permute-start.14 = (f32[2,128]{1,0:T(2,128)S(1)}, f32[2,128]{1,0:T(2,128)S(1)}, u32[]{:S(2)}, u32[]{:S(2)}) collective-permute-start(f32[2,128]{1,0:T(2,128)S(1)} %pad_maximum_fusion), channel_id=1, source_target_pairs={{0,2},{1,3},{2,0},{3,1},{4,6},{5,7},{6,4},{7,5},{8,10},{9,11},{10,... | collective-permute-start | bytes 3080 | tf_op jit(solution)/shard_map/ppermute | solution.py:108
  91.0 2.1 %collective-permute-done.14 = f32[2,128]{1,0:T(2,128)S(1)} collective-permute-done((f32[2,128]{1,0:T(2,128)S(1)}, f32[2,128]{1,0:T(2,128)S(1)}, u32[]{:S(2)}, u32[]{:S(2)}) %collective-permute-start.14) | collective-permute-done | bytes 1056 | tf_op jit(solution)/shard_map/ppermute | solution.py:108
  93.2 3.6 %collective-permute-done.15 = f32[2,128]{1,0:T(2,128)S(1)} collective-permute-done((f32[2,128]{1,0:T(2,128)S(1)}, f32[2,128]{1,0:T(2,128)S(1)}, u32[]{:S(2)}, u32[]{:S(2)}) %collective-permute-start.15) | collective-permute-done | bytes 1056 | tf_op jit(solution)/shard_map/ppermute | solution.py:108
  96.9 4.5 %collective-permute-done.16 = f32[2,128]{1,0:T(2,128)S(1)} collective-permute-done((f32[2,128]{1,0:T(2,128)S(1)}, f32[2,128]{1,0:T(2,128)S(1)}, u32[]{:S(2)}, u32[]{:S(2)}) %collective-permute-start.16) | collective-permute-done | bytes 1056 | tf_op jit(solution)/shard_map/ppermute | solution.py:108
  (39 shorter events, 4.3 us)
Async XLA Ops:
  1.6 11.0 %copy-start = (bf16[128,1024]{1,0:T(8,128)(2,1)S(1)}, bf16[128,1024]{1,0:T(8,128)(2,1)}, u32[]{:S(2)}) copy-start(bf16[128,1024]{1,0:T(8,128)(2,1)} %refs_5_.1) | copy-start | bytes 786436
  1.6 11.0 %copy-start.1 = (bf16[2,1024]{1,0:T(2,128)(2,1)S(1)}, bf16[2,1024]{1,0:T(2,128)(2,1)}, u32[]{:S(2)}) copy-start(bf16[2,1024]{1,0:T(2,128)(2,1)} %refs_6_.1) | copy-start | bytes 12292
  1.7 11.0 %copy-start.2 = (f32[1024]{0:T(1024)S(1)}, f32[1024]{0:T(1024)}, u32[]{:S(2)}) copy-start(f32[1024]{0:T(1024)} %refs_9_.1) | copy-start | bytes 12292
  1.7 11.0 %copy-start.3 = (f32[1024]{0:T(1024)S(1)}, f32[1024]{0:T(1024)}, u32[]{:S(2)}) copy-start(f32[1024]{0:T(1024)} %refs_10_.1) | copy-start | bytes 12292
  1.7 11.0 %copy-start.4 = (f32[128]{0:T(128)S(1)}, f32[128]{0:T(128)}, u32[]{:S(2)}) copy-start(f32[128]{0:T(128)} %refs_7_.1) | copy-start | bytes 1540
  1.7 11.0 %copy-start.5 = (f32[128]{0:T(128)S(1)}, f32[128]{0:T(128)}, u32[]{:S(2)}) copy-start(f32[128]{0:T(128)} %refs_8_.1) | copy-start | bytes 1540
  1.7 10.9 %collective-permute-start.1 = (bf16[80,1024]{1,0:T(8,128)(2,1)S(1)}, bf16[80,1024]{1,0:T(8,128)(2,1)S(1)}, u32[]{:S(2)}, u32[]{:S(2)}) collective-permute-start(bf16[80,1024]{1,0:T(8,128)(2,1)S(1)} %shard_map.123.refs_2_), channel_id=1, source_target_pairs={{1,8},{3,10},{5,12},{7,14},{8,1},{10,3},{12,5},{14,7},{17,24},{19,... | collective-permute-start | bytes 491528 | tf_op jit(solution)/shard_map/ppermute | solution.py:108
  2.5 10.1 %collective-permute-start = (bf16[80,1024]{1,0:T(8,128)(2,1)S(1)}, bf16[80,1024]{1,0:T(8,128)(2,1)S(1)}, u32[]{:S(2)}, u32[]{:S(2)}) collective-permute-start(bf16[80,1024]{1,0:T(8,128)(2,1)S(1)} %shard_map.123.refs_2_), channel_id=1, source_target_pairs={{0,8},{2,10},{4,12},{6,14},{9,1},{11,3},{13,5},{15,7},{1,0},{3,2},... | collective-permute-start | bytes 491528 | tf_op jit(solution)/shard_map/ppermute | solution.py:108
  13.5 11.7 %collective-permute-start.4 = (bf16[144,1024]{1,0:T(8,128)(2,1)S(1)}, bf16[144,1024]{1,0:T(8,128)(2,1)S(1)}, u32[]{:S(2)}, u32[]{:S(2)}) collective-permute-start(bf16[144,1024]{1,0:T(8,128)(2,1)S(1)} %get-tuple-element.39.refs_2_), channel_id=1, source_target_pairs={{0,4},{1,5},{2,6},{3,7},{4,0},{5,1},{6,2},{7,3},{8,12},{9,13},{10,... | collective-permute-start | bytes 884744 | tf_op jit(solution)/shard_map/ppermute | solution.py:108
  17.7 14.0 %collective-permute-start.3 = (bf16[144,1024]{1,0:T(8,128)(2,1)S(1)}, bf16[144,1024]{1,0:T(8,128)(2,1)S(1)}, u32[]{:S(2)}, u32[]{:S(2)}) collective-permute-start(bf16[144,1024]{1,0:T(8,128)(2,1)S(1)} %get-tuple-element.39.refs_2_), channel_id=1, source_target_pairs={{0,2},{1,3},{2,0},{3,1},{4,6},{5,7},{6,4},{7,5},{8,10},{9,11},{10,... | collective-permute-start | bytes 884744 | tf_op jit(solution)/shard_map/ppermute | solution.py:108
  19.2 17.3 %collective-permute-start.2 = (bf16[144,1024]{1,0:T(8,128)(2,1)S(1)}, bf16[144,1024]{1,0:T(8,128)(2,1)S(1)}, u32[]{:S(2)}, u32[]{:S(2)}) collective-permute-start(bf16[144,1024]{1,0:T(8,128)(2,1)S(1)} %get-tuple-element.39.refs_2_), channel_id=1, source_target_pairs={{0,6},{1,7},{2,4},{3,5},{4,2},{5,3},{6,0},{7,1},{8,14},{9,15},{10,... | collective-permute-start | bytes 884744 | tf_op jit(solution)/shard_map/ppermute | solution.py:108
  39.3 3.5 %collective-permute-start.5 = (bf16[2,144,1536]{2,1,0:T(8,128)(2,1)S(1)}, bf16[2,144,1536]{2,1,0:T(8,128)(2,1)S(1)}, u32[]{:S(2)}, u32[]{:S(2)}) collective-permute-start(bf16[2,144,1536]{2,1,0:T(8,128)(2,1)S(1)} %get-tuple-element.54), channel_id=1, source_target_pairs={{0,1},{1,0},{2,3},{3,2},{4,5},{5,4},{6,7},{7,6},{8,9},{9,8},{10,11... | collective-permute-start | bytes 2654216 | tf_op jit(solution)/shard_map/ppermute | solution.py:108
  42.3 3.5 %collective-permute-start.6 = (bf16[2,144,1536]{2,1,0:T(8,128)(2,1)S(1)}, bf16[2,144,1536]{2,1,0:T(8,128)(2,1)S(1)}, u32[]{:S(2)}, u32[]{:S(2)}) collective-permute-start(bf16[2,144,1536]{2,1,0:T(8,128)(2,1)S(1)} %get-tuple-element.58), channel_id=1, source_target_pairs={{0,1},{1,0},{2,3},{3,2},{4,5},{5,4},{6,7},{7,6},{8,9},{9,8},{10,11... | collective-permute-start | bytes 2654216 | tf_op jit(solution)/shard_map/ppermute | solution.py:108
  50.5 13.9 %collective-permute-start.9 = (bf16[128,2048]{1,0:T(8,128)(2,1)S(1)}, bf16[128,2048]{1,0:T(8,128)(2,1)S(1)}, u32[]{:S(2)}, u32[]{:S(2)}) collective-permute-start(bf16[128,2048]{1,0:T(8,128)(2,1)S(1)} %shard_map.134), channel_id=1, source_target_pairs={{0,4},{1,5},{2,6},{3,7},{4,0},{5,1},{6,2},{7,3},{8,12},{9,13},{10,... | collective-permute-start | bytes 1572872 | tf_op jit(solution)/shard_map/ppermute | solution.py:108
  51.8 15.2 %collective-permute-start.7 = (bf16[128,2048]{1,0:T(8,128)(2,1)S(1)}, bf16[128,2048]{1,0:T(8,128)(2,1)S(1)}, u32[]{:S(2)}, u32[]{:S(2)}) collective-permute-start(bf16[128,2048]{1,0:T(8,128)(2,1)S(1)} %get-tuple-element.64), channel_id=1, source_target_pairs={{0,2},{1,3},{2,0},{3,1},{4,6},{5,7},{6,4},{7,5},{8,10},{9,11},{10,... | collective-permute-start | bytes 1572872 | tf_op jit(solution)/shard_map/ppermute | solution.py:108
  64.5 8.2 %collective-permute-start.10 = (bf16[128,1024]{1,0:T(8,128)(2,1)S(1)}, bf16[128,1024]{1,0:T(8,128)(2,1)S(1)}, u32[]{:S(2)}, u32[]{:S(2)}) collective-permute-start(bf16[128,1024]{1,0:T(8,128)(2,1)S(1)} %add_convert_fusion.2), channel_id=1, source_target_pairs={{0,2},{1,3},{2,0},{3,1},{4,6},{5,7},{6,4},{7,5},{8,10},{9,11},{10,... | collective-permute-start | bytes 786440 | tf_op jit(solution)/shard_map/ppermute | solution.py:108
  67.1 7.2 %collective-permute-start.8 = (bf16[128,1024]{1,0:T(8,128)(2,1)S(1)}, bf16[128,1024]{1,0:T(8,128)(2,1)S(1)}, u32[]{:S(2)}, u32[]{:S(2)}) collective-permute-start(bf16[128,1024]{1,0:T(8,128)(2,1)S(1)} %add_convert_fusion.4), channel_id=1, source_target_pairs={{0,4},{1,5},{2,6},{3,7},{4,0},{5,1},{6,2},{7,3},{8,12},{9,13},{10,... | collective-permute-start | bytes 786440 | tf_op jit(solution)/shard_map/ppermute | solution.py:108
  72.8 4.7 %collective-permute-start.13 = (bf16[128,1024]{1,0:T(8,128)(2,1)S(1)}, bf16[128,1024]{1,0:T(8,128)(2,1)S(1)}, u32[]{:S(2)}, u32[]{:S(2)}) collective-permute-start(bf16[128,1024]{1,0:T(8,128)(2,1)S(1)} %add_convert_fusion.1), channel_id=1, source_target_pairs={{1,9},{3,11},{5,13},{7,15},{8,1},{10,3},{12,5},{14,7},{17,25},{19,... | collective-permute-start | bytes 786440 | tf_op jit(solution)/shard_map/ppermute | solution.py:108
  74.4 3.1 %collective-permute-start.11 = (bf16[128,1024]{1,0:T(8,128)(2,1)S(1)}, bf16[128,1024]{1,0:T(8,128)(2,1)S(1)}, u32[]{:S(2)}, u32[]{:S(2)}) collective-permute-start(bf16[128,1024]{1,0:T(8,128)(2,1)S(1)} %broadcast_select_fusion), channel_id=1, source_target_pairs={{0,1},{2,3},{4,5},{6,7},{9,8},{11,10},{13,12},{15,14},{16,17},{18,... | collective-permute-start | bytes 786440 | tf_op jit(solution)/shard_map/ppermute | solution.py:108
  76.2 12.4 %collective-permute-start.12 = (bf16[128,1024]{1,0:T(8,128)(2,1)S(1)}, bf16[128,1024]{1,0:T(8,128)(2,1)S(1)}, u32[]{:S(2)}, u32[]{:S(2)}) collective-permute-start(bf16[128,1024]{1,0:T(8,128)(2,1)S(1)} %add_convert_fusion.3), channel_id=1, source_target_pairs={{1,8},{3,10},{5,12},{7,14},{8,0},{10,2},{12,4},{14,6},{17,24},{19,... | collective-permute-start | bytes 786440 | tf_op jit(solution)/shard_map/ppermute | solution.py:108
  89.5 3.6 %collective-permute-start.14 = (f32[2,128]{1,0:T(2,128)S(1)}, f32[2,128]{1,0:T(2,128)S(1)}, u32[]{:S(2)}, u32[]{:S(2)}) collective-permute-start(f32[2,128]{1,0:T(2,128)S(1)} %pad_maximum_fusion), channel_id=1, source_target_pairs={{0,2},{1,3},{2,0},{3,1},{4,6},{5,7},{6,4},{7,5},{8,10},{9,11},{10,... | collective-permute-start | bytes 3080 | tf_op jit(solution)/shard_map/ppermute | solution.py:108
  93.2 3.6 %collective-permute-start.15 = (f32[2,128]{1,0:T(2,128)S(1)}, f32[2,128]{1,0:T(2,128)S(1)}, u32[]{:S(2)}, u32[]{:S(2)}) collective-permute-start(f32[2,128]{1,0:T(2,128)S(1)} %fusion.2), channel_id=1, source_target_pairs={{0,4},{1,5},{2,6},{3,7},{4,0},{5,1},{6,2},{7,3},{8,12},{9,13},{10,... | collective-permute-start | bytes 3080 | tf_op jit(solution)/shard_map/ppermute | solution.py:108
  96.8 4.5 %collective-permute-start.16 = (f32[2,128]{1,0:T(2,128)S(1)}, f32[2,128]{1,0:T(2,128)S(1)}, u32[]{:S(2)}, u32[]{:S(2)}) collective-permute-start(f32[2,128]{1,0:T(2,128)S(1)} %fusion.3), channel_id=1, source_target_pairs={{0,8},{1,9},{2,10},{3,11},{4,12},{5,13},{6,14},{7,15},{8,0},{9,1},... | collective-permute-start | bytes 3080 | tf_op jit(solution)/shard_map/ppermute | solution.py:108

commit v10 on v9

--- a/solution.py
+++ b/solution.py
@@ -122,7 +122,7 @@
     return place if k == 0 else 3 - place
 
 
-def stage(loads, ins, outs, compute, scratch=(), limit=3, flops=0, alias=None, manual=False):
+def stage(loads, ins, outs, compute, scratch=(), limit=2, flops=0, alias=None, manual=False):
     vmem = pl.BlockSpec(memory_space=pltpu.VMEM)
     count = len(ins)
     shapes, sources, flat = list(outs), [], []
@@ -183,7 +183,9 @@
         scratch_shapes=([pltpu.SemaphoreType.DMA((n * SPLIT,))] if n else []) + list(scratch),
         input_output_aliases={} if alias is None else {n + alias: 0},
         compiler_params=pltpu.CompilerParams(vmem_limit_bytes=limit * MIB),
-        cost_estimate=pl.CostEstimate(flops=flops, bytes_accessed=loaded, transcendentals=0),
+        cost_estimate=pl.CostEstimate(
+            flops=flops, bytes_accessed=0 if manual else loaded, transcendentals=0
+        ),
     )(*sources, *ins)
 
 
@@ -531,25 +533,25 @@
 
     span = (0, units)
     basis, square, *held = basis_stage(
-        pair(2), [block], held, None, span, features, [], False
-    )
-    basis, square, *held = basis_stage(
-        pair(1), [near[2]], held, basis, span, features, [square], False
-    )
-    basis, square, *held = basis_stage(
-        pair(3), [near[1]], held, basis, span, features, [square], False
+        pair(2) + pair(1), [block], held, None, span, features, [], False
+    )
+    basis, square, *last = basis_stage(
+        pair(3), [near[2]], held[:2], basis, span, features, [square], False
+    )
+    basis, square, down_diagonal = basis_stage(
+        [column(3)], [near[1]], held[2:], basis, span, features, [square], False
     )
     cut = units // 2
-    own_a, narrow_a, square, down_diagonal = basis_stage(
-        [column(3)], [near[3]], held, basis, (0, cut), features, [square], True
+    own_a, narrow_a, square, down_x = basis_stage(
+        [column(1)], [near[3]], last, basis, (0, cut), features, [square], True
     )
     other_a = send(narrow_a, swap_core)
-    own_b, narrow_b, down_x = basis_stage(
-        [column(1)], [near[3]], held, basis, (cut, units), features, None, True
+    own_b, narrow_b, down_z = basis_stage(
+        [column(2)], [near[3]], last, basis, (cut, units), features, None, True
     )
     other_b = send(narrow_b, swap_core)
-    hidden_a, scale, down_z = hidden_stage(
-        [column(2)], own_a, other_a, features, square, None, full_width
+    hidden_a, scale = hidden_stage(
+        [], own_a, other_a, features, square, None, full_width
     )
     (hidden_b,) = hidden_stage([], own_b, other_b, features, None, scale, full_width)
     hidden = [hidden_a, hidden_b]

time: 102 us -> 105 us (1.029)
  waiting for transfers between devices: 32.1 us -> 34.4 us
    ppermute x17, waiting for transfers between devices: 32.1 us -> 34.4 us  [send(): lax.ppermute(array, ('tp', 'dp'), [(2 * st + sd, 2 * dt + dd) for (st, sd...]
where the time goes in v10:
time: 105 us; the launch traced here: 104 us
  Pallas kernels  42 us (40%)
  waiting for transfers between devices  34.4 us (33%)
  starting transfers between devices  24.9 us (24%)
  other arithmetic  1.43 us (1%)
    pallas_call x11, Pallas kernels, stage(): pl.pallas_call(body, out_shape=shapes, in_specs=[pl.BlockSpec(memory_spac...  40.2 us
    ppermute x17, waiting for transfers between devices, send(): lax.ppermute(array, ('tp', 'dp'), [(2 * st + sd, 2 * dt + dd) for (st, sd...  34.4 us
    ppermute x17, starting transfers between devices, send(): lax.ppermute(array, ('tp', 'dp'), [(2 * st + sd, 2 * dt + dd) for (st, sd...  24.9 us
  transfers between devices with their start and end apart: 17, of which 9 were waited for; matrix products, arithmetic and copies ran while one was open for 0% of the time, Pallas kernels for 31%

profile of v10, /device:TPU:0, one launch (start us, length us, event | category | flops | bytes accessed | tf_op | source)
XLA Modules:
  0.0 104.4 jit_solution(3518139382252754871)
XLA Ops:
  0.6 1.0 shard_map.123.refs_2_
  1.7 4.1 %collective-permute-start = (bf16[80,1024]{1,0:T(8,128)(2,1)S(1)}, bf16[80,1024]{1,0:T(8,128)(2,1)S(1)}, u32[]{:S(2)}, u32[]{:S(2)}) collective-permute-start(bf16[80,1024]{1,0:T(8,128)(2,1)S(1)} %shard_map.123.refs_2_), channel_id=1, source_target_pairs={{0,8},{2,10},{4,12},{6,14},{9,1},{11,3},{13,5},{15,7},{1,0},{3,2},... | collective-permute-start | bytes 491528 | tf_op jit(solution)/shard_map/ppermute | solution.py:108
  6.5 4.7 %shard_map.122 = (bf16[1024,3072]{1,0:T(8,128)(2,1)S(1)}, bf16[1024,3072]{1,0:T(8,128)(2,1)S(1)}) custom-call(bf16[4096,3072]{1,0:T(8,128)(2,1)} %refs_0_.11, bf16[4096,3072]{1,0:T(8,128)(2,1)} %refs_1_.7), custom_call_target="tpu_custom_call" | custom-call | bytes 12582912 | tf_op jit(solution)/shard_map/pallas_call | solution.py:178
  12.1 4.1 %collective-permute-start.3 = (bf16[144,1024]{1,0:T(8,128)(2,1)S(1)}, bf16[144,1024]{1,0:T(8,128)(2,1)S(1)}, u32[]{:S(2)}, u32[]{:S(2)}) collective-permute-start(bf16[144,1024]{1,0:T(8,128)(2,1)S(1)} %get-tuple-element.39.refs_4_), channel_id=1, source_target_pairs={{0,4},{1,5},{2,6},{3,7},{4,0},{5,1},{6,2},{7,3},{8,12},{9,13},{10,... | collective-permute-start | bytes 884744 | tf_op jit(solution)/shard_map/ppermute | solution.py:108
  16.2 1.5 %collective-permute-start.4 = (bf16[144,1024]{1,0:T(8,128)(2,1)S(1)}, bf16[144,1024]{1,0:T(8,128)(2,1)S(1)}, u32[]{:S(2)}, u32[]{:S(2)}) collective-permute-start(bf16[144,1024]{1,0:T(8,128)(2,1)S(1)} %get-tuple-element.39.refs_4_), channel_id=1, source_target_pairs={{0,2},{1,3},{2,0},{3,1},{4,6},{5,7},{6,4},{7,5},{8,10},{9,11},{10,... | collective-permute-start | bytes 884744 | tf_op jit(solution)/shard_map/ppermute | solution.py:108
  17.8 8.5 %shard_map.125 = (f32[2,144,3072]{2,1,0:T(8,128)S(1)}, f32[256,128]{1,0:T(8,128)S(1)}, bf16[1024,3072]{1,0:T(8,128)(2,1)S(1)}, bf16[1024,3072]{1,0:T(8,128)(2,1)...) custom-call(bf16[4096,3072]{1,0:T(8,128)(2,1)} %refs_0_.11, bf16[4096,3072]{1,0:T(8,128)(2,1)} %refs_1_.7, ...), custom_call_target="tpu_custom_call" | custom-call | flops 1811939328 | bytes 25165824 | tf_op jit(solution)/shard_map/pallas_call | solution.py:178
  26.3 4.7 %shard_map.126 = (f32[2,144,3072]{2,1,0:T(8,128)S(1)}, f32[256,128]{1,0:T(8,128)S(1)}, bf16[1024,3072]{1,0:T(8,128)(2,1)S(1)}, bf16[1024,3072]{1,0:T(8,128)(2,1)S(1)}) custom-call(bf16[4096,3072]{1,0:T(8,128)(2,1)} %refs_0_.11, bf16[4096,3072]{1,0:T(8,128)(2,1)} %refs_1_.7, ...), custom_call_target="tpu_custom_call", output_to_operand_aliasing={{0}: (5, {})} | custom-call | flops 1811939328 | bytes 12582912 | tf_op jit(solution)/shard_map/pallas_call | solution.py:178
  31.5 3.5 %shard_map.127 = (f32[2,144,3072]{2,1,0:T(8,128)S(1)}, f32[256,128]{1,0:T(8,128)S(1)}, bf16[3072,1024]{1,0:T(8,128)(2,1)S(1)}) custom-call(bf16[3072,4096]{1,0:T(8,128)(2,1)} %refs_0_.15, bf16[144,1024]{1,0:T(8,128)(2,1)S(1)} %collective-permute-done.4.refs_1_, bf16[1024,3072]{1,0:T(8,128)(2,1)S(1)} %get-tuple-element.47.refs_2_, ...), custom_call_target="tpu_custom_call", output_to_operand_aliasing={{0}: (4, {})} | custom-call | flops 1811939328 | bytes 6291456 | tf_op jit(solution)/shard_map/pallas_call | solution.py:178
  35.0 2.9 %shard_map.128 = (f32[2,144,1536]{2,1,0:T(8,128)S(1)}, bf16[2,144,1536]{2,1,0:T(8,128)(2,1)S(1)}, f32[256,128]{1,0:T(8,128)S(1)}, bf16[3072,1024]{1,0:T(8,128)(2,1)S(1)}) custom-call(bf16[3072,4096]{1,0:T(8,128)(2,1)} %refs_0_.15, bf16[144,1024]{1,0:T(8,128)(2,1)S(1)} %collective-permute-done.2.refs_1_, bf16[1024,3072]{1,0:T(8,128)(2,1)S(1)} %get-tuple-element.45.refs_2_, ...), custom_call_target="tpu_custom_call" | custom-call | flops 905969664 | bytes 6291456 | tf_op jit(solution)/shard_map/pallas_call | solution.py:178
  38.0 2.9 %shard_map.130 = (f32[2,144,1536]{2,1,0:T(8,128)S(1)}, bf16[2,144,1536]{2,1,0:T(8,128)(2,1)S(1)}, bf16[3072,1024]{1,0:T(8,128)(2,1)S(1)}) custom-call(bf16[3072,4096]{1,0:T(8,128)(2,1)} %refs_0_.15, bf16[144,1024]{1,0:T(8,128)(2,1)S(1)} %collective-permute-done.2.refs_1_, bf16[1024,3072]{1,0:T(8,128)(2,1)S(1)} %get-tuple-element.45.refs_2_, ...), custom_call_target="tpu_custom_call" | custom-call | flops 905969664 | bytes 6291456 | tf_op jit(solution)/shard_map/pallas_call | solution.py:178
  41.4 1.2 %shard_map.129 = (bf16[256,1536]{1,0:T(8,128)(2,1)S(1)}, f32[256,128]{1,0:T(8,128)S(1)}) custom-call(f32[2,144,1536]{2,1,0:T(8,128)S(1)} %get-tuple-element.53.refs_0_, bf16[2,144,1536]{2,1,0:T(8,128)(2,1)S(1)} %collective-permute-done.5.refs_1_, bf16[256,144]{1,0:T(8,128)(2,1)S(1)} %get-tuple-element.40.refs_7_.refs_6_.refs_5_.refs_2_, ...), custom_call_target="tpu_custom_call" | custom-call | flops 226492416 | tf_op jit(solution)/shard_map/pallas_call | solution.py:178
  42.6 0.9 collective-permute-done.6.refs_1_
  43.5 1.1 %shard_map.131.refs_2_.refs_1_ = bf16[256,1536]{1,0:T(8,128)(2,1)S(1)} custom-call(f32[2,144,1536]{2,1,0:T(8,128)S(1)} %get-tuple-element.57.refs_0_, bf16[2,144,1536]{2,1,0:T(8,128)(2,1)S(1)} %collective-permute-done.6.refs_1_, bf16[256,144]{1,0:T(8,128)(2,1)S(1)} %get-tuple-element.40.refs_7_.refs_6_.refs_5_.refs_2_, f32[256,128]{1,0:T(8,128)S(1)} %get-tuple-element.59.refs_3_), custom_call_target="tpu_custom_call" | custom-call | flops 226492416 | tf_op jit(solution)/shard_map/pallas_call | solution.py:178
  44.5 2.6 %shard_map.133 = (bf16[128,2048]{1,0:T(8,128)(2,1)S(1)}, bf16[128,1024]{1,0:T(8,128)(2,1)S(1)}) custom-call(bf16[256,1536]{1,0:T(8,128)(2,1)S(1)} %get-tuple-element.56.refs_1_.refs_0_, bf16[256,1536]{1,0:T(8,128)(2,1)S(1)} %shard_map.131.refs_2_.refs_1_, bf16[3072,1024]{1,0:T(8,128)(2,1)S(1)} %get-tuple-element.63.refs_2_, ...), custom_call_target="tpu_custom_call" | custom-call | flops 150994944 | tf_op jit(solution)/shard_map/pallas_call | solution.py:178
  47.1 1.0 shard_map.134
  48.1 1.7 %collective-permute-start.9 = (bf16[128,2048]{1,0:T(8,128)(2,1)S(1)}, bf16[128,2048]{1,0:T(8,128)(2,1)S(1)}, u32[]{:S(2)}, u32[]{:S(2)}) collective-permute-start(bf16[128,2048]{1,0:T(8,128)(2,1)S(1)} %shard_map.134), channel_id=1, source_target_pairs={{0,4},{1,5},{2,6},{3,7},{4,0},{5,1},{6,2},{7,3},{8,12},{9,13},{10,... | collective-permute-start | bytes 1572872 | tf_op jit(solution)/shard_map/ppermute | solution.py:108
  49.8 1.4 %collective-permute-start.7 = (bf16[128,2048]{1,0:T(8,128)(2,1)S(1)}, bf16[128,2048]{1,0:T(8,128)(2,1)S(1)}, u32[]{:S(2)}, u32[]{:S(2)}) collective-permute-start(bf16[128,2048]{1,0:T(8,128)(2,1)S(1)} %get-tuple-element.64), channel_id=1, source_target_pairs={{0,2},{1,3},{2,0},{3,1},{4,6},{5,7},{6,4},{7,5},{8,10},{9,11},{10,... | collective-permute-start | bytes 1572872 | tf_op jit(solution)/shard_map/ppermute | solution.py:108
  51.2 7.2 %shard_map.132 = (bf16[128,1024]{1,0:T(8,128)(2,1)S(1)}, bf16[128,1024]{1,0:T(8,128)(2,1)S(1)}, bf16[128,1024]{1,0:T(8,128)(2,1)S(1)}, bf16[128,1024]{1,0:T(8,128)(2,1)S(1)}, bf16[3072,1024]{1,0:T(8,128)(2,1)}) custom-call(bf16[3072,4096]{1,0:T(8,128)(2,1)} %refs_0_.15, bf16[256,1536]{1,0:T(8,128)(2,1)S(1)} %get-tuple-element.56.refs_1_.refs_0_, ...), custom_call_target="tpu_custom_call" | custom-call | flops 201326592 | tf_op jit(solution)/shard_map/pallas_call | solution.py:178
  58.4 4.0 %collective-permute-done.9 = bf16[128,2048]{1,0:T(8,128)(2,1)S(1)} collective-permute-done((bf16[128,2048]{1,0:T(8,128)(2,1)S(1)}, bf16[128,2048]{1,0:T(8,128)(2,1)S(1)}, u32[]{:S(2)}, u32[]{:S(2)}) %collective-permute-start.9) | collective-permute-done | bytes 524320 | tf_op jit(solution)/shard_map/ppermute | solution.py:108
  62.5 1.5 %collective-permute-start.10 = (bf16[128,1024]{1,0:T(8,128)(2,1)S(1)}, bf16[128,1024]{1,0:T(8,128)(2,1)S(1)}, u32[]{:S(2)}, u32[]{:S(2)}) collective-permute-start(bf16[128,1024]{1,0:T(8,128)(2,1)S(1)} %add_convert_fusion.2), channel_id=1, source_target_pairs={{0,2},{1,3},{2,0},{3,1},{4,6},{5,7},{6,4},{7,5},{8,10},{9,11},{10,... | collective-permute-start | bytes 786440 | tf_op jit(solution)/shard_map/ppermute | solution.py:108
  64.1 1.6 %collective-permute-start.8 = (bf16[128,1024]{1,0:T(8,128)(2,1)S(1)}, bf16[128,1024]{1,0:T(8,128)(2,1)S(1)}, u32[]{:S(2)}, u32[]{:S(2)}) collective-permute-start(bf16[128,1024]{1,0:T(8,128)(2,1)S(1)} %add_convert_fusion.4), channel_id=1, source_target_pairs={{0,4},{1,5},{2,6},{3,7},{4,0},{5,1},{6,2},{7,3},{8,12},{9,13},{10,... | collective-permute-start | bytes 786440 | tf_op jit(solution)/shard_map/ppermute | solution.py:108
  65.6 4.7 %collective-permute-done.10 = bf16[128,1024]{1,0:T(8,128)(2,1)S(1)} collective-permute-done((bf16[128,1024]{1,0:T(8,128)(2,1)S(1)}, bf16[128,1024]{1,0:T(8,128)(2,1)S(1)}, u32[]{:S(2)}, u32[]{:S(2)}) %collective-permute-start.10) | collective-permute-done | bytes 262176 | tf_op jit(solution)/shard_map/ppermute | solution.py:108
  70.4 1.2 %collective-permute-done.8 = bf16[128,1024]{1,0:T(8,128)(2,1)S(1)} collective-permute-done((bf16[128,1024]{1,0:T(8,128)(2,1)S(1)}, bf16[128,1024]{1,0:T(8,128)(2,1)S(1)}, u32[]{:S(2)}, u32[]{:S(2)}) %collective-permute-start.8) | collective-permute-done | bytes 262176 | tf_op jit(solution)/shard_map/ppermute | solution.py:108
  71.8 1.3 %collective-permute-start.11 = (bf16[128,1024]{1,0:T(8,128)(2,1)S(1)}, bf16[128,1024]{1,0:T(8,128)(2,1)S(1)}, u32[]{:S(2)}, u32[]{:S(2)}) collective-permute-start(bf16[128,1024]{1,0:T(8,128)(2,1)S(1)} %broadcast_select_fusion), channel_id=1, source_target_pairs={{0,1},{2,3},{4,5},{6,7},{9,8},{11,10},{13,12},{15,14},{16,17},{18,... | collective-permute-start | bytes 786440 | tf_op jit(solution)/shard_map/ppermute | solution.py:108
  73.8 1.3 %collective-permute-start.12 = (bf16[128,1024]{1,0:T(8,128)(2,1)S(1)}, bf16[128,1024]{1,0:T(8,128)(2,1)S(1)}, u32[]{:S(2)}, u32[]{:S(2)}) collective-permute-start(bf16[128,1024]{1,0:T(8,128)(2,1)S(1)} %add_convert_fusion.3), channel_id=1, source_target_pairs={{1,8},{3,10},{5,12},{7,14},{8,0},{10,2},{12,4},{14,6},{17,24},{19,... | collective-permute-start | bytes 786440 | tf_op jit(solution)/shard_map/ppermute | solution.py:108
  75.1 15.5 %collective-permute-done.12 = bf16[128,1024]{1,0:T(8,128)(2,1)S(1)} collective-permute-done((bf16[128,1024]{1,0:T(8,128)(2,1)S(1)}, bf16[128,1024]{1,0:T(8,128)(2,1)S(1)}, u32[]{:S(2)}, u32[]{:S(2)}) %collective-permute-start.12) | collective-permute-done | bytes 262176 | tf_op jit(solution)/shard_map/ppermute | solution.py:108
  90.7 1.0 fusion
  91.7 1.1 %collective-permute-start.14 = (f32[2,128]{1,0:T(2,128)S(1)}, f32[2,128]{1,0:T(2,128)S(1)}, u32[]{:S(2)}, u32[]{:S(2)}) collective-permute-start(f32[2,128]{1,0:T(2,128)S(1)} %pad_maximum_fusion), channel_id=1, source_target_pairs={{0,2},{1,3},{2,0},{3,1},{4,6},{5,7},{6,4},{7,5},{8,10},{9,11},{10,... | collective-permute-start | bytes 3080 | tf_op jit(solution)/shard_map/ppermute | solution.py:108
  92.8 2.5 %collective-permute-done.14 = f32[2,128]{1,0:T(2,128)S(1)} collective-permute-done((f32[2,128]{1,0:T(2,128)S(1)}, f32[2,128]{1,0:T(2,128)S(1)}, u32[]{:S(2)}, u32[]{:S(2)}) %collective-permute-start.14) | collective-permute-done | bytes 1056 | tf_op jit(solution)/shard_map/ppermute | solution.py:108
  95.4 3.6 %collective-permute-done.15 = f32[2,128]{1,0:T(2,128)S(1)} collective-permute-done((f32[2,128]{1,0:T(2,128)S(1)}, f32[2,128]{1,0:T(2,128)S(1)}, u32[]{:S(2)}, u32[]{:S(2)}) %collective-permute-start.15) | collective-permute-done | bytes 1056 | tf_op jit(solution)/shard_map/ppermute | solution.py:108
  98.9 3.2 %collective-permute-start.16 = (f32[2,128]{1,0:T(2,128)S(1)}, f32[2,128]{1,0:T(2,128)S(1)}, u32[]{:S(2)}, u32[]{:S(2)}) collective-permute-start(f32[2,128]{1,0:T(2,128)S(1)} %fusion.3), channel_id=1, source_target_pairs={{0,8},{1,9},{2,10},{3,11},{4,12},{5,13},{6,14},{7,15},{8,0},{9,1},... | collective-permute-start | bytes 3080 | tf_op jit(solution)/shard_map/ppermute | solution.py:108
  102.2 1.5 %collective-permute-done.16 = f32[2,128]{1,0:T(2,128)S(1)} collective-permute-done((f32[2,128]{1,0:T(2,128)S(1)}, f32[2,128]{1,0:T(2,128)S(1)}, u32[]{:S(2)}, u32[]{:S(2)}) %collective-permute-start.16) | collective-permute-done | bytes 1056 | tf_op jit(solution)/shard_map/ppermute | solution.py:108
  (39 shorter events, 4.5 us)
Async XLA Ops:
  1.6 9.6 %copy-start = (bf16[128,1024]{1,0:T(8,128)(2,1)S(1)}, bf16[128,1024]{1,0:T(8,128)(2,1)}, u32[]{:S(2)}) copy-start(bf16[128,1024]{1,0:T(8,128)(2,1)} %refs_5_.1) | copy-start | bytes 786436
  1.6 9.6 %copy-start.1 = (bf16[2,1024]{1,0:T(2,128)(2,1)S(1)}, bf16[2,1024]{1,0:T(2,128)(2,1)}, u32[]{:S(2)}) copy-start(bf16[2,1024]{1,0:T(2,128)(2,1)} %refs_6_.1) | copy-start | bytes 12292
  1.7 9.6 %copy-start.2 = (f32[1024]{0:T(1024)S(1)}, f32[1024]{0:T(1024)}, u32[]{:S(2)}) copy-start(f32[1024]{0:T(1024)} %refs_9_.1) | copy-start | bytes 12292
  1.7 9.6 %copy-start.3 = (f32[1024]{0:T(1024)S(1)}, f32[1024]{0:T(1024)}, u32[]{:S(2)}) copy-start(f32[1024]{0:T(1024)} %refs_10_.1) | copy-start | bytes 12292
  1.7 9.6 %copy-start.4 = (f32[128]{0:T(128)S(1)}, f32[128]{0:T(128)}, u32[]{:S(2)}) copy-start(f32[128]{0:T(128)} %refs_7_.1) | copy-start | bytes 1540
  1.7 9.6 %copy-start.5 = (f32[128]{0:T(128)S(1)}, f32[128]{0:T(128)}, u32[]{:S(2)}) copy-start(f32[128]{0:T(128)} %refs_8_.1) | copy-start | bytes 1540
  1.7 9.5 %collective-permute-start = (bf16[80,1024]{1,0:T(8,128)(2,1)S(1)}, bf16[80,1024]{1,0:T(8,128)(2,1)S(1)}, u32[]{:S(2)}, u32[]{:S(2)}) collective-permute-start(bf16[80,1024]{1,0:T(8,128)(2,1)S(1)} %shard_map.123.refs_2_), channel_id=1, source_target_pairs={{0,8},{2,10},{4,12},{6,14},{9,1},{11,3},{13,5},{15,7},{1,0},{3,2},... | collective-permute-start | bytes 491528 | tf_op jit(solution)/shard_map/ppermute | solution.py:108
  5.8 5.4 %collective-permute-start.1 = (bf16[80,1024]{1,0:T(8,128)(2,1)S(1)}, bf16[80,1024]{1,0:T(8,128)(2,1)S(1)}, u32[]{:S(2)}, u32[]{:S(2)}) collective-permute-start(bf16[80,1024]{1,0:T(8,128)(2,1)S(1)} %shard_map.123.refs_2_), channel_id=1, source_target_pairs={{1,8},{3,10},{5,12},{7,14},{8,1},{10,3},{12,5},{14,7},{17,24},{19,... | collective-permute-start | bytes 491528 | tf_op jit(solution)/shard_map/ppermute | solution.py:108
  12.1 14.2 %collective-permute-start.3 = (bf16[144,1024]{1,0:T(8,128)(2,1)S(1)}, bf16[144,1024]{1,0:T(8,128)(2,1)S(1)}, u32[]{:S(2)}, u32[]{:S(2)}) collective-permute-start(bf16[144,1024]{1,0:T(8,128)(2,1)S(1)} %get-tuple-element.39.refs_4_), channel_id=1, source_target_pairs={{0,4},{1,5},{2,6},{3,7},{4,0},{5,1},{6,2},{7,3},{8,12},{9,13},{10,... | collective-permute-start | bytes 884744 | tf_op jit(solution)/shard_map/ppermute | solution.py:108
  16.2 15.2 %collective-permute-start.4 = (bf16[144,1024]{1,0:T(8,128)(2,1)S(1)}, bf16[144,1024]{1,0:T(8,128)(2,1)S(1)}, u32[]{:S(2)}, u32[]{:S(2)}) collective-permute-start(bf16[144,1024]{1,0:T(8,128)(2,1)S(1)} %get-tuple-element.39.refs_4_), channel_id=1, source_target_pairs={{0,2},{1,3},{2,0},{3,1},{4,6},{5,7},{6,4},{7,5},{8,10},{9,11},{10,... | collective-permute-start | bytes 884744 | tf_op jit(solution)/shard_map/ppermute | solution.py:108
  17.7 17.2 %collective-permute-start.2 = (bf16[144,1024]{1,0:T(8,128)(2,1)S(1)}, bf16[144,1024]{1,0:T(8,128)(2,1)S(1)}, u32[]{:S(2)}, u32[]{:S(2)}) collective-permute-start(bf16[144,1024]{1,0:T(8,128)(2,1)S(1)} %get-tuple-element.39.refs_4_), channel_id=1, source_target_pairs={{0,6},{1,7},{2,4},{3,5},{4,2},{5,3},{6,0},{7,1},{8,14},{9,15},{10,... | collective-permute-start | bytes 884744 | tf_op jit(solution)/shard_map/ppermute | solution.py:108
  37.9 3.5 %collective-permute-start.5 = (bf16[2,144,1536]{2,1,0:T(8,128)(2,1)S(1)}, bf16[2,144,1536]{2,1,0:T(8,128)(2,1)S(1)}, u32[]{:S(2)}, u32[]{:S(2)}) collective-permute-start(bf16[2,144,1536]{2,1,0:T(8,128)(2,1)S(1)} %get-tuple-element.54), channel_id=1, source_target_pairs={{0,1},{1,0},{2,3},{3,2},{4,5},{5,4},{6,7},{7,6},{8,9},{9,8},{10,11... | collective-permute-start | bytes 2654216 | tf_op jit(solution)/shard_map/ppermute | solution.py:108
  40.9 2.6 %collective-permute-start.6 = (bf16[2,144,1536]{2,1,0:T(8,128)(2,1)S(1)}, bf16[2,144,1536]{2,1,0:T(8,128)(2,1)S(1)}, u32[]{:S(2)}, u32[]{:S(2)}) collective-permute-start(bf16[2,144,1536]{2,1,0:T(8,128)(2,1)S(1)} %get-tuple-element.58), channel_id=1, source_target_pairs={{0,1},{1,0},{2,3},{3,2},{4,5},{5,4},{6,7},{7,6},{8,9},{9,8},{10,11... | collective-permute-start | bytes 2654216 | tf_op jit(solution)/shard_map/ppermute | solution.py:108
  48.1 14.3 %collective-permute-start.9 = (bf16[128,2048]{1,0:T(8,128)(2,1)S(1)}, bf16[128,2048]{1,0:T(8,128)(2,1)S(1)}, u32[]{:S(2)}, u32[]{:S(2)}) collective-permute-start(bf16[128,2048]{1,0:T(8,128)(2,1)S(1)} %shard_map.134), channel_id=1, source_target_pairs={{0,4},{1,5},{2,6},{3,7},{4,0},{5,1},{6,2},{7,3},{8,12},{9,13},{10,... | collective-permute-start | bytes 1572872 | tf_op jit(solution)/shard_map/ppermute | solution.py:108
  49.8 14.2 %collective-permute-start.7 = (bf16[128,2048]{1,0:T(8,128)(2,1)S(1)}, bf16[128,2048]{1,0:T(8,128)(2,1)S(1)}, u32[]{:S(2)}, u32[]{:S(2)}) collective-permute-start(bf16[128,2048]{1,0:T(8,128)(2,1)S(1)} %get-tuple-element.64), channel_id=1, source_target_pairs={{0,2},{1,3},{2,0},{3,1},{4,6},{5,7},{6,4},{7,5},{8,10},{9,11},{10,... | collective-permute-start | bytes 1572872 | tf_op jit(solution)/shard_map/ppermute | solution.py:108
  62.5 7.8 %collective-permute-start.10 = (bf16[128,1024]{1,0:T(8,128)(2,1)S(1)}, bf16[128,1024]{1,0:T(8,128)(2,1)S(1)}, u32[]{:S(2)}, u32[]{:S(2)}) collective-permute-start(bf16[128,1024]{1,0:T(8,128)(2,1)S(1)} %add_convert_fusion.2), channel_id=1, source_target_pairs={{0,2},{1,3},{2,0},{3,1},{4,6},{5,7},{6,4},{7,5},{8,10},{9,11},{10,... | collective-permute-start | bytes 786440 | tf_op jit(solution)/shard_map/ppermute | solution.py:108
  64.1 7.5 %collective-permute-start.8 = (bf16[128,1024]{1,0:T(8,128)(2,1)S(1)}, bf16[128,1024]{1,0:T(8,128)(2,1)S(1)}, u32[]{:S(2)}, u32[]{:S(2)}) collective-permute-start(bf16[128,1024]{1,0:T(8,128)(2,1)S(1)} %add_convert_fusion.4), channel_id=1, source_target_pairs={{0,4},{1,5},{2,6},{3,7},{4,0},{5,1},{6,2},{7,3},{8,12},{9,13},{10,... | collective-permute-start | bytes 786440 | tf_op jit(solution)/shard_map/ppermute | solution.py:108
  71.8 3.3 %collective-permute-start.11 = (bf16[128,1024]{1,0:T(8,128)(2,1)S(1)}, bf16[128,1024]{1,0:T(8,128)(2,1)S(1)}, u32[]{:S(2)}, u32[]{:S(2)}) collective-permute-start(bf16[128,1024]{1,0:T(8,128)(2,1)S(1)} %broadcast_select_fusion), channel_id=1, source_target_pairs={{0,1},{2,3},{4,5},{6,7},{9,8},{11,10},{13,12},{15,14},{16,17},{18,... | collective-permute-start | bytes 786440 | tf_op jit(solution)/shard_map/ppermute | solution.py:108
  73.1 2.0 %collective-permute-start.13 = (bf16[128,1024]{1,0:T(8,128)(2,1)S(1)}, bf16[128,1024]{1,0:T(8,128)(2,1)S(1)}, u32[]{:S(2)}, u32[]{:S(2)}) collective-permute-start(bf16[128,1024]{1,0:T(8,128)(2,1)S(1)} %add_convert_fusion.1), channel_id=1, source_target_pairs={{1,9},{3,11},{5,13},{7,15},{8,1},{10,3},{12,5},{14,7},{17,25},{19,... | collective-permute-start | bytes 786440 | tf_op jit(solution)/shard_map/ppermute | solution.py:108
  73.8 16.9 %collective-permute-start.12 = (bf16[128,1024]{1,0:T(8,128)(2,1)S(1)}, bf16[128,1024]{1,0:T(8,128)(2,1)S(1)}, u32[]{:S(2)}, u32[]{:S(2)}) collective-permute-start(bf16[128,1024]{1,0:T(8,128)(2,1)S(1)} %add_convert_fusion.3), channel_id=1, source_target_pairs={{1,8},{3,10},{5,12},{7,14},{8,0},{10,2},{12,4},{14,6},{17,24},{19,... | collective-permute-start | bytes 786440 | tf_op jit(solution)/shard_map/ppermute | solution.py:108
  91.7 3.6 %collective-permute-start.14 = (f32[2,128]{1,0:T(2,128)S(1)}, f32[2,128]{1,0:T(2,128)S(1)}, u32[]{:S(2)}, u32[]{:S(2)}) collective-permute-start(f32[2,128]{1,0:T(2,128)S(1)} %pad_maximum_fusion), channel_id=1, source_target_pairs={{0,2},{1,3},{2,0},{3,1},{4,6},{5,7},{6,4},{7,5},{8,10},{9,11},{10,... | collective-permute-start | bytes 3080 | tf_op jit(solution)/shard_map/ppermute | solution.py:108
  95.3 3.6 %collective-permute-start.15 = (f32[2,128]{1,0:T(2,128)S(1)}, f32[2,128]{1,0:T(2,128)S(1)}, u32[]{:S(2)}, u32[]{:S(2)}) collective-permute-start(f32[2,128]{1,0:T(2,128)S(1)} %fusion.2), channel_id=1, source_target_pairs={{0,4},{1,5},{2,6},{3,7},{4,0},{5,1},{6,2},{7,3},{8,12},{9,13},{10,... | collective-permute-start | bytes 3080 | tf_op jit(solution)/shard_map/ppermute | solution.py:108
  98.9 4.8 %collective-permute-start.16 = (f32[2,128]{1,0:T(2,128)S(1)}, f32[2,128]{1,0:T(2,128)S(1)}, u32[]{:S(2)}, u32[]{:S(2)}) collective-permute-start(f32[2,128]{1,0:T(2,128)S(1)} %fusion.3), channel_id=1, source_target_pairs={{0,8},{1,9},{2,10},{3,11},{4,12},{5,13},{6,14},{7,15},{8,0},{9,1},... | collective-permute-start | bytes 3080 | tf_op jit(solution)/shard_map/ppermute | solution.py:108

commit v11 on v10

--- a/solution.py
+++ b/solution.py
@@ -184,7 +184,7 @@
         input_output_aliases={} if alias is None else {n + alias: 0},
         compiler_params=pltpu.CompilerParams(vmem_limit_bytes=limit * MIB),
         cost_estimate=pl.CostEstimate(
-            flops=flops, bytes_accessed=0 if manual else loaded, transcendentals=0
+            flops=flops, bytes_accessed=loaded, transcendentals=0
         ),
     )(*sources, *ins)
 

time: 105 us -> 105 us (level)
  no operation moved by 1% of the time
where the time goes in v11:
time: 105 us; the launch traced here: 104 us
  Pallas kernels  42 us (40%)
  waiting for transfers between devices  34.4 us (33%)
  starting transfers between devices  24.9 us (24%)
  other arithmetic  1.43 us (1%)
    pallas_call x11, Pallas kernels, stage(): pl.pallas_call(body, out_shape=shapes, in_specs=[pl.BlockSpec(memory_spac...  40.2 us
    ppermute x17, waiting for transfers between devices, send(): lax.ppermute(array, ('tp', 'dp'), [(2 * st + sd, 2 * dt + dd) for (st, sd...  34.4 us
    ppermute x17, starting transfers between devices, send(): lax.ppermute(array, ('tp', 'dp'), [(2 * st + sd, 2 * dt + dd) for (st, sd...  24.9 us
  transfers between devices with their start and end apart: 17, of which 9 were waited for; matrix products, arithmetic and copies ran while one was open for 0% of the time, Pallas kernels for 31%

profile of v11, /device:TPU:0, one launch (start us, length us, event | category | flops | bytes accessed | tf_op | source)
XLA Modules:
  0.0 104.4 jit_solution(3518139382252754871)
XLA Ops:
  0.6 1.0 shard_map.123.refs_2_
  1.7 4.1 %collective-permute-start = (bf16[80,1024]{1,0:T(8,128)(2,1)S(1)}, bf16[80,1024]{1,0:T(8,128)(2,1)S(1)}, u32[]{:S(2)}, u32[]{:S(2)}) collective-permute-start(bf16[80,1024]{1,0:T(8,128)(2,1)S(1)} %shard_map.123.refs_2_), channel_id=1, source_target_pairs={{0,8},{2,10},{4,12},{6,14},{9,1},{11,3},{13,5},{15,7},{1,0},{3,2},... | collective-permute-start | bytes 491528 | tf_op jit(solution)/shard_map/ppermute | solution.py:108
  6.5 4.7 %shard_map.122 = (bf16[1024,3072]{1,0:T(8,128)(2,1)S(1)}, bf16[1024,3072]{1,0:T(8,128)(2,1)S(1)}) custom-call(bf16[4096,3072]{1,0:T(8,128)(2,1)} %refs_0_.11, bf16[4096,3072]{1,0:T(8,128)(2,1)} %refs_1_.7), custom_call_target="tpu_custom_call" | custom-call | bytes 12582912 | tf_op jit(solution)/shard_map/pallas_call | solution.py:178
  12.1 4.1 %collective-permute-start.3 = (bf16[144,1024]{1,0:T(8,128)(2,1)S(1)}, bf16[144,1024]{1,0:T(8,128)(2,1)S(1)}, u32[]{:S(2)}, u32[]{:S(2)}) collective-permute-start(bf16[144,1024]{1,0:T(8,128)(2,1)S(1)} %get-tuple-element.39.refs_4_), channel_id=1, source_target_pairs={{0,4},{1,5},{2,6},{3,7},{4,0},{5,1},{6,2},{7,3},{8,12},{9,13},{10,... | collective-permute-start | bytes 884744 | tf_op jit(solution)/shard_map/ppermute | solution.py:108
  16.2 1.5 %collective-permute-start.4 = (bf16[144,1024]{1,0:T(8,128)(2,1)S(1)}, bf16[144,1024]{1,0:T(8,128)(2,1)S(1)}, u32[]{:S(2)}, u32[]{:S(2)}) collective-permute-start(bf16[144,1024]{1,0:T(8,128)(2,1)S(1)} %get-tuple-element.39.refs_4_), channel_id=1, source_target_pairs={{0,2},{1,3},{2,0},{3,1},{4,6},{5,7},{6,4},{7,5},{8,10},{9,11},{10,... | collective-permute-start | bytes 884744 | tf_op jit(solution)/shard_map/ppermute | solution.py:108
  17.8 8.5 %shard_map.125 = (f32[2,144,3072]{2,1,0:T(8,128)S(1)}, f32[256,128]{1,0:T(8,128)S(1)}, bf16[1024,3072]{1,0:T(8,128)(2,1)S(1)}, bf16[1024,3072]{1,0:T(8,128)(2,1)...) custom-call(bf16[4096,3072]{1,0:T(8,128)(2,1)} %refs_0_.11, bf16[4096,3072]{1,0:T(8,128)(2,1)} %refs_1_.7, ...), custom_call_target="tpu_custom_call" | custom-call | flops 1811939328 | bytes 25165824 | tf_op jit(solution)/shard_map/pallas_call | solution.py:178
  26.3 4.7 %shard_map.126 = (f32[2,144,3072]{2,1,0:T(8,128)S(1)}, f32[256,128]{1,0:T(8,128)S(1)}, bf16[1024,3072]{1,0:T(8,128)(2,1)S(1)}, bf16[1024,3072]{1,0:T(8,128)(2,1)S(1)}) custom-call(bf16[4096,3072]{1,0:T(8,128)(2,1)} %refs_0_.11, bf16[4096,3072]{1,0:T(8,128)(2,1)} %refs_1_.7, ...), custom_call_target="tpu_custom_call", output_to_operand_aliasing={{0}: (5, {})} | custom-call | flops 1811939328 | bytes 12582912 | tf_op jit(solution)/shard_map/pallas_call | solution.py:178
  31.5 3.5 %shard_map.127 = (f32[2,144,3072]{2,1,0:T(8,128)S(1)}, f32[256,128]{1,0:T(8,128)S(1)}, bf16[3072,1024]{1,0:T(8,128)(2,1)S(1)}) custom-call(bf16[3072,4096]{1,0:T(8,128)(2,1)} %refs_0_.15, bf16[144,1024]{1,0:T(8,128)(2,1)S(1)} %collective-permute-done.4.refs_1_, bf16[1024,3072]{1,0:T(8,128)(2,1)S(1)} %get-tuple-element.47.refs_2_, ...), custom_call_target="tpu_custom_call", output_to_operand_aliasing={{0}: (4, {})} | custom-call | flops 1811939328 | bytes 6291456 | tf_op jit(solution)/shard_map/pallas_call | solution.py:178
  35.0 2.9 %shard_map.128 = (f32[2,144,1536]{2,1,0:T(8,128)S(1)}, bf16[2,144,1536]{2,1,0:T(8,128)(2,1)S(1)}, f32[256,128]{1,0:T(8,128)S(1)}, bf16[3072,1024]{1,0:T(8,128)(2,1)S(1)}) custom-call(bf16[3072,4096]{1,0:T(8,128)(2,1)} %refs_0_.15, bf16[144,1024]{1,0:T(8,128)(2,1)S(1)} %collective-permute-done.2.refs_1_, bf16[1024,3072]{1,0:T(8,128)(2,1)S(1)} %get-tuple-element.45.refs_2_, ...), custom_call_target="tpu_custom_call" | custom-call | flops 905969664 | bytes 6291456 | tf_op jit(solution)/shard_map/pallas_call | solution.py:178
  38.0 2.9 %shard_map.130 = (f32[2,144,1536]{2,1,0:T(8,128)S(1)}, bf16[2,144,1536]{2,1,0:T(8,128)(2,1)S(1)}, bf16[3072,1024]{1,0:T(8,128)(2,1)S(1)}) custom-call(bf16[3072,4096]{1,0:T(8,128)(2,1)} %refs_0_.15, bf16[144,1024]{1,0:T(8,128)(2,1)S(1)} %collective-permute-done.2.refs_1_, bf16[1024,3072]{1,0:T(8,128)(2,1)S(1)} %get-tuple-element.45.refs_2_, ...), custom_call_target="tpu_custom_call" | custom-call | flops 905969664 | bytes 6291456 | tf_op jit(solution)/shard_map/pallas_call | solution.py:178
  41.4 1.2 %shard_map.129 = (bf16[256,1536]{1,0:T(8,128)(2,1)S(1)}, f32[256,128]{1,0:T(8,128)S(1)}) custom-call(f32[2,144,1536]{2,1,0:T(8,128)S(1)} %get-tuple-element.53.refs_0_, bf16[2,144,1536]{2,1,0:T(8,128)(2,1)S(1)} %collective-permute-done.5.refs_1_, bf16[256,144]{1,0:T(8,128)(2,1)S(1)} %get-tuple-element.40.refs_7_.refs_6_.refs_5_.refs_2_, ...), custom_call_target="tpu_custom_call" | custom-call | flops 226492416 | tf_op jit(solution)/shard_map/pallas_call | solution.py:178
  42.6 0.9 collective-permute-done.6.refs_1_
  43.5 1.1 %shard_map.131.refs_2_.refs_1_ = bf16[256,1536]{1,0:T(8,128)(2,1)S(1)} custom-call(f32[2,144,1536]{2,1,0:T(8,128)S(1)} %get-tuple-element.57.refs_0_, bf16[2,144,1536]{2,1,0:T(8,128)(2,1)S(1)} %collective-permute-done.6.refs_1_, bf16[256,144]{1,0:T(8,128)(2,1)S(1)} %get-tuple-element.40.refs_7_.refs_6_.refs_5_.refs_2_, f32[256,128]{1,0:T(8,128)S(1)} %get-tuple-element.59.refs_3_), custom_call_target="tpu_custom_call" | custom-call | flops 226492416 | tf_op jit(solution)/shard_map/pallas_call | solution.py:178
  44.5 2.6 %shard_map.133 = (bf16[128,2048]{1,0:T(8,128)(2,1)S(1)}, bf16[128,1024]{1,0:T(8,128)(2,1)S(1)}) custom-call(bf16[256,1536]{1,0:T(8,128)(2,1)S(1)} %get-tuple-element.56.refs_1_.refs_0_, bf16[256,1536]{1,0:T(8,128)(2,1)S(1)} %shard_map.131.refs_2_.refs_1_, bf16[3072,1024]{1,0:T(8,128)(2,1)S(1)} %get-tuple-element.63.refs_2_, ...), custom_call_target="tpu_custom_call" | custom-call | flops 150994944 | tf_op jit(solution)/shard_map/pallas_call | solution.py:178
  47.1 1.0 shard_map.134
  48.1 1.7 %collective-permute-start.9 = (bf16[128,2048]{1,0:T(8,128)(2,1)S(1)}, bf16[128,2048]{1,0:T(8,128)(2,1)S(1)}, u32[]{:S(2)}, u32[]{:S(2)}) collective-permute-start(bf16[128,2048]{1,0:T(8,128)(2,1)S(1)} %shard_map.134), channel_id=1, source_target_pairs={{0,4},{1,5},{2,6},{3,7},{4,0},{5,1},{6,2},{7,3},{8,12},{9,13},{10,... | collective-permute-start | bytes 1572872 | tf_op jit(solution)/shard_map/ppermute | solution.py:108
  49.8 1.4 %collective-permute-start.7 = (bf16[128,2048]{1,0:T(8,128)(2,1)S(1)}, bf16[128,2048]{1,0:T(8,128)(2,1)S(1)}, u32[]{:S(2)}, u32[]{:S(2)}) collective-permute-start(bf16[128,2048]{1,0:T(8,128)(2,1)S(1)} %get-tuple-element.64), channel_id=1, source_target_pairs={{0,2},{1,3},{2,0},{3,1},{4,6},{5,7},{6,4},{7,5},{8,10},{9,11},{10,... | collective-permute-start | bytes 1572872 | tf_op jit(solution)/shard_map/ppermute | solution.py:108
  51.2 7.2 %shard_map.132 = (bf16[128,1024]{1,0:T(8,128)(2,1)S(1)}, bf16[128,1024]{1,0:T(8,128)(2,1)S(1)}, bf16[128,1024]{1,0:T(8,128)(2,1)S(1)}, bf16[128,1024]{1,0:T(8,128)(2,1)S(1)}, bf16[3072,1024]{1,0:T(8,128)(2,1)}) custom-call(bf16[3072,4096]{1,0:T(8,128)(2,1)} %refs_0_.15, bf16[256,1536]{1,0:T(8,128)(2,1)S(1)} %get-tuple-element.56.refs_1_.refs_0_, ...), custom_call_target="tpu_custom_call" | custom-call | flops 201326592 | bytes 6291456 | tf_op jit(solution)/shard_map/pallas_call | solution.py:178
  58.4 4.0 %collective-permute-done.9 = bf16[128,2048]{1,0:T(8,128)(2,1)S(1)} collective-permute-done((bf16[128,2048]{1,0:T(8,128)(2,1)S(1)}, bf16[128,2048]{1,0:T(8,128)(2,1)S(1)}, u32[]{:S(2)}, u32[]{:S(2)}) %collective-permute-start.9) | collective-permute-done | bytes 524320 | tf_op jit(solution)/shard_map/ppermute | solution.py:108
  62.5 1.5 %collective-permute-start.10 = (bf16[128,1024]{1,0:T(8,128)(2,1)S(1)}, bf16[128,1024]{1,0:T(8,128)(2,1)S(1)}, u32[]{:S(2)}, u32[]{:S(2)}) collective-permute-start(bf16[128,1024]{1,0:T(8,128)(2,1)S(1)} %add_convert_fusion.2), channel_id=1, source_target_pairs={{0,2},{1,3},{2,0},{3,1},{4,6},{5,7},{6,4},{7,5},{8,10},{9,11},{10,... | collective-permute-start | bytes 786440 | tf_op jit(solution)/shard_map/ppermute | solution.py:108
  64.1 1.6 %collective-permute-start.8 = (bf16[128,1024]{1,0:T(8,128)(2,1)S(1)}, bf16[128,1024]{1,0:T(8,128)(2,1)S(1)}, u32[]{:S(2)}, u32[]{:S(2)}) collective-permute-start(bf16[128,1024]{1,0:T(8,128)(2,1)S(1)} %add_convert_fusion.4), channel_id=1, source_target_pairs={{0,4},{1,5},{2,6},{3,7},{4,0},{5,1},{6,2},{7,3},{8,12},{9,13},{10,... | collective-permute-start | bytes 786440 | tf_op jit(solution)/shard_map/ppermute | solution.py:108
  65.6 4.7 %collective-permute-done.10 = bf16[128,1024]{1,0:T(8,128)(2,1)S(1)} collective-permute-done((bf16[128,1024]{1,0:T(8,128)(2,1)S(1)}, bf16[128,1024]{1,0:T(8,128)(2,1)S(1)}, u32[]{:S(2)}, u32[]{:S(2)}) %collective-permute-start.10) | collective-permute-done | bytes 262176 | tf_op jit(solution)/shard_map/ppermute | solution.py:108
  70.4 1.2 %collective-permute-done.8 = bf16[128,1024]{1,0:T(8,128)(2,1)S(1)} collective-permute-done((bf16[128,1024]{1,0:T(8,128)(2,1)S(1)}, bf16[128,1024]{1,0:T(8,128)(2,1)S(1)}, u32[]{:S(2)}, u32[]{:S(2)}) %collective-permute-start.8) | collective-permute-done | bytes 262176 | tf_op jit(solution)/shard_map/ppermute | solution.py:108
  71.8 1.3 %collective-permute-start.11 = (bf16[128,1024]{1,0:T(8,128)(2,1)S(1)}, bf16[128,1024]{1,0:T(8,128)(2,1)S(1)}, u32[]{:S(2)}, u32[]{:S(2)}) collective-permute-start(bf16[128,1024]{1,0:T(8,128)(2,1)S(1)} %broadcast_select_fusion), channel_id=1, source_target_pairs={{0,1},{2,3},{4,5},{6,7},{9,8},{11,10},{13,12},{15,14},{16,17},{18,... | collective-permute-start | bytes 786440 | tf_op jit(solution)/shard_map/ppermute | solution.py:108
  73.8 1.3 %collective-permute-start.12 = (bf16[128,1024]{1,0:T(8,128)(2,1)S(1)}, bf16[128,1024]{1,0:T(8,128)(2,1)S(1)}, u32[]{:S(2)}, u32[]{:S(2)}) collective-permute-start(bf16[128,1024]{1,0:T(8,128)(2,1)S(1)} %add_convert_fusion.3), channel_id=1, source_target_pairs={{1,8},{3,10},{5,12},{7,14},{8,0},{10,2},{12,4},{14,6},{17,24},{19,... | collective-permute-start | bytes 786440 | tf_op jit(solution)/shard_map/ppermute | solution.py:108
  75.1 15.5 %collective-permute-done.12 = bf16[128,1024]{1,0:T(8,128)(2,1)S(1)} collective-permute-done((bf16[128,1024]{1,0:T(8,128)(2,1)S(1)}, bf16[128,1024]{1,0:T(8,128)(2,1)S(1)}, u32[]{:S(2)}, u32[]{:S(2)}) %collective-permute-start.12) | collective-permute-done | bytes 262176 | tf_op jit(solution)/shard_map/ppermute | solution.py:108
  90.7 1.0 fusion
  91.7 1.1 %collective-permute-start.14 = (f32[2,128]{1,0:T(2,128)S(1)}, f32[2,128]{1,0:T(2,128)S(1)}, u32[]{:S(2)}, u32[]{:S(2)}) collective-permute-start(f32[2,128]{1,0:T(2,128)S(1)} %pad_maximum_fusion), channel_id=1, source_target_pairs={{0,2},{1,3},{2,0},{3,1},{4,6},{5,7},{6,4},{7,5},{8,10},{9,11},{10,... | collective-permute-start | bytes 3080 | tf_op jit(solution)/shard_map/ppermute | solution.py:108
  92.8 2.5 %collective-permute-done.14 = f32[2,128]{1,0:T(2,128)S(1)} collective-permute-done((f32[2,128]{1,0:T(2,128)S(1)}, f32[2,128]{1,0:T(2,128)S(1)}, u32[]{:S(2)}, u32[]{:S(2)}) %collective-permute-start.14) | collective-permute-done | bytes 1056 | tf_op jit(solution)/shard_map/ppermute | solution.py:108
  95.4 3.6 %collective-permute-done.15 = f32[2,128]{1,0:T(2,128)S(1)} collective-permute-done((f32[2,128]{1,0:T(2,128)S(1)}, f32[2,128]{1,0:T(2,128)S(1)}, u32[]{:S(2)}, u32[]{:S(2)}) %collective-permute-start.15) | collective-permute-done | bytes 1056 | tf_op jit(solution)/shard_map/ppermute | solution.py:108
  98.9 3.2 %collective-permute-start.16 = (f32[2,128]{1,0:T(2,128)S(1)}, f32[2,128]{1,0:T(2,128)S(1)}, u32[]{:S(2)}, u32[]{:S(2)}) collective-permute-start(f32[2,128]{1,0:T(2,128)S(1)} %fusion.3), channel_id=1, source_target_pairs={{0,8},{1,9},{2,10},{3,11},{4,12},{5,13},{6,14},{7,15},{8,0},{9,1},... | collective-permute-start | bytes 3080 | tf_op jit(solution)/shard_map/ppermute | solution.py:108
  102.2 1.5 %collective-permute-done.16 = f32[2,128]{1,0:T(2,128)S(1)} collective-permute-done((f32[2,128]{1,0:T(2,128)S(1)}, f32[2,128]{1,0:T(2,128)S(1)}, u32[]{:S(2)}, u32[]{:S(2)}) %collective-permute-start.16) | collective-permute-done | bytes 1056 | tf_op jit(solution)/shard_map/ppermute | solution.py:108
  (39 shorter events, 4.5 us)
Async XLA Ops:
  1.6 9.6 %copy-start = (bf16[128,1024]{1,0:T(8,128)(2,1)S(1)}, bf16[128,1024]{1,0:T(8,128)(2,1)}, u32[]{:S(2)}) copy-start(bf16[128,1024]{1,0:T(8,128)(2,1)} %refs_5_.1) | copy-start | bytes 786436
  1.6 9.6 %copy-start.1 = (bf16[2,1024]{1,0:T(2,128)(2,1)S(1)}, bf16[2,1024]{1,0:T(2,128)(2,1)}, u32[]{:S(2)}) copy-start(bf16[2,1024]{1,0:T(2,128)(2,1)} %refs_6_.1) | copy-start | bytes 12292
  1.7 9.6 %copy-start.2 = (f32[1024]{0:T(1024)S(1)}, f32[1024]{0:T(1024)}, u32[]{:S(2)}) copy-start(f32[1024]{0:T(1024)} %refs_9_.1) | copy-start | bytes 12292
  1.7 9.6 %copy-start.3 = (f32[1024]{0:T(1024)S(1)}, f32[1024]{0:T(1024)}, u32[]{:S(2)}) copy-start(f32[1024]{0:T(1024)} %refs_10_.1) | copy-start | bytes 12292
  1.7 9.6 %copy-start.4 = (f32[128]{0:T(128)S(1)}, f32[128]{0:T(128)}, u32[]{:S(2)}) copy-start(f32[128]{0:T(128)} %refs_7_.1) | copy-start | bytes 1540
  1.7 9.6 %copy-start.5 = (f32[128]{0:T(128)S(1)}, f32[128]{0:T(128)}, u32[]{:S(2)}) copy-start(f32[128]{0:T(128)} %refs_8_.1) | copy-start | bytes 1540
  1.7 9.5 %collective-permute-start = (bf16[80,1024]{1,0:T(8,128)(2,1)S(1)}, bf16[80,1024]{1,0:T(8,128)(2,1)S(1)}, u32[]{:S(2)}, u32[]{:S(2)}) collective-permute-start(bf16[80,1024]{1,0:T(8,128)(2,1)S(1)} %shard_map.123.refs_2_), channel_id=1, source_target_pairs={{0,8},{2,10},{4,12},{6,14},{9,1},{11,3},{13,5},{15,7},{1,0},{3,2},... | collective-permute-start | bytes 491528 | tf_op jit(solution)/shard_map/ppermute | solution.py:108
  5.8 5.4 %collective-permute-start.1 = (bf16[80,1024]{1,0:T(8,128)(2,1)S(1)}, bf16[80,1024]{1,0:T(8,128)(2,1)S(1)}, u32[]{:S(2)}, u32[]{:S(2)}) collective-permute-start(bf16[80,1024]{1,0:T(8,128)(2,1)S(1)} %shard_map.123.refs_2_), channel_id=1, source_target_pairs={{1,8},{3,10},{5,12},{7,14},{8,1},{10,3},{12,5},{14,7},{17,24},{19,... | collective-permute-start | bytes 491528 | tf_op jit(solution)/shard_map/ppermute | solution.py:108
  12.1 14.2 %collective-permute-start.3 = (bf16[144,1024]{1,0:T(8,128)(2,1)S(1)}, bf16[144,1024]{1,0:T(8,128)(2,1)S(1)}, u32[]{:S(2)}, u32[]{:S(2)}) collective-permute-start(bf16[144,1024]{1,0:T(8,128)(2,1)S(1)} %get-tuple-element.39.refs_4_), channel_id=1, source_target_pairs={{0,4},{1,5},{2,6},{3,7},{4,0},{5,1},{6,2},{7,3},{8,12},{9,13},{10,... | collective-permute-start | bytes 884744 | tf_op jit(solution)/shard_map/ppermute | solution.py:108
  16.2 15.2 %collective-permute-start.4 = (bf16[144,1024]{1,0:T(8,128)(2,1)S(1)}, bf16[144,1024]{1,0:T(8,128)(2,1)S(1)}, u32[]{:S(2)}, u32[]{:S(2)}) collective-permute-start(bf16[144,1024]{1,0:T(8,128)(2,1)S(1)} %get-tuple-element.39.refs_4_), channel_id=1, source_target_pairs={{0,2},{1,3},{2,0},{3,1},{4,6},{5,7},{6,4},{7,5},{8,10},{9,11},{10,... | collective-permute-start | bytes 884744 | tf_op jit(solution)/shard_map/ppermute | solution.py:108
  17.7 17.2 %collective-permute-start.2 = (bf16[144,1024]{1,0:T(8,128)(2,1)S(1)}, bf16[144,1024]{1,0:T(8,128)(2,1)S(1)}, u32[]{:S(2)}, u32[]{:S(2)}) collective-permute-start(bf16[144,1024]{1,0:T(8,128)(2,1)S(1)} %get-tuple-element.39.refs_4_), channel_id=1, source_target_pairs={{0,6},{1,7},{2,4},{3,5},{4,2},{5,3},{6,0},{7,1},{8,14},{9,15},{10,... | collective-permute-start | bytes 884744 | tf_op jit(solution)/shard_map/ppermute | solution.py:108
  37.9 3.5 %collective-permute-start.5 = (bf16[2,144,1536]{2,1,0:T(8,128)(2,1)S(1)}, bf16[2,144,1536]{2,1,0:T(8,128)(2,1)S(1)}, u32[]{:S(2)}, u32[]{:S(2)}) collective-permute-start(bf16[2,144,1536]{2,1,0:T(8,128)(2,1)S(1)} %get-tuple-element.54), channel_id=1, source_target_pairs={{0,1},{1,0},{2,3},{3,2},{4,5},{5,4},{6,7},{7,6},{8,9},{9,8},{10,11... | collective-permute-start | bytes 2654216 | tf_op jit(solution)/shard_map/ppermute | solution.py:108
  40.9 2.6 %collective-permute-start.6 = (bf16[2,144,1536]{2,1,0:T(8,128)(2,1)S(1)}, bf16[2,144,1536]{2,1,0:T(8,128)(2,1)S(1)}, u32[]{:S(2)}, u32[]{:S(2)}) collective-permute-start(bf16[2,144,1536]{2,1,0:T(8,128)(2,1)S(1)} %get-tuple-element.58), channel_id=1, source_target_pairs={{0,1},{1,0},{2,3},{3,2},{4,5},{5,4},{6,7},{7,6},{8,9},{9,8},{10,11... | collective-permute-start | bytes 2654216 | tf_op jit(solution)/shard_map/ppermute | solution.py:108
  48.1 14.3 %collective-permute-start.9 = (bf16[128,2048]{1,0:T(8,128)(2,1)S(1)}, bf16[128,2048]{1,0:T(8,128)(2,1)S(1)}, u32[]{:S(2)}, u32[]{:S(2)}) collective-permute-start(bf16[128,2048]{1,0:T(8,128)(2,1)S(1)} %shard_map.134), channel_id=1, source_target_pairs={{0,4},{1,5},{2,6},{3,7},{4,0},{5,1},{6,2},{7,3},{8,12},{9,13},{10,... | collective-permute-start | bytes 1572872 | tf_op jit(solution)/shard_map/ppermute | solution.py:108
  49.8 14.2 %collective-permute-start.7 = (bf16[128,2048]{1,0:T(8,128)(2,1)S(1)}, bf16[128,2048]{1,0:T(8,128)(2,1)S(1)}, u32[]{:S(2)}, u32[]{:S(2)}) collective-permute-start(bf16[128,2048]{1,0:T(8,128)(2,1)S(1)} %get-tuple-element.64), channel_id=1, source_target_pairs={{0,2},{1,3},{2,0},{3,1},{4,6},{5,7},{6,4},{7,5},{8,10},{9,11},{10,... | collective-permute-start | bytes 1572872 | tf_op jit(solution)/shard_map/ppermute | solution.py:108
  62.5 7.8 %collective-permute-start.10 = (bf16[128,1024]{1,0:T(8,128)(2,1)S(1)}, bf16[128,1024]{1,0:T(8,128)(2,1)S(1)}, u32[]{:S(2)}, u32[]{:S(2)}) collective-permute-start(bf16[128,1024]{1,0:T(8,128)(2,1)S(1)} %add_convert_fusion.2), channel_id=1, source_target_pairs={{0,2},{1,3},{2,0},{3,1},{4,6},{5,7},{6,4},{7,5},{8,10},{9,11},{10,... | collective-permute-start | bytes 786440 | tf_op jit(solution)/shard_map/ppermute | solution.py:108
  64.1 7.5 %collective-permute-start.8 = (bf16[128,1024]{1,0:T(8,128)(2,1)S(1)}, bf16[128,1024]{1,0:T(8,128)(2,1)S(1)}, u32[]{:S(2)}, u32[]{:S(2)}) collective-permute-start(bf16[128,1024]{1,0:T(8,128)(2,1)S(1)} %add_convert_fusion.4), channel_id=1, source_target_pairs={{0,4},{1,5},{2,6},{3,7},{4,0},{5,1},{6,2},{7,3},{8,12},{9,13},{10,... | collective-permute-start | bytes 786440 | tf_op jit(solution)/shard_map/ppermute | solution.py:108
  71.8 3.3 %collective-permute-start.11 = (bf16[128,1024]{1,0:T(8,128)(2,1)S(1)}, bf16[128,1024]{1,0:T(8,128)(2,1)S(1)}, u32[]{:S(2)}, u32[]{:S(2)}) collective-permute-start(bf16[128,1024]{1,0:T(8,128)(2,1)S(1)} %broadcast_select_fusion), channel_id=1, source_target_pairs={{0,1},{2,3},{4,5},{6,7},{9,8},{11,10},{13,12},{15,14},{16,17},{18,... | collective-permute-start | bytes 786440 | tf_op jit(solution)/shard_map/ppermute | solution.py:108
  73.1 2.0 %collective-permute-start.13 = (bf16[128,1024]{1,0:T(8,128)(2,1)S(1)}, bf16[128,1024]{1,0:T(8,128)(2,1)S(1)}, u32[]{:S(2)}, u32[]{:S(2)}) collective-permute-start(bf16[128,1024]{1,0:T(8,128)(2,1)S(1)} %add_convert_fusion.1), channel_id=1, source_target_pairs={{1,9},{3,11},{5,13},{7,15},{8,1},{10,3},{12,5},{14,7},{17,25},{19,... | collective-permute-start | bytes 786440 | tf_op jit(solution)/shard_map/ppermute | solution.py:108
  73.8 16.9 %collective-permute-start.12 = (bf16[128,1024]{1,0:T(8,128)(2,1)S(1)}, bf16[128,1024]{1,0:T(8,128)(2,1)S(1)}, u32[]{:S(2)}, u32[]{:S(2)}) collective-permute-start(bf16[128,1024]{1,0:T(8,128)(2,1)S(1)} %add_convert_fusion.3), channel_id=1, source_target_pairs={{1,8},{3,10},{5,12},{7,14},{8,0},{10,2},{12,4},{14,6},{17,24},{19,... | collective-permute-start | bytes 786440 | tf_op jit(solution)/shard_map/ppermute | solution.py:108
  91.7 3.6 %collective-permute-start.14 = (f32[2,128]{1,0:T(2,128)S(1)}, f32[2,128]{1,0:T(2,128)S(1)}, u32[]{:S(2)}, u32[]{:S(2)}) collective-permute-start(f32[2,128]{1,0:T(2,128)S(1)} %pad_maximum_fusion), channel_id=1, source_target_pairs={{0,2},{1,3},{2,0},{3,1},{4,6},{5,7},{6,4},{7,5},{8,10},{9,11},{10,... | collective-permute-start | bytes 3080 | tf_op jit(solution)/shard_map/ppermute | solution.py:108
  95.3 3.6 %collective-permute-start.15 = (f32[2,128]{1,0:T(2,128)S(1)}, f32[2,128]{1,0:T(2,128)S(1)}, u32[]{:S(2)}, u32[]{:S(2)}) collective-permute-start(f32[2,128]{1,0:T(2,128)S(1)} %fusion.2), channel_id=1, source_target_pairs={{0,4},{1,5},{2,6},{3,7},{4,0},{5,1},{6,2},{7,3},{8,12},{9,13},{10,... | collective-permute-start | bytes 3080 | tf_op jit(solution)/shard_map/ppermute | solution.py:108
  98.9 4.8 %collective-permute-start.16 = (f32[2,128]{1,0:T(2,128)S(1)}, f32[2,128]{1,0:T(2,128)S(1)}, u32[]{:S(2)}, u32[]{:S(2)}) collective-permute-start(f32[2,128]{1,0:T(2,128)S(1)} %fusion.3), channel_id=1, source_target_pairs={{0,8},{1,9},{2,10},{3,11},{4,12},{5,13},{6,14},{7,15},{8,0},{9,1},... | collective-permute-start | bytes 3080 | tf_op jit(solution)/shard_map/ppermute | solution.py:108
